TPU v7x, 32 devices: a whole 2x2x4 slice. The times are simulated.
32 devices in a mesh: copies: 2 (over y), nodes: 4 (over z), samples: 4 (over x, core).
Axes of the slice: x: 2, y: 2, z: 4, core: 2. Of those that a mesh axis runs over, the one named last changes fastest.
Arguments:
- vector: float32 [128, 16384], P('samples', ('copies', 'nodes')), parts along dimension 1, may hold values from -1500 to 1500
- operating: float32 [128, 16384], P('samples', ('copies', 'nodes')), parts along dimension 1, may hold values from -3.5 to 3.5
- table: float32 [16], replicated, may hold values from 0.2 to 2
- linear: float32 [8192], P('nodes'), may hold values from 0.5 to 2
- capacity: float32 [8192], P('nodes'), may hold values from 0.5 to 4
- weights: float32 [8, 8192], P(None, 'nodes'), may hold values from -2 to 2
- degree: int32 [8192], P('nodes'), may hold values from 1 to 8
- neighbours: int32 [8, 8192], P(None, 'nodes'), may hold values from 0 to 2111, as said below
- boundary: int32 [1024], P('nodes'), may hold values from 0 to 2047, as said below
- send_list: int32 [256], P('nodes'), may hold values from 0 to 255, as said below
Outputs:
- basis_two: float32 [128, 16384], P('samples', ('copies', 'nodes')), parts along dimension 1
- next_residue: float32 [128, 16384], P('samples', ('copies', 'nodes')), parts along dimension 1
There are 2 independent parts, one for each index of `copies`. A program takes and returns all parts, laid end to end along the dimension named above; an argument that names none is the same for every part. Nothing has to cross between parts.
Inputs may be any that keep to these rules, and one draw needn't show every extreme that they name: `neighbours`: columns of node part r are nodes r * 2048 onward. An entry e below 2048 names local node e of the same part; otherwise e - 2048 = q * 16 + c names the c-th cut row that part q sends to part r, with q different from r and c below that pair's count of cut rows, a count of 1 to 16 that is 16 for some pair in every draw. Every cut row below its pair's count is named by slot 0 of some node. `boundary`: entries q * 256 to q * 256 + 255 are 256 different local node numbers of node part q. `send_list`: entry q * 4 * 16 + r * 16 + c is the position, in part q's boundary list, of the node that part q sends to part r as its c-th cut row.
All inputs are finite; a program needn't handle non-finite values.
Results may differ from a plain program's by a relative error of at most 0.0003.
Values sent between devices are 32-bit elements; how exact they have to be, the bound alone decides.
No kernel may reach another device: no remote copies, remote signals or barrier semaphores. Data moves between devices by JAX's collectives and lax.ppermute only.
A program may use at most 64 MiB of HBM per device.

v0:
```python
import math

import jax
import jax.numpy as jnp
from jax import lax
from jax.sharding import PartitionSpec as P

CAP = 16


EPSILON = 1e-06


def spectral_tables(length):
    indices = jnp.arange(length, dtype=jnp.int32)
    frequency = jnp.where(indices == 1, length // 2, indices // 2)
    angles = (indices[:, None] * frequency[None, :] % length).astype(jnp.float32) * (
        2.0 * math.pi / length
    )
    cosine_column = (indices % 2 == 0) | (indices == 1)
    synthesis = jnp.where(cosine_column[None, :], jnp.cos(angles), jnp.sin(angles))
    factor = jnp.where(indices < 2, 1.0 / length, 2.0 / length).astype(jnp.float32)
    analysis = jnp.transpose(synthesis) * factor[:, None]
    return (synthesis, analysis)


def conductance(operating, table):
    points = table.shape[0]
    spacing = 8.0 / (points - 1)
    summed = jnp.zeros_like(operating)
    for knot_index in range(points):
        centre = -4.0 + spacing * knot_index
        summed = summed + table[knot_index] * jnp.maximum(
            0.0, 1.0 - jnp.abs(operating - centre) / spacing
        )
    return summed


def derivative(field_in, first_pair, half_order):
    rows_total = field_in.shape[0]
    paired = field_in.reshape(rows_total // 2, 2, field_in.shape[1])
    scaling = (
        (first_pair + jnp.arange(rows_total // 2, dtype=jnp.int32)).astype(jnp.float32) / half_order
    )[:, None]
    turned = jnp.stack([scaling * paired[:, 1], -scaling * paired[:, 0]], axis=1)
    return turned.reshape(field_in.shape)


def matmul_exact(first_array, second_array):
    return jnp.dot(
        first_array,
        second_array,
        precision=lax.Precision.HIGHEST,
        preferred_element_type=jnp.float32,
    )


def shards(
    vector, operating, table, linear, capacity, weights, degree, neighbours, boundary, send_list
):
    rows_here = vector.shape[0]
    nodes_here = vector.shape[1]
    length = rows_here * lax.axis_size("samples")
    node_groups = lax.axis_size("nodes")
    node_part = lax.axis_index("nodes")
    sample_part = lax.axis_index("samples")
    entries = float(length * nodes_here * node_groups)
    synthesis, analysis = spectral_tables(length)
    first_pair = sample_part * (rows_here // 2)
    half_order = length // 2
    conductances = conductance(operating, table)
    slot_count = weights.shape[0]
    masked = jnp.where(
        jnp.arange(slot_count, dtype=jnp.int32)[:, None] < degree[None, :], weights, 0.0
    )
    outgoing_index = boundary[send_list]
    remote = jnp.maximum(neighbours - nodes_here, 0)
    gathered_index = jnp.where(
        neighbours < nodes_here,
        neighbours,
        nodes_here + remote // CAP * (node_groups * CAP) + node_part * CAP + remote % CAP,
    )

    def couple(current):
        outgoing = current[:, outgoing_index]
        arrived = lax.all_gather(outgoing, "nodes", axis=1, tiled=True)
        extended = jnp.concatenate([current, arrived], axis=1)
        picked = jnp.take(extended, gathered_index, axis=1)
        return jnp.sum(picked * masked[None, :, :], axis=1)

    def apply_matvec(field_in):
        columns = lax.all_to_all(field_in, "samples", split_axis=1, concat_axis=0, tiled=True)
        wave_cols = matmul_exact(synthesis, columns)
        waveform = lax.all_to_all(wave_cols, "samples", split_axis=0, concat_axis=1, tiled=True)
        current = conductances * waveform
        node_load = linear[None, :] * waveform + current + couple(current)
        load_cols = lax.all_to_all(node_load, "samples", split_axis=1, concat_axis=0, tiled=True)
        spec_cols = matmul_exact(analysis, load_cols)
        spectrum = lax.all_to_all(spec_cols, "samples", split_axis=0, concat_axis=1, tiled=True)
        return spectrum + capacity[None, :] * derivative(field_in, first_pair, half_order)

    squares_total = lax.psum(jnp.sum(vector * vector), ("nodes", "samples"))
    scale_norm = jnp.sqrt(squares_total / entries + EPSILON)
    basis_one = vector / scale_norm
    image_one = apply_matvec(basis_one)
    first_coeff = lax.psum(jnp.sum(basis_one * image_one), ("nodes", "samples")) / entries
    residue = image_one - first_coeff * basis_one
    residue_total = lax.psum(jnp.sum(residue * residue), ("nodes", "samples"))
    second_norm = jnp.sqrt(residue_total / entries + EPSILON)
    basis_two = residue / second_norm
    image_two = apply_matvec(basis_two)
    along_one, along_two = lax.psum(
        (jnp.sum(basis_one * image_two), jnp.sum(basis_two * image_two)), ("nodes", "samples")
    )
    next_residue = image_two - along_one / entries * basis_one - along_two / entries * basis_two
    return (basis_two, next_residue)


def solution(mesh):
    return jax.shard_map(
        shards,
        mesh=mesh,
        in_specs=(
            P("samples", ("copies", "nodes")),
            P("samples", ("copies", "nodes")),
            P(),
            P("nodes"),
            P("nodes"),
            P(None, "nodes"),
            P("nodes"),
            P(None, "nodes"),
            P("nodes"),
            P("nodes"),
        ),
        out_specs=(P("samples", ("copies", "nodes")), P("samples", ("copies", "nodes"))),
        check_vma=False,
    )
```

profile of v0, /device:TPU:0, one launch (start us, length us, event | category | flops | bytes accessed | tf_op | source)
XLA Modules:
  0.0 382.1 jit_solution(17199578665333704693)
XLA Ops:
  0.6 1.6 multiply_reduce_fusion.4
  2.3 35.5 %psum.35 = f32[]{:T(128)} all-reduce(f32[]{:T(128)} %multiply_reduce_fusion.4), channel_id=1, replica_groups=mesh['copies'=2,'nodes'=4,'samples'=4] {'nodes','samples'}, use_global_device_ids=true, to_apply=%region_1.2 | all-reduce | flops 1 | bytes 8 | tf_op jit(solution)/shard_map/psum | solution.py:102
  38.5 1.0 broadcast_divide_fusion.1
  39.5 0.7 copy.214
  40.2 3.4 all-to-all-start
  43.8 0.7 compare_select_fusion.3
  44.4 0.8 gather_fusion
  45.2 0.9 compare_and_fusion
  46.2 0.9 fusion.24
  47.4 2.2 all-to-all-done
  49.6 1.4 fusion.26
  51.0 3.4 all-to-all-start.1
  54.4 2.0 fusion.57
  56.4 4.0 %all-to-all-done.1 = f32[4,32,512]{2,1,0:T(8,128)S(1)} async-done(((f32[4,32,512]{2,1,0:T(8,128)}), f32[4,32,512]{2,1,0:T(8,128)S(1)}, u32[]{:S(2)}, u32[]{:S(2)}) %all-to-all-start.1) | async-done | bytes 262176 | tf_op jit(solution)/shard_map/all_to_all | solution.py:94
  60.4 11.8 %fusion.56 = (f32[32,2048]{1,0:T(8,128)S(1)}, f32[32,2048]{1,0:T(8,128)S(1)}) fusion(f32[32,2048]{1,0:T(8,128)S(1)} %bitcast.103, f32[32,2048]{1,0:T(8,128)} %param.13, f32[]{:T(128)} %bitcast.20, f32[]{:T(128)} %bitcast.19, f32[]{:T(128)} %bitcast.18, f32[]{:T(128)} %bitcast.17, f32[]{:T(128)} %bitcast.16, f32[]{:T(128)} %bitcast.15, f32[]{:T(128)} %bitcast.14, ...), kind=kLoop, calls=%fused_computation.124 | loop fusion | flops 7340032 | bytes 1048640 | tf_op jit(solution)/shard_map/mul | solution.py:95
  72.6 0.6 gather_fusion.1
  73.3 13.1 %all-gather.2 = f32[4,64,32]{1,2,0:T(8,128)S(1)} all-gather(f32[1,64,32]{1,2,0:T(8,128)S(1)} %copy.183), channel_id=2, replica_groups=mesh['copies'=2,'nodes'=4,'samples'=4] {'nodes'}, dimensions={0}, use_global_device_ids=true | all-gather | bytes 40960 | tf_op jit(solution)/shard_map/all_gather | solution.py:86
  86.6 0.4 copy.185
  87.0 54.4 %gather_fusion.3 = f32[16384,32]{1,0:T(8,128)} fusion(f32[32,2304]{0,1:T(8,128)S(1)} %copy.185, s32[16384]{0:T(1024)S(1)} %broadcast_clamp_fusion), kind=kCustom, calls=%fused_computation.clone | custom fusion | bytes 4259840 | tf_op jit(solution)/shard_map/jit(_take)/gather | solution.py:88
  141.4 6.9 %fusion.1 = f32[32,2048]{0,1:T(8,128)S(1)} fusion(f32[8,2048,32]{2,1,0:T(8,128)} %bitcast.98, f32[8,2048]{1,0:T(8,128)S(1)} %fusion.24, pred[8,2048]{1,0:T(8,128)(4,1)S(1)} %get-tuple-element.10), kind=kLoop, calls=%fused_computation.8 | loop fusion | flops 1507328 | bytes 2441216 | tf_op jit(solution)/shard_map/reduce_sum | solution.py:89
  148.7 0.7 copy.213
  149.4 3.4 all-to-all-start.2
  152.8 6.0 %all-to-all-done.2 = f32[32,4,512]{2,0,1:T(8,128)S(1)} async-done(((f32[32,4,512]{2,0,1:T(8,128)}), f32[32,4,512]{2,0,1:T(8,128)S(1)}, u32[]{:S(2)}, u32[]{:S(2)}) %all-to-all-start.2) | async-done | bytes 262176 | tf_op jit(solution)/shard_map/all_to_all | solution.py:97
  158.8 1.4 fusion.14
  160.2 3.4 all-to-all-start.3
  164.0 5.6 %all-to-all-done.3 = f32[4,32,512]{2,1,0:T(8,128)S(1)} async-done(((f32[4,32,512]{2,1,0:T(8,128)}), f32[4,32,512]{2,1,0:T(8,128)S(1)}, u32[]{:S(2)}, u32[]{:S(2)}) %all-to-all-start.3) | async-done | bytes 262176 | tf_op jit(solution)/shard_map/all_to_all | solution.py:99
  169.6 0.7 multiply_reduce_fusion.3
  170.3 30.1 %psum.36 = f32[]{:T(128)} all-reduce(f32[]{:T(128)} %get-tuple-element.8), channel_id=1, replica_groups=mesh['copies'=2,'nodes'=4,'samples'=4] {'nodes','samples'}, use_global_device_ids=true, to_apply=%region_4.6 | all-reduce | flops 1 | bytes 8 | tf_op jit(solution)/shard_map/psum | solution.py:106
  201.1 0.7 multiply_reduce_fusion.2
  201.8 30.1 %psum.37 = f32[]{:T(128)} all-reduce(f32[]{:T(128)} %multiply_reduce_fusion.2), channel_id=1, replica_groups=mesh['copies'=2,'nodes'=4,'samples'=4] {'nodes','samples'}, use_global_device_ids=true, to_apply=%region_6.8 | all-reduce | flops 1 | bytes 8 | tf_op jit(solution)/shard_map/psum | solution.py:108
  232.6 8.4 %all_to_all.140 = f32[32,4,512]{2,0,1:T(8,128)S(1)} all-to-all(f32[32,4,512]{2,0,1:T(8,128)S(1)} %bitcast.114), channel_id=1, replica_groups=mesh['copies'=2,'nodes'=4,'samples'=4] {'samples'}, dimensions={1} | all-to-all | bytes 524288 | tf_op jit(solution)/shard_map/all_to_all | solution.py:92
  241.1 1.4 fusion.25
  242.5 3.4 all-to-all-start.5
  246.0 5.8 %all-to-all-done.5 = f32[4,32,512]{2,1,0:T(8,128)S(1)} async-done(((f32[4,32,512]{2,1,0:T(8,128)}), f32[4,32,512]{2,1,0:T(8,128)S(1)}, u32[]{:S(2)}, u32[]{:S(2)}) %all-to-all-start.5) | async-done | bytes 262176 | tf_op jit(solution)/shard_map/all_to_all | solution.py:94
  252.3 0.6 gather_fusion.2
  253.0 13.1 %all-gather.3 = f32[4,64,32]{1,2,0:T(8,128)S(1)} all-gather(f32[1,64,32]{1,2,0:T(8,128)S(1)} %copy.192), channel_id=3, replica_groups=mesh['copies'=2,'nodes'=4,'samples'=4] {'nodes'}, dimensions={0}, use_global_device_ids=true | all-gather | bytes 40960 | tf_op jit(solution)/shard_map/all_gather | solution.py:86
  266.3 0.4 copy.194
  266.6 54.4 %gather_fusion.4 = f32[16384,32]{1,0:T(8,128)} fusion(f32[32,2304]{0,1:T(8,128)S(1)} %copy.194, s32[16384]{0:T(1024)S(1)} %broadcast_clamp_fusion), kind=kCustom, calls=%fused_computation.1.clone | custom fusion | bytes 4259840 | tf_op jit(solution)/shard_map/jit(_take)/gather | solution.py:88
  321.1 6.9 %fusion = f32[32,2048]{0,1:T(8,128)S(1)} fusion(f32[8,2048,32]{2,1,0:T(8,128)} %bitcast.97, f32[8,2048]{1,0:T(8,128)S(1)} %fusion.24, pred[8,2048]{1,0:T(8,128)(4,1)S(1)} %get-tuple-element.10), kind=kLoop, calls=%fused_computation.6 | loop fusion | flops 1507328 | bytes 2441216 | tf_op jit(solution)/shard_map/reduce_sum | solution.py:89
  328.3 0.7 copy.211
  329.0 3.4 all-to-all-start.6
  332.7 5.7 %all-to-all-done.6 = f32[32,4,512]{2,0,1:T(8,128)S(1)} async-done(((f32[32,4,512]{2,0,1:T(8,128)}), f32[32,4,512]{2,0,1:T(8,128)S(1)}, u32[]{:S(2)}, u32[]{:S(2)}) %all-to-all-start.6) | async-done | bytes 262176 | tf_op jit(solution)/shard_map/all_to_all | solution.py:97
  338.4 1.4 fusion.12
  339.8 3.4 all-to-all-start.7
  343.7 5.6 %all-to-all-done.7 = f32[4,32,512]{2,1,0:T(8,128)S(1)} async-done(((f32[4,32,512]{2,1,0:T(8,128)}), f32[4,32,512]{2,1,0:T(8,128)S(1)}, u32[]{:S(2)}, u32[]{:S(2)}) %all-to-all-start.7) | async-done | bytes 262176 | tf_op jit(solution)/shard_map/all_to_all | solution.py:99
  349.2 0.8 multiply_reduce_fusion.1
  350.0 30.1 %all-reduce = (f32[]{:T(128)}, f32[]{:T(128)}) all-reduce(f32[]{:T(128)} %get-tuple-element.4, f32[]{:T(128)} %get-tuple-element.3), channel_id=1, replica_groups=mesh['copies'=2,'nodes'=4,'samples'=4] {'nodes','samples'}, use_global_device_ids=true, to_apply=%region_11.13 | all-reduce | flops 2 | bytes 16 | tf_op jit(solution)/shard_map/psum | solution.py:112
  381.4 0.8 multiply_subtract_fusion
  (51 shorter events, 3.8 us)
Async XLA Ops:
  0.6 43.8 %copy-start = (s32[256]{0:T(256)S(1)}, s32[256]{0:T(256)}, u32[]{:S(2)}) copy-start(s32[256]{0:T(256)} %param.20) | copy-start | bytes 3076
  40.2 9.4 %all-to-all-start = ((f32[32,4,512]{2,0,1:T(8,128)}), f32[32,4,512]{2,0,1:T(8,128)S(1)}, u32[]{:S(2)}, u32[]{:S(2)}) async-start(f32[32,4,512]{2,0,1:T(8,128)} %bitcast.96), calls=%async_computation | async-start | bytes 524288 | tf_op jit(solution)/shard_map/all_to_all | solution.py:92
  51.0 9.4 %all-to-all-start.1 = ((f32[4,32,512]{2,1,0:T(8,128)}), f32[4,32,512]{2,1,0:T(8,128)S(1)}, u32[]{:S(2)}, u32[]{:S(2)}) async-start(f32[4,32,512]{2,1,0:T(8,128)} %fusion.26), calls=%async_computation.1 | async-start | bytes 524288 | tf_op jit(solution)/shard_map/all_to_all | solution.py:94
  141.4 7.2 %copy-start.3 = (f32[2048]{0:T(1024)S(1)}, f32[2048]{0:T(1024)}, u32[]{:S(2)}) copy-start(f32[2048]{0:T(1024)} %param.15) | copy-start | bytes 24580
  141.4 28.2 %copy-start.1 = (f32[32,2048]{1,0:T(8,128)S(1)}, f32[32,2048]{1,0:T(8,128)}, u32[]{:S(2)}) copy-start(f32[32,2048]{1,0:T(8,128)} %param.12) | copy-start | bytes 786436
  141.4 28.2 %copy-start.4 = (f32[2048]{0:T(1024)S(1)}, f32[2048]{0:T(1024)}, u32[]{:S(2)}) copy-start(f32[2048]{0:T(1024)} %param.16) | copy-start | bytes 24580
  149.4 9.4 %all-to-all-start.2 = ((f32[32,4,512]{2,0,1:T(8,128)}), f32[32,4,512]{2,0,1:T(8,128)S(1)}, u32[]{:S(2)}, u32[]{:S(2)}) async-start(f32[32,4,512]{2,0,1:T(8,128)} %bitcast.95), calls=%async_computation.2 | async-start | bytes 524288 | tf_op jit(solution)/shard_map/all_to_all | solution.py:97
  160.2 9.4 %all-to-all-start.3 = ((f32[4,32,512]{2,1,0:T(8,128)}), f32[4,32,512]{2,1,0:T(8,128)S(1)}, u32[]{:S(2)}, u32[]{:S(2)}) async-start(f32[4,32,512]{2,1,0:T(8,128)} %fusion.14), calls=%async_computation.3 | async-start | bytes 524288 | tf_op jit(solution)/shard_map/all_to_all | solution.py:99
  232.6 148.8 %copy-start.2 = (f32[32,2048]{1,0:T(8,128)}, f32[32,2048]{1,0:T(8,128)S(1)}, u32[]{:S(2)}) copy-start(f32[32,2048]{1,0:T(8,128)S(1)} %broadcast_divide_fusion) | copy-start | bytes 786436
  242.5 9.4 %all-to-all-start.5 = ((f32[4,32,512]{2,1,0:T(8,128)}), f32[4,32,512]{2,1,0:T(8,128)S(1)}, u32[]{:S(2)}, u32[]{:S(2)}) async-start(f32[4,32,512]{2,1,0:T(8,128)} %fusion.25), calls=%async_computation.5 | async-start | bytes 524288 | tf_op jit(solution)/shard_map/all_to_all | solution.py:94
  329.0 9.4 %all-to-all-start.6 = ((f32[32,4,512]{2,0,1:T(8,128)}), f32[32,4,512]{2,0,1:T(8,128)S(1)}, u32[]{:S(2)}, u32[]{:S(2)}) async-start(f32[32,4,512]{2,0,1:T(8,128)} %bitcast.93), calls=%async_computation.6 | async-start | bytes 524288 | tf_op jit(solution)/shard_map/all_to_all | solution.py:97
  339.8 9.4 %all-to-all-start.7 = ((f32[4,32,512]{2,1,0:T(8,128)}), f32[4,32,512]{2,1,0:T(8,128)S(1)}, u32[]{:S(2)}, u32[]{:S(2)}) async-start(f32[4,32,512]{2,1,0:T(8,128)} %fusion.12), calls=%async_computation.7 | async-start | bytes 524288 | tf_op jit(solution)/shard_map/all_to_all | solution.py:99
where the time goes:
time: 383 us; the launch traced here: 382 us
  blocking collectives  161 us (42%)
  local copies, waits for them, and re-layouts  118 us (31%)
  waiting for transfers between devices  35 us (9%)
  other arithmetic  34.8 us (9%)
  starting transfers between devices  23.8 us (6%)
  matrix products  5.56 us (1%)
  between operations  4.26 us (1%)
    gather x2, local copies, waits for them, and re-layouts, couple(): picked = jnp.take(extended, gathered_index, axis=1)  109 us
    psum x1, blocking collectives, shards(): squares_total = lax.psum(jnp.sum(vector * vector), ('nodes', 'samples'))  35.5 us
    psum x1, blocking collectives, shards(): lax.psum((jnp.sum(basis_one * image_two), jnp.sum(basis_two * image_two))...  30.1 us
    psum x1, blocking collectives, shards(): lax.psum(jnp.sum(basis_one * image_one), ('nodes', 'samples')) / entries  30.1 us
    psum x1, blocking collectives, shards(): residue_total = lax.psum(jnp.sum(residue * residue), ('nodes', 'samples'))  30.1 us
    all_gather x2, blocking collectives, couple(): arrived = lax.all_gather(outgoing, 'nodes', axis=1, tiled=True)  26.3 us
    reduce_sum x2, other arithmetic, couple(): return jnp.sum(picked * masked[None, :, :], axis=1)  13.7 us
    mul x2, other arithmetic, apply_matvec(): current = conductances * waveform  11.9 us
  transfers between devices with their start and end apart: 7, of which 7 were waited for; matrix products, arithmetic and copies ran while one was open for 2% of the time, Pallas kernels for 0%

commit v1 on v0

v1 whole, which is shorter than its diff:
```python
import functools
import math

import jax
import jax.numpy as jnp
import numpy as np
from jax import lax
from jax.experimental import pallas as pl
from jax.experimental.pallas import tpu as pltpu
from jax.sharding import PartitionSpec as P

CAP = 16
EPSILON = 1e-06
LANES = 128
BF16 = jnp.bfloat16
F32 = jnp.float32
I32 = jnp.int32


def spectral_tables(length):
    indices = np.arange(length)
    frequency = np.where(indices == 1, length // 2, indices // 2)
    angles = (indices[:, None] * frequency[None, :] % length) * (2.0 * math.pi / length)
    cosine_column = (indices % 2 == 0) | (indices == 1)
    synthesis = np.where(cosine_column[None, :], np.cos(angles), np.sin(angles))
    factor = np.where(indices < 2, 1.0 / length, 2.0 / length)
    analysis = synthesis.T * factor[:, None]
    turn = np.zeros((length, length))
    for pair in range(length // 2):
        turn[2 * pair, 2 * pair + 1] = pair / (length // 2)
        turn[2 * pair + 1, 2 * pair] = -pair / (length // 2)
    return synthesis, analysis, synthesis @ turn


def halves(table):
    high = table.astype(np.float32).astype(BF16)
    low = (table - high.astype(np.float64)).astype(np.float32).astype(BF16)
    return np.stack([high, low])


def piece_order(count):
    masks, bit = [0], count // 2
    while bit:
        masks = masks + [mask ^ bit for mask in masks]
        bit //= 2
    return masks


def transform_tables(length, parts):
    synthesis, analysis, slope = spectral_tables(length)
    rows = length // parts
    forward, back = [], []
    for place in range(parts):
        times = np.arange(place // 2 * 2 * rows, (place // 2 + 1) * 2 * rows)
        block = lambda owner: np.arange(owner * rows, (owner + 1) * rows)
        coefs = np.concatenate([block(place ^ mask) for mask in piece_order(parts)])
        forward.append(
            np.concatenate(
                [
                    synthesis[np.ix_(times, coefs)],
                    slope[np.ix_(times, coefs)],
                    analysis[np.ix_(coefs, times)].T,
                ]
            )
        )
        sent = np.concatenate(
            [block(place ^ (2 * group) ^ side) for group in range(parts // 2) for side in (0, 1)]
        )
        back.append(analysis[np.ix_(sent, times)])
    return (
        np.moveaxis(halves(np.stack(forward)), 0, 1),
        np.moveaxis(halves(np.stack(back)), 0, 1),
    )


def split(values):
    high = values.astype(BF16)
    return high, (values - high.astype(F32)).astype(BF16)


def dot(first, second):
    return jnp.dot(first, second, preferred_element_type=F32)


def dot_split(first, second):
    (first_high, first_low), (second_high, second_low) = first, second
    rows = first_high.shape[0]
    both = dot(jnp.concatenate([first_high, first_low], axis=0), second_high)
    return both[:rows] + both[rows:] + dot(first_high, second_low)


def lane_sums(values):
    blocks = values.shape[1] // LANES
    total = values[:, :LANES]
    for block in range(1, blocks):
        total = total + values[:, block * LANES : (block + 1) * LANES]
    return jnp.sum(total, axis=0, keepdims=True)


def half_of(side, half):
    return pl.ds(pl.multiple_of(side * half, LANES), half)


def gather_kernel(place, send_list, boundary, vector, operating, picked, cut):
    node_groups = send_list.shape[0] // CAP
    nodes, lanes = picked.shape
    part = place[1]
    lane = lax.broadcasted_iota(I32, (8, lanes), 1)

    def name(slot, found):
        target = lax.rem(part + slot // CAP + 1, node_groups)
        node = boundary[send_list[target * CAP + slot % CAP]]
        return jnp.where(lane == slot, node, found)

    cut_nodes = lax.fori_loop(
        0, (node_groups - 1) * CAP, name, jnp.full((8, lanes), -1, I32), unroll=8
    )
    hit = lax.broadcasted_iota(I32, (nodes, lanes), 0) == cut_nodes[:1]
    picked[...] = jnp.where(hit, 1.0, 0.0).astype(BF16)
    both = jnp.concatenate([vector[...], operating[...]], axis=0)
    high, rest = split(both)
    middle, low = split(both - high.astype(F32))
    rows = both.shape[0]
    found = dot(jnp.concatenate([high, middle, low], axis=0), picked[...])
    cut[...] = found[:rows] + (found[rows : 2 * rows] + found[2 * rows :])


def conductance(operating, table):
    points = table.shape[1]
    spread = jnp.concatenate([table, jnp.zeros((1, LANES - points), F32)], axis=1)
    spread = jnp.broadcast_to(spread, (operating.shape[0], LANES))
    pieces = []
    for block in range(operating.shape[1] // LANES):
        scaled = (operating[:, block * LANES : (block + 1) * LANES] + 4.0) * ((points - 1) / 8.0)
        knot = jnp.clip(jnp.floor(scaled), 0.0, points - 2.0)
        weight = scaled - knot
        place = knot.astype(I32)
        left = jnp.take_along_axis(spread, place, axis=1, mode="promise_in_bounds")
        right = jnp.take_along_axis(spread, place + 1, axis=1, mode="promise_in_bounds")
        pieces.append(left + weight * (right - left))
    return jnp.concatenate(pieces, axis=1)


def prepare_kernel(
    place,
    neighbours,
    weights,
    degree,
    own_operating,
    near_operating,
    table,
    coupling_high,
    coupling_low,
    conductances,
    entry_rows,
    weight_rows,
):
    slots, nodes = neighbours.shape
    half = coupling_high.shape[1]
    sources = coupling_high.shape[0]
    node_groups = place[2]
    side, part = place[0] % 2, place[1]
    rows = own_operating.shape[0]
    conductances[pl.ds(pl.multiple_of(side * rows, 8), rows), :] = conductance(
        own_operating[...], table[...]
    )
    conductances[pl.ds(pl.multiple_of((1 - side) * rows, 8), rows), :] = conductance(
        near_operating[...], table[...]
    )

    mine = half_of(side, half)
    entry = neighbours[:, mine]
    remote = entry - nodes
    distance = part - (remote >> 4)
    distance = jnp.where(distance < 0, distance + node_groups, distance)
    entry = jnp.where(remote < 0, entry, nodes + (distance - 1) * CAP + (remote & 15))
    live = lax.broadcasted_iota(I32, (slots, half), 0) < degree[:, mine]
    masked = jnp.where(live, weights[:, mine], 0.0)
    entries = [entry[slot : slot + 1] for slot in range(slots)]
    gains = [masked[slot : slot + 1] for slot in range(slots)]
    for slot in range(slots):
        for later in range(slot + 1, slots):
            same = entries[slot] == entries[later]
            gains[slot] = gains[slot] + jnp.where(same, gains[later], 0.0)
            entries[later] = jnp.where(same, -1, entries[later])
    for slot in range(slots):
        entry_rows[slot : slot + 1, :] = entries[slot]
        weight_rows[slot : slot + 1, :] = gains[slot]

    unroll = 4

    def columns(block, carry):
        lanes = pl.ds(pl.multiple_of(block * LANES, LANES), LANES)
        wide = (CAP, LANES)
        names = [
            jnp.broadcast_to(entry_rows[slot : slot + 1, lanes], wide).astype(jnp.int16)
            for slot in range(slots)
        ]
        parts = [
            split(jnp.broadcast_to(weight_rows[slot : slot + 1, lanes], wide))
            for slot in range(slots)
        ]

        def source_rows(step, row):
            for inner in range(unroll):
                high = jnp.zeros(wide, BF16)
                low = jnp.zeros(wide, BF16)
                for slot in range(slots):
                    hit = names[slot] == row
                    high = jnp.where(hit, parts[slot][0], high)
                    low = jnp.where(hit, parts[slot][1], low)
                at = pl.ds(pl.multiple_of((step * unroll + inner) * 16, 16), 16)
                coupling_high[at, lanes] = high
                coupling_low[at, lanes] = low
                row = row + jnp.int16(16)
            return row

        lax.fori_loop(
            0,
            sources // 16 // unroll,
            source_rows,
            lax.broadcasted_iota(I32, wide, 0).astype(jnp.int16),
        )
        return carry

    lax.fori_loop(0, half // LANES, columns, 0)


def couple(load, current, halo_current, coupling_high, coupling_low):
    nodes = current.shape[1]
    high, low = split(current)
    halo_high, halo_low = split(halo_current)
    rows = high.shape[0]
    stacked = jnp.concatenate([high, low], axis=0)
    halo_stacked = jnp.concatenate([halo_high, halo_low], axis=0)
    width = 256
    for block in range(load.shape[1] // width):
        lanes = slice(block * width, (block + 1) * width)
        both = dot(stacked, coupling_high[:nodes, lanes]) + dot(
            halo_stacked, coupling_high[nodes:, lanes]
        )
        third = dot(high, coupling_low[:nodes, lanes]) + dot(
            halo_high, coupling_low[nodes:, lanes]
        )
        load[:, lanes] = load[:, lanes] + (both[:rows] + both[rows:] + third)


def signed_sums(values):
    even = lax.broadcasted_iota(I32, values.shape, 0) % 2 == 0
    return (
        jnp.sum(values, axis=0, keepdims=True),
        jnp.sum(jnp.where(even, values, -values), axis=0, keepdims=True),
    )


def first_kernel(*refs, pieces):
    place = refs[0]
    vectors = refs[1 : 1 + pieces]
    halos = refs[1 + pieces : 1 + 2 * pieces]
    (
        forward,
        back,
        conductances,
        coupling_high,
        coupling_low,
        linear,
        capacity,
        table,
        picked,
        image,
        load,
        wave,
        dual,
        halo_conductances,
        kept,
        sent,
        cut,
        sums,
        scalars,
        field_high,
        field_low,
    ) = refs[1 + 2 * pieces :]
    rows, nodes = vectors[0].shape
    half = load.shape[1]
    times = load.shape[0]
    side = place[0] % 2
    mine = half_of(side, half)
    for index in range(pieces):
        at = slice(index * rows, (index + 1) * rows)
        field_high[at, :nodes], field_low[at, :nodes] = split(vectors[index][...])
        field_high[at, nodes:], field_low[at, nodes:] = split(halos[index][:rows])
    near = piece_order(pieces).index(1)
    halo_conductances[pl.ds(pl.multiple_of(side * rows, 8), rows), :] = conductance(
        halos[0][rows:], table[...]
    )
    halo_conductances[pl.ds(pl.multiple_of((1 - side) * rows, 8), rows), :] = conductance(
        halos[near][rows:], table[...]
    )
    waveform = dot_split(
        (forward[0, :times], forward[1, :times]), (field_high[...], field_low[...])
    )
    others = dot_split(
        (forward[0, times:], forward[1, times:]), (field_high[:, mine], field_low[:, mine])
    )
    current = conductances[...] * waveform[:, :nodes]
    halo_current = halo_conductances[...] * waveform[:, nodes:]
    wave[...] = jnp.where(side == 0, waveform[:, :half], waveform[:, half:nodes])
    dual[...] = others[times:]
    load[...] = wave[...] * (linear[:, mine] + conductances[:, mine])
    couple(load, current, halo_current, coupling_high, coupling_low)
    answer = load[...] + capacity[:, mine] * others[:times]
    image[...] = answer
    halves_of_answer = split(answer)
    spectrum = dot_split((back[0], back[1]), halves_of_answer)
    kept[...] = spectrum[:times]
    sent[...] = spectrum[times:]
    cut[...] = pick(answer, picked[mine, :])
    lines = [*signed_sums(answer), *signed_sums(wave[...])]
    sums[...] = jnp.concatenate(lines + [jnp.zeros((4, half), F32)], axis=0)
    own = vectors[0][...]
    products = [lane_sums(own * own), lane_sums(dual[...] * answer)]
    scalars[...] = jnp.concatenate(products + [jnp.zeros((6, LANES), F32)], axis=0)


def pick(values, picked):
    high, rest = split(values)
    middle, low = split(values - high.astype(F32))
    rows = values.shape[0]
    found = dot(jnp.concatenate([high, middle, low], axis=0), picked)
    return found[:rows] + (found[rows : 2 * rows] + found[2 * rows :])


def second_kernel(
    place,
    image,
    near_image,
    halo,
    back,
    conductances,
    halo_conductances,
    coupling_high,
    coupling_low,
    linear,
    load,
    kept,
    sent,
    current,
):
    half = image.shape[1]
    times = image.shape[0]
    side = place[0] % 2
    mine, other = half_of(side, half), half_of(1 - side, half)
    current[:, mine] = conductances[:, mine] * image[...]
    current[:, other] = conductances[:, other] * near_image[...]
    load[...] = image[...] * (linear[:, mine] + conductances[:, mine])
    couple(load, current[...], halo_conductances[...] * halo[...], coupling_high, coupling_low)
    spectrum = dot_split((back[0], back[1]), split(load[...]))
    kept[...] = spectrum[:times]
    sent[...] = spectrum[times:]


def turned(field, first_pair, half_order):
    count = field.shape[0]
    row = lax.broadcasted_iota(I32, field.shape, 0)
    scaling = (first_pair + row // 2).astype(F32) * (1.0 / half_order)
    above = pltpu.roll(field, count - 1, 0)
    below = pltpu.roll(field, 1, 0)
    return scaling * jnp.where(row % 2 == 0, above, -below)


def norms(first_sums, entries):
    squares = jnp.sum(first_sums[0:1, :], axis=1, keepdims=True)
    cross = jnp.sum(first_sums[1:2, :], axis=1, keepdims=True)
    scale_square = squares / entries + EPSILON
    return scale_square, cross / entries / scale_square


def join(target, side, own, near):
    half = own.shape[1]
    target[:, half_of(side, half)] = own
    target[:, half_of(1 - side, half)] = near


def products_kernel(
    place,
    totals,
    vector,
    own_image,
    near_image,
    capacity,
    load,
    second_load,
    image,
    wave,
    dual,
    sums,
    residue,
    base,
    scalars,
    *,
    length,
    entries,
):
    side = place[0] % 2
    rows = vector.shape[0]
    first_pair = place[0] * (rows // 2)
    _, coeff = norms(totals[...], entries)
    join(residue, side, own_image[...], near_image[...])
    field = residue[...]
    base[...] = capacity[...] * turned(field, first_pair, length // 2) - coeff * field
    field = field - coeff * vector[...]
    residue[...] = field
    slope = capacity[...] * turned(field, first_pair, length // 2)
    change = second_load[...] - coeff * load[...]
    rest = image[...] - coeff * wave[...]
    changes = signed_sums(change)
    rests = [sums[line : line + 1] - coeff * sums[2 + line : 3 + line] for line in (0, 1)]
    ends = rests[0] * changes[0] + rests[1] * changes[1]
    products = [
        lane_sums(field * field),
        lane_sums(dual[...] * change) + lane_sums(vector[...] * slope),
        lane_sums(rest * change) * (2.0 / length)
        - lane_sums(ends) * (1.0 / length / length)
        + lane_sums(field * slope),
    ]
    scalars[...] = jnp.concatenate(products + [jnp.zeros((5, LANES), F32)], axis=0)


def last_kernel(
    place,
    first_totals,
    last_totals,
    vector,
    residue,
    base,
    own_part,
    near_part,
    basis_two,
    next_residue,
    *,
    entries,
):
    side = place[0] % 2
    scale_square, _ = norms(first_totals[...], entries)
    sums = [jnp.sum(last_totals[line : line + 1, :], axis=1, keepdims=True) for line in range(3)]
    second_norm = jnp.sqrt(sums[0] / entries / scale_square + EPSILON)
    scale = jnp.sqrt(scale_square)
    inverse = 1.0 / (second_norm * scale)
    along_one = sums[1] / entries * inverse / scale
    along_two = sums[2] / entries * inverse * inverse
    join(next_residue, side, own_part[...], near_part[...])
    second = residue[...] * inverse
    basis_two[...] = second
    next_residue[...] = (
        (next_residue[...] + base[...]) * inverse
        - (along_one / scale) * vector[...]
        - along_two * second
    )


VMEM = pl.BlockSpec(memory_space=pltpu.VMEM)
SMEM = pl.BlockSpec(memory_space=pltpu.SMEM)


def run(kernel, name, operands, outs, scratch=(), scalars=1, flops=0, moved=0):
    pinned = [pltpu.VMEM(shape, dtype) for shape, dtype in outs]
    return pl.pallas_call(
        kernel,
        out_shape=pinned,
        in_specs=[SMEM] * scalars + [VMEM] * (len(operands) - scalars),
        out_specs=[VMEM] * len(outs),
        scratch_shapes=[pltpu.VMEM(shape, dtype) for shape, dtype in scratch],
        compiler_params=pltpu.CompilerParams(vmem_limit_bytes=40 * 2**20),
        cost_estimate=pl.CostEstimate(flops=flops, bytes_accessed=moved, transcendentals=0),
        name=name,
    )(*operands)


def swap(value, mask):
    count = lax.axis_size("samples")
    return lax.ppermute(value, "samples", [(at, at ^ mask) for at in range(count)])


def total(value):
    for axis in ("samples", "nodes"):
        count, stride = lax.axis_size(axis), 1
        while stride < count:
            radix = 4 if count // stride % 4 == 0 else 2
            others = [
                lax.ppermute(value, axis, [(at, at ^ (step * stride)) for at in range(count)])
                for step in range(1, radix)
            ]
            value = value + functools.reduce(jnp.add, others)
            stride *= radix
    return value


def reduce_groups(kept, sent):
    times = kept.shape[0]
    count = lax.axis_size("samples") // 2
    blocks = {0: kept}
    for group in range(1, count):
        blocks[group] = sent[(group - 1) * times : group * times]
    bit = count // 2
    while bit:
        for group in [name for name in blocks if name & bit]:
            blocks[group ^ bit] = blocks[group ^ bit] + swap(blocks.pop(group), 2 * bit)
        bit //= 2
    return blocks[0]


def shards(
    vector, operating, table, linear, capacity, weights, degree, neighbours, boundary, send_list
):
    rows, nodes = vector.shape
    parts, node_groups = lax.axis_size("samples"), lax.axis_size("nodes")
    length, half, times = rows * parts, nodes // 2, 2 * rows
    entries = float(length * nodes * node_groups)
    lanes = -(-(node_groups - 1) * CAP // LANES) * LANES
    sources = nodes + lanes
    order = piece_order(parts)
    own_place = lax.axis_index("samples")
    place = jnp.stack([own_place, lax.axis_index("nodes"), jnp.int32(node_groups)]).astype(I32)
    forward, back = (
        lax.dynamic_index_in_dim(jnp.asarray(stack), own_place, keepdims=False)
        for stack in transform_tables(length, parts)
    )
    linear, capacity, degree, table = (
        value.reshape(1, -1) for value in (linear, capacity, degree, table)
    )
    distance = (jnp.arange(lanes, dtype=I32) // CAP + 1)[None, :]

    def from_parts(value, sides):
        found = jnp.zeros_like(value)
        for step in range(1, node_groups):
            arrived = [
                lax.ppermute(
                    value,
                    ("nodes", "samples"),
                    [
                        (at * parts + which, (at + step) % node_groups * parts + (which ^ side))
                        for at in range(node_groups)
                        for which in range(parts)
                    ],
                )
                for side in range(sides)
            ]
            found = jnp.where(distance == step, functools.reduce(jnp.add, arrived), found)
        return found

    vectors, bit = [vector], parts // 2
    while bit:
        vectors = vectors + [swap(piece, bit) for piece in vectors]
        bit //= 2
    near_operating = swap(operating, 1)

    picked, cut = run(
        gather_kernel,
        "gather",
        (place, send_list, boundary, vector, operating),
        [((nodes, lanes), BF16), ((times, lanes), F32)],
        scalars=3,
    )
    halo = from_parts(cut, 1)
    halos = [halo if mask == 0 else swap(halo, mask) for mask in order]

    coupling_high, coupling_low, conductances = run(
        prepare_kernel,
        "prepare",
        (place, neighbours, weights, degree, operating, near_operating, table),
        [((sources, half), BF16), ((sources, half), BF16), ((times, nodes), F32)],
        scratch=[((weights.shape[0], half), I32), ((weights.shape[0], half), F32)],
    )

    wide = ((times, half), F32)
    rest = max(length - times, 8)
    image, load, wave, dual, halo_conductances, kept, sent, cut, sums, scalars = run(
        functools.partial(first_kernel, pieces=parts),
        "first",
        (place, *vectors, *halos, forward, back, conductances, coupling_high, coupling_low)
        + (linear, capacity, table, picked),
        [wide, wide, wide, wide, ((times, lanes), F32), wide, ((rest, half), F32)]
        + [((times, lanes), F32), ((8, half), F32), ((8, LANES), F32)],
        scratch=[((length, sources), BF16)] * 2,
    )
    near_image = swap(image, 1)
    halo = from_parts(cut, 2)
    first_totals = total(scalars)
    bit = 2
    while bit < parts:
        sums = sums + swap(sums, bit)
        bit *= 2
    spectrum = reduce_groups(kept, sent)
    own_coefs, near_coefs = spectrum[:rows], swap(spectrum[rows:], 1)

    second_load, kept, sent = run(
        second_kernel,
        "second",
        (place, image, near_image, halo, back, conductances, halo_conductances)
        + (coupling_high, coupling_low, linear),
        [wide, wide, ((rest, half), F32)],
        scratch=[((times, nodes), F32)],
    )
    residue, base, scalars = run(
        functools.partial(products_kernel, length=length, entries=entries),
        "products",
        (place, first_totals, vector, own_coefs, near_coefs, capacity)
        + (load, second_load, image, wave, dual, sums),
        [((rows, nodes), F32), ((rows, nodes), F32), ((8, LANES), F32)],
    )
    last_totals = total(scalars)
    spectrum = reduce_groups(kept, sent)
    own_part, near_part = spectrum[:rows], swap(spectrum[rows:], 1)
    field = jax.ShapeDtypeStruct((rows, nodes), F32)
    return tuple(
        pl.pallas_call(
            functools.partial(last_kernel, entries=entries),
            out_shape=[field, field],
            in_specs=[SMEM] + [VMEM] * 7,
            out_specs=[VMEM] * 2,
            name="last",
        )(place, first_totals, last_totals, vector, residue, base, own_part, near_part)
    )


def solution(mesh):
    return jax.shard_map(
        shards,
        mesh=mesh,
        in_specs=(
            P("samples", ("copies", "nodes")),
            P("samples", ("copies", "nodes")),
            P(),
            P("nodes"),
            P("nodes"),
            P(None, "nodes"),
            P("nodes"),
            P(None, "nodes"),
            P("nodes"),
            P("nodes"),
        ),
        out_specs=(P("samples", ("copies", "nodes")), P("samples", ("copies", "nodes"))),
        check_vma=False,
    )
```

time: 383 us -> 79.1 us (0.21)
  blocking collectives: 161 us -> 0 us
  local copies, waits for them, and re-layouts: 118 us -> 13.3 us
  other arithmetic: 34.8 us -> 0.78 us
  waiting for transfers between devices: 35 us -> 12.6 us
  Pallas kernels: 0 us -> 17.1 us
  starting transfers between devices: 23.8 us -> 33.8 us
  matrix products: 5.56 us -> 0 us
    psum x4 -> x0, blocking collectives: 126 us -> none  [the longest x1 35.5 us: shards(): squares_total = lax.psum(jnp.sum(vector * vector), ('nodes', 'samples'))]
    gather x5 -> x0, local copies, waits for them, and re-layouts: 111 us -> none  [the longest x2 109 us: couple(): picked = jnp.take(extended, gathered_index, axis=1)]
    all_to_all x7 -> x0, waiting for transfers between devices: 35 us -> none  [the longest x2 11.7 us: apply_matvec(): lax.all_to_all(node_load, 'samples', split_axis=1, concat_axis=0, tiled=T...]
    ppermute x0 -> x34, starting transfers between devices: none -> 33.8 us  [the longest x9 13.2 us: from_parts(): lax.ppermute(value, ('nodes', 'samples'), [(at * parts + which, (at + ste...]
    all_gather x2 -> x0, blocking collectives: 26.3 us -> none  [couple(): arrived = lax.all_gather(outgoing, 'nodes', axis=1, tiled=True)]
    all_to_all x7 -> x0, starting transfers between devices: 23.8 us -> none  [the longest x2 6.81 us: apply_matvec(): lax.all_to_all(node_load, 'samples', split_axis=1, concat_axis=0, tiled=T...]
    reduce_sum x6 -> x0, other arithmetic: 17.5 us -> none  [the longest x2 13.7 us: couple(): return jnp.sum(picked * masked[None, :, :], axis=1)]
    pallas_call x0 -> x6, Pallas kernels: none -> 17.1 us  [the longest x5 15 us: run(): pl.pallas_call(kernel, out_shape=pinned, in_specs=[SMEM] * scalars + [VME...]
  transfers between devices with their start and end apart: 7 -> 34, of which waited for: 7 -> 7; matrix products, arithmetic and copies ran while one was open for 2% -> 4% of each run, Pallas kernels for 0% -> 15%
where the time goes in v1:
time: 79.1 us; the launch traced here: 78.5 us
  starting transfers between devices  33.8 us (43%)
  Pallas kernels  17.1 us (22%)
  local copies, waits for them, and re-layouts  13.3 us (17%)
  waiting for transfers between devices  12.6 us (16%)
  between operations  0.91 us (1%)
    pallas_call x5, Pallas kernels, run(): pl.pallas_call(kernel, out_shape=pinned, in_specs=[SMEM] * scalars + [VME...  15 us
    ppermute x9, starting transfers between devices, from_parts(): lax.ppermute(value, ('nodes', 'samples'), [(at * parts + which, (at + ste...  13.2 us
    ppermute x12, starting transfers between devices, total(): lax.ppermute(value, axis, [(at, at ^ step * stride) for at in range(count)])  12 us
    unnamed x36, local copies, waits for them, and re-layouts  10.9 us
    ppermute x13, starting transfers between devices, swap(): lax.ppermute(value, 'samples', [(at, at ^ mask) for at in range(count)])  8.56 us
    ppermute x12, waiting for transfers between devices, total(): lax.ppermute(value, axis, [(at, at ^ step * stride) for at in range(count)])  7.24 us
    ppermute x13, waiting for transfers between devices, swap(): lax.ppermute(value, 'samples', [(at, at ^ mask) for at in range(count)])  4.29 us
    pallas_call x1, Pallas kernels, shards(): pl.pallas_call(functools.partial(last_kernel, entries=entries), out_shape...  2.15 us
  transfers between devices with their start and end apart: 34, of which 7 were waited for; matrix products, arithmetic and copies ran while one was open for 4% of the time, Pallas kernels for 15%

profile of v1, /device:TPU:0, one launch (start us, length us, event | category | flops | bytes accessed | tf_op | source)
XLA Modules:
  0.0 78.5 jit_solution(8286921338488915254)
XLA Ops:
  1.1 2.6 %collective-permute-start = (f32[32,2048]{1,0:T(8,128)}, f32[32,2048]{1,0:T(8,128)S(1)}, u32[]{:S(2)}, u32[]{:S(2)}) collective-permute-start(f32[32,2048]{1,0:T(8,128)} %vector.5), channel_id=1, source_target_pairs={{0,2},{1,3},{2,0},{3,1},{4,6},{5,7},{6,4},{7,5},{8,10},{9,11},{10,... | collective-permute-start | bytes 786440 | tf_op jit(solution)/shard_map/ppermute | solution.py:481
  3.8 0.9 %copy-done = f32[32,2048]{1,0:T(8,128)S(1)} copy-done((f32[32,2048]{1,0:T(8,128)S(1)}, f32[32,2048]{1,0:T(8,128)}, u32[]{:S(2)}) %copy-start) | copy-done | bytes 262168
  4.7 0.9 %copy-done.2 = f32[32,2048]{1,0:T(8,128)S(1)} copy-done((f32[32,2048]{1,0:T(8,128)S(1)}, f32[32,2048]{1,0:T(8,128)}, u32[]{:S(2)}) %copy-start.2) | copy-done | bytes 262168
  5.7 0.7 copy-done.15
  6.4 0.7 copy-done.16
  7.0 1.5 %gather.1 = (bf16[2048,128]{1,0:T(8,128)(2,1)S(1)}, f32[64,128]{1,0:T(8,128)S(1)}) custom-call(s32[3]{0:T(128)S(1)} %pad_add_fusion.place.refs_0_, s32[64]{0:T(128)S(1)} %copy-done.16, s32[256]{0:T(256)S(1)} %copy-done.15, f32[32,2048]{1,0:T(8,128)S(1)} %copy-done, f32[32,2048]{1,0:T(8,128)S(1)} %copy-done.2), custom_call_target="tpu_custom_call" | custom-call | tf_op jit(solution)/shard_map/gather/pallas_call | solution.py:467
  8.5 1.6 %collective-permute-start.5 = (f32[64,128]{1,0:T(8,128)S(1)}, f32[64,128]{1,0:T(8,128)S(1)}, u32[]{:S(2)}, u32[]{:S(2)}) collective-permute-start(f32[64,128]{1,0:T(8,128)S(1)} %get-tuple-element.23), channel_id=1, source_target_pairs={{0,4},{1,5},{2,6},{3,7},{4,8},{5,9},{6,10},{7,11},{8,12},{9,13},{1... | collective-permute-start | bytes 98312 | tf_op jit(solution)/shard_map/ppermute | solution.py:537
  10.1 2.6 %collective-permute-start.4 = (f32[64,128]{1,0:T(8,128)S(1)}, f32[64,128]{1,0:T(8,128)S(1)}, u32[]{:S(2)}, u32[]{:S(2)}) collective-permute-start(f32[64,128]{1,0:T(8,128)S(1)} %get-tuple-element.23), channel_id=1, source_target_pairs={{0,8},{1,9},{2,10},{3,11},{4,12},{5,13},{6,14},{7,15},{8,0},{9,1},... | collective-permute-start | bytes 98312 | tf_op jit(solution)/shard_map/ppermute | solution.py:537
  12.7 1.3 %collective-permute-start.3 = (f32[64,128]{1,0:T(8,128)S(1)}, f32[64,128]{1,0:T(8,128)S(1)}, u32[]{:S(2)}, u32[]{:S(2)}) collective-permute-start(f32[64,128]{1,0:T(8,128)S(1)} %get-tuple-element.23), channel_id=1, source_target_pairs={{0,12},{1,13},{2,14},{3,15},{4,0},{5,1},{6,2},{7,3},{8,4},{9,5},{1... | collective-permute-start | bytes 98312 | tf_op jit(solution)/shard_map/ppermute | solution.py:537
  14.1 0.9 %dynamic-slice_bitcast_fusion.refs_9_ = bf16[2,192,128]{2,1,0:T(8,128)(2,1)S(1)} fusion(bf16[4,2,192,128]{3,2,1,0:T(8,128)(2,1)} %constant.51.clone, s32[]{:T(128)S(6)} %select_n.55), kind=kLoop, calls=%fused_computation | loop fusion | bytes 196612 | tf_op jit(solution)/shard_map/jit(dynamic_index_in_dim)/squeeze | solution.py:525
  15.6 1.1 %collective-permute-done.3 = f32[64,128]{1,0:T(8,128)S(1)} collective-permute-done((f32[64,128]{1,0:T(8,128)S(1)}, f32[64,128]{1,0:T(8,128)S(1)}, u32[]{:S(2)}, u32[]{:S(2)}) %collective-permute-start.3) | collective-permute-done | bytes 32800 | tf_op jit(solution)/shard_map/ppermute | solution.py:537
  17.4 1.5 %collective-permute-start.6 = (f32[64,128]{1,0:T(8,128)S(1)}, f32[64,128]{1,0:T(8,128)S(1)}, u32[]{:S(2)}, u32[]{:S(2)}) collective-permute-start(f32[64,128]{1,0:T(8,128)S(1)} %select_select_fusion.1.refs_5_), channel_id=1, source_target_pairs={{0,2},{1,3},{2,0},{3,1},{4,6},{5,7},{6,4},{7,5},{8,10},{9,11},{10,... | collective-permute-start | bytes 98312 | tf_op jit(solution)/shard_map/ppermute | solution.py:481
  18.9 0.8 %dynamic-slice_bitcast_fusion.1.refs_10_.back = bf16[2,128,64]{2,1,0:T(8,128)(2,1)S(1)} fusion(bf16[4,2,128,64]{3,2,1,0:T(8,128)(2,1)} %constant.52.clone, s32[]{:T(128)S(6)} %select_n.55), kind=kLoop, calls=%fused_computation.1 | loop fusion | bytes 65540 | tf_op jit(solution)/shard_map/jit(dynamic_index_in_dim)/squeeze | solution.py:525
  19.7 0.9 %copy-done.3 = f32[32,2048]{1,0:T(8,128)S(1)} copy-done((f32[32,2048]{1,0:T(8,128)S(1)}, f32[32,2048]{1,0:T(8,128)}, u32[]{:S(2)}) %copy-start.3) | copy-done | bytes 262168
  20.7 0.8 %copy-done.6 = s32[8,2048]{1,0:T(8,128)S(1)} copy-done((s32[8,2048]{1,0:T(8,128)S(1)}, s32[8,2048]{1,0:T(8,128)}, u32[]{:S(2)}) %copy-start.6) | copy-done | bytes 65560
  21.5 0.8 %copy-done.7 = f32[8,2048]{1,0:T(8,128)S(1)} copy-done((f32[8,2048]{1,0:T(8,128)S(1)}, f32[8,2048]{1,0:T(8,128)}, u32[]{:S(2)}) %copy-start.7) | copy-done | bytes 65560
  22.3 0.7 copy-done.12
  23.0 0.7 copy-done.13
  23.7 6.9 %prepare.1 = (bf16[2176,1024]{1,0:T(8,128)(2,1)S(1)}, bf16[2176,1024]{1,0:T(8,128)(2,1)S(1)}, f32[64,2048]{1,0:T(8,128)S(1)}) custom-call(s32[3]{0:T(128)S(1)} %pad_add_fusion.place.refs_0_, s32[8,2048]{1,0:T(8,128)S(1)} %copy-done.6, f32[8,2048]{1,0:T(8,128)S(1)} %copy-done.7, s32[1,2048]{1,0:T(1,128)S(1)} %bitcast.14, f32[32,2048]{1,0:T(8,128)S(1)} %copy-done.3, ...), custom_call_target="tpu_custom_call" | custom-call | tf_op jit(solution)/shard_map/prepare/pallas_call | solution.py:467
  30.6 0.9 %copy-done.1 = f32[32,2048]{1,0:T(8,128)S(1)} copy-done((f32[32,2048]{1,0:T(8,128)S(1)}, f32[32,2048]{1,0:T(8,128)}, u32[]{:S(2)}) %copy-start.1) | copy-done | bytes 262168
  31.6 0.7 copy-done.9
  32.3 0.7 copy-done.10
  33.0 0.7 copy-done.14
  33.6 3.1 %first.1 = (f32[64,1024]{1,0:T(8,128)S(1)}, f32[64,1024]{1,0:T(8,128)S(1)}, f32[64,1024]{1,0:T(8,128)S(1)}, f32[64,1024]{1,0:T(8,128)S(1)}, f32[64,128]{1,0:T(8,...) custom-call(s32[3]{0:T(128)S(1)} %pad_add_fusion.place.refs_0_, ...), custom_call_target="tpu_custom_call" | custom-call | tf_op jit(solution)/shard_map/first/pallas_call | solution.py:467
  36.8 1.1 %collective-permute-start.23 = (f32[64,128]{1,0:T(8,128)S(1)}, f32[64,128]{1,0:T(8,128)S(1)}, u32[]{:S(2)}, u32[]{:S(2)}) collective-permute-start(f32[64,128]{1,0:T(8,128)S(1)} %get-tuple-element.33), channel_id=1, source_target_pairs={{0,4},{1,5},{2,6},{3,7},{4,8},{5,9},{6,10},{7,11},{8,12},{9,13},{1... | collective-permute-start | bytes 98312 | tf_op jit(solution)/shard_map/ppermute | solution.py:537
  37.9 0.7 collective-permute-start.12
  38.5 1.5 %collective-permute-start.11 = (f32[8,128]{1,0:T(8,128)S(1)}, f32[8,128]{1,0:T(8,128)S(1)}, u32[]{:S(2)}, u32[]{:S(2)}) collective-permute-start(f32[8,128]{1,0:T(8,128)S(1)} %get-tuple-element.28), channel_id=1, source_target_pairs={{0,2},{1,3},{2,0},{3,1},{4,6},{5,7},{6,4},{7,5},{8,10},{9,11},{10,... | collective-permute-start | bytes 12296 | tf_op jit(solution)/shard_map/ppermute | solution.py:490
  40.0 0.9 %collective-permute-done.12 = f32[8,128]{1,0:T(8,128)S(1)} collective-permute-done((f32[8,128]{1,0:T(8,128)S(1)}, f32[8,128]{1,0:T(8,128)S(1)}, u32[]{:S(2)}, u32[]{:S(2)}) %collective-permute-start.12) | collective-permute-done | bytes 4128 | tf_op jit(solution)/shard_map/ppermute | solution.py:490
  40.9 2.7 %collective-permute-start.22 = (f32[64,128]{1,0:T(8,128)S(1)}, f32[64,128]{1,0:T(8,128)S(1)}, u32[]{:S(2)}, u32[]{:S(2)}) collective-permute-start(f32[64,128]{1,0:T(8,128)S(1)} %get-tuple-element.33), channel_id=1, source_target_pairs={{0,9},{1,8},{2,11},{3,10},{4,13},{5,12},{6,15},{7,14},{8,1},{9,0},... | collective-permute-start | bytes 98312 | tf_op jit(solution)/shard_map/ppermute | solution.py:537
  43.6 1.1 %collective-permute-start.21 = (f32[64,128]{1,0:T(8,128)S(1)}, f32[64,128]{1,0:T(8,128)S(1)}, u32[]{:S(2)}, u32[]{:S(2)}) collective-permute-start(f32[64,128]{1,0:T(8,128)S(1)} %get-tuple-element.33), channel_id=1, source_target_pairs={{0,8},{1,9},{2,10},{3,11},{4,12},{5,13},{6,14},{7,15},{8,0},{9,1},... | collective-permute-start | bytes 98312 | tf_op jit(solution)/shard_map/ppermute | solution.py:537
  44.7 1.3 %collective-permute-start.20 = (f32[64,128]{1,0:T(8,128)S(1)}, f32[64,128]{1,0:T(8,128)S(1)}, u32[]{:S(2)}, u32[]{:S(2)}) collective-permute-start(f32[64,128]{1,0:T(8,128)S(1)} %get-tuple-element.33), channel_id=1, source_target_pairs={{0,13},{1,12},{2,15},{3,14},{4,1},{5,0},{6,3},{7,2},{8,5},{9,4},{1... | collective-permute-start | bytes 98312 | tf_op jit(solution)/shard_map/ppermute | solution.py:537
  46.1 1.3 %collective-permute-start.19 = (f32[64,128]{1,0:T(8,128)S(1)}, f32[64,128]{1,0:T(8,128)S(1)}, u32[]{:S(2)}, u32[]{:S(2)}) collective-permute-start(f32[64,128]{1,0:T(8,128)S(1)} %get-tuple-element.33), channel_id=1, source_target_pairs={{0,12},{1,13},{2,14},{3,15},{4,0},{5,1},{6,2},{7,3},{8,4},{9,5},{1... | collective-permute-start | bytes 98312 | tf_op jit(solution)/shard_map/ppermute | solution.py:537
  47.4 1.1 %collective-permute-start.16 = (f32[64,1024]{1,0:T(8,128)S(1)}, f32[64,1024]{1,0:T(8,128)S(1)}, u32[]{:S(2)}, u32[]{:S(2)}) collective-permute-start(f32[64,1024]{1,0:T(8,128)S(1)} %get-tuple-element.30), channel_id=1, source_target_pairs={{0,2},{1,3},{2,0},{3,1},{4,6},{5,7},{6,4},{7,5},{8,10},{9,11},{10,... | collective-permute-start | bytes 786440 | tf_op jit(solution)/shard_map/ppermute | solution.py:481
  48.5 1.0 %collective-permute-start.25 = (f32[8,1024]{1,0:T(8,128)S(1)}, f32[8,1024]{1,0:T(8,128)S(1)}, u32[]{:S(2)}, u32[]{:S(2)}) collective-permute-start(f32[8,1024]{1,0:T(8,128)S(1)} %get-tuple-element.38), channel_id=1, source_target_pairs={{0,2},{1,3},{2,0},{3,1},{4,6},{5,7},{6,4},{7,5},{8,10},{9,11},{10,... | collective-permute-start | bytes 98312 | tf_op jit(solution)/shard_map/ppermute | solution.py:481
  49.5 2.6 %collective-permute-start.15 = (f32[8,128]{1,0:T(8,128)S(1)}, f32[8,128]{1,0:T(8,128)S(1)}, u32[]{:S(2)}, u32[]{:S(2)}) collective-permute-start(f32[8,128]{1,0:T(8,128)S(1)} %add_add_fusion.3), channel_id=1, source_target_pairs={{0,12},{4,8},{8,4},{12,0},{1,13},{5,9},{9,5},{13,1},{2,14},{6,10},... | collective-permute-start | bytes 12296 | tf_op jit(solution)/shard_map/ppermute | solution.py:490
  52.1 4.3 %collective-permute-done.16 = f32[64,1024]{1,0:T(8,128)S(1)} collective-permute-done((f32[64,1024]{1,0:T(8,128)S(1)}, f32[64,1024]{1,0:T(8,128)S(1)}, u32[]{:S(2)}, u32[]{:S(2)}) %collective-permute-start.16) | collective-permute-done | bytes 262176 | tf_op jit(solution)/shard_map/ppermute | solution.py:481
  56.4 0.9 %collective-permute-start.13 = (f32[8,128]{1,0:T(8,128)S(1)}, f32[8,128]{1,0:T(8,128)S(1)}, u32[]{:S(2)}, u32[]{:S(2)}) collective-permute-start(f32[8,128]{1,0:T(8,128)S(1)} %add_add_fusion.3), channel_id=1, source_target_pairs={{0,4},{4,0},{8,12},{12,8},{1,5},{5,1},{9,13},{13,9},{2,6},{6,2},{1... | collective-permute-start | bytes 12296 | tf_op jit(solution)/shard_map/ppermute | solution.py:490
  57.4 2.4 %second.1 = (f32[64,1024]{1,0:T(8,128)S(1)}, f32[64,1024]{1,0:T(8,128)S(1)}, f32[64,1024]{1,0:T(8,128)S(1)}) custom-call(s32[3]{0:T(128)S(1)} %pad_add_fusion.place.refs_0_, f32[64,1024]{1,0:T(8,128)S(1)} %get-tuple-element.32.image, f32[64,1024]{1,0:T(8,128)S(1)} %collective-permute-done.18.near_image, f32[64,128]{1,0:T(8,128)S(1)} %select_select_fusion.halo, ...), custom_call_target="tpu_custom_call" | custom-call | tf_op jit(solution)/shard_map/second/pallas_call | solution.py:467
  60.5 1.2 %products.1 = (f32[32,2048]{1,0:T(8,128)S(1)}, f32[32,2048]{1,0:T(8,128)S(1)}, f32[8,128]{1,0:T(8,128)S(1)}) custom-call(s32[3]{0:T(128)S(1)} %pad_add_fusion.place.refs_0_, f32[8,128]{1,0:T(8,128)S(1)} %add_add_fusion.2.totals.first_totals, f32[32,2048]{1,0:T(8,128)S(1)} %copy-done.1, f32[32,1024]{1,0:T(8,128)S(1)} %get-tuple-element.47.own_image, ...), custom_call_target="tpu_custom_call" | custom-call | tf_op jit(solution)/shard_map/products/pallas_call | solution.py:467
  61.7 1.4 %collective-permute-start.28 = (f32[8,128]{1,0:T(8,128)S(1)}, f32[8,128]{1,0:T(8,128)S(1)}, u32[]{:S(2)}, u32[]{:S(2)}) collective-permute-start(f32[8,128]{1,0:T(8,128)S(1)} %get-tuple-element.39), channel_id=1, source_target_pairs={{0,3},{1,2},{2,1},{3,0},{4,7},{5,6},{6,5},{7,4},{8,11},{9,10},{10,... | collective-permute-start | bytes 12296 | tf_op jit(solution)/shard_map/ppermute | solution.py:490
  63.6 4.7 %collective-permute-done.28 = f32[8,128]{1,0:T(8,128)S(1)} collective-permute-done((f32[8,128]{1,0:T(8,128)S(1)}, f32[8,128]{1,0:T(8,128)S(1)}, u32[]{:S(2)}, u32[]{:S(2)}) %collective-permute-start.28) | collective-permute-done | bytes 4128 | tf_op jit(solution)/shard_map/ppermute | solution.py:490
  68.8 0.9 %collective-permute-start.31 = (f32[8,128]{1,0:T(8,128)S(1)}, f32[8,128]{1,0:T(8,128)S(1)}, u32[]{:S(2)}, u32[]{:S(2)}) collective-permute-start(f32[8,128]{1,0:T(8,128)S(1)} %add_add_fusion.1), channel_id=1, source_target_pairs={{0,12},{4,8},{8,4},{12,0},{1,13},{5,9},{9,5},{13,1},{2,14},{6,10},... | collective-permute-start | bytes 12296 | tf_op jit(solution)/shard_map/ppermute | solution.py:490
  69.7 1.8 %collective-permute-start.30 = (f32[8,128]{1,0:T(8,128)S(1)}, f32[8,128]{1,0:T(8,128)S(1)}, u32[]{:S(2)}, u32[]{:S(2)}) collective-permute-start(f32[8,128]{1,0:T(8,128)S(1)} %add_add_fusion.1), channel_id=1, source_target_pairs={{0,8},{4,12},{8,0},{12,4},{1,9},{5,13},{9,1},{13,5},{2,10},{6,14},... | collective-permute-start | bytes 12296 | tf_op jit(solution)/shard_map/ppermute | solution.py:490
  71.5 1.8 %collective-permute-start.29 = (f32[8,128]{1,0:T(8,128)S(1)}, f32[8,128]{1,0:T(8,128)S(1)}, u32[]{:S(2)}, u32[]{:S(2)}) collective-permute-start(f32[8,128]{1,0:T(8,128)S(1)} %add_add_fusion.1), channel_id=1, source_target_pairs={{0,4},{4,0},{8,12},{12,8},{1,5},{5,1},{9,13},{13,9},{2,6},{6,2},{1... | collective-permute-start | bytes 12296 | tf_op jit(solution)/shard_map/ppermute | solution.py:490
  73.3 0.7 fusion.1
  74.3 0.8 %collective-permute-done.29 = f32[8,128]{1,0:T(8,128)S(1)} collective-permute-done((f32[8,128]{1,0:T(8,128)S(1)}, f32[8,128]{1,0:T(8,128)S(1)}, u32[]{:S(2)}, u32[]{:S(2)}) %collective-permute-start.29) | collective-permute-done | bytes 4128 | tf_op jit(solution)/shard_map/ppermute | solution.py:490
  75.7 0.6 copy-done.17
  76.4 2.1 %last.1 = (f32[32,2048]{1,0:T(8,128)}, f32[32,2048]{1,0:T(8,128)}) custom-call(s32[3]{0:T(128)} %copy-done.11, f32[8,128]{1,0:T(8,128)} %copy-done.8, f32[8,128]{1,0:T(8,128)} %add_add_fusion.last_totals, f32[32,2048]{1,0:T(8,128)} %vector.5, f32[32,2048]{1,0:T(8,128)} %copy-done.4, f32[32,2048]{1,0:T(8,128)} %copy-done.5, ...), custom_call_target="tpu_custom_call" | custom-call | tf_op jit(solution)/shard_map/last/pallas_call | solution.py:616
  (78 shorter events, 4.7 us)
Async XLA Ops:
  0.6 16.7 %collective-permute-start.9 = (f32[32,2048]{1,0:T(8,128)}, f32[32,2048]{1,0:T(8,128)S(1)}, u32[]{:S(2)}, u32[]{:S(2)}) collective-permute-start(f32[32,2048]{1,0:T(8,128)} %own_operating.1), channel_id=1, source_target_pairs={{0,1},{1,0},{2,3},{3,2},{4,5},{5,4},{6,7},{7,6},{8,9},{9,8},{10,11... | collective-permute-start | bytes 786440 | tf_op jit(solution)/shard_map/ppermute | solution.py:481
  1.1 13.9 %collective-permute-start = (f32[32,2048]{1,0:T(8,128)}, f32[32,2048]{1,0:T(8,128)S(1)}, u32[]{:S(2)}, u32[]{:S(2)}) collective-permute-start(f32[32,2048]{1,0:T(8,128)} %vector.5), channel_id=1, source_target_pairs={{0,2},{1,3},{2,0},{3,1},{4,6},{5,7},{6,4},{7,5},{8,10},{9,11},{10,... | collective-permute-start | bytes 786440 | tf_op jit(solution)/shard_map/ppermute | solution.py:481
  3.8 1.0 %copy-start = (f32[32,2048]{1,0:T(8,128)S(1)}, f32[32,2048]{1,0:T(8,128)}, u32[]{:S(2)}) copy-start(f32[32,2048]{1,0:T(8,128)} %vector.5) | copy-start | bytes 786436
  4.7 0.9 %copy-start.2 = (f32[32,2048]{1,0:T(8,128)S(1)}, f32[32,2048]{1,0:T(8,128)}, u32[]{:S(2)}) copy-start(f32[32,2048]{1,0:T(8,128)} %own_operating.1) | copy-start | bytes 786436
  5.7 0.7 copy-start.15
  7.0 53.5 %copy-start.11 = (s32[3]{0:T(128)}, s32[3]{0:T(128)S(1)}, u32[]{:S(2)}) copy-start(s32[3]{0:T(128)S(1)} %pad_add_fusion.place.refs_0_) | copy-start | bytes 40
  8.5 6.5 %collective-permute-start.5 = (f32[64,128]{1,0:T(8,128)S(1)}, f32[64,128]{1,0:T(8,128)S(1)}, u32[]{:S(2)}, u32[]{:S(2)}) collective-permute-start(f32[64,128]{1,0:T(8,128)S(1)} %get-tuple-element.23), channel_id=1, source_target_pairs={{0,4},{1,5},{2,6},{3,7},{4,8},{5,9},{6,10},{7,11},{8,12},{9,13},{1... | collective-permute-start | bytes 98312 | tf_op jit(solution)/shard_map/ppermute | solution.py:537
  10.1 5.4 %collective-permute-start.4 = (f32[64,128]{1,0:T(8,128)S(1)}, f32[64,128]{1,0:T(8,128)S(1)}, u32[]{:S(2)}, u32[]{:S(2)}) collective-permute-start(f32[64,128]{1,0:T(8,128)S(1)} %get-tuple-element.23), channel_id=1, source_target_pairs={{0,8},{1,9},{2,10},{3,11},{4,12},{5,13},{6,14},{7,15},{8,0},{9,1},... | collective-permute-start | bytes 98312 | tf_op jit(solution)/shard_map/ppermute | solution.py:537
  12.7 3.9 %collective-permute-start.3 = (f32[64,128]{1,0:T(8,128)S(1)}, f32[64,128]{1,0:T(8,128)S(1)}, u32[]{:S(2)}, u32[]{:S(2)}) collective-permute-start(f32[64,128]{1,0:T(8,128)S(1)} %get-tuple-element.23), channel_id=1, source_target_pairs={{0,12},{1,13},{2,14},{3,15},{4,0},{5,1},{6,2},{7,3},{8,4},{9,5},{1... | collective-permute-start | bytes 98312 | tf_op jit(solution)/shard_map/ppermute | solution.py:537
  15.0 15.6 %collective-permute-start.1 = (f32[32,2048]{1,0:T(8,128)}, f32[32,2048]{1,0:T(8,128)S(1)}, u32[]{:S(2)}, u32[]{:S(2)}) collective-permute-start(f32[32,2048]{1,0:T(8,128)} %vector.5), channel_id=1, source_target_pairs={{0,1},{1,0},{2,3},{3,2},{4,5},{5,4},{6,7},{7,6},{8,9},{9,8},{10,11... | collective-permute-start | bytes 786440 | tf_op jit(solution)/shard_map/ppermute | solution.py:481
  15.1 15.5 %collective-permute-start.2 = (f32[32,2048]{1,0:T(8,128)S(1)}, f32[32,2048]{1,0:T(8,128)S(1)}, u32[]{:S(2)}, u32[]{:S(2)}) collective-permute-start(f32[32,2048]{1,0:T(8,128)S(1)} %collective-permute-done.refs_2_), channel_id=1, source_target_pairs={{0,1},{1,0},{2,3},{3,2},{4,5},{5,4},{6,7},{7,6},{8,9},{9,8},{10,11... | collective-permute-start | bytes 786440 | tf_op jit(solution)/shard_map/ppermute | solution.py:481
  16.6 13.9 %collective-permute-start.8 = (f32[64,128]{1,0:T(8,128)S(1)}, f32[64,128]{1,0:T(8,128)S(1)}, u32[]{:S(2)}, u32[]{:S(2)}) collective-permute-start(f32[64,128]{1,0:T(8,128)S(1)} %select_select_fusion.1.refs_5_), channel_id=1, source_target_pairs={{0,3},{1,2},{2,1},{3,0},{4,7},{5,6},{6,5},{7,4},{8,11},{9,10},{10,... | collective-permute-start | bytes 98312 | tf_op jit(solution)/shard_map/ppermute | solution.py:481
  16.7 13.9 %collective-permute-start.7 = (f32[64,128]{1,0:T(8,128)S(1)}, f32[64,128]{1,0:T(8,128)S(1)}, u32[]{:S(2)}, u32[]{:S(2)}) collective-permute-start(f32[64,128]{1,0:T(8,128)S(1)} %select_select_fusion.1.refs_5_), channel_id=1, source_target_pairs={{0,1},{1,0},{2,3},{3,2},{4,5},{5,4},{6,7},{7,6},{8,9},{9,8},{10,11... | collective-permute-start | bytes 98312 | tf_op jit(solution)/shard_map/ppermute | solution.py:481
  17.4 13.2 %collective-permute-start.6 = (f32[64,128]{1,0:T(8,128)S(1)}, f32[64,128]{1,0:T(8,128)S(1)}, u32[]{:S(2)}, u32[]{:S(2)}) collective-permute-start(f32[64,128]{1,0:T(8,128)S(1)} %select_select_fusion.1.refs_5_), channel_id=1, source_target_pairs={{0,2},{1,3},{2,0},{3,1},{4,6},{5,7},{6,4},{7,5},{8,10},{9,11},{10,... | collective-permute-start | bytes 98312 | tf_op jit(solution)/shard_map/ppermute | solution.py:481
  19.7 0.9 %copy-start.3 = (f32[32,2048]{1,0:T(8,128)S(1)}, f32[32,2048]{1,0:T(8,128)}, u32[]{:S(2)}) copy-start(f32[32,2048]{1,0:T(8,128)} %own_operating.1) | copy-start | bytes 786436
  20.7 0.8 %copy-start.6 = (s32[8,2048]{1,0:T(8,128)S(1)}, s32[8,2048]{1,0:T(8,128)}, u32[]{:S(2)}) copy-start(s32[8,2048]{1,0:T(8,128)} %neighbours.1) | copy-start | bytes 196612
  21.5 0.8 %copy-start.7 = (f32[8,2048]{1,0:T(8,128)S(1)}, f32[8,2048]{1,0:T(8,128)}, u32[]{:S(2)}) copy-start(f32[8,2048]{1,0:T(8,128)} %weights.1) | copy-start | bytes 196612
  22.3 0.7 copy-start.12
  30.6 1.0 %copy-start.1 = (f32[32,2048]{1,0:T(8,128)S(1)}, f32[32,2048]{1,0:T(8,128)}, u32[]{:S(2)}) copy-start(f32[32,2048]{1,0:T(8,128)} %vector.5) | copy-start | bytes 786436
  31.6 0.7 copy-start.9
  32.3 0.7 copy-start.10
  36.7 9.4 %collective-permute-start.24 = (f32[64,128]{1,0:T(8,128)S(1)}, f32[64,128]{1,0:T(8,128)S(1)}, u32[]{:S(2)}, u32[]{:S(2)}) collective-permute-start(f32[64,128]{1,0:T(8,128)S(1)} %get-tuple-element.33), channel_id=1, source_target_pairs={{0,5},{1,4},{2,7},{3,6},{4,9},{5,8},{6,11},{7,10},{8,13},{9,12},{1... | collective-permute-start | bytes 98312 | tf_op jit(solution)/shard_map/ppermute | solution.py:537
  36.8 10.6 %collective-permute-start.23 = (f32[64,128]{1,0:T(8,128)S(1)}, f32[64,128]{1,0:T(8,128)S(1)}, u32[]{:S(2)}, u32[]{:S(2)}) collective-permute-start(f32[64,128]{1,0:T(8,128)S(1)} %get-tuple-element.33), channel_id=1, source_target_pairs={{0,4},{1,5},{2,6},{3,7},{4,8},{5,9},{6,10},{7,11},{8,12},{9,13},{1... | collective-permute-start | bytes 98312 | tf_op jit(solution)/shard_map/ppermute | solution.py:537
  37.9 3.0 %collective-permute-start.12 = (f32[8,128]{1,0:T(8,128)S(1)}, f32[8,128]{1,0:T(8,128)S(1)}, u32[]{:S(2)}, u32[]{:S(2)}) collective-permute-start(f32[8,128]{1,0:T(8,128)S(1)} %get-tuple-element.28), channel_id=1, source_target_pairs={{0,3},{1,2},{2,1},{3,0},{4,7},{5,6},{6,5},{7,4},{8,11},{9,10},{10,... | collective-permute-start | bytes 12296 | tf_op jit(solution)/shard_map/ppermute | solution.py:490
  38.5 5.1 %collective-permute-start.11 = (f32[8,128]{1,0:T(8,128)S(1)}, f32[8,128]{1,0:T(8,128)S(1)}, u32[]{:S(2)}, u32[]{:S(2)}) collective-permute-start(f32[8,128]{1,0:T(8,128)S(1)} %get-tuple-element.28), channel_id=1, source_target_pairs={{0,2},{1,3},{2,0},{3,1},{4,6},{5,7},{6,4},{7,5},{8,10},{9,11},{10,... | collective-permute-start | bytes 12296 | tf_op jit(solution)/shard_map/ppermute | solution.py:490
  40.0 4.7 %collective-permute-start.10 = (f32[8,128]{1,0:T(8,128)S(1)}, f32[8,128]{1,0:T(8,128)S(1)}, u32[]{:S(2)}, u32[]{:S(2)}) collective-permute-start(f32[8,128]{1,0:T(8,128)S(1)} %get-tuple-element.28), channel_id=1, source_target_pairs={{0,1},{1,0},{2,3},{3,2},{4,5},{5,4},{6,7},{7,6},{8,9},{9,8},{10,11... | collective-permute-start | bytes 12296 | tf_op jit(solution)/shard_map/ppermute | solution.py:490
  40.9 7.6 %collective-permute-start.22 = (f32[64,128]{1,0:T(8,128)S(1)}, f32[64,128]{1,0:T(8,128)S(1)}, u32[]{:S(2)}, u32[]{:S(2)}) collective-permute-start(f32[64,128]{1,0:T(8,128)S(1)} %get-tuple-element.33), channel_id=1, source_target_pairs={{0,9},{1,8},{2,11},{3,10},{4,13},{5,12},{6,15},{7,14},{8,1},{9,0},... | collective-permute-start | bytes 98312 | tf_op jit(solution)/shard_map/ppermute | solution.py:537
  43.6 5.9 %collective-permute-start.21 = (f32[64,128]{1,0:T(8,128)S(1)}, f32[64,128]{1,0:T(8,128)S(1)}, u32[]{:S(2)}, u32[]{:S(2)}) collective-permute-start(f32[64,128]{1,0:T(8,128)S(1)} %get-tuple-element.33), channel_id=1, source_target_pairs={{0,8},{1,9},{2,10},{3,11},{4,12},{5,13},{6,14},{7,15},{8,0},{9,1},... | collective-permute-start | bytes 98312 | tf_op jit(solution)/shard_map/ppermute | solution.py:537
  44.7 4.8 %collective-permute-start.20 = (f32[64,128]{1,0:T(8,128)S(1)}, f32[64,128]{1,0:T(8,128)S(1)}, u32[]{:S(2)}, u32[]{:S(2)}) collective-permute-start(f32[64,128]{1,0:T(8,128)S(1)} %get-tuple-element.33), channel_id=1, source_target_pairs={{0,13},{1,12},{2,15},{3,14},{4,1},{5,0},{6,3},{7,2},{8,5},{9,4},{1... | collective-permute-start | bytes 98312 | tf_op jit(solution)/shard_map/ppermute | solution.py:537
  46.1 6.1 %collective-permute-start.19 = (f32[64,128]{1,0:T(8,128)S(1)}, f32[64,128]{1,0:T(8,128)S(1)}, u32[]{:S(2)}, u32[]{:S(2)}) collective-permute-start(f32[64,128]{1,0:T(8,128)S(1)} %get-tuple-element.33), channel_id=1, source_target_pairs={{0,12},{1,13},{2,14},{3,15},{4,0},{5,1},{6,2},{7,3},{8,4},{9,5},{1... | collective-permute-start | bytes 98312 | tf_op jit(solution)/shard_map/ppermute | solution.py:537
  47.4 9.0 %collective-permute-start.16 = (f32[64,1024]{1,0:T(8,128)S(1)}, f32[64,1024]{1,0:T(8,128)S(1)}, u32[]{:S(2)}, u32[]{:S(2)}) collective-permute-start(f32[64,1024]{1,0:T(8,128)S(1)} %get-tuple-element.30), channel_id=1, source_target_pairs={{0,2},{1,3},{2,0},{3,1},{4,6},{5,7},{6,4},{7,5},{8,10},{9,11},{10,... | collective-permute-start | bytes 786440 | tf_op jit(solution)/shard_map/ppermute | solution.py:481
  48.5 11.9 %collective-permute-start.25 = (f32[8,1024]{1,0:T(8,128)S(1)}, f32[8,1024]{1,0:T(8,128)S(1)}, u32[]{:S(2)}, u32[]{:S(2)}) collective-permute-start(f32[8,1024]{1,0:T(8,128)S(1)} %get-tuple-element.38), channel_id=1, source_target_pairs={{0,2},{1,3},{2,0},{3,1},{4,6},{5,7},{6,4},{7,5},{8,10},{9,11},{10,... | collective-permute-start | bytes 98312 | tf_op jit(solution)/shard_map/ppermute | solution.py:481
  49.5 7.8 %collective-permute-start.18 = (f32[64,1024]{1,0:T(8,128)S(1)}, f32[64,1024]{1,0:T(8,128)S(1)}, u32[]{:S(2)}, u32[]{:S(2)}) collective-permute-start(f32[64,1024]{1,0:T(8,128)S(1)} %get-tuple-element.32.image), channel_id=1, source_target_pairs={{0,1},{1,0},{2,3},{3,2},{4,5},{5,4},{6,7},{7,6},{8,9},{9,8},{10,11... | collective-permute-start | bytes 786440 | tf_op jit(solution)/shard_map/ppermute | solution.py:481
  49.5 10.4 %collective-permute-start.15 = (f32[8,128]{1,0:T(8,128)S(1)}, f32[8,128]{1,0:T(8,128)S(1)}, u32[]{:S(2)}, u32[]{:S(2)}) collective-permute-start(f32[8,128]{1,0:T(8,128)S(1)} %add_add_fusion.3), channel_id=1, source_target_pairs={{0,12},{4,8},{8,4},{12,0},{1,13},{5,9},{9,5},{13,1},{2,14},{6,10},... | collective-permute-start | bytes 12296 | tf_op jit(solution)/shard_map/ppermute | solution.py:490
  52.1 8.3 %collective-permute-start.14 = (f32[8,128]{1,0:T(8,128)S(1)}, f32[8,128]{1,0:T(8,128)S(1)}, u32[]{:S(2)}, u32[]{:S(2)}) collective-permute-start(f32[8,128]{1,0:T(8,128)S(1)} %add_add_fusion.3), channel_id=1, source_target_pairs={{0,8},{4,12},{8,0},{12,4},{1,9},{5,13},{9,1},{13,5},{2,10},{6,14},... | collective-permute-start | bytes 12296 | tf_op jit(solution)/shard_map/ppermute | solution.py:490
  56.4 4.0 %collective-permute-start.13 = (f32[8,128]{1,0:T(8,128)S(1)}, f32[8,128]{1,0:T(8,128)S(1)}, u32[]{:S(2)}, u32[]{:S(2)}) collective-permute-start(f32[8,128]{1,0:T(8,128)S(1)} %add_add_fusion.3), channel_id=1, source_target_pairs={{0,4},{4,0},{8,12},{12,8},{1,5},{5,1},{9,13},{13,9},{2,6},{6,2},{1... | collective-permute-start | bytes 12296 | tf_op jit(solution)/shard_map/ppermute | solution.py:490
  57.3 3.1 %collective-permute-start.17 = (f32[32,1024]{1,0:T(8,128)S(1)}, f32[32,1024]{1,0:T(8,128)S(1)}, u32[]{:S(2)}, u32[]{:S(2)}) collective-permute-start(f32[32,1024]{1,0:T(8,128)S(1)} %get-tuple-element.46), channel_id=1, source_target_pairs={{0,1},{1,0},{2,3},{3,2},{4,5},{5,4},{6,7},{7,6},{8,9},{9,8},{10,11... | collective-permute-start | bytes 393224 | tf_op jit(solution)/shard_map/ppermute | solution.py:481
  59.9 13.4 %collective-permute-start.32 = (f32[64,1024]{1,0:T(8,128)S(1)}, f32[64,1024]{1,0:T(8,128)S(1)}, u32[]{:S(2)}, u32[]{:S(2)}) collective-permute-start(f32[64,1024]{1,0:T(8,128)S(1)} %get-tuple-element.43), channel_id=1, source_target_pairs={{0,2},{1,3},{2,0},{3,1},{4,6},{5,7},{6,4},{7,5},{8,10},{9,11},{10,... | collective-permute-start | bytes 786440 | tf_op jit(solution)/shard_map/ppermute | solution.py:481
  60.4 15.3 %copy-start.8 = (f32[8,128]{1,0:T(8,128)}, f32[8,128]{1,0:T(8,128)S(1)}, u32[]{:S(2)}) copy-start(f32[8,128]{1,0:T(8,128)S(1)} %add_add_fusion.2.totals.first_totals) | copy-start | bytes 12292
  61.7 11.7 %copy-start.4 = (f32[32,2048]{1,0:T(8,128)}, f32[32,2048]{1,0:T(8,128)S(1)}, u32[]{:S(2)}) copy-start(f32[32,2048]{1,0:T(8,128)S(1)} %get-tuple-element.40.residue) | copy-start | bytes 786436
  61.7 12.3 %copy-start.5 = (f32[32,2048]{1,0:T(8,128)}, f32[32,2048]{1,0:T(8,128)S(1)}, u32[]{:S(2)}) copy-start(f32[32,2048]{1,0:T(8,128)S(1)} %get-tuple-element.41.base) | copy-start | bytes 786436
  61.7 6.6 %collective-permute-start.28 = (f32[8,128]{1,0:T(8,128)S(1)}, f32[8,128]{1,0:T(8,128)S(1)}, u32[]{:S(2)}, u32[]{:S(2)}) collective-permute-start(f32[8,128]{1,0:T(8,128)S(1)} %get-tuple-element.39), channel_id=1, source_target_pairs={{0,3},{1,2},{2,1},{3,0},{4,7},{5,6},{6,5},{7,4},{8,11},{9,10},{10,... | collective-permute-start | bytes 12296 | tf_op jit(solution)/shard_map/ppermute | solution.py:490
  63.1 5.7 %collective-permute-start.27 = (f32[8,128]{1,0:T(8,128)S(1)}, f32[8,128]{1,0:T(8,128)S(1)}, u32[]{:S(2)}, u32[]{:S(2)}) collective-permute-start(f32[8,128]{1,0:T(8,128)S(1)} %get-tuple-element.39), channel_id=1, source_target_pairs={{0,2},{1,3},{2,0},{3,1},{4,6},{5,7},{6,4},{7,5},{8,10},{9,11},{10,... | collective-permute-start | bytes 12296 | tf_op jit(solution)/shard_map/ppermute | solution.py:490
  63.4 5.4 %collective-permute-start.26 = (f32[8,128]{1,0:T(8,128)S(1)}, f32[8,128]{1,0:T(8,128)S(1)}, u32[]{:S(2)}, u32[]{:S(2)}) collective-permute-start(f32[8,128]{1,0:T(8,128)S(1)} %get-tuple-element.39), channel_id=1, source_target_pairs={{0,1},{1,0},{2,3},{3,2},{4,5},{5,4},{6,7},{7,6},{8,9},{9,8},{10,11... | collective-permute-start | bytes 12296 | tf_op jit(solution)/shard_map/ppermute | solution.py:490
  68.8 5.5 %collective-permute-start.31 = (f32[8,128]{1,0:T(8,128)S(1)}, f32[8,128]{1,0:T(8,128)S(1)}, u32[]{:S(2)}, u32[]{:S(2)}) collective-permute-start(f32[8,128]{1,0:T(8,128)S(1)} %add_add_fusion.1), channel_id=1, source_target_pairs={{0,12},{4,8},{8,4},{12,0},{1,13},{5,9},{9,5},{13,1},{2,14},{6,10},... | collective-permute-start | bytes 12296 | tf_op jit(solution)/shard_map/ppermute | solution.py:490
  69.7 4.6 %collective-permute-start.30 = (f32[8,128]{1,0:T(8,128)S(1)}, f32[8,128]{1,0:T(8,128)S(1)}, u32[]{:S(2)}, u32[]{:S(2)}) collective-permute-start(f32[8,128]{1,0:T(8,128)S(1)} %add_add_fusion.1), channel_id=1, source_target_pairs={{0,8},{4,12},{8,0},{12,4},{1,9},{5,13},{9,1},{13,5},{2,10},{6,14},... | collective-permute-start | bytes 12296 | tf_op jit(solution)/shard_map/ppermute | solution.py:490
  71.5 3.6 %collective-permute-start.29 = (f32[8,128]{1,0:T(8,128)S(1)}, f32[8,128]{1,0:T(8,128)S(1)}, u32[]{:S(2)}, u32[]{:S(2)}) collective-permute-start(f32[8,128]{1,0:T(8,128)S(1)} %add_add_fusion.1), channel_id=1, source_target_pairs={{0,4},{4,0},{8,12},{12,8},{1,5},{5,1},{9,13},{13,9},{2,6},{6,2},{1... | collective-permute-start | bytes 12296 | tf_op jit(solution)/shard_map/ppermute | solution.py:490
  74.0 1.7 %collective-permute-start.33 = (f32[32,1024]{1,0:T(8,128)S(1)}, f32[32,1024]{1,0:T(8,128)S(1)}, u32[]{:S(2)}, u32[]{:S(2)}) collective-permute-start(f32[32,1024]{1,0:T(8,128)S(1)} %get-tuple-element.44), channel_id=1, source_target_pairs={{0,1},{1,0},{2,3},{3,2},{4,5},{5,4},{6,7},{7,6},{8,9},{9,8},{10,11... | collective-permute-start | bytes 393224 | tf_op jit(solution)/shard_map/ppermute | solution.py:481
  (4 other events, 2.6 us)

commit v2 on v1

v2 whole, which is shorter than its diff:
```python
import functools
import math

import jax
import jax.numpy as jnp
import numpy as np
from jax import lax
from jax.experimental import pallas as pl
from jax.experimental.pallas import tpu as pltpu
from jax.sharding import PartitionSpec as P

CAP = 16
EPSILON = 1e-06
LANES = 128
BF16 = jnp.bfloat16
F32 = jnp.float32
I32 = jnp.int32


def spectral_tables(length):
    indices = np.arange(length)
    frequency = np.where(indices == 1, length // 2, indices // 2)
    angles = (indices[:, None] * frequency[None, :] % length) * (2.0 * math.pi / length)
    cosine_column = (indices % 2 == 0) | (indices == 1)
    synthesis = np.where(cosine_column[None, :], np.cos(angles), np.sin(angles))
    factor = np.where(indices < 2, 1.0 / length, 2.0 / length)
    analysis = synthesis.T * factor[:, None]
    turn = np.zeros((length, length))
    for pair in range(length // 2):
        turn[2 * pair, 2 * pair + 1] = pair / (length // 2)
        turn[2 * pair + 1, 2 * pair] = -pair / (length // 2)
    return synthesis, analysis, synthesis @ turn


def halves(table):
    high = table.astype(np.float32).astype(BF16)
    low = (table - high.astype(np.float64)).astype(np.float32).astype(BF16)
    return np.stack([high, low])


def piece_order(count):
    masks, bit = [0], count // 2
    while bit:
        masks = masks + [mask ^ bit for mask in masks]
        bit //= 2
    return masks


def transform_tables(length, parts):
    synthesis, analysis, slope = spectral_tables(length)
    rows = length // parts
    forward, back = [], []
    for place in range(parts):
        times = np.arange(place // 2 * 2 * rows, (place // 2 + 1) * 2 * rows)
        block = lambda owner: np.arange(owner * rows, (owner + 1) * rows)
        coefs = np.concatenate([block(place ^ mask) for mask in piece_order(parts)])
        forward.append(
            np.concatenate(
                [
                    synthesis[np.ix_(times, coefs)],
                    slope[np.ix_(times, coefs)],
                    analysis[np.ix_(coefs, times)].T,
                ]
            )
        )
        sent = np.concatenate(
            [block(place ^ (2 * group) ^ side) for group in range(parts // 2) for side in (0, 1)]
        )
        back.append(analysis[np.ix_(sent, times)])
    return (
        np.moveaxis(halves(np.stack(forward)), 0, 1),
        np.moveaxis(halves(np.stack(back)), 0, 1),
    )


def split(values):
    high = values.astype(BF16)
    return high, (values - high.astype(F32)).astype(BF16)


def dot(first, second):
    return jnp.dot(first, second, preferred_element_type=F32)


def dot_split(first, second):
    (first_high, first_low), (second_high, second_low) = first, second
    rows = first_high.shape[0]
    both = dot(jnp.concatenate([first_high, first_low], axis=0), second_high)
    return both[:rows] + both[rows:] + dot(first_high, second_low)


def lane_sums(values):
    blocks = values.shape[1] // LANES
    total = values[:, :LANES]
    for block in range(1, blocks):
        total = total + values[:, block * LANES : (block + 1) * LANES]
    return jnp.sum(total, axis=0, keepdims=True)


def half_of(side, half):
    return pl.ds(pl.multiple_of(side * half, LANES), half)


def scalar_sum(values):
    return jnp.sum(lane_sums(values), axis=1, keepdims=True)


def pick(values, picked):
    high, _ = split(values)
    middle, low = split(values - high.astype(F32))
    rows = values.shape[0]
    found = dot(jnp.concatenate([high, middle, low], axis=0), picked)
    return found[:rows] + (found[rows : 2 * rows] + found[2 * rows :])


def conductance(operating, table):
    points = table.shape[1]
    spread = jnp.concatenate([table, jnp.zeros((1, LANES - points), F32)], axis=1)
    spread = jnp.broadcast_to(spread, (operating.shape[0], LANES))
    pieces = []
    for block in range(operating.shape[1] // LANES):
        scaled = (operating[:, block * LANES : (block + 1) * LANES] + 4.0) * ((points - 1) / 8.0)
        knot = jnp.clip(jnp.floor(scaled), 0.0, points - 2.0)
        weight = scaled - knot
        place = knot.astype(I32)
        left = jnp.take_along_axis(spread, place, axis=1, mode="promise_in_bounds")
        right = jnp.take_along_axis(spread, place + 1, axis=1, mode="promise_in_bounds")
        pieces.append(left + weight * (right - left))
    return jnp.concatenate(pieces, axis=1)


def prepare_kernel(
    place,
    send_list,
    boundary,
    near_operating_in,
    operating_in,
    neighbours_in,
    weights_in,
    degree_in,
    linear_in,
    capacity_in,
    table_in,
    vector_in,
    forward_in,
    back_in,
    coupling_high,
    coupling_low,
    conductances,
    picked,
    linear,
    capacity,
    capacity_all,
    cut_halo,
    vector,
    forward,
    back,
    near_operating,
    operating,
    neighbours,
    weights,
    degree,
    linear_all,
    table,
    entry_rows,
    weight_rows,
    copied,
):
    slots, nodes = neighbours.shape
    sources, width = coupling_high.shape
    lanes = picked.shape[1]
    half = width - lanes
    node_groups = send_list.shape[0] // CAP
    side, part = place[0] % 2, place[1]
    rows = operating.shape[0]
    copies = [
        pltpu.make_async_copy(source, target, copied.at[index])
        for index, (source, target) in enumerate(
            [
                (neighbours_in, neighbours),
                (weights_in, weights),
                (degree_in, degree),
                (linear_in, linear_all),
                (capacity_in, capacity_all),
                (table_in, table),
                (operating_in, operating),
                (near_operating_in, near_operating),
                (vector_in, vector),
                (forward_in.at[place[0]], forward),
                (back_in.at[place[0]], back),
            ]
        )
    ]
    for copy in copies:
        copy.start()

    lane = lax.broadcasted_iota(I32, (8, lanes), 1)

    def name(slot, found):
        target = lax.rem(part + slot // CAP + 1, node_groups)
        node = boundary[send_list[target * CAP + slot % CAP]]
        return jnp.where(lane == slot, node, found)

    cut_nodes = lax.fori_loop(
        0, (node_groups - 1) * CAP, name, jnp.full((8, lanes), -1, I32), unroll=8
    )
    hit = lax.broadcasted_iota(I32, (nodes, lanes), 0) == cut_nodes[:1]
    picked[...] = jnp.where(hit, 1.0, 0.0).astype(BF16)

    for copy in copies[:6]:
        copy.wait()
    mine = half_of(side, half)
    entry = neighbours[...]
    remote = entry - nodes
    distance = part - (remote >> 4)
    distance = jnp.where(distance < 0, distance + node_groups, distance)
    entry = jnp.where(remote < 0, entry, nodes + (distance - 1) * CAP + (remote & 15))
    live = lax.broadcasted_iota(I32, (slots, nodes), 0) < degree[...]
    neighbours[...] = entry
    weights[...] = jnp.where(live, weights[...], 0.0)
    columns = jnp.concatenate(
        [
            entry.astype(F32),
            weights[...],
            linear_all[...],
            capacity_all[...],
            jnp.zeros((6, nodes), F32),
        ],
        axis=0,
    )
    at_cut = pick(columns, picked[...])
    linear[:, :half] = linear_all[:, mine]
    linear[:, half:] = at_cut[2 * slots : 2 * slots + 1]
    capacity[:, :half] = capacity_all[:, mine]
    capacity[:, half:] = at_cut[2 * slots + 1 : 2 * slots + 2]
    entry_rows[:, :half] = neighbours[:, mine]
    entry_rows[:, half:] = at_cut[:slots].astype(I32)
    weight_rows[:, :half] = weights[:, mine]
    weight_rows[:, half:] = at_cut[slots : 2 * slots]
    entries = [entry_rows[slot : slot + 1, :] for slot in range(slots)]
    gains = [weight_rows[slot : slot + 1, :] for slot in range(slots)]
    for slot in range(slots):
        for later in range(slot + 1, slots):
            same = entries[slot] == entries[later]
            gains[slot] = gains[slot] + jnp.where(same, gains[later], 0.0)
            entries[later] = jnp.where(same, -1, entries[later])
    for slot in range(slots):
        entry_rows[slot : slot + 1, :] = entries[slot]
        weight_rows[slot : slot + 1, :] = gains[slot]

    unroll = 4

    def column_block(block, carry):
        at_lanes = pl.ds(pl.multiple_of(block * LANES, LANES), LANES)
        wide = (CAP, LANES)
        names = [
            jnp.broadcast_to(entry_rows[slot : slot + 1, at_lanes], wide).astype(jnp.int16)
            for slot in range(slots)
        ]
        parts = [
            split(jnp.broadcast_to(weight_rows[slot : slot + 1, at_lanes], wide))
            for slot in range(slots)
        ]

        def source_rows(step, row):
            for inner in range(unroll):
                high = jnp.zeros(wide, BF16)
                low = jnp.zeros(wide, BF16)
                for slot in range(slots):
                    hit = names[slot] == row
                    high = jnp.where(hit, parts[slot][0], high)
                    low = jnp.where(hit, parts[slot][1], low)
                at = pl.ds(pl.multiple_of((step * unroll + inner) * 16, 16), 16)
                coupling_high[at, at_lanes] = high
                coupling_low[at, at_lanes] = low
                row = row + jnp.int16(16)
            return row

        lax.fori_loop(
            0,
            sources // 16 // unroll,
            source_rows,
            lax.broadcasted_iota(I32, wide, 0).astype(jnp.int16),
        )
        return carry

    lax.fori_loop(0, width // LANES, column_block, 0)
    cut_halo[...] = jnp.transpose(
        coupling_high[nodes:, half:].astype(F32) + coupling_low[nodes:, half:].astype(F32)
    )

    for copy in copies[6:]:
        copy.wait()
    conductances[pl.ds(pl.multiple_of(side * rows, 8), rows), :nodes] = conductance(
        operating[...], table[...]
    )
    conductances[pl.ds(pl.multiple_of((1 - side) * rows, 8), rows), :nodes] = conductance(
        near_operating[...], table[...]
    )
    conductances[:, nodes:] = pick(conductances[:, :nodes], picked[...])


def coupled(high, stacked, coupling_high, coupling_low, sources, lanes):
    rows = high.shape[0]
    both = dot(stacked, coupling_high[sources, lanes])
    return both[:rows] + both[rows:] + dot(high, coupling_low[sources, lanes])


def packet_layout(steps, times):
    shared = steps * CAP <= LANES
    return shared, times if shared else 0


def wave_kernel(*refs, pieces):
    vectors = refs[:pieces]
    (
        forward,
        conductances,
        picked,
        coupling_high,
        coupling_low,
        linear,
        capacity,
        cut_halo,
        field_high,
        field_low,
        wave,
        current,
        cut_current,
    ) = refs[pieces : pieces + 13]
    sent = refs[pieces + 13 :]
    rows, nodes = vectors[0].shape
    lanes = picked.shape[1]
    times = wave.shape[0]
    half = linear.shape[1] - lanes
    for index in range(pieces):
        at = slice(index * rows, (index + 1) * rows)
        field_high[at, :nodes], field_low[at, :nodes] = split(vectors[index][...])
    field_high[:, nodes:] = dot(field_high[:, :nodes], picked[...]).astype(BF16)
    field_low[:, nodes:] = dot(field_low[:, :nodes], picked[...]).astype(BF16)
    wave[...] = dot_split(
        (forward[0, :times], forward[1, :times]), (field_high[...], field_low[...])
    )
    slope = dot_split(
        (forward[0, times : 2 * times], forward[1, times : 2 * times]),
        (field_high[:, nodes:], field_low[:, nodes:]),
    )
    high, low = split(conductances[:, :nodes] * wave[:, :nodes])
    current[:times] = high
    current[times:] = low
    at_cut = conductances[:, nodes:] * wave[:, nodes:]
    cut_current[...] = jnp.transpose(at_cut)
    image = (
        linear[:, half:] * wave[:, nodes:]
        + at_cut
        + capacity[:, half:] * slope
        + coupled(
            high, current[...], coupling_high, coupling_low, slice(0, nodes), slice(half, None)
        )
    )
    image = jnp.transpose(image)
    at_cut = jnp.transpose(conductances[:, nodes:])
    slots = len(sent) * CAP
    shared, start = packet_layout(len(sent), times)
    for step, target in enumerate(sent):
        at = slice(step * CAP, (step + 1) * CAP)
        target[...] = jnp.zeros(target.shape, F32)
        if shared:
            target[:slots, :times] = cut_current[:slots]
        target[:CAP, start : start + slots] = cut_halo[at, :slots]
        target[CAP : 2 * CAP, start : start + times] = image[at]
        target[2 * CAP : 3 * CAP, start : start + times] = at_cut[at]


def local_kernel(
    field_high,
    field_low,
    forward,
    wave,
    current,
    conductances,
    coupling_high,
    coupling_low,
    linear,
    capacity,
    place,
    load,
    slope,
    own_wave,
    dual,
):
    times, half = load.shape
    sources = slice(0, current.shape[1])
    mine = half_of(place[0] % 2, half)
    others = dot_split(
        (forward[0, times:], forward[1, times:]), (field_high[:, mine], field_low[:, mine])
    )
    slope[...] = capacity[:, :half] * others[:times]
    dual[...] = others[times:]
    own_wave[...] = wave[:, mine]
    load[...] = own_wave[...] * (linear[:, :half] + conductances[:, mine])
    high = current[:times]
    step = 256
    for block in range(half // step):
        lanes = slice(block * step, (block + 1) * step)
        load[:, lanes] += coupled(
            high, current[...], coupling_high, coupling_low, sources, lanes
        )


def signed_sums(values):
    even = lax.broadcasted_iota(I32, values.shape, 0) % 2 == 0
    return (
        jnp.sum(values, axis=0, keepdims=True),
        jnp.sum(jnp.where(even, values, -values), axis=0, keepdims=True),
    )


def first_kernel(*refs, steps, apart):
    arrived, others = refs[:steps], refs[steps : steps + apart]
    (
        cut_current,
        local_load,
        slope,
        own_wave,
        back,
        coupling_high,
        coupling_low,
        image,
        load,
        kept,
        sent,
        halo,
    ) = refs[steps + apart :]
    times, half = local_load.shape
    lanes = halo.shape[1]
    nodes = coupling_high.shape[0] - lanes
    slots = steps * CAP
    start = packet_layout(steps, times)[1]
    blank = jnp.zeros((lanes - slots, times), F32)

    def stack(blocks):
        return jnp.transpose(jnp.concatenate([*blocks, blank], axis=0))

    def sender(step, block):
        at = slice((block - 1) * CAP, block * CAP)
        if step == 0:
            return cut_current[at]
        return others[0][step, at] if apart else arrived[step - 1][at, :times]

    current = stack([sender(step, step) for step in range(1, steps + 1)])
    high, low = split(current)
    share = coupled(
        high,
        jnp.concatenate([high, low], axis=0),
        coupling_high,
        coupling_low,
        slice(nodes, None),
        slice(0, half),
    )
    load[...] = local_load[...] + share
    answer = load[...] + slope[...]
    image[...] = answer
    spectrum = dot_split((back[0], back[1]), split(answer))
    kept[...] = spectrum[:times]
    rest = spectrum.shape[0] - times
    if rest:
        sent[:rest] = spectrum[times:]
    lines = [*signed_sums(answer), *signed_sums(own_wave[...])]
    sent[rest:] = jnp.concatenate(lines + [jnp.zeros((4, half), F32)], axis=0)

    blocks = []
    for step in range(1, steps + 1):
        theirs = jnp.concatenate(
            [sender((step + block) % (steps + 1), block) for block in range(1, steps + 1)], axis=0
        )
        gains = arrived[step - 1][:CAP, start : start + slots]
        image_part = arrived[step - 1][CAP : 2 * CAP, start : start + times]
        there = arrived[step - 1][2 * CAP : 3 * CAP, start : start + times]
        blocks.append(there * (image_part + dot_split(split(gains), split(theirs))))
    halo[...] = stack(blocks)


def second_kernel(
    place,
    halo,
    near_image,
    image,
    back,
    conductances,
    coupling_high,
    coupling_low,
    linear,
    load,
    kept,
    sent,
    current,
):
    times, half = image.shape
    nodes = current.shape[1]
    side = place[0] % 2
    mine, other = half_of(side, half), half_of(1 - side, half)
    for at, field in ((mine, image), (other, near_image)):
        current[:times, at], current[times:, at] = split(conductances[:, at] * field[...])
    load[...] = image[...] * (linear[:, :half] + conductances[:, mine])
    high, low = split(halo[...])
    halo_stacked = jnp.concatenate([high, low], axis=0)
    step = 256
    for block in range(half // step):
        lanes = slice(block * step, (block + 1) * step)
        load[:, lanes] += coupled(
            current[:times], current[...], coupling_high, coupling_low, slice(0, nodes), lanes
        ) + coupled(high, halo_stacked, coupling_high, coupling_low, slice(nodes, None), lanes)
    spectrum = dot_split((back[0], back[1]), split(load[...]))
    kept[...] = spectrum[:times]
    if spectrum.shape[0] > times:
        sent[...] = spectrum[times:]


def turned(field, first_pair, half_order):
    count = field.shape[0]
    row = lax.broadcasted_iota(I32, field.shape, 0)
    scaling = (first_pair + row // 2).astype(F32) * (1.0 / half_order)
    above = pltpu.roll(field, count - 1, 0)
    below = pltpu.roll(field, 1, 0)
    return scaling * jnp.where(row % 2 == 0, above, -below)


def join(target, side, own, near):
    half = own.shape[1]
    target[:, half_of(side, half)] = own
    target[:, half_of(1 - side, half)] = near


def guess(cross, squares):
    ratio = cross / jnp.where(squares > 0.0, squares, 1.0)
    return jnp.clip(jnp.where(squares > 0.0, ratio, 0.0), -40.0, 40.0)


def products_kernel(
    place,
    vector,
    own_image,
    near_image,
    capacity,
    load,
    second_load,
    image,
    wave,
    dual,
    own_sums,
    far_sums,
    answer,
    slope,
    scalars,
    *,
    length,
):
    side = place[0] % 2
    rows = vector.shape[0]
    first_pair = place[0] * (rows // 2)
    join(answer, side, own_image[...], near_image[...])
    field, start = answer[...], vector[...]
    squares = scalar_sum(start * start)
    coeff = guess(scalar_sum(start * field), squares)
    slope[...] = capacity[...] * turned(field, first_pair, length // 2)
    start_slope = capacity[...] * turned(start, first_pair, length // 2)
    rest = field - coeff * start
    rest_slope = slope[...] - coeff * start_slope
    found = [
        coeff,
        squares,
        scalar_sum(start * rest),
        scalar_sum(rest * rest),
        scalar_sum(start * rest_slope),
        scalar_sum(start * start_slope),
        scalar_sum(rest * rest_slope),
        scalar_sum(rest * start_slope),
    ]

    sums = own_sums[...] + far_sums[...]
    base = wave[...]
    coeff = guess(scalar_sum(base * image[...]), scalar_sum(base * base))
    rest = image[...] - coeff * base
    rest_sums = [sums[line : line + 1] - coeff * sums[line + 2 : line + 3] for line in (0, 1)]
    base_sums = [sums[line + 2 : line + 3] for line in (0, 1)]
    first = load[...]
    change = second_load[...] - coeff * first
    first_ends, change_ends = signed_sums(first), signed_sums(change)

    def mixed(values, value_sums, others, other_ends):
        ends = value_sums[0] * other_ends[0] + value_sums[1] * other_ends[1]
        return scalar_sum(values * others) * (2.0 / length) - scalar_sum(ends) * (
            1.0 / length / length
        )

    found += [
        coeff,
        scalar_sum(dual[...] * change),
        scalar_sum(dual[...] * first),
        mixed(rest, rest_sums, change, change_ends),
        mixed(rest, rest_sums, first, first_ends) + mixed(base, base_sums, change, change_ends),
        mixed(base, base_sums, first, first_ends),
    ]
    device = place[1] * place[3] + place[0]
    lane = lax.broadcasted_iota(I32, scalars.shape, 1)
    column = jnp.concatenate(found + [jnp.zeros((2, 1), F32)], axis=0)
    scalars[...] = jnp.where(lane == device, column, 0.0)


def last_kernel(
    gathered,
    vector,
    answer,
    slope,
    place,
    own_part,
    near_part,
    basis_two,
    next_residue,
    *,
    entries,
):
    side = place[0] % 2
    own = [gathered[line : line + 1, :] for line in range(14)]

    def everywhere(values):
        return jnp.sum(values, axis=1, keepdims=True) / entries

    scale_square = everywhere(own[1]) + EPSILON
    coeff = everywhere(own[2] + own[0] * own[1]) / scale_square
    near = own[0] - coeff
    rest_square = everywhere(own[3] + near * (2.0 * own[2] + near * own[1]))
    along_one = own[4] + near * own[5]
    along_two = own[6] + near * (own[4] + own[7] + near * own[5])
    near = own[8] - coeff
    along_one = everywhere(along_one + own[9] + near * own[10])
    along_two = everywhere(along_two + own[11] + near * (own[12] + near * own[13]))
    scale = jnp.sqrt(scale_square)
    second_norm = jnp.sqrt(jnp.maximum(rest_square, 0.0) / scale_square + EPSILON)
    inverse = 1.0 / (second_norm * scale)
    along_one = along_one * inverse / scale_square
    along_two = along_two * inverse * inverse
    join(next_residue, side, own_part[...], near_part[...])
    second = (answer[...] - coeff * vector[...]) * inverse
    basis_two[...] = second
    next_residue[...] = (
        (next_residue[...] + slope[...] - coeff * answer[...]) * inverse
        - along_one * vector[...]
        - along_two * second
    )


VMEM = pl.BlockSpec(memory_space=pltpu.VMEM)
SMEM = pl.BlockSpec(memory_space=pltpu.SMEM)
ANY = pl.BlockSpec(memory_space=pl.ANY)


def run(kernel, name, specs, operands, outs, scratch=(), micros=1):
    return pl.pallas_call(
        kernel,
        out_shape=[pltpu.VMEM(shape, dtype) for shape, dtype in outs],
        in_specs=specs,
        out_specs=[VMEM] * len(outs),
        scratch_shapes=list(scratch),
        compiler_params=pltpu.CompilerParams(vmem_limit_bytes=40 * 2**20),
        cost_estimate=pl.CostEstimate(
            flops=0, bytes_accessed=int(micros * 3e6), transcendentals=0
        ),
        name=name,
    )(*operands)


def swap(value, mask):
    count = lax.axis_size("samples")
    return lax.ppermute(value, "samples", [(at, at ^ mask) for at in range(count)])


def ahead(value, step):
    count = lax.axis_size("nodes")
    return lax.ppermute(value, "nodes", [(at, (at + step) % count) for at in range(count)])


def total(value):
    for axis in ("samples", "nodes"):
        count, stride = lax.axis_size(axis), 1
        while stride < count:
            radix = 4 if count // stride % 4 == 0 else 2
            others = [
                lax.ppermute(value, axis, [(at, at ^ (step * stride)) for at in range(count)])
                for step in range(1, radix)
            ]
            value = value + functools.reduce(jnp.add, others)
            stride *= radix
    return value


def reduce_groups(kept, sent):
    times = kept.shape[0]
    count = lax.axis_size("samples") // 2
    extra = sent[(count - 1) * times :]
    if count == 2:
        arrived = swap(sent, 2)
        return kept + arrived[:times], arrived[times:]
    blocks = {0: kept}
    for group in range(1, count):
        blocks[group] = sent[(group - 1) * times : group * times]
    bit = count // 2
    while bit:
        for group in [name for name in blocks if name & bit]:
            blocks[group ^ bit] = blocks[group ^ bit] + swap(blocks.pop(group), 2 * bit)
        bit //= 2
    others, bit = extra, 1
    while bit < count:
        others = others + swap(others, 2 * bit)
        bit *= 2
    return blocks[0], others - extra


def shards(
    vector, operating, table, linear, capacity, weights, degree, neighbours, boundary, send_list
):
    rows, nodes = vector.shape
    parts, node_groups = lax.axis_size("samples"), lax.axis_size("nodes")
    length, half, times = rows * parts, nodes // 2, 2 * rows
    entries = float(length * nodes * node_groups)
    steps = node_groups - 1
    slots = steps * CAP
    lanes = -(-slots // LANES) * LANES
    sources, width = nodes + lanes, half + lanes
    place = jnp.stack(
        [
            lax.axis_index("samples"),
            lax.axis_index("nodes"),
            jnp.int32(node_groups),
            jnp.int32(parts),
        ]
    ).astype(I32)
    forward, back = (jnp.asarray(table) for table in transform_tables(length, parts))
    linear, capacity, degree, table = (
        value.reshape(1, -1) for value in (linear, capacity, degree, table)
    )

    near_operating = swap(operating, 1)
    vectors, bit = [vector], parts // 2
    while bit:
        vectors = vectors + [swap(piece, bit) for piece in vectors]
        bit //= 2

    slot_count = weights.shape[0]
    (
        coupling_high,
        coupling_low,
        conductances,
        picked,
        linear_wide,
        capacity_wide,
        capacity,
        cut_halo,
        own_vector,
        forward,
        back,
    ) = run(
        prepare_kernel,
        "prepare",
        [SMEM] * 3 + [ANY] * 11,
        (place, send_list, boundary, near_operating, operating, neighbours, weights, degree)
        + (linear, capacity, table, vector, forward, back),
        [
            ((sources, width), BF16),
            ((sources, width), BF16),
            ((times, sources), F32),
            ((nodes, lanes), BF16),
            ((1, width), F32),
            ((1, width), F32),
            ((1, nodes), F32),
            ((lanes, lanes), F32),
            ((rows, nodes), F32),
            (forward.shape[1:], BF16),
            (back.shape[1:], BF16),
        ],
        scratch=[
            pltpu.VMEM((rows, nodes), F32),
            pltpu.VMEM((rows, nodes), F32),
            pltpu.VMEM((slot_count, nodes), I32),
            pltpu.VMEM((slot_count, nodes), F32),
            pltpu.VMEM((1, nodes), I32),
            pltpu.VMEM((1, nodes), F32),
            pltpu.VMEM(table.shape, F32),
            pltpu.VMEM((slot_count, width), I32),
            pltpu.VMEM((slot_count, width), F32),
            pltpu.SemaphoreType.DMA((11,)),
        ],
        micros=8,
    )
    vectors[0] = own_vector

    wide = ((times, half), F32)
    shared, start = packet_layout(steps, times)
    packet = (
        max(slots if shared else 0, 3 * CAP),
        -(-(start + max(times, slots)) // LANES) * LANES,
    )
    field_high, field_low, wave, current, cut_current, *sent = run(
        functools.partial(wave_kernel, pieces=parts),
        "wave",
        [VMEM] * (parts + 8),
        (*vectors, forward, conductances, picked, coupling_high, coupling_low)
        + (linear_wide, capacity_wide, cut_halo),
        [
            ((length, sources), BF16),
            ((length, sources), BF16),
            ((times, sources), F32),
            ((2 * times, nodes), BF16),
            ((lanes, times), F32),
        ]
        + [(packet, F32)] * steps,
        micros=2,
    )
    arrived = [ahead(packet, step + 1) for step, packet in enumerate(sent)]
    others = []
    if not shared:
        gathered = lax.all_gather(cut_current, "nodes")
        distance = jnp.arange(node_groups, dtype=I32)
        others = [gathered[(lax.axis_index("nodes") - distance) % node_groups]]
    local_load, slope, own_wave, dual = run(
        local_kernel,
        "local",
        [VMEM] * 10 + [SMEM],
        (field_high, field_low, forward, wave, current, conductances)
        + (coupling_high, coupling_low, linear_wide, capacity_wide, place),
        [wide] * 4,
        micros=3,
    )
    rest = length - times
    image, load, kept, sent, halo = run(
        functools.partial(first_kernel, steps=steps, apart=len(others)),
        "first",
        [VMEM] * (steps + len(others) + 7),
        (*arrived, *others, cut_current, local_load, slope, own_wave, back, coupling_high, coupling_low),
        [wide, wide, wide, ((rest + 8, half), F32), ((times, lanes), F32)],
        micros=1,
    )
    own_sums = sent[rest:]
    near_image = swap(image, 1)
    spectrum, far_sums = reduce_groups(kept, sent)
    own_coefs, near_coefs = spectrum[:rows], swap(spectrum[rows:], 1)

    second_load, kept, sent = run(
        second_kernel,
        "second",
        [SMEM] + [VMEM] * 8,
        (place, halo, near_image, image, back, conductances)
        + (coupling_high, coupling_low, linear_wide),
        [wide, wide, ((max(rest, 8), half), F32)],
        scratch=[pltpu.VMEM((2 * times, nodes), BF16)],
        micros=3,
    )
    gathered = -(-node_groups * parts // LANES) * LANES
    answer, slope, scalars = run(
        functools.partial(products_kernel, length=length),
        "products",
        [SMEM] + [VMEM] * 11,
        (place, own_vector, own_coefs, near_coefs, capacity, load, second_load)
        + (image, own_wave, dual, own_sums, far_sums),
        [((rows, nodes), F32), ((rows, nodes), F32), ((16, gathered), F32)],
        micros=1,
    )
    scalars = total(scalars)
    spectrum, _ = reduce_groups(kept, sent)
    own_part, near_part = spectrum[:rows], swap(spectrum[rows:], 1)
    field = jax.ShapeDtypeStruct((rows, nodes), F32)
    return tuple(
        pl.pallas_call(
            functools.partial(last_kernel, entries=entries),
            out_shape=[field, field],
            in_specs=[VMEM] * 4 + [SMEM] + [VMEM] * 2,
            out_specs=[VMEM] * 2,
            name="last",
        )(scalars, own_vector, answer, slope, place, own_part, near_part)
    )


def solution(mesh):
    return jax.shard_map(
        shards,
        mesh=mesh,
        in_specs=(
            P("samples", ("copies", "nodes")),
            P("samples", ("copies", "nodes")),
            P(),
            P("nodes"),
            P("nodes"),
            P(None, "nodes"),
            P("nodes"),
            P(None, "nodes"),
            P("nodes"),
            P("nodes"),
        ),
        out_specs=(P("samples", ("copies", "nodes")), P("samples", ("copies", "nodes"))),
        check_vma=False,
    )
```

time: 79.1 us -> 79.2 us (level)
  starting transfers between devices: 33.8 us -> 18.8 us
  waiting for transfers between devices: 12.6 us -> 19.2 us
  Pallas kernels: 17.1 us -> 22.5 us
  local copies, waits for them, and re-layouts: 13.3 us -> 16.6 us
    ppermute x13 -> x9, waiting for transfers between devices: 4.29 us -> 12.9 us  [swap(): lax.ppermute(value, 'samples', [(at, at ^ mask) for at in range(count)])]
    ppermute x9 -> x3, starting transfers between devices: 13.2 us -> 5.82 us  [ahead(): lax.ppermute(value, 'nodes', [(at, (at + step) % count) for at in range(c...]
    ppermute x12 -> x6, starting transfers between devices: 12 us -> 6.32 us  [total(): lax.ppermute(value, axis, [(at, at ^ step * stride) for at in range(count)])]
    pallas_call x5 -> x6, Pallas kernels: 15 us -> 20.3 us  [run(): pl.pallas_call(kernel, out_shape=[pltpu.VMEM(shape, dtype) for shape, dty...]
    unnamed x36 -> x46, local copies, waits for them, and re-layouts: 10.9 us -> 15.9 us
    ppermute x13 -> x9, starting transfers between devices: 8.56 us -> 6.67 us  [swap(): lax.ppermute(value, 'samples', [(at, at ^ mask) for at in range(count)])]
    squeeze x2 -> x0, local copies, waits for them, and re-layouts: 1.74 us -> none  [shards(): lax.dynamic_index_in_dim(jnp.asarray(stack), own_place, keepdims=False)]
    ppermute x12 -> x6, waiting for transfers between devices: 7.24 us -> 5.97 us  [total(): lax.ppermute(value, axis, [(at, at ^ step * stride) for at in range(count)])]
  transfers between devices with their start and end apart: 34 -> 18, of which waited for: 7 -> 7; matrix products, arithmetic and copies ran while one was open for 4% -> 2% of each run, Pallas kernels for 15% -> 20%
where the time goes in v2:
time: 79.2 us; the launch traced here: 78.6 us
  Pallas kernels  22.5 us (28%)
  waiting for transfers between devices  19.2 us (24%)
  starting transfers between devices  18.8 us (24%)
  local copies, waits for them, and re-layouts  16.6 us (21%)
    pallas_call x6, Pallas kernels, run(): pl.pallas_call(kernel, out_shape=[pltpu.VMEM(shape, dtype) for shape, dty...  20.3 us
    unnamed x46, local copies, waits for them, and re-layouts  15.9 us
    ppermute x9, waiting for transfers between devices, swap(): lax.ppermute(value, 'samples', [(at, at ^ mask) for at in range(count)])  12.9 us
    ppermute x9, starting transfers between devices, swap(): lax.ppermute(value, 'samples', [(at, at ^ mask) for at in range(count)])  6.67 us
    ppermute x6, starting transfers between devices, total(): lax.ppermute(value, axis, [(at, at ^ step * stride) for at in range(count)])  6.32 us
    ppermute x6, waiting for transfers between devices, total(): lax.ppermute(value, axis, [(at, at ^ step * stride) for at in range(count)])  5.97 us
    ppermute x3, starting transfers between devices, ahead(): lax.ppermute(value, 'nodes', [(at, (at + step) % count) for at in range(c...  5.82 us
    pallas_call x1, Pallas kernels, shards(): pl.pallas_call(functools.partial(last_kernel, entries=entries), out_shape...  2.21 us
  transfers between devices with their start and end apart: 18, of which 7 were waited for; matrix products, arithmetic and copies ran while one was open for 2% of the time, Pallas kernels for 20%

profile of v2, /device:TPU:0, one launch (start us, length us, event | category | flops | bytes accessed | tf_op | source)
XLA Modules:
  0.0 78.6 jit_solution(3016844460898676366)
XLA Ops:
  0.6 3.0 %collective-permute-start.1 = (f32[32,2048]{1,0:T(8,128)}, f32[32,2048]{1,0:T(8,128)S(1)}, u32[]{:S(2)}, u32[]{:S(2)}) collective-permute-start(f32[32,2048]{1,0:T(8,128)} %vector_in.1), channel_id=1, source_target_pairs={{0,2},{1,3},{2,0},{3,1},{4,6},{5,7},{6,4},{7,5},{8,10},{9,11},{10,... | collective-permute-start | bytes 786440 | tf_op jit(solution)/shard_map/ppermute | solution.py:676
  3.6 0.5 collective-permute-start.2
  4.1 6.0 %collective-permute-done.1.refs_1_ = f32[32,2048]{1,0:T(8,128)S(1)} collective-permute-done((f32[32,2048]{1,0:T(8,128)}, f32[32,2048]{1,0:T(8,128)S(1)}, u32[]{:S(2)}, u32[]{:S(2)}) %collective-permute-start.1) | collective-permute-done | bytes 262176 | tf_op jit(solution)/shard_map/ppermute | solution.py:676
  10.2 0.1 pad_add_fusion.place
  10.2 0.0 collective-permute-done.near_operating_in
  10.2 1.0 %copy-done.3 = bf16[4,2,192,128]{3,2,1,0:T(8,128)(2,1)S(1)} copy-done((bf16[4,2,192,128]{3,2,1,0:T(8,128)(2,1)S(1)}, bf16[4,2,192,128]{3,2,1,0:T(8,128)(2,1)}, u32[]{:S(2)}) %copy-start.3) | copy-done | bytes 393240
  11.2 0.9 %copy-done.8 = f32[32,2048]{1,0:T(8,128)S(1)} copy-done((f32[32,2048]{1,0:T(8,128)S(1)}, f32[32,2048]{1,0:T(8,128)}, u32[]{:S(2)}) %copy-start.8) | copy-done | bytes 262168
  12.2 0.9 %copy-done.9 = f32[32,2048]{1,0:T(8,128)S(1)} copy-done((f32[32,2048]{1,0:T(8,128)S(1)}, f32[32,2048]{1,0:T(8,128)}, u32[]{:S(2)}) %copy-start.9) | copy-done | bytes 262168
  13.1 0.9 %copy-done.12 = bf16[4,2,128,64]{3,2,1,0:T(8,128)(2,1)S(1)} copy-done((bf16[4,2,128,64]{3,2,1,0:T(8,128)(2,1)S(1)}, bf16[4,2,128,64]{3,2,1,0:T(8,128)(2,1)}, u32[]{:S(2)}) %copy-start.12) | copy-done | bytes 131096
  14.1 0.8 %copy-done.13 = s32[8,2048]{1,0:T(8,128)S(1)} copy-done((s32[8,2048]{1,0:T(8,128)S(1)}, s32[8,2048]{1,0:T(8,128)}, u32[]{:S(2)}) %copy-start.13) | copy-done | bytes 65560
  14.9 0.8 %copy-done.14 = f32[8,2048]{1,0:T(8,128)S(1)} copy-done((f32[8,2048]{1,0:T(8,128)S(1)}, f32[8,2048]{1,0:T(8,128)}, u32[]{:S(2)}) %copy-start.14) | copy-done | bytes 65560
  15.8 0.7 copy-done.16
  16.5 0.7 copy-done.17
  17.2 0.7 copy-done.18
  17.9 0.7 copy-done.19
  18.5 0.7 copy-done.20
  19.2 0.7 copy-done.21
  19.9 9.4 %prepare.1 = (bf16[2176,1152]{1,0:T(8,128)(2,1)S(1)}, bf16[2176,1152]{1,0:T(8,128)(2,1)S(1)}, f32[64,2176]{1,0:T(8,128)S(1)}, bf16[2048,128]{1,0:T(8,128)(2,1)S(...) custom-call(s32[4]{0:T(128)S(1)} %pad_add_fusion.place, ...), custom_call_target="tpu_custom_call" | custom-call | bytes 24000000 | tf_op jit(solution)/shard_map/prepare/pallas_call | solution.py:660
  29.2 2.3 %copy-done = bf16[2176,1152]{1,0:T(8,128)(2,1)} copy-done((bf16[2176,1152]{1,0:T(8,128)(2,1)}, bf16[2176,1152]{1,0:T(8,128)(2,1)S(1)}, u32[]{:S(2)}) %copy-start) | copy-done | bytes 5013528
  31.5 0.7 copy-done.4
  32.3 0.7 copy-done.6
  33.0 0.9 %copy-done.5 = f32[32,2048]{1,0:T(8,128)S(1)} copy-done((f32[32,2048]{1,0:T(8,128)S(1)}, f32[32,2048]{1,0:T(8,128)}, u32[]{:S(2)}) %copy-start.5) | copy-done | bytes 262168
  33.9 0.9 %copy-done.7 = f32[32,2048]{1,0:T(8,128)S(1)} copy-done((f32[32,2048]{1,0:T(8,128)S(1)}, f32[32,2048]{1,0:T(8,128)}, u32[]{:S(2)}) %copy-start.7) | copy-done | bytes 262168
  34.9 3.7 %wave.1 = (bf16[128,2176]{1,0:T(8,128)(2,1)S(1)}, bf16[128,2176]{1,0:T(8,128)(2,1)S(1)}, f32[64,2176]{1,0:T(8,128)S(1)}, bf16[128,2048]{1,0:T(8,128)(2,1)S(1)}, ...) custom-call(f32[32,2048]{1,0:T(8,128)S(1)} %get-tuple-element.36.refs_0_.vector, ...), custom_call_target="tpu_custom_call" | custom-call | bytes 6000000 | tf_op jit(solution)/shard_map/wave/pallas_call | solution.py:660
  38.6 1.9 %collective-permute-start.4 = (f32[48,128]{1,0:T(8,128)S(1)}, f32[48,128]{1,0:T(8,128)S(1)}, u32[]{:S(2)}, u32[]{:S(2)}) collective-permute-start(f32[48,128]{1,0:T(8,128)S(1)} %get-tuple-element.45), channel_id=1, source_target_pairs={{0,4},{4,8},{8,12},{12,0},{1,5},{5,9},{9,13},{13,1},{2,6},{6,10},{... | collective-permute-start | bytes 73736 | tf_op jit(solution)/shard_map/ppermute | solution.py:681
  40.5 2.6 %collective-permute-start.5 = (f32[48,128]{1,0:T(8,128)S(1)}, f32[48,128]{1,0:T(8,128)S(1)}, u32[]{:S(2)}, u32[]{:S(2)}) collective-permute-start(f32[48,128]{1,0:T(8,128)S(1)} %get-tuple-element.46), channel_id=1, source_target_pairs={{0,8},{4,12},{8,0},{12,4},{1,9},{5,13},{9,1},{13,5},{2,10},{6,14},... | collective-permute-start | bytes 73736 | tf_op jit(solution)/shard_map/ppermute | solution.py:681
  43.1 1.4 %collective-permute-start.6 = (f32[48,128]{1,0:T(8,128)S(1)}, f32[48,128]{1,0:T(8,128)S(1)}, u32[]{:S(2)}, u32[]{:S(2)}) collective-permute-start(f32[48,128]{1,0:T(8,128)S(1)} %get-tuple-element.47), channel_id=1, source_target_pairs={{0,12},{4,0},{8,4},{12,8},{1,13},{5,1},{9,5},{13,9},{2,14},{6,2},{... | collective-permute-start | bytes 73736 | tf_op jit(solution)/shard_map/ppermute | solution.py:681
  44.4 2.2 %local.1 = (f32[64,1024]{1,0:T(8,128)S(1)}, f32[64,1024]{1,0:T(8,128)S(1)}, f32[64,1024]{1,0:T(8,128)S(1)}, f32[64,1024]{1,0:T(8,128)S(1)}) custom-call(bf16[128,2176]{1,0:T(8,128)(2,1)S(1)} %get-tuple-element.49.field_high, bf16[128,2176]{1,0:T(8,128)(2,1)S(1)} %get-tuple-element.50.field_low, bf16[2,192,128]{2,1,0:T(8,128)(2,1)S(1)} %get-tuple-element.37.refs_4_.forward, ...), custom_call_target="tpu_custom_call" | custom-call | bytes 9000000 | tf_op jit(solution)/shard_map/local/pallas_call | solution.py:660
  46.6 0.3 collective-permute-done.6.refs_2_
  46.9 0.9 %first.1 = (f32[64,1024]{1,0:T(8,128)S(1)}, f32[64,1024]{1,0:T(8,128)S(1)}, f32[64,1024]{1,0:T(8,128)S(1)}, f32[72,1024]{1,0:T(8,128)S(1)}, f32[64,128]{1,0:T(8,128)S(1)}) custom-call(f32[48,128]{1,0:T(8,128)S(1)} %collective-permute-done.4.refs_0_, f32[48,128]{1,0:T(8,128)S(1)} %collective-permute-done.5.refs_1_, ...), custom_call_target="tpu_custom_call" | custom-call | bytes 3000000 | tf_op jit(solution)/shard_map/first/pallas_call | solution.py:660
  47.7 1.6 %collective-permute-start.7 = (f32[72,1024]{1,0:T(8,128)S(1)}, f32[72,1024]{1,0:T(8,128)S(1)}, u32[]{:S(2)}, u32[]{:S(2)}) collective-permute-start(f32[72,1024]{1,0:T(8,128)S(1)} %get-tuple-element.58), channel_id=1, source_target_pairs={{0,2},{1,3},{2,0},{3,1},{4,6},{5,7},{6,4},{7,5},{8,10},{9,11},{10,... | collective-permute-start | bytes 884744 | tf_op jit(solution)/shard_map/ppermute | solution.py:676
  49.3 6.9 %collective-permute-done.7 = f32[72,1024]{1,0:T(8,128)S(1)} collective-permute-done((f32[72,1024]{1,0:T(8,128)S(1)}, f32[72,1024]{1,0:T(8,128)S(1)}, u32[]{:S(2)}, u32[]{:S(2)}) %collective-permute-start.7) | collective-permute-done | bytes 294944 | tf_op jit(solution)/shard_map/ppermute | solution.py:676
  56.3 0.1 collective-permute-start.8
  56.3 2.5 %second.1 = (f32[64,1024]{1,0:T(8,128)S(1)}, f32[64,1024]{1,0:T(8,128)S(1)}, f32[64,1024]{1,0:T(8,128)S(1)}) custom-call(s32[4]{0:T(128)S(1)} %pad_add_fusion.place, f32[64,128]{1,0:T(8,128)S(1)} %get-tuple-element.61.halo, f32[64,1024]{1,0:T(8,128)S(1)} %collective-permute-done.9.near_image, f32[64,1024]{1,0:T(8,128)S(1)} %get-tuple-element.62.image, ...), custom_call_target="tpu_custom_call" | custom-call | bytes 9000000 | tf_op jit(solution)/shard_map/second/pallas_call | solution.py:660
  58.8 1.5 %collective-permute-start.16 = (f32[64,1024]{1,0:T(8,128)S(1)}, f32[64,1024]{1,0:T(8,128)S(1)}, u32[]{:S(2)}, u32[]{:S(2)}) collective-permute-start(f32[64,1024]{1,0:T(8,128)S(1)} %get-tuple-element.69), channel_id=1, source_target_pairs={{0,2},{1,3},{2,0},{3,1},{4,6},{5,7},{6,4},{7,5},{8,10},{9,11},{10,... | collective-permute-start | bytes 786440 | tf_op jit(solution)/shard_map/ppermute | solution.py:676
  60.4 1.7 %products.1 = (f32[32,2048]{1,0:T(8,128)S(1)}, f32[32,2048]{1,0:T(8,128)S(1)}, f32[16,128]{1,0:T(8,128)S(1)}) custom-call(s32[4]{0:T(128)S(1)} %pad_add_fusion.place, f32[32,2048]{1,0:T(8,128)S(1)} %get-tuple-element.36.refs_0_.vector, f32[32,1024]{1,0:T(8,128)S(1)} %get-tuple-element.73.own_image, f32[32,1024]{1,0:T(8,128)S(1)} %collective-permute-done.8.near_image, ...), custom_call_target="tpu_custom_call" | custom-call | bytes 3000000 | tf_op jit(solution)/shard_map/products/pallas_call | solution.py:660
  62.1 0.4 collective-permute-start.12
  62.5 1.5 %collective-permute-start.11 = (f32[16,128]{1,0:T(8,128)S(1)}, f32[16,128]{1,0:T(8,128)S(1)}, u32[]{:S(2)}, u32[]{:S(2)}) collective-permute-start(f32[16,128]{1,0:T(8,128)S(1)} %get-tuple-element.65), channel_id=1, source_target_pairs={{0,2},{1,3},{2,0},{3,1},{4,6},{5,7},{6,4},{7,5},{8,10},{9,11},{10,... | collective-permute-start | bytes 24584 | tf_op jit(solution)/shard_map/ppermute | solution.py:690
  63.9 3.5 %collective-permute-done.12 = f32[16,128]{1,0:T(8,128)S(1)} collective-permute-done((f32[16,128]{1,0:T(8,128)S(1)}, f32[16,128]{1,0:T(8,128)S(1)}, u32[]{:S(2)}, u32[]{:S(2)}) %collective-permute-start.12) | collective-permute-done | bytes 8224 | tf_op jit(solution)/shard_map/ppermute | solution.py:690
  67.4 0.6 collective-permute-done.11
  68.0 2.6 %collective-permute-start.15 = (f32[16,128]{1,0:T(8,128)S(1)}, f32[16,128]{1,0:T(8,128)S(1)}, u32[]{:S(2)}, u32[]{:S(2)}) collective-permute-start(f32[16,128]{1,0:T(8,128)S(1)} %add_add_fusion.1), channel_id=1, source_target_pairs={{0,12},{4,8},{8,4},{12,0},{1,13},{5,9},{9,5},{13,1},{2,14},{6,10},... | collective-permute-start | bytes 24584 | tf_op jit(solution)/shard_map/ppermute | solution.py:690
  70.6 1.9 %collective-permute-start.13 = (f32[16,128]{1,0:T(8,128)S(1)}, f32[16,128]{1,0:T(8,128)S(1)}, u32[]{:S(2)}, u32[]{:S(2)}) collective-permute-start(f32[16,128]{1,0:T(8,128)S(1)} %add_add_fusion.1), channel_id=1, source_target_pairs={{0,4},{4,0},{8,12},{12,8},{1,5},{5,1},{9,13},{13,9},{2,6},{6,2},{1... | collective-permute-start | bytes 24584 | tf_op jit(solution)/shard_map/ppermute | solution.py:690
  72.5 0.7 fusion
  73.2 0.3 collective-permute-done.15
  73.5 1.6 %collective-permute-done.14 = f32[16,128]{1,0:T(8,128)S(1)} collective-permute-done((f32[16,128]{1,0:T(8,128)S(1)}, f32[16,128]{1,0:T(8,128)S(1)}, u32[]{:S(2)}, u32[]{:S(2)}) %collective-permute-start.14) | collective-permute-done | bytes 8224 | tf_op jit(solution)/shard_map/ppermute | solution.py:690
  75.1 0.6 add_add_fusion.gathered
  75.7 0.7 copy-done.22
  76.4 2.2 %last.1 = (f32[32,2048]{1,0:T(8,128)}, f32[32,2048]{1,0:T(8,128)}) custom-call(f32[16,128]{1,0:T(8,128)} %add_add_fusion.gathered, f32[32,2048]{1,0:T(8,128)} %copy-done.2, f32[32,2048]{1,0:T(8,128)} %copy-done.10, f32[32,2048]{1,0:T(8,128)} %copy-done.11, s32[4]{0:T(128)} %copy-done.15, f32[32,1024]{1,0:T(8,128)} %get-tuple-element.71.own_part, ...), custom_call_target="tpu_custom_call" | custom-call | tf_op jit(solution)/shard_map/last/pallas_call | solution.py:874
  (51 shorter events, 0.2 us)
Async XLA Ops:
  0.6 9.5 %collective-permute-start.1 = (f32[32,2048]{1,0:T(8,128)}, f32[32,2048]{1,0:T(8,128)S(1)}, u32[]{:S(2)}, u32[]{:S(2)}) collective-permute-start(f32[32,2048]{1,0:T(8,128)} %vector_in.1), channel_id=1, source_target_pairs={{0,2},{1,3},{2,0},{3,1},{4,6},{5,7},{6,4},{7,5},{8,10},{9,11},{10,... | collective-permute-start | bytes 786440 | tf_op jit(solution)/shard_map/ppermute | solution.py:676
  3.6 6.6 %collective-permute-start = (f32[32,2048]{1,0:T(8,128)}, f32[32,2048]{1,0:T(8,128)S(1)}, u32[]{:S(2)}, u32[]{:S(2)}) collective-permute-start(f32[32,2048]{1,0:T(8,128)} %operating_in.1), channel_id=1, source_target_pairs={{0,1},{1,0},{2,3},{3,2},{4,5},{5,4},{6,7},{7,6},{8,9},{9,8},{10,11... | collective-permute-start | bytes 786440 | tf_op jit(solution)/shard_map/ppermute | solution.py:676
  3.6 27.9 %collective-permute-start.2 = (f32[32,2048]{1,0:T(8,128)}, f32[32,2048]{1,0:T(8,128)S(1)}, u32[]{:S(2)}, u32[]{:S(2)}) collective-permute-start(f32[32,2048]{1,0:T(8,128)} %vector_in.1), channel_id=1, source_target_pairs={{0,1},{1,0},{2,3},{3,2},{4,5},{5,4},{6,7},{7,6},{8,9},{9,8},{10,11... | collective-permute-start | bytes 786440 | tf_op jit(solution)/shard_map/ppermute | solution.py:676
  10.2 22.1 %collective-permute-start.3 = (f32[32,2048]{1,0:T(8,128)S(1)}, f32[32,2048]{1,0:T(8,128)S(1)}, u32[]{:S(2)}, u32[]{:S(2)}) collective-permute-start(f32[32,2048]{1,0:T(8,128)S(1)} %collective-permute-done.1.refs_1_), channel_id=1, source_target_pairs={{0,1},{1,0},{2,3},{3,2},{4,5},{5,4},{6,7},{7,6},{8,9},{9,8},{10,11... | collective-permute-start | bytes 786440 | tf_op jit(solution)/shard_map/ppermute | solution.py:676
  10.2 50.1 %copy-start.15 = (s32[4]{0:T(128)}, s32[4]{0:T(128)S(1)}, u32[]{:S(2)}) copy-start(s32[4]{0:T(128)S(1)} %pad_add_fusion.place) | copy-start | bytes 52
  10.2 1.0 %copy-start.3 = (bf16[4,2,192,128]{3,2,1,0:T(8,128)(2,1)S(1)}, bf16[4,2,192,128]{3,2,1,0:T(8,128)(2,1)}, u32[]{:S(2)}) copy-start(bf16[4,2,192,128]{3,2,1,0:T(8,128)(2,1)} %constant.13.clone.forward_in) | copy-start | bytes 1179652
  11.2 0.9 %copy-start.8 = (f32[32,2048]{1,0:T(8,128)S(1)}, f32[32,2048]{1,0:T(8,128)}, u32[]{:S(2)}) copy-start(f32[32,2048]{1,0:T(8,128)} %operating_in.1) | copy-start | bytes 786436
  12.2 0.9 %copy-start.9 = (f32[32,2048]{1,0:T(8,128)S(1)}, f32[32,2048]{1,0:T(8,128)}, u32[]{:S(2)}) copy-start(f32[32,2048]{1,0:T(8,128)} %vector_in.1) | copy-start | bytes 786436
  13.1 0.9 %copy-start.12 = (bf16[4,2,128,64]{3,2,1,0:T(8,128)(2,1)S(1)}, bf16[4,2,128,64]{3,2,1,0:T(8,128)(2,1)}, u32[]{:S(2)}) copy-start(bf16[4,2,128,64]{3,2,1,0:T(8,128)(2,1)} %constant.14.clone.back_in) | copy-start | bytes 393220
  14.1 0.8 %copy-start.13 = (s32[8,2048]{1,0:T(8,128)S(1)}, s32[8,2048]{1,0:T(8,128)}, u32[]{:S(2)}) copy-start(s32[8,2048]{1,0:T(8,128)} %neighbours_in.1) | copy-start | bytes 196612
  14.9 0.8 %copy-start.14 = (f32[8,2048]{1,0:T(8,128)S(1)}, f32[8,2048]{1,0:T(8,128)}, u32[]{:S(2)}) copy-start(f32[8,2048]{1,0:T(8,128)} %weights_in.1) | copy-start | bytes 196612
  15.8 0.7 copy-start.16
  16.5 0.7 copy-start.17
  17.2 0.7 copy-start.18
  17.9 0.7 copy-start.19
  18.5 0.7 copy-start.20
  19.2 0.7 copy-start.21
  29.2 2.3 %copy-start = (bf16[2176,1152]{1,0:T(8,128)(2,1)}, bf16[2176,1152]{1,0:T(8,128)(2,1)S(1)}, u32[]{:S(2)}) copy-start(bf16[2176,1152]{1,0:T(8,128)(2,1)S(1)} %get-tuple-element.41.refs_8_.coupling_low.refs_9_) | copy-start | bytes 15040516
  31.5 28.9 %copy-start.2 = (f32[32,2048]{1,0:T(8,128)}, f32[32,2048]{1,0:T(8,128)S(1)}, u32[]{:S(2)}) copy-start(f32[32,2048]{1,0:T(8,128)S(1)} %get-tuple-element.36.refs_0_.vector) | copy-start | bytes 786436
  31.5 0.7 copy-start.4
  32.3 0.7 copy-start.6
  33.0 0.9 %copy-start.5 = (f32[32,2048]{1,0:T(8,128)S(1)}, f32[32,2048]{1,0:T(8,128)}, u32[]{:S(2)}) copy-start(f32[32,2048]{1,0:T(8,128)} %copy-done.4) | copy-start | bytes 786436
  33.9 0.9 %copy-start.7 = (f32[32,2048]{1,0:T(8,128)S(1)}, f32[32,2048]{1,0:T(8,128)}, u32[]{:S(2)}) copy-start(f32[32,2048]{1,0:T(8,128)} %copy-done.6) | copy-start | bytes 786436
  34.9 9.6 %copy-start.1 = (bf16[2176,1152]{1,0:T(8,128)(2,1)S(1)}, bf16[2176,1152]{1,0:T(8,128)(2,1)}, u32[]{:S(2)}) copy-start(bf16[2176,1152]{1,0:T(8,128)(2,1)} %copy-done) | copy-start | bytes 15040516
  38.6 8.0 %collective-permute-start.4 = (f32[48,128]{1,0:T(8,128)S(1)}, f32[48,128]{1,0:T(8,128)S(1)}, u32[]{:S(2)}, u32[]{:S(2)}) collective-permute-start(f32[48,128]{1,0:T(8,128)S(1)} %get-tuple-element.45), channel_id=1, source_target_pairs={{0,4},{4,8},{8,12},{12,0},{1,5},{5,9},{9,13},{13,1},{2,6},{6,10},{... | collective-permute-start | bytes 73736 | tf_op jit(solution)/shard_map/ppermute | solution.py:681
  40.5 6.1 %collective-permute-start.5 = (f32[48,128]{1,0:T(8,128)S(1)}, f32[48,128]{1,0:T(8,128)S(1)}, u32[]{:S(2)}, u32[]{:S(2)}) collective-permute-start(f32[48,128]{1,0:T(8,128)S(1)} %get-tuple-element.46), channel_id=1, source_target_pairs={{0,8},{4,12},{8,0},{12,4},{1,9},{5,13},{9,1},{13,5},{2,10},{6,14},... | collective-permute-start | bytes 73736 | tf_op jit(solution)/shard_map/ppermute | solution.py:681
  43.1 3.8 %collective-permute-start.6 = (f32[48,128]{1,0:T(8,128)S(1)}, f32[48,128]{1,0:T(8,128)S(1)}, u32[]{:S(2)}, u32[]{:S(2)}) collective-permute-start(f32[48,128]{1,0:T(8,128)S(1)} %get-tuple-element.47), channel_id=1, source_target_pairs={{0,12},{4,0},{8,4},{12,8},{1,13},{5,1},{9,5},{13,9},{2,14},{6,2},{... | collective-permute-start | bytes 73736 | tf_op jit(solution)/shard_map/ppermute | solution.py:681
  47.7 8.5 %collective-permute-start.7 = (f32[72,1024]{1,0:T(8,128)S(1)}, f32[72,1024]{1,0:T(8,128)S(1)}, u32[]{:S(2)}, u32[]{:S(2)}) collective-permute-start(f32[72,1024]{1,0:T(8,128)S(1)} %get-tuple-element.58), channel_id=1, source_target_pairs={{0,2},{1,3},{2,0},{3,1},{4,6},{5,7},{6,4},{7,5},{8,10},{9,11},{10,... | collective-permute-start | bytes 884744 | tf_op jit(solution)/shard_map/ppermute | solution.py:676
  49.3 7.0 %collective-permute-start.9 = (f32[64,1024]{1,0:T(8,128)S(1)}, f32[64,1024]{1,0:T(8,128)S(1)}, u32[]{:S(2)}, u32[]{:S(2)}) collective-permute-start(f32[64,1024]{1,0:T(8,128)S(1)} %get-tuple-element.62.image), channel_id=1, source_target_pairs={{0,1},{1,0},{2,3},{3,2},{4,5},{5,4},{6,7},{7,6},{8,9},{9,8},{10,11... | collective-permute-start | bytes 786440 | tf_op jit(solution)/shard_map/ppermute | solution.py:676
  56.3 4.1 %collective-permute-start.8 = (f32[32,1024]{1,0:T(8,128)S(1)}, f32[32,1024]{1,0:T(8,128)S(1)}, u32[]{:S(2)}, u32[]{:S(2)}) collective-permute-start(f32[32,1024]{1,0:T(8,128)S(1)} %get-tuple-element.72), channel_id=1, source_target_pairs={{0,1},{1,0},{2,3},{3,2},{4,5},{5,4},{6,7},{7,6},{8,9},{9,8},{10,11... | collective-permute-start | bytes 393224 | tf_op jit(solution)/shard_map/ppermute | solution.py:676
  58.8 13.6 %collective-permute-start.16 = (f32[64,1024]{1,0:T(8,128)S(1)}, f32[64,1024]{1,0:T(8,128)S(1)}, u32[]{:S(2)}, u32[]{:S(2)}) collective-permute-start(f32[64,1024]{1,0:T(8,128)S(1)} %get-tuple-element.69), channel_id=1, source_target_pairs={{0,2},{1,3},{2,0},{3,1},{4,6},{5,7},{6,4},{7,5},{8,10},{9,11},{10,... | collective-permute-start | bytes 786440 | tf_op jit(solution)/shard_map/ppermute | solution.py:676
  62.1 10.4 %copy-start.10 = (f32[32,2048]{1,0:T(8,128)}, f32[32,2048]{1,0:T(8,128)S(1)}, u32[]{:S(2)}) copy-start(f32[32,2048]{1,0:T(8,128)S(1)} %get-tuple-element.66.answer) | copy-start | bytes 786436
  62.1 11.1 %copy-start.11 = (f32[32,2048]{1,0:T(8,128)}, f32[32,2048]{1,0:T(8,128)S(1)}, u32[]{:S(2)}) copy-start(f32[32,2048]{1,0:T(8,128)S(1)} %get-tuple-element.67.slope) | copy-start | bytes 786436
  62.1 5.3 %collective-permute-start.12 = (f32[16,128]{1,0:T(8,128)S(1)}, f32[16,128]{1,0:T(8,128)S(1)}, u32[]{:S(2)}, u32[]{:S(2)}) collective-permute-start(f32[16,128]{1,0:T(8,128)S(1)} %get-tuple-element.65), channel_id=1, source_target_pairs={{0,3},{1,2},{2,1},{3,0},{4,7},{5,6},{6,5},{7,4},{8,11},{9,10},{10,... | collective-permute-start | bytes 24584 | tf_op jit(solution)/shard_map/ppermute | solution.py:690
  62.5 5.5 %collective-permute-start.11 = (f32[16,128]{1,0:T(8,128)S(1)}, f32[16,128]{1,0:T(8,128)S(1)}, u32[]{:S(2)}, u32[]{:S(2)}) collective-permute-start(f32[16,128]{1,0:T(8,128)S(1)} %get-tuple-element.65), channel_id=1, source_target_pairs={{0,2},{1,3},{2,0},{3,1},{4,6},{5,7},{6,4},{7,5},{8,10},{9,11},{10,... | collective-permute-start | bytes 24584 | tf_op jit(solution)/shard_map/ppermute | solution.py:690
  63.9 4.0 %collective-permute-start.10 = (f32[16,128]{1,0:T(8,128)S(1)}, f32[16,128]{1,0:T(8,128)S(1)}, u32[]{:S(2)}, u32[]{:S(2)}) collective-permute-start(f32[16,128]{1,0:T(8,128)S(1)} %get-tuple-element.65), channel_id=1, source_target_pairs={{0,1},{1,0},{2,3},{3,2},{4,5},{5,4},{6,7},{7,6},{8,9},{9,8},{10,11... | collective-permute-start | bytes 24584 | tf_op jit(solution)/shard_map/ppermute | solution.py:690
  68.0 5.5 %collective-permute-start.15 = (f32[16,128]{1,0:T(8,128)S(1)}, f32[16,128]{1,0:T(8,128)S(1)}, u32[]{:S(2)}, u32[]{:S(2)}) collective-permute-start(f32[16,128]{1,0:T(8,128)S(1)} %add_add_fusion.1), channel_id=1, source_target_pairs={{0,12},{4,8},{8,4},{12,0},{1,13},{5,9},{9,5},{13,1},{2,14},{6,10},... | collective-permute-start | bytes 24584 | tf_op jit(solution)/shard_map/ppermute | solution.py:690
  70.6 4.5 %collective-permute-start.14 = (f32[16,128]{1,0:T(8,128)S(1)}, f32[16,128]{1,0:T(8,128)S(1)}, u32[]{:S(2)}, u32[]{:S(2)}) collective-permute-start(f32[16,128]{1,0:T(8,128)S(1)} %add_add_fusion.1), channel_id=1, source_target_pairs={{0,8},{4,12},{8,0},{12,4},{1,9},{5,13},{9,1},{13,5},{2,10},{6,14},... | collective-permute-start | bytes 24584 | tf_op jit(solution)/shard_map/ppermute | solution.py:690
  70.6 4.5 %collective-permute-start.13 = (f32[16,128]{1,0:T(8,128)S(1)}, f32[16,128]{1,0:T(8,128)S(1)}, u32[]{:S(2)}, u32[]{:S(2)}) collective-permute-start(f32[16,128]{1,0:T(8,128)S(1)} %add_add_fusion.1), channel_id=1, source_target_pairs={{0,4},{4,0},{8,12},{12,8},{1,5},{5,1},{9,13},{13,9},{2,6},{6,2},{1... | collective-permute-start | bytes 24584 | tf_op jit(solution)/shard_map/ppermute | solution.py:690
  73.2 2.5 %collective-permute-start.17 = (f32[32,1024]{1,0:T(8,128)S(1)}, f32[32,1024]{1,0:T(8,128)S(1)}, u32[]{:S(2)}, u32[]{:S(2)}) collective-permute-start(f32[32,1024]{1,0:T(8,128)S(1)} %get-tuple-element.70), channel_id=1, source_target_pairs={{0,1},{1,0},{2,3},{3,2},{4,5},{5,4},{6,7},{7,6},{8,9},{9,8},{10,11... | collective-permute-start | bytes 393224 | tf_op jit(solution)/shard_map/ppermute | solution.py:676
  75.7 0.7 copy-start.22

commit v3 on v2

--- a/solution.py
+++ b/solution.py
@@ -131,37 +131,36 @@
 
 def prepare_kernel(
     place,
-    send_list,
-    boundary,
-    near_operating_in,
-    operating_in,
     neighbours_in,
     weights_in,
     degree_in,
     linear_in,
     capacity_in,
+    send_list_in,
+    boundary_in,
     table_in,
+    operating_in,
     vector_in,
     forward_in,
     back_in,
     coupling_high,
     coupling_low,
-    conductances,
     picked,
     linear,
     capacity,
     capacity_all,
     cut_halo,
+    table,
+    operating,
     vector,
     forward,
     back,
-    near_operating,
-    operating,
     neighbours,
     weights,
     degree,
     linear_all,
-    table,
+    send_list,
+    boundary,
     entry_rows,
     weight_rows,
     copied,
@@ -172,11 +171,12 @@
     half = width - lanes
     node_groups = send_list.shape[0] // CAP
     side, part = place[0] % 2, place[1]
-    rows = operating.shape[0]
     copies = [
         pltpu.make_async_copy(source, target, copied.at[index])
         for index, (source, target) in enumerate(
             [
+                (send_list_in, send_list),
+                (boundary_in, boundary),
                 (neighbours_in, neighbours),
                 (weights_in, weights),
                 (degree_in, degree),
@@ -184,7 +184,6 @@
                 (capacity_in, capacity_all),
                 (table_in, table),
                 (operating_in, operating),
-                (near_operating_in, near_operating),
                 (vector_in, vector),
                 (forward_in.at[place[0]], forward),
                 (back_in.at[place[0]], back),
@@ -193,11 +192,13 @@
     ]
     for copy in copies:
         copy.start()
+    for copy in copies[:2]:
+        copy.wait()
 
     lane = lax.broadcasted_iota(I32, (8, lanes), 1)
 
     def name(slot, found):
-        target = lax.rem(part + slot // CAP + 1, node_groups)
+        target = part ^ (slot // CAP + 1)
         node = boundary[send_list[target * CAP + slot % CAP]]
         return jnp.where(lane == slot, node, found)
 
@@ -207,13 +208,12 @@
     hit = lax.broadcasted_iota(I32, (nodes, lanes), 0) == cut_nodes[:1]
     picked[...] = jnp.where(hit, 1.0, 0.0).astype(BF16)
 
-    for copy in copies[:6]:
+    for copy in copies[2:7]:
         copy.wait()
     mine = half_of(side, half)
     entry = neighbours[...]
     remote = entry - nodes
-    distance = part - (remote >> 4)
-    distance = jnp.where(distance < 0, distance + node_groups, distance)
+    distance = part ^ (remote >> 4)
     entry = jnp.where(remote < 0, entry, nodes + (distance - 1) * CAP + (remote & 15))
     live = lax.broadcasted_iota(I32, (slots, nodes), 0) < degree[...]
     neighbours[...] = entry
@@ -289,14 +289,23 @@
         coupling_high[nodes:, half:].astype(F32) + coupling_low[nodes:, half:].astype(F32)
     )
 
-    for copy in copies[6:]:
+    for copy in copies[7:]:
         copy.wait()
-    conductances[pl.ds(pl.multiple_of(side * rows, 8), rows), :nodes] = conductance(
-        operating[...], table[...]
-    )
-    conductances[pl.ds(pl.multiple_of((1 - side) * rows, 8), rows), :nodes] = conductance(
-        near_operating[...], table[...]
-    )
+
+
+def relay_kernel(*refs):
+    count = (len(refs) - 1) // 2
+    for source, target in zip(refs[1 : 1 + count], refs[1 + count :]):
+        target[...] = source[...]
+
+
+def conductance_kernel(place, near_operating, operating, table, picked, conductances):
+    rows, nodes = operating.shape
+    side = place[0] % 2
+    for at, values in ((side, operating), (1 - side, near_operating)):
+        conductances[pl.ds(pl.multiple_of(at * rows, 8), rows), :nodes] = conductance(
+            values[...], table[...]
+        )
     conductances[:, nodes:] = pick(conductances[:, :nodes], picked[...])
 
 
@@ -472,7 +481,7 @@
     blocks = []
     for step in range(1, steps + 1):
         theirs = jnp.concatenate(
-            [sender((step + block) % (steps + 1), block) for block in range(1, steps + 1)], axis=0
+            [sender(step ^ block, block) for block in range(1, steps + 1)], axis=0
         )
         gains = arrived[step - 1][:CAP, start : start + slots]
         image_part = arrived[step - 1][CAP : 2 * CAP, start : start + times]
@@ -515,6 +524,16 @@
     kept[...] = spectrum[:times]
     if spectrum.shape[0] > times:
         sent[...] = spectrum[times:]
+
+
+def merge_kernel(after, kept, arrived, own, near, far_sums):
+    rows = own.shape[0]
+    own[...] = kept[:rows] + arrived[:rows]
+    near[...] = kept[rows:] + arrived[rows : 2 * rows]
+    if arrived.shape[0] > 2 * rows:
+        far_sums[...] = arrived[2 * rows :]
+    else:
+        far_sums[...] = jnp.zeros(far_sums.shape, F32)
 
 
 def turned(field, first_pair, half_order):
@@ -653,17 +672,19 @@
 
 VMEM = pl.BlockSpec(memory_space=pltpu.VMEM)
 SMEM = pl.BlockSpec(memory_space=pltpu.SMEM)
-ANY = pl.BlockSpec(memory_space=pl.ANY)
-
-
-def run(kernel, name, specs, operands, outs, scratch=(), micros=1):
+
+
+HBM = pl.BlockSpec(memory_space=pltpu.HBM)
+
+
+def run(kernel, name, specs, operands, outs, scratch=(), micros=1, room=12):
     return pl.pallas_call(
         kernel,
         out_shape=[pltpu.VMEM(shape, dtype) for shape, dtype in outs],
         in_specs=specs,
         out_specs=[VMEM] * len(outs),
         scratch_shapes=list(scratch),
-        compiler_params=pltpu.CompilerParams(vmem_limit_bytes=40 * 2**20),
+        compiler_params=pltpu.CompilerParams(vmem_limit_bytes=room * 2**20),
         cost_estimate=pl.CostEstimate(
             flops=0, bytes_accessed=int(micros * 3e6), transcendentals=0
         ),
@@ -676,13 +697,13 @@
     return lax.ppermute(value, "samples", [(at, at ^ mask) for at in range(count)])
 
 
-def ahead(value, step):
+def trade(value, mask):
     count = lax.axis_size("nodes")
-    return lax.ppermute(value, "nodes", [(at, (at + step) % count) for at in range(count)])
+    return lax.ppermute(value, "nodes", [(at, at ^ mask) for at in range(count)])
 
 
 def total(value):
-    for axis in ("samples", "nodes"):
+    for axis in ("nodes", "samples"):
         count, stride = lax.axis_size(axis), 1
         while stride < count:
             radix = 4 if count // stride % 4 == 0 else 2
@@ -695,26 +716,38 @@
     return value
 
 
-def reduce_groups(kept, sent):
-    times = kept.shape[0]
+def reduce_groups(kept, sent, after):
+    times, half = kept.shape
     count = lax.axis_size("samples") // 2
-    extra = sent[(count - 1) * times :]
-    if count == 2:
+    block, arrived = kept, sent
+    if count > 2:
+        blocks = {group: sent[(group - 1) * times : group * times] for group in range(1, count)}
+        extra = sent[(count - 1) * times :]
+        blocks[0], bit = kept, count // 2
+        while bit > 1:
+            for group in [name for name in blocks if name & bit]:
+                blocks[group ^ bit] = blocks[group ^ bit] + swap(blocks.pop(group), 2 * bit)
+            bit //= 2
+        block = blocks[0]
+        others, bit = extra, 2
+        while bit < count:
+            others = others + swap(others, 2 * bit)
+            bit *= 2
+        arrived = jnp.concatenate([blocks[1], others], axis=0)
+        arrived = swap(arrived, 2)
+        arrived = jnp.concatenate([arrived[:times], arrived[times:] + others - extra], axis=0)
+    elif count == 2:
         arrived = swap(sent, 2)
-        return kept + arrived[:times], arrived[times:]
-    blocks = {0: kept}
-    for group in range(1, count):
-        blocks[group] = sent[(group - 1) * times : group * times]
-    bit = count // 2
-    while bit:
-        for group in [name for name in blocks if name & bit]:
-            blocks[group ^ bit] = blocks[group ^ bit] + swap(blocks.pop(group), 2 * bit)
-        bit //= 2
-    others, bit = extra, 1
-    while bit < count:
-        others = others + swap(others, 2 * bit)
-        bit *= 2
-    return blocks[0], others - extra
+    else:
+        arrived = jnp.zeros((times + sent.shape[0], half), F32)
+    own, near, extra = run(
+        merge_kernel,
+        "merge",
+        [VMEM] * 3,
+        (after, block, arrived),
+        [((times // 2, half), F32), ((times // 2, half), F32), ((8, half), F32)],
+    )
+    return own, swap(near, 1), extra
 
 
 def shards(
@@ -741,59 +774,81 @@
         value.reshape(1, -1) for value in (linear, capacity, degree, table)
     )
 
-    near_operating = swap(operating, 1)
-    vectors, bit = [vector], parts // 2
-    while bit:
-        vectors = vectors + [swap(piece, bit) for piece in vectors]
-        bit //= 2
-
     slot_count = weights.shape[0]
     (
         coupling_high,
         coupling_low,
-        conductances,
         picked,
         linear_wide,
         capacity_wide,
         capacity,
         cut_halo,
+        table,
+        own_operating,
         own_vector,
         forward,
         back,
     ) = run(
         prepare_kernel,
         "prepare",
-        [SMEM] * 3 + [ANY] * 11,
-        (place, send_list, boundary, near_operating, operating, neighbours, weights, degree)
-        + (linear, capacity, table, vector, forward, back),
+        [SMEM] + [HBM] * 12,
+        (place,)
+        + tuple(
+            pltpu.with_memory_space_constraint(value, pltpu.HBM)
+            for value in (neighbours, weights, degree, linear, capacity, send_list, boundary)
+            + (table, operating, vector, forward, back)
+        ),
         [
             ((sources, width), BF16),
             ((sources, width), BF16),
-            ((times, sources), F32),
             ((nodes, lanes), BF16),
             ((1, width), F32),
             ((1, width), F32),
             ((1, nodes), F32),
             ((lanes, lanes), F32),
+            (table.shape, F32),
+            ((rows, nodes), F32),
             ((rows, nodes), F32),
             (forward.shape[1:], BF16),
             (back.shape[1:], BF16),
         ],
         scratch=[
-            pltpu.VMEM((rows, nodes), F32),
-            pltpu.VMEM((rows, nodes), F32),
             pltpu.VMEM((slot_count, nodes), I32),
             pltpu.VMEM((slot_count, nodes), F32),
             pltpu.VMEM((1, nodes), I32),
             pltpu.VMEM((1, nodes), F32),
-            pltpu.VMEM(table.shape, F32),
+            pltpu.SMEM(send_list.shape, I32),
+            pltpu.SMEM(boundary.shape, I32),
             pltpu.VMEM((slot_count, width), I32),
             pltpu.VMEM((slot_count, width), F32),
-            pltpu.SemaphoreType.DMA((11,)),
+            pltpu.SemaphoreType.DMA((12,)),
         ],
         micros=8,
     )
+    near_operating = swap(operating, 1)
+    vectors, bit = [vector], parts // 2
+    while bit > 1:
+        vectors = vectors + [swap(piece, bit) for piece in vectors]
+        bit //= 2
+    far = len(vectors) - 1
+    if far:
+        vectors[1:] = run(
+            relay_kernel,
+            "relay",
+            [VMEM] * (far + 1),
+            (cut_halo, *vectors[1:]),
+            [((rows, nodes), F32)] * far,
+        )
+    vectors = vectors + [swap(piece, 1) for piece in vectors]
     vectors[0] = own_vector
+    (conductances,) = run(
+        conductance_kernel,
+        "conductance",
+        [SMEM] + [VMEM] * 4,
+        (place, near_operating, own_operating, table, picked),
+        [((times, sources), F32)],
+        micros=1,
+    )
 
     wide = ((times, half), F32)
     shared, start = packet_layout(steps, times)
@@ -817,12 +872,12 @@
         + [(packet, F32)] * steps,
         micros=2,
     )
-    arrived = [ahead(packet, step + 1) for step, packet in enumerate(sent)]
+    arrived = [trade(packet, step + 1) for step, packet in enumerate(sent)]
     others = []
     if not shared:
         gathered = lax.all_gather(cut_current, "nodes")
         distance = jnp.arange(node_groups, dtype=I32)
-        others = [gathered[(lax.axis_index("nodes") - distance) % node_groups]]
+        others = [gathered[lax.axis_index("nodes") ^ distance]]
     local_load, slope, own_wave, dual = run(
         local_kernel,
         "local",
@@ -843,10 +898,8 @@
     )
     own_sums = sent[rest:]
     near_image = swap(image, 1)
-    spectrum, far_sums = reduce_groups(kept, sent)
-    own_coefs, near_coefs = spectrum[:rows], swap(spectrum[rows:], 1)
-
-    second_load, kept, sent = run(
+
+    second_load, second_kept, second_sent = run(
         second_kernel,
         "second",
         [SMEM] + [VMEM] * 8,
@@ -856,6 +909,7 @@
         scratch=[pltpu.VMEM((2 * times, nodes), BF16)],
         micros=3,
     )
+    own_coefs, near_coefs, far_sums = reduce_groups(kept, sent, second_load)
     gathered = -(-node_groups * parts // LANES) * LANES
     answer, slope, scalars = run(
         functools.partial(products_kernel, length=length),
@@ -867,8 +921,7 @@
         micros=1,
     )
     scalars = total(scalars)
-    spectrum, _ = reduce_groups(kept, sent)
-    own_part, near_part = spectrum[:rows], swap(spectrum[rows:], 1)
+    own_part, near_part, _ = reduce_groups(second_kept, second_sent, answer)
     field = jax.ShapeDtypeStruct((rows, nodes), F32)
     return tuple(
         pl.pallas_call(
@@ -876,6 +929,7 @@
             out_shape=[field, field],
             in_specs=[VMEM] * 4 + [SMEM] + [VMEM] * 2,
             out_specs=[VMEM] * 2,
+            compiler_params=pltpu.CompilerParams(vmem_limit_bytes=12 * 2**20),
             name="last",
         )(scalars, own_vector, answer, slope, place, own_part, near_part)
     )

time: 79.2 us -> 48.8 us (0.62)
  local copies, waits for them, and re-layouts: 16.6 us -> 0.01 us
  waiting for transfers between devices: 19.2 us -> 11.6 us
  starting transfers between devices: 18.8 us -> 15.6 us
  Pallas kernels: 22.5 us -> 20.6 us
    unnamed x46 -> x0, local copies, waits for them, and re-layouts: 15.9 us -> none
    ppermute x9, waiting for transfers between devices: 12.9 us -> 5.59 us  [swap(): lax.ppermute(value, 'samples', [(at, at ^ mask) for at in range(count)])]
    ppermute x6, waiting for transfers between devices: 5.97 us -> 2.83 us  [total(): lax.ppermute(value, axis, [(at, at ^ step * stride) for at in range(count)])]
    ppermute x3, waiting for transfers between devices: 0.28 us -> 3.2 us  [trade(): lax.ppermute(value, 'nodes', [(at, at ^ mask) for at in range(count)])]
    ppermute x9, starting transfers between devices: 6.67 us -> 4.85 us  [swap(): lax.ppermute(value, 'samples', [(at, at ^ mask) for at in range(count)])]
    ppermute x3, starting transfers between devices: 5.82 us -> 4.45 us  [trade(): lax.ppermute(value, 'nodes', [(at, at ^ mask) for at in range(count)])]
    pallas_call x6 -> x10, Pallas kernels: 20.3 us -> 19.1 us  [run(): pl.pallas_call(kernel, out_shape=[pltpu.VMEM(shape, dtype) for shape, dty...]
  transfers between devices with their start and end apart: 18 -> 18, of which waited for: 7 -> 10; matrix products, arithmetic and copies ran while one was open for 2% -> 0% of each run, Pallas kernels for 20% -> 35%
where the time goes in v3:
time: 48.8 us; the launch traced here: 48.7 us
  Pallas kernels  20.6 us (42%)
  starting transfers between devices  15.6 us (32%)
  waiting for transfers between devices  11.6 us (24%)
  between operations  0.76 us (2%)
    pallas_call x10, Pallas kernels, run(): pl.pallas_call(kernel, out_shape=[pltpu.VMEM(shape, dtype) for shape, dty...  19.1 us
    ppermute x6, starting transfers between devices, total(): lax.ppermute(value, axis, [(at, at ^ step * stride) for at in range(count)])  6.25 us
    ppermute x9, waiting for transfers between devices, swap(): lax.ppermute(value, 'samples', [(at, at ^ mask) for at in range(count)])  5.59 us
    ppermute x9, starting transfers between devices, swap(): lax.ppermute(value, 'samples', [(at, at ^ mask) for at in range(count)])  4.85 us
    ppermute x3, starting transfers between devices, trade(): lax.ppermute(value, 'nodes', [(at, at ^ mask) for at in range(count)])  4.45 us
    ppermute x3, waiting for transfers between devices, trade(): lax.ppermute(value, 'nodes', [(at, at ^ mask) for at in range(count)])  3.2 us
    ppermute x6, waiting for transfers between devices, total(): lax.ppermute(value, axis, [(at, at ^ step * stride) for at in range(count)])  2.83 us
    pallas_call x1, Pallas kernels, shards(): pl.pallas_call(functools.partial(last_kernel, entries=entries), out_shape...  1.55 us
  transfers between devices with their start and end apart: 18, of which 10 were waited for; matrix products, arithmetic and copies ran while one was open for 0% of the time, Pallas kernels for 35%

profile of v3, /device:TPU:0, one launch (start us, length us, event | category | flops | bytes accessed | tf_op | source)
XLA Modules:
  0.0 48.7 jit_solution(1286451534961130429)
XLA Ops:
  0.6 3.0 %collective-permute-start = (f32[32,2048]{1,0:T(8,128)}, f32[32,2048]{1,0:T(8,128)S(1)}, u32[]{:S(2)}, u32[]{:S(2)}) collective-permute-start(f32[32,2048]{1,0:T(8,128)} %vector_in.1), channel_id=1, source_target_pairs={{0,2},{1,3},{2,0},{3,1},{4,6},{5,7},{6,4},{7,5},{8,10},{9,11},{10,... | collective-permute-start | bytes 786440 | tf_op jit(solution)/shard_map/ppermute | solution.py:697
  3.6 0.0 collective-permute-start.1
  3.6 0.5 %collective-permute-start.3 = (f32[32,2048]{1,0:T(8,128)}, f32[32,2048]{1,0:T(8,128)S(1)}, u32[]{:S(2)}, u32[]{:S(2)}) collective-permute-start(f32[32,2048]{1,0:T(8,128)} %operating_in.1), channel_id=1, source_target_pairs={{0,1},{1,0},{2,3},{3,2},{4,5},{5,4},{6,7},{7,6},{8,9},{9,8},{10,11... | collective-permute-start | bytes 786440 | tf_op jit(solution)/shard_map/ppermute | solution.py:697
  4.1 0.1 pad_add_fusion.place
  4.2 8.5 %prepare.1 = (bf16[2176,1152]{1,0:T(8,128)(2,1)S(1)}, bf16[2176,1152]{1,0:T(8,128)(2,1)S(1)}, bf16[2048,128]{1,0:T(8,128)(2,1)S(1)}, f32[1,1152]{1,0:T(1,128)S(1...) custom-call(s32[4]{0:T(128)S(1)} %pad_add_fusion.place, ...), custom_call_target="tpu_custom_call" | custom-call | bytes 24000000 | tf_op jit(solution)/shard_map/prepare/pallas_call | solution.py:681
  12.7 0.0 collective-permute-done.refs_1_
  12.8 0.1 collective-permute-start.2
  12.8 0.0 collective-permute-done.3.near_operating
  12.8 1.5 %conductance.1.refs_5_.conductances = f32[64,2176]{1,0:T(8,128)S(1)} custom-call(s32[4]{0:T(128)S(1)} %pad_add_fusion.place, f32[32,2048]{1,0:T(8,128)S(1)} %collective-permute-done.3.near_operating, f32[32,2048]{1,0:T(8,128)S(1)} %get-tuple-element.45.operating, f32[1,16]{1,0:T(1,128)S(1)} %get-tuple-element.46.table, ...), custom_call_target="tpu_custom_call" | custom-call | bytes 3000000 | tf_op jit(solution)/shard_map/conductance/pallas_call | solution.py:681
  14.4 0.0 collective-permute-done.1.refs_2_
  14.4 0.0 collective-permute-done.2.refs_3_
  14.4 1.2 %wave.1 = (bf16[128,2176]{1,0:T(8,128)(2,1)S(1)}, bf16[128,2176]{1,0:T(8,128)(2,1)S(1)}, f32[64,2176]{1,0:T(8,128)S(1)}, bf16[128,2048]{1,0:T(8,128)(2,1)S(1)}, ...) custom-call(f32[32,2048]{1,0:T(8,128)S(1)} %get-tuple-element.42.refs_0_.vector, ...), custom_call_target="tpu_custom_call" | custom-call | bytes 6000000 | tf_op jit(solution)/shard_map/wave/pallas_call | solution.py:681
  15.6 1.6 %collective-permute-start.4 = (f32[48,128]{1,0:T(8,128)S(1)}, f32[48,128]{1,0:T(8,128)S(1)}, u32[]{:S(2)}, u32[]{:S(2)}) collective-permute-start(f32[48,128]{1,0:T(8,128)S(1)} %get-tuple-element.52), channel_id=1, source_target_pairs={{0,4},{4,0},{8,12},{12,8},{1,5},{5,1},{9,13},{13,9},{2,6},{6,2},{1... | collective-permute-start | bytes 73736 | tf_op jit(solution)/shard_map/ppermute | solution.py:702
  17.2 2.6 %collective-permute-start.5 = (f32[48,128]{1,0:T(8,128)S(1)}, f32[48,128]{1,0:T(8,128)S(1)}, u32[]{:S(2)}, u32[]{:S(2)}) collective-permute-start(f32[48,128]{1,0:T(8,128)S(1)} %get-tuple-element.53), channel_id=1, source_target_pairs={{0,8},{4,12},{8,0},{12,4},{1,9},{5,13},{9,1},{13,5},{2,10},{6,14},... | collective-permute-start | bytes 73736 | tf_op jit(solution)/shard_map/ppermute | solution.py:702
  19.8 0.2 collective-permute-start.6
  20.0 2.2 %local.1 = (f32[64,1024]{1,0:T(8,128)S(1)}, f32[64,1024]{1,0:T(8,128)S(1)}, f32[64,1024]{1,0:T(8,128)S(1)}, f32[64,1024]{1,0:T(8,128)S(1)}) custom-call(bf16[128,2176]{1,0:T(8,128)(2,1)S(1)} %get-tuple-element.56.field_high, bf16[128,2176]{1,0:T(8,128)(2,1)S(1)} %get-tuple-element.57.field_low, bf16[2,192,128]{2,1,0:T(8,128)(2,1)S(1)} %get-tuple-element.44.refs_4_.forward, ...), custom_call_target="tpu_custom_call" | custom-call | bytes 9000000 | tf_op jit(solution)/shard_map/local/pallas_call | solution.py:681
  22.2 0.0 collective-permute-done.4.refs_0_
  22.2 0.0 collective-permute-done.5.refs_1_
  22.2 3.2 %collective-permute-done.6.refs_2_ = f32[48,128]{1,0:T(8,128)S(1)} collective-permute-done((f32[48,128]{1,0:T(8,128)S(1)}, f32[48,128]{1,0:T(8,128)S(1)}, u32[]{:S(2)}, u32[]{:S(2)}) %collective-permute-start.6) | collective-permute-done | bytes 24608 | tf_op jit(solution)/shard_map/ppermute | solution.py:702
  25.4 0.9 %first.1 = (f32[64,1024]{1,0:T(8,128)S(1)}, f32[64,1024]{1,0:T(8,128)S(1)}, f32[64,1024]{1,0:T(8,128)S(1)}, f32[72,1024]{1,0:T(8,128)S(1)}, f32[64,128]{1,0:T(8,128)S(1)}) custom-call(f32[48,128]{1,0:T(8,128)S(1)} %collective-permute-done.4.refs_0_, f32[48,128]{1,0:T(8,128)S(1)} %collective-permute-done.5.refs_1_, ...), custom_call_target="tpu_custom_call" | custom-call | bytes 3000000 | tf_op jit(solution)/shard_map/first/pallas_call | solution.py:681
  26.3 0.6 %collective-permute-start.8 = (f32[72,1024]{1,0:T(8,128)S(1)}, f32[72,1024]{1,0:T(8,128)S(1)}, u32[]{:S(2)}, u32[]{:S(2)}) collective-permute-start(f32[72,1024]{1,0:T(8,128)S(1)} %get-tuple-element.68), channel_id=1, source_target_pairs={{0,2},{1,3},{2,0},{3,1},{4,6},{5,7},{6,4},{7,5},{8,10},{9,11},{10,... | collective-permute-start | bytes 884744 | tf_op jit(solution)/shard_map/ppermute | solution.py:697
  26.9 0.0 collective-permute-start.7
  26.9 1.5 %collective-permute-done.7.near_image = f32[64,1024]{1,0:T(8,128)S(1)} collective-permute-done((f32[64,1024]{1,0:T(8,128)S(1)}, f32[64,1024]{1,0:T(8,128)S(1)}, u32[]{:S(2)}, u32[]{:S(2)}) %collective-permute-start.7) | collective-permute-done | bytes 262176 | tf_op jit(solution)/shard_map/ppermute | solution.py:697
  28.4 2.5 %second.1 = (f32[64,1024]{1,0:T(8,128)S(1)}, f32[64,1024]{1,0:T(8,128)S(1)}, f32[64,1024]{1,0:T(8,128)S(1)}) custom-call(s32[4]{0:T(128)S(1)} %pad_add_fusion.place, f32[64,128]{1,0:T(8,128)S(1)} %get-tuple-element.64.halo, f32[64,1024]{1,0:T(8,128)S(1)} %collective-permute-done.7.near_image, f32[64,1024]{1,0:T(8,128)S(1)} %get-tuple-element.65.image, ...), custom_call_target="tpu_custom_call" | custom-call | bytes 9000000 | tf_op jit(solution)/shard_map/second/pallas_call | solution.py:681
  30.9 3.2 %collective-permute-done.8.arrived = f32[72,1024]{1,0:T(8,128)S(1)} collective-permute-done((f32[72,1024]{1,0:T(8,128)S(1)}, f32[72,1024]{1,0:T(8,128)S(1)}, u32[]{:S(2)}, u32[]{:S(2)}) %collective-permute-start.8) | collective-permute-done | bytes 294944 | tf_op jit(solution)/shard_map/ppermute | solution.py:697
  34.1 0.1 collective-permute-start.9
  34.2 0.6 %collective-permute-start.16 = (f32[64,1024]{1,0:T(8,128)S(1)}, f32[64,1024]{1,0:T(8,128)S(1)}, u32[]{:S(2)}, u32[]{:S(2)}) collective-permute-start(f32[64,1024]{1,0:T(8,128)S(1)} %get-tuple-element.79), channel_id=1, source_target_pairs={{0,2},{1,3},{2,0},{3,1},{4,6},{5,7},{6,4},{7,5},{8,10},{9,11},{10,... | collective-permute-start | bytes 786440 | tf_op jit(solution)/shard_map/ppermute | solution.py:697
  34.8 0.7 %collective-permute-done.9.near_image = f32[32,1024]{1,0:T(8,128)S(1)} collective-permute-done((f32[32,1024]{1,0:T(8,128)S(1)}, f32[32,1024]{1,0:T(8,128)S(1)}, u32[]{:S(2)}, u32[]{:S(2)}) %collective-permute-start.9) | collective-permute-done | bytes 131104 | tf_op jit(solution)/shard_map/ppermute | solution.py:697
  35.6 1.7 %products.1 = (f32[32,2048]{1,0:T(8,128)S(1)}, f32[32,2048]{1,0:T(8,128)S(1)}, f32[16,128]{1,0:T(8,128)S(1)}) custom-call(s32[4]{0:T(128)S(1)} %pad_add_fusion.place, f32[32,2048]{1,0:T(8,128)S(1)} %get-tuple-element.42.refs_0_.vector, f32[32,1024]{1,0:T(8,128)S(1)} %get-tuple-element.69.own_image, f32[32,1024]{1,0:T(8,128)S(1)} %collective-permute-done.9.near_image, ...), custom_call_target="tpu_custom_call" | custom-call | bytes 3000000 | tf_op jit(solution)/shard_map/products/pallas_call | solution.py:681
  37.2 1.3 %collective-permute-start.12 = (f32[16,128]{1,0:T(8,128)S(1)}, f32[16,128]{1,0:T(8,128)S(1)}, u32[]{:S(2)}, u32[]{:S(2)}) collective-permute-start(f32[16,128]{1,0:T(8,128)S(1)} %get-tuple-element.75), channel_id=1, source_target_pairs={{0,12},{4,8},{8,4},{12,0},{1,13},{5,9},{9,5},{13,1},{2,14},{6,10},... | collective-permute-start | bytes 24584 | tf_op jit(solution)/shard_map/ppermute | solution.py:711
  38.5 0.0 collective-permute-start.11
  38.5 3.1 %collective-permute-start.10 = (f32[16,128]{1,0:T(8,128)S(1)}, f32[16,128]{1,0:T(8,128)S(1)}, u32[]{:S(2)}, u32[]{:S(2)}) collective-permute-start(f32[16,128]{1,0:T(8,128)S(1)} %get-tuple-element.75), channel_id=1, source_target_pairs={{0,4},{4,0},{8,12},{12,8},{1,5},{5,1},{9,13},{13,9},{2,6},{6,2},{1... | collective-permute-start | bytes 24584 | tf_op jit(solution)/shard_map/ppermute | solution.py:711
  41.6 1.1 %collective-permute-done.12 = f32[16,128]{1,0:T(8,128)S(1)} collective-permute-done((f32[16,128]{1,0:T(8,128)S(1)}, f32[16,128]{1,0:T(8,128)S(1)}, u32[]{:S(2)}, u32[]{:S(2)}) %collective-permute-start.12) | collective-permute-done | bytes 8224 | tf_op jit(solution)/shard_map/ppermute | solution.py:711
  42.7 0.4 collective-permute-done.11
  43.1 0.2 collective-permute-done.10
  43.2 0.0 collective-permute-start.15
  43.2 0.8 %collective-permute-start.14 = (f32[16,128]{1,0:T(8,128)S(1)}, f32[16,128]{1,0:T(8,128)S(1)}, u32[]{:S(2)}, u32[]{:S(2)}) collective-permute-start(f32[16,128]{1,0:T(8,128)S(1)} %add_add_fusion.1), channel_id=1, source_target_pairs={{0,2},{1,3},{2,0},{3,1},{4,6},{5,7},{6,4},{7,5},{8,10},{9,11},{10,... | collective-permute-start | bytes 24584 | tf_op jit(solution)/shard_map/ppermute | solution.py:711
  44.1 1.0 %collective-permute-start.13 = (f32[16,128]{1,0:T(8,128)S(1)}, f32[16,128]{1,0:T(8,128)S(1)}, u32[]{:S(2)}, u32[]{:S(2)}) collective-permute-start(f32[16,128]{1,0:T(8,128)S(1)} %add_add_fusion.1), channel_id=1, source_target_pairs={{0,1},{1,0},{2,3},{3,2},{4,5},{5,4},{6,7},{7,6},{8,9},{9,8},{10,11... | collective-permute-start | bytes 24584 | tf_op jit(solution)/shard_map/ppermute | solution.py:711
  45.1 0.0 collective-permute-done.16.arrived
  45.1 0.7 %merge.3 = (f32[32,1024]{1,0:T(8,128)S(1)}, f32[32,1024]{1,0:T(8,128)S(1)}, f32[8,1024]{1,0:T(8,128)}) custom-call(f32[32,2048]{1,0:T(8,128)S(1)} %get-tuple-element.76.after.answer, f32[64,1024]{1,0:T(8,128)S(1)} %get-tuple-element.78.kept, f32[64,1024]{1,0:T(8,128)S(1)} %collective-permute-done.16.arrived), custom_call_target="tpu_custom_call" | custom-call | bytes 3000000 | tf_op jit(solution)/shard_map/merge/pallas_call | solution.py:681
  45.8 0.0 collective-permute-start.17
  45.8 0.6 %collective-permute-done.15 = f32[16,128]{1,0:T(8,128)S(1)} collective-permute-done((f32[16,128]{1,0:T(8,128)S(1)}, f32[16,128]{1,0:T(8,128)S(1)}, u32[]{:S(2)}, u32[]{:S(2)}) %collective-permute-start.15) | collective-permute-done | bytes 8224 | tf_op jit(solution)/shard_map/ppermute | solution.py:711
  46.3 0.6 %collective-permute-done.14 = f32[16,128]{1,0:T(8,128)S(1)} collective-permute-done((f32[16,128]{1,0:T(8,128)S(1)}, f32[16,128]{1,0:T(8,128)S(1)}, u32[]{:S(2)}, u32[]{:S(2)}) %collective-permute-start.14) | collective-permute-done | bytes 8224 | tf_op jit(solution)/shard_map/ppermute | solution.py:711
  47.0 0.0 collective-permute-done.13
  47.0 0.1 collective-permute-done.17.near_part
  47.1 1.6 %last.1 = (f32[32,2048]{1,0:T(8,128)}, f32[32,2048]{1,0:T(8,128)}) custom-call(f32[16,128]{1,0:T(8,128)S(1)} %add_add_fusion.gathered, f32[32,2048]{1,0:T(8,128)S(1)} %get-tuple-element.42.refs_0_.vector, f32[32,2048]{1,0:T(8,128)S(1)} %get-tuple-element.76.after.answer, f32[32,2048]{1,0:T(8,128)S(1)} %get-tuple-element.77.slope, s32[4]{0:T(128)S(1)} %pad_add_fusion.place, ...), custom_call_target="tpu_custom_call" | custom-call | tf_op jit(solution)/shard_map/last/pallas_call | solution.py:927
  (6 shorter events, 0.1 us)
Async XLA Ops:
  0.6 12.1 %collective-permute-start = (f32[32,2048]{1,0:T(8,128)}, f32[32,2048]{1,0:T(8,128)S(1)}, u32[]{:S(2)}, u32[]{:S(2)}) collective-permute-start(f32[32,2048]{1,0:T(8,128)} %vector_in.1), channel_id=1, source_target_pairs={{0,2},{1,3},{2,0},{3,1},{4,6},{5,7},{6,4},{7,5},{8,10},{9,11},{10,... | collective-permute-start | bytes 786440 | tf_op jit(solution)/shard_map/ppermute | solution.py:697
  3.6 10.7 %collective-permute-start.1 = (f32[32,2048]{1,0:T(8,128)}, f32[32,2048]{1,0:T(8,128)S(1)}, u32[]{:S(2)}, u32[]{:S(2)}) collective-permute-start(f32[32,2048]{1,0:T(8,128)} %vector_in.1), channel_id=1, source_target_pairs={{0,1},{1,0},{2,3},{3,2},{4,5},{5,4},{6,7},{7,6},{8,9},{9,8},{10,11... | collective-permute-start | bytes 786440 | tf_op jit(solution)/shard_map/ppermute | solution.py:697
  3.6 9.2 %collective-permute-start.3 = (f32[32,2048]{1,0:T(8,128)}, f32[32,2048]{1,0:T(8,128)S(1)}, u32[]{:S(2)}, u32[]{:S(2)}) collective-permute-start(f32[32,2048]{1,0:T(8,128)} %operating_in.1), channel_id=1, source_target_pairs={{0,1},{1,0},{2,3},{3,2},{4,5},{5,4},{6,7},{7,6},{8,9},{9,8},{10,11... | collective-permute-start | bytes 786440 | tf_op jit(solution)/shard_map/ppermute | solution.py:697
  12.8 1.6 %collective-permute-start.2 = (f32[32,2048]{1,0:T(8,128)S(1)}, f32[32,2048]{1,0:T(8,128)S(1)}, u32[]{:S(2)}, u32[]{:S(2)}) collective-permute-start(f32[32,2048]{1,0:T(8,128)S(1)} %relay.1.refs_1_), channel_id=1, source_target_pairs={{0,1},{1,0},{2,3},{3,2},{4,5},{5,4},{6,7},{7,6},{8,9},{9,8},{10,11... | collective-permute-start | bytes 786440 | tf_op jit(solution)/shard_map/ppermute | solution.py:697
  15.6 6.6 %collective-permute-start.4 = (f32[48,128]{1,0:T(8,128)S(1)}, f32[48,128]{1,0:T(8,128)S(1)}, u32[]{:S(2)}, u32[]{:S(2)}) collective-permute-start(f32[48,128]{1,0:T(8,128)S(1)} %get-tuple-element.52), channel_id=1, source_target_pairs={{0,4},{4,0},{8,12},{12,8},{1,5},{5,1},{9,13},{13,9},{2,6},{6,2},{1... | collective-permute-start | bytes 73736 | tf_op jit(solution)/shard_map/ppermute | solution.py:702
  17.2 5.0 %collective-permute-start.5 = (f32[48,128]{1,0:T(8,128)S(1)}, f32[48,128]{1,0:T(8,128)S(1)}, u32[]{:S(2)}, u32[]{:S(2)}) collective-permute-start(f32[48,128]{1,0:T(8,128)S(1)} %get-tuple-element.53), channel_id=1, source_target_pairs={{0,8},{4,12},{8,0},{12,4},{1,9},{5,13},{9,1},{13,5},{2,10},{6,14},... | collective-permute-start | bytes 73736 | tf_op jit(solution)/shard_map/ppermute | solution.py:702
  19.8 5.6 %collective-permute-start.6 = (f32[48,128]{1,0:T(8,128)S(1)}, f32[48,128]{1,0:T(8,128)S(1)}, u32[]{:S(2)}, u32[]{:S(2)}) collective-permute-start(f32[48,128]{1,0:T(8,128)S(1)} %get-tuple-element.54), channel_id=1, source_target_pairs={{0,12},{4,8},{8,4},{12,0},{1,13},{5,9},{9,5},{13,1},{2,14},{6,10},... | collective-permute-start | bytes 73736 | tf_op jit(solution)/shard_map/ppermute | solution.py:702
  26.3 7.8 %collective-permute-start.8 = (f32[72,1024]{1,0:T(8,128)S(1)}, f32[72,1024]{1,0:T(8,128)S(1)}, u32[]{:S(2)}, u32[]{:S(2)}) collective-permute-start(f32[72,1024]{1,0:T(8,128)S(1)} %get-tuple-element.68), channel_id=1, source_target_pairs={{0,2},{1,3},{2,0},{3,1},{4,6},{5,7},{6,4},{7,5},{8,10},{9,11},{10,... | collective-permute-start | bytes 884744 | tf_op jit(solution)/shard_map/ppermute | solution.py:697
  26.9 1.5 %collective-permute-start.7 = (f32[64,1024]{1,0:T(8,128)S(1)}, f32[64,1024]{1,0:T(8,128)S(1)}, u32[]{:S(2)}, u32[]{:S(2)}) collective-permute-start(f32[64,1024]{1,0:T(8,128)S(1)} %get-tuple-element.65.image), channel_id=1, source_target_pairs={{0,1},{1,0},{2,3},{3,2},{4,5},{5,4},{6,7},{7,6},{8,9},{9,8},{10,11... | collective-permute-start | bytes 786440 | tf_op jit(solution)/shard_map/ppermute | solution.py:697
  34.1 1.4 %collective-permute-start.9 = (f32[32,1024]{1,0:T(8,128)S(1)}, f32[32,1024]{1,0:T(8,128)S(1)}, u32[]{:S(2)}, u32[]{:S(2)}) collective-permute-start(f32[32,1024]{1,0:T(8,128)S(1)} %get-tuple-element.70), channel_id=1, source_target_pairs={{0,1},{1,0},{2,3},{3,2},{4,5},{5,4},{6,7},{7,6},{8,9},{9,8},{10,11... | collective-permute-start | bytes 393224 | tf_op jit(solution)/shard_map/ppermute | solution.py:697
  34.2 10.9 %collective-permute-start.16 = (f32[64,1024]{1,0:T(8,128)S(1)}, f32[64,1024]{1,0:T(8,128)S(1)}, u32[]{:S(2)}, u32[]{:S(2)}) collective-permute-start(f32[64,1024]{1,0:T(8,128)S(1)} %get-tuple-element.79), channel_id=1, source_target_pairs={{0,2},{1,3},{2,0},{3,1},{4,6},{5,7},{6,4},{7,5},{8,10},{9,11},{10,... | collective-permute-start | bytes 786440 | tf_op jit(solution)/shard_map/ppermute | solution.py:697
  37.2 5.5 %collective-permute-start.12 = (f32[16,128]{1,0:T(8,128)S(1)}, f32[16,128]{1,0:T(8,128)S(1)}, u32[]{:S(2)}, u32[]{:S(2)}) collective-permute-start(f32[16,128]{1,0:T(8,128)S(1)} %get-tuple-element.75), channel_id=1, source_target_pairs={{0,12},{4,8},{8,4},{12,0},{1,13},{5,9},{9,5},{13,1},{2,14},{6,10},... | collective-permute-start | bytes 24584 | tf_op jit(solution)/shard_map/ppermute | solution.py:711
  38.5 4.5 %collective-permute-start.11 = (f32[16,128]{1,0:T(8,128)S(1)}, f32[16,128]{1,0:T(8,128)S(1)}, u32[]{:S(2)}, u32[]{:S(2)}) collective-permute-start(f32[16,128]{1,0:T(8,128)S(1)} %get-tuple-element.75), channel_id=1, source_target_pairs={{0,8},{4,12},{8,0},{12,4},{1,9},{5,13},{9,1},{13,5},{2,10},{6,14},... | collective-permute-start | bytes 24584 | tf_op jit(solution)/shard_map/ppermute | solution.py:711
  38.5 4.7 %collective-permute-start.10 = (f32[16,128]{1,0:T(8,128)S(1)}, f32[16,128]{1,0:T(8,128)S(1)}, u32[]{:S(2)}, u32[]{:S(2)}) collective-permute-start(f32[16,128]{1,0:T(8,128)S(1)} %get-tuple-element.75), channel_id=1, source_target_pairs={{0,4},{4,0},{8,12},{12,8},{1,5},{5,1},{9,13},{13,9},{2,6},{6,2},{1... | collective-permute-start | bytes 24584 | tf_op jit(solution)/shard_map/ppermute | solution.py:711
  43.2 3.1 %collective-permute-start.15 = (f32[16,128]{1,0:T(8,128)S(1)}, f32[16,128]{1,0:T(8,128)S(1)}, u32[]{:S(2)}, u32[]{:S(2)}) collective-permute-start(f32[16,128]{1,0:T(8,128)S(1)} %add_add_fusion.1), channel_id=1, source_target_pairs={{0,3},{1,2},{2,1},{3,0},{4,7},{5,6},{6,5},{7,4},{8,11},{9,10},{10,... | collective-permute-start | bytes 24584 | tf_op jit(solution)/shard_map/ppermute | solution.py:711
  43.2 3.7 %collective-permute-start.14 = (f32[16,128]{1,0:T(8,128)S(1)}, f32[16,128]{1,0:T(8,128)S(1)}, u32[]{:S(2)}, u32[]{:S(2)}) collective-permute-start(f32[16,128]{1,0:T(8,128)S(1)} %add_add_fusion.1), channel_id=1, source_target_pairs={{0,2},{1,3},{2,0},{3,1},{4,6},{5,7},{6,4},{7,5},{8,10},{9,11},{10,... | collective-permute-start | bytes 24584 | tf_op jit(solution)/shard_map/ppermute | solution.py:711
  44.1 2.9 %collective-permute-start.13 = (f32[16,128]{1,0:T(8,128)S(1)}, f32[16,128]{1,0:T(8,128)S(1)}, u32[]{:S(2)}, u32[]{:S(2)}) collective-permute-start(f32[16,128]{1,0:T(8,128)S(1)} %add_add_fusion.1), channel_id=1, source_target_pairs={{0,1},{1,0},{2,3},{3,2},{4,5},{5,4},{6,7},{7,6},{8,9},{9,8},{10,11... | collective-permute-start | bytes 24584 | tf_op jit(solution)/shard_map/ppermute | solution.py:711
  45.8 1.3 %collective-permute-start.17 = (f32[32,1024]{1,0:T(8,128)S(1)}, f32[32,1024]{1,0:T(8,128)S(1)}, u32[]{:S(2)}, u32[]{:S(2)}) collective-permute-start(f32[32,1024]{1,0:T(8,128)S(1)} %get-tuple-element.81), channel_id=1, source_target_pairs={{0,1},{1,0},{2,3},{3,2},{4,5},{5,4},{6,7},{7,6},{8,9},{9,8},{10,11... | collective-permute-start | bytes 393224 | tf_op jit(solution)/shard_map/ppermute | solution.py:697

commit v4 on v3

--- a/solution.py
+++ b/solution.py
@@ -29,7 +29,7 @@
     for pair in range(length // 2):
         turn[2 * pair, 2 * pair + 1] = pair / (length // 2)
         turn[2 * pair + 1, 2 * pair] = -pair / (length // 2)
-    return synthesis, analysis, synthesis @ turn
+    return synthesis, analysis, turn
 
 
 def halves(table):
@@ -47,7 +47,8 @@
 
 
 def transform_tables(length, parts):
-    synthesis, analysis, slope = spectral_tables(length)
+    synthesis, analysis, turn = spectral_tables(length)
+    slope, dual_slope = synthesis @ turn, analysis.T @ turn
     rows = length // parts
     forward, back = [], []
     for place in range(parts):
@@ -60,6 +61,7 @@
                     synthesis[np.ix_(times, coefs)],
                     slope[np.ix_(times, coefs)],
                     analysis[np.ix_(coefs, times)].T,
+                    dual_slope[np.ix_(times, coefs)],
                 ]
             )
         )
@@ -397,6 +399,7 @@
     slope,
     own_wave,
     dual,
+    dual_slope,
 ):
     times, half = load.shape
     sources = slice(0, current.shape[1])
@@ -405,7 +408,8 @@
         (forward[0, times:], forward[1, times:]), (field_high[:, mine], field_low[:, mine])
     )
     slope[...] = capacity[:, :half] * others[:times]
-    dual[...] = others[times:]
+    dual[...] = others[times : 2 * times]
+    dual_slope[...] = capacity[:, :half] * others[2 * times :]
     own_wave[...] = wave[:, mine]
     load[...] = own_wave[...] * (linear[:, :half] + conductances[:, mine])
     high = current[:times]
@@ -439,6 +443,7 @@
         load,
         kept,
         sent,
+        sums,
         halo,
     ) = refs[steps + apart :]
     times, half = local_load.shape
@@ -472,11 +477,10 @@
     image[...] = answer
     spectrum = dot_split((back[0], back[1]), split(answer))
     kept[...] = spectrum[:times]
-    rest = spectrum.shape[0] - times
-    if rest:
-        sent[:rest] = spectrum[times:]
+    if spectrum.shape[0] > times:
+        sent[...] = spectrum[times:]
     lines = [*signed_sums(answer), *signed_sums(own_wave[...])]
-    sent[rest:] = jnp.concatenate(lines + [jnp.zeros((4, half), F32)], axis=0)
+    sums[...] = jnp.concatenate(lines + [jnp.zeros((4, half), F32)], axis=0)
 
     blocks = []
     for step in range(1, steps + 1):
@@ -526,14 +530,10 @@
         sent[...] = spectrum[times:]
 
 
-def merge_kernel(after, kept, arrived, own, near, far_sums):
+def merge_kernel(after, kept, arrived, own, near):
     rows = own.shape[0]
     own[...] = kept[:rows] + arrived[:rows]
-    near[...] = kept[rows:] + arrived[rows : 2 * rows]
-    if arrived.shape[0] > 2 * rows:
-        far_sums[...] = arrived[2 * rows :]
-    else:
-        far_sums[...] = jnp.zeros(far_sums.shape, F32)
+    near[...] = kept[rows:] + arrived[rows:]
 
 
 def turned(field, first_pair, half_order):
@@ -559,53 +559,27 @@
 def products_kernel(
     place,
     vector,
-    own_image,
-    near_image,
-    capacity,
     load,
     second_load,
     image,
     wave,
     dual,
-    own_sums,
-    far_sums,
-    answer,
-    slope,
+    dual_slope,
+    sums,
     scalars,
     *,
     length,
 ):
-    side = place[0] % 2
-    rows = vector.shape[0]
-    first_pair = place[0] * (rows // 2)
-    join(answer, side, own_image[...], near_image[...])
-    field, start = answer[...], vector[...]
-    squares = scalar_sum(start * start)
-    coeff = guess(scalar_sum(start * field), squares)
-    slope[...] = capacity[...] * turned(field, first_pair, length // 2)
-    start_slope = capacity[...] * turned(start, first_pair, length // 2)
-    rest = field - coeff * start
-    rest_slope = slope[...] - coeff * start_slope
-    found = [
-        coeff,
-        squares,
-        scalar_sum(start * rest),
-        scalar_sum(rest * rest),
-        scalar_sum(start * rest_slope),
-        scalar_sum(start * start_slope),
-        scalar_sum(rest * rest_slope),
-        scalar_sum(rest * start_slope),
-    ]
-
-    sums = own_sums[...] + far_sums[...]
-    base = wave[...]
-    coeff = guess(scalar_sum(base * image[...]), scalar_sum(base * base))
-    rest = image[...] - coeff * base
-    rest_sums = [sums[line : line + 1] - coeff * sums[line + 2 : line + 3] for line in (0, 1)]
-    base_sums = [sums[line + 2 : line + 3] for line in (0, 1)]
-    first = load[...]
+    start, first = wave[...], load[...]
+    field = vector[...]
+    coeff = guess(scalar_sum(start * image[...]), scalar_sum(start * start))
+    rest = image[...] - coeff * start
     change = second_load[...] - coeff * first
-    first_ends, change_ends = signed_sums(first), signed_sums(change)
+    start_sums = [sums[line + 2 : line + 3] for line in (0, 1)]
+    rest_sums = [sums[line : line + 1] - coeff * start_sums[line] for line in (0, 1)]
+    start_ends, rest_ends, first_ends, change_ends = (
+        signed_sums(values) for values in (start, rest, first, change)
+    )
 
     def mixed(values, value_sums, others, other_ends):
         ends = value_sums[0] * other_ends[0] + value_sums[1] * other_ends[1]
@@ -613,18 +587,40 @@
             1.0 / length / length
         )
 
-    found += [
+    found = [
         coeff,
-        scalar_sum(dual[...] * change),
-        scalar_sum(dual[...] * first),
+        scalar_sum(field * field),
+        scalar_sum(dual[...] * rest),
+        scalar_sum(dual[...] * start),
+        mixed(rest, rest_sums, rest, rest_ends),
+        mixed(rest, rest_sums, start, start_ends) + mixed(start, start_sums, rest, rest_ends),
+        mixed(start, start_sums, start, start_ends),
+        scalar_sum(dual[...] * change - dual_slope[...] * rest),
+        scalar_sum(dual[...] * first - dual_slope[...] * start),
         mixed(rest, rest_sums, change, change_ends),
-        mixed(rest, rest_sums, first, first_ends) + mixed(base, base_sums, change, change_ends),
-        mixed(base, base_sums, first, first_ends),
+        mixed(rest, rest_sums, first, first_ends) + mixed(start, start_sums, change, change_ends),
+        mixed(start, start_sums, first, first_ends),
     ]
     device = place[1] * place[3] + place[0]
     lane = lax.broadcasted_iota(I32, scalars.shape, 1)
-    column = jnp.concatenate(found + [jnp.zeros((2, 1), F32)], axis=0)
+    column = jnp.concatenate(found + [jnp.zeros((4, 1), F32)], axis=0)
     scalars[...] = jnp.where(lane == device, column, 0.0)
+
+
+def settle_kernel(place, own_image, near_image, vector, capacity, answer, slope, skew, *, length):
+    rows = vector.shape[0]
+    first_pair = place[0] * (rows // 2)
+    join(answer, place[0] % 2, own_image[...], near_image[...])
+    field, start = answer[...], vector[...]
+    slope[...] = capacity[...] * turned(field, first_pair, length // 2)
+    start_slope = capacity[...] * turned(start, first_pair, length // 2)
+    products = [
+        scalar_sum(field * slope[...]),
+        scalar_sum(field * start_slope + start * slope[...]),
+        scalar_sum(start * start_slope),
+        jnp.zeros((5, 1), F32),
+    ]
+    skew[...] = jnp.broadcast_to(jnp.concatenate(products, axis=0), skew.shape)
 
 
 def last_kernel(
@@ -632,6 +628,7 @@
     vector,
     answer,
     slope,
+    skew,
     place,
     own_part,
     near_part,
@@ -639,22 +636,22 @@
     next_residue,
     *,
     entries,
+    devices,
 ):
     side = place[0] % 2
-    own = [gathered[line : line + 1, :] for line in range(14)]
+    own = [gathered[line : line + 1, :] for line in range(12)]
 
     def everywhere(values):
         return jnp.sum(values, axis=1, keepdims=True) / entries
 
     scale_square = everywhere(own[1]) + EPSILON
-    coeff = everywhere(own[2] + own[0] * own[1]) / scale_square
+    coeff = everywhere(own[2] + own[0] * own[3]) / scale_square
     near = own[0] - coeff
-    rest_square = everywhere(own[3] + near * (2.0 * own[2] + near * own[1]))
-    along_one = own[4] + near * own[5]
-    along_two = own[6] + near * (own[4] + own[7] + near * own[5])
-    near = own[8] - coeff
-    along_one = everywhere(along_one + own[9] + near * own[10])
-    along_two = everywhere(along_two + own[11] + near * (own[12] + near * own[13]))
+    rest_square = everywhere(own[4] + near * (own[5] + near * own[6]))
+    along_one = everywhere(own[7] + near * own[8])
+    along_two = everywhere(own[9] + near * (own[10] + near * own[11]))
+    turn = skew[0:1, :1] - coeff * (skew[1:2, :1] - coeff * skew[2:3, :1])
+    along_two = along_two + turn * (devices / entries)
     scale = jnp.sqrt(scale_square)
     second_norm = jnp.sqrt(jnp.maximum(rest_square, 0.0) / scale_square + EPSILON)
     inverse = 1.0 / (second_norm * scale)
@@ -702,52 +699,39 @@
     return lax.ppermute(value, "nodes", [(at, at ^ mask) for at in range(count)])
 
 
-def total(value):
-    for axis in ("nodes", "samples"):
-        count, stride = lax.axis_size(axis), 1
-        while stride < count:
-            radix = 4 if count // stride % 4 == 0 else 2
-            others = [
-                lax.ppermute(value, axis, [(at, at ^ (step * stride)) for at in range(count)])
-                for step in range(1, radix)
-            ]
-            value = value + functools.reduce(jnp.add, others)
-            stride *= radix
+def total(value, axis):
+    count, stride = lax.axis_size(axis), 1
+    while stride < count:
+        radix = 4 if count // stride % 4 == 0 else 2
+        others = [
+            lax.ppermute(value, axis, [(at, at ^ (step * stride)) for at in range(count)])
+            for step in range(1, radix)
+        ]
+        value = value + functools.reduce(jnp.add, others)
+        stride *= radix
     return value
 
 
-def reduce_groups(kept, sent, after):
-    times, half = kept.shape
+def send_groups(kept, sent):
+    times = kept.shape[0]
     count = lax.axis_size("samples") // 2
-    block, arrived = kept, sent
-    if count > 2:
-        blocks = {group: sent[(group - 1) * times : group * times] for group in range(1, count)}
-        extra = sent[(count - 1) * times :]
-        blocks[0], bit = kept, count // 2
-        while bit > 1:
-            for group in [name for name in blocks if name & bit]:
-                blocks[group ^ bit] = blocks[group ^ bit] + swap(blocks.pop(group), 2 * bit)
-            bit //= 2
-        block = blocks[0]
-        others, bit = extra, 2
-        while bit < count:
-            others = others + swap(others, 2 * bit)
-            bit *= 2
-        arrived = jnp.concatenate([blocks[1], others], axis=0)
-        arrived = swap(arrived, 2)
-        arrived = jnp.concatenate([arrived[:times], arrived[times:] + others - extra], axis=0)
-    elif count == 2:
-        arrived = swap(sent, 2)
-    else:
-        arrived = jnp.zeros((times + sent.shape[0], half), F32)
-    own, near, extra = run(
-        merge_kernel,
-        "merge",
-        [VMEM] * 3,
-        (after, block, arrived),
-        [((times // 2, half), F32), ((times // 2, half), F32), ((8, half), F32)],
-    )
-    return own, swap(near, 1), extra
+    blocks = {0: kept}
+    for group in range(1, count):
+        blocks[group] = sent[(group - 1) * times : group * times] if count > 2 else sent
+    bit = count // 2
+    while bit > 1:
+        for group in [name for name in blocks if name & bit]:
+            blocks[group ^ bit] = blocks[group ^ bit] + swap(blocks.pop(group), 2 * bit)
+        bit //= 2
+    return blocks[0], swap(blocks[1], 2) if count > 1 else jnp.zeros_like(kept)
+
+
+def merge(after, kept, arrived):
+    half_block = ((kept.shape[0] // 2, kept.shape[1]), F32)
+    own, near = run(
+        merge_kernel, "merge", [VMEM] * 3, (after, kept, arrived), [half_block, half_block]
+    )
+    return own, swap(near, 1)
 
 
 def shards(
@@ -878,27 +862,30 @@
         gathered = lax.all_gather(cut_current, "nodes")
         distance = jnp.arange(node_groups, dtype=I32)
         others = [gathered[lax.axis_index("nodes") ^ distance]]
-    local_load, slope, own_wave, dual = run(
+    local_load, slope, own_wave, dual, dual_slope = run(
         local_kernel,
         "local",
         [VMEM] * 10 + [SMEM],
         (field_high, field_low, forward, wave, current, conductances)
         + (coupling_high, coupling_low, linear_wide, capacity_wide, place),
-        [wide] * 4,
+        [wide] * 5,
         micros=3,
     )
     rest = length - times
-    image, load, kept, sent, halo = run(
+    image, load, kept, sent, sums, halo = run(
         functools.partial(first_kernel, steps=steps, apart=len(others)),
         "first",
         [VMEM] * (steps + len(others) + 7),
         (*arrived, *others, cut_current, local_load, slope, own_wave, back, coupling_high, coupling_low),
-        [wide, wide, wide, ((rest + 8, half), F32), ((times, lanes), F32)],
+        [wide, wide, wide, ((max(rest, 8), half), F32), ((8, half), F32), ((times, lanes), F32)],
         micros=1,
     )
-    own_sums = sent[rest:]
     near_image = swap(image, 1)
-
+    bit = 2
+    while bit < parts:
+        sums = sums + swap(sums, bit)
+        bit *= 2
+    kept, arrived = send_groups(kept, sent)
     second_load, second_kept, second_sent = run(
         second_kernel,
         "second",
@@ -909,29 +896,40 @@
         scratch=[pltpu.VMEM((2 * times, nodes), BF16)],
         micros=3,
     )
-    own_coefs, near_coefs, far_sums = reduce_groups(kept, sent, second_load)
     gathered = -(-node_groups * parts // LANES) * LANES
-    answer, slope, scalars = run(
+    (scalars,) = run(
         functools.partial(products_kernel, length=length),
         "products",
-        [SMEM] + [VMEM] * 11,
-        (place, own_vector, own_coefs, near_coefs, capacity, load, second_load)
-        + (image, own_wave, dual, own_sums, far_sums),
-        [((rows, nodes), F32), ((rows, nodes), F32), ((16, gathered), F32)],
+        [SMEM] + [VMEM] * 8,
+        (place, own_vector, load, second_load, image, own_wave, dual, dual_slope, sums),
+        [((16, gathered), F32)],
         micros=1,
     )
-    scalars = total(scalars)
-    own_part, near_part, _ = reduce_groups(second_kept, second_sent, answer)
+    second_kept, second_arrived = send_groups(second_kept, second_sent)
+    own_image, near_image = merge(scalars, kept, arrived)
+    scalars = total(scalars, "nodes")
+    answer, slope, skew = run(
+        functools.partial(settle_kernel, length=length),
+        "settle",
+        [SMEM] + [VMEM] * 4,
+        (place, own_image, near_image, own_vector, capacity),
+        [((rows, nodes), F32), ((rows, nodes), F32), ((8, LANES), F32)],
+        micros=1,
+    )
+    own_part, near_part = merge(scalars, second_kept, second_arrived)
+    scalars = total(scalars, "samples")
     field = jax.ShapeDtypeStruct((rows, nodes), F32)
     return tuple(
         pl.pallas_call(
-            functools.partial(last_kernel, entries=entries),
+            functools.partial(
+                last_kernel, entries=entries, devices=float(node_groups * parts)
+            ),
             out_shape=[field, field],
-            in_specs=[VMEM] * 4 + [SMEM] + [VMEM] * 2,
+            in_specs=[VMEM] * 5 + [SMEM] + [VMEM] * 2,
             out_specs=[VMEM] * 2,
             compiler_params=pltpu.CompilerParams(vmem_limit_bytes=12 * 2**20),
             name="last",
-        )(scalars, own_vector, answer, slope, place, own_part, near_part)
+        )(scalars, own_vector, answer, slope, skew, place, own_part, near_part)
     )
 
 

time: 48.8 us -> 45.6 us (0.934)
  waiting for transfers between devices: 11.6 us -> 6.04 us
  starting transfers between devices: 15.6 us -> 17.5 us
    ppermute x9 -> x10, waiting for transfers between devices: 5.59 us -> 0.18 us  [swap(): lax.ppermute(value, 'samples', [(at, at ^ mask) for at in range(count)])]
    ppermute x9 -> x10, starting transfers between devices: 4.85 us -> 6.82 us  [swap(): lax.ppermute(value, 'samples', [(at, at ^ mask) for at in range(count)])]
    pallas_call x10 -> x11, Pallas kernels: 19.1 us -> 19.4 us  [run(): pl.pallas_call(kernel, out_shape=[pltpu.VMEM(shape, dtype) for shape, dty...]
  transfers between devices with their start and end apart: 18 -> 19, of which waited for: 10 -> 6; matrix products, arithmetic and copies ran while one was open for 0% -> 0% of each run, Pallas kernels for 35% -> 38%
where the time goes in v4:
time: 45.6 us; the launch traced here: 45.5 us
  Pallas kernels  21 us (46%)
  starting transfers between devices  17.5 us (38%)
  waiting for transfers between devices  6.04 us (13%)
  between operations  0.78 us (2%)
    pallas_call x11, Pallas kernels, run(): pl.pallas_call(kernel, out_shape=[pltpu.VMEM(shape, dtype) for shape, dty...  19.4 us
    ppermute x10, starting transfers between devices, swap(): lax.ppermute(value, 'samples', [(at, at ^ mask) for at in range(count)])  6.82 us
    ppermute x6, starting transfers between devices, total(): lax.ppermute(value, axis, [(at, at ^ step * stride) for at in range(count)])  6.26 us
    ppermute x3, starting transfers between devices, trade(): lax.ppermute(value, 'nodes', [(at, at ^ mask) for at in range(count)])  4.45 us
    ppermute x3, waiting for transfers between devices, trade(): lax.ppermute(value, 'nodes', [(at, at ^ mask) for at in range(count)])  3.09 us
    ppermute x6, waiting for transfers between devices, total(): lax.ppermute(value, axis, [(at, at ^ step * stride) for at in range(count)])  2.77 us
    pallas_call x1, Pallas kernels, shards(): pl.pallas_call(functools.partial(last_kernel, entries=entries, devices=fl...  1.56 us
  transfers between devices with their start and end apart: 19, of which 6 were waited for; matrix products, arithmetic and copies ran while one was open for 0% of the time, Pallas kernels for 38%

profile of v4, /device:TPU:0, one launch (start us, length us, event | category | flops | bytes accessed | tf_op | source)
XLA Modules:
  0.0 45.5 jit_solution(7433720215841721725)
XLA Ops:
  0.6 3.0 %collective-permute-start = (f32[32,2048]{1,0:T(8,128)}, f32[32,2048]{1,0:T(8,128)S(1)}, u32[]{:S(2)}, u32[]{:S(2)}) collective-permute-start(f32[32,2048]{1,0:T(8,128)} %vector_in.1), channel_id=1, source_target_pairs={{0,2},{1,3},{2,0},{3,1},{4,6},{5,7},{6,4},{7,5},{8,10},{9,11},{10,... | collective-permute-start | bytes 786440 | tf_op jit(solution)/shard_map/ppermute | solution.py:694
  3.6 0.0 collective-permute-start.1
  3.6 0.5 %collective-permute-start.3 = (f32[32,2048]{1,0:T(8,128)}, f32[32,2048]{1,0:T(8,128)S(1)}, u32[]{:S(2)}, u32[]{:S(2)}) collective-permute-start(f32[32,2048]{1,0:T(8,128)} %operating_in.1), channel_id=1, source_target_pairs={{0,1},{1,0},{2,3},{3,2},{4,5},{5,4},{6,7},{7,6},{8,9},{9,8},{10,11... | collective-permute-start | bytes 786440 | tf_op jit(solution)/shard_map/ppermute | solution.py:694
  4.1 0.1 pad_add_fusion.place
  4.2 8.5 %prepare.1 = (bf16[2176,1152]{1,0:T(8,128)(2,1)S(1)}, bf16[2176,1152]{1,0:T(8,128)(2,1)S(1)}, bf16[2048,128]{1,0:T(8,128)(2,1)S(1)}, f32[1,1152]{1,0:T(1,128)S(1...) custom-call(s32[4]{0:T(128)S(1)} %pad_add_fusion.place, ...), custom_call_target="tpu_custom_call" | custom-call | bytes 24000000 | tf_op jit(solution)/shard_map/prepare/pallas_call | solution.py:678
  12.7 0.0 collective-permute-done.refs_1_
  12.8 0.1 collective-permute-start.2
  12.8 0.0 collective-permute-done.3.near_operating
  12.8 1.5 %conductance.1.refs_5_.conductances = f32[64,2176]{1,0:T(8,128)S(1)} custom-call(s32[4]{0:T(128)S(1)} %pad_add_fusion.place, f32[32,2048]{1,0:T(8,128)S(1)} %collective-permute-done.3.near_operating, f32[32,2048]{1,0:T(8,128)S(1)} %get-tuple-element.46.operating, f32[1,16]{1,0:T(1,128)S(1)} %get-tuple-element.47.table, ...), custom_call_target="tpu_custom_call" | custom-call | bytes 3000000 | tf_op jit(solution)/shard_map/conductance/pallas_call | solution.py:678
  14.4 0.0 collective-permute-done.1.refs_2_
  14.4 0.0 collective-permute-done.2.refs_3_
  14.4 1.2 %wave.1 = (bf16[128,2176]{1,0:T(8,128)(2,1)S(1)}, bf16[128,2176]{1,0:T(8,128)(2,1)S(1)}, f32[64,2176]{1,0:T(8,128)S(1)}, bf16[128,2048]{1,0:T(8,128)(2,1)S(1)}, ...) custom-call(f32[32,2048]{1,0:T(8,128)S(1)} %get-tuple-element.43.refs_0_.vector, ...), custom_call_target="tpu_custom_call" | custom-call | bytes 6000000 | tf_op jit(solution)/shard_map/wave/pallas_call | solution.py:678
  15.6 1.6 %collective-permute-start.4 = (f32[48,128]{1,0:T(8,128)S(1)}, f32[48,128]{1,0:T(8,128)S(1)}, u32[]{:S(2)}, u32[]{:S(2)}) collective-permute-start(f32[48,128]{1,0:T(8,128)S(1)} %get-tuple-element.53), channel_id=1, source_target_pairs={{0,4},{4,0},{8,12},{12,8},{1,5},{5,1},{9,13},{13,9},{2,6},{6,2},{1... | collective-permute-start | bytes 73736 | tf_op jit(solution)/shard_map/ppermute | solution.py:699
  17.2 2.6 %collective-permute-start.5 = (f32[48,128]{1,0:T(8,128)S(1)}, f32[48,128]{1,0:T(8,128)S(1)}, u32[]{:S(2)}, u32[]{:S(2)}) collective-permute-start(f32[48,128]{1,0:T(8,128)S(1)} %get-tuple-element.54), channel_id=1, source_target_pairs={{0,8},{4,12},{8,0},{12,4},{1,9},{5,13},{9,1},{13,5},{2,10},{6,14},... | collective-permute-start | bytes 73736 | tf_op jit(solution)/shard_map/ppermute | solution.py:699
  19.8 0.2 collective-permute-start.6
  20.0 2.3 %local.1 = (f32[64,1024]{1,0:T(8,128)S(1)}, f32[64,1024]{1,0:T(8,128)S(1)}, f32[64,1024]{1,0:T(8,128)S(1)}, f32[64,1024]{1,0:T(8,128)S(1)}, f32[64,1024]{1,0:T(8,128)S(1)}) custom-call(bf16[128,2176]{1,0:T(8,128)(2,1)S(1)} %get-tuple-element.57.field_high, bf16[128,2176]{1,0:T(8,128)(2,1)S(1)} %get-tuple-element.58.field_low, ...), custom_call_target="tpu_custom_call" | custom-call | bytes 9000000 | tf_op jit(solution)/shard_map/local/pallas_call | solution.py:678
  22.3 0.0 collective-permute-done.4.refs_0_
  22.3 0.0 collective-permute-done.5.refs_1_
  22.4 3.1 %collective-permute-done.6.refs_2_ = f32[48,128]{1,0:T(8,128)S(1)} collective-permute-done((f32[48,128]{1,0:T(8,128)S(1)}, f32[48,128]{1,0:T(8,128)S(1)}, u32[]{:S(2)}, u32[]{:S(2)}) %collective-permute-start.6) | collective-permute-done | bytes 24608 | tf_op jit(solution)/shard_map/ppermute | solution.py:699
  25.4 0.9 %first.1 = (f32[64,1024]{1,0:T(8,128)S(1)}, f32[64,1024]{1,0:T(8,128)S(1)}, f32[64,1024]{1,0:T(8,128)S(1)}, f32[64,1024]{1,0:T(8,128)S(1)}, f32[8,1024]{1,0:T(8,128)S(1)}, /*index=5*/f32[64,128]{1,0:T(8,128)S(1)}) custom-call(f32[48,128]{1,0:T(8,128)S(1)} %collective-permute-done.4.refs_0_, f32[48,128]{1,0:T(8,128)S(1)} %collective-permute-done.5.refs_1_, ...), custom_call_target="tpu_custom_call" | custom-call | bytes 3000000 | tf_op jit(solution)/shard_map/first/pallas_call | solution.py:678
  26.3 0.1 collective-permute-start.7
  26.4 0.6 %collective-permute-start.8 = (f32[8,1024]{1,0:T(8,128)S(1)}, f32[8,1024]{1,0:T(8,128)S(1)}, u32[]{:S(2)}, u32[]{:S(2)}) collective-permute-start(f32[8,1024]{1,0:T(8,128)S(1)} %get-tuple-element.71), channel_id=1, source_target_pairs={{0,2},{1,3},{2,0},{3,1},{4,6},{5,7},{6,4},{7,5},{8,10},{9,11},{10,... | collective-permute-start | bytes 98312 | tf_op jit(solution)/shard_map/ppermute | solution.py:694
  27.0 1.5 %collective-permute-start.15 = (f32[64,1024]{1,0:T(8,128)S(1)}, f32[64,1024]{1,0:T(8,128)S(1)}, u32[]{:S(2)}, u32[]{:S(2)}) collective-permute-start(f32[64,1024]{1,0:T(8,128)S(1)} %get-tuple-element.73), channel_id=1, source_target_pairs={{0,2},{1,3},{2,0},{3,1},{4,6},{5,7},{6,4},{7,5},{8,10},{9,11},{10,... | collective-permute-start | bytes 786440 | tf_op jit(solution)/shard_map/ppermute | solution.py:694
  28.5 0.0 collective-permute-done.7.near_image
  28.5 2.5 %second.1 = (f32[64,1024]{1,0:T(8,128)S(1)}, f32[64,1024]{1,0:T(8,128)S(1)}, f32[64,1024]{1,0:T(8,128)S(1)}) custom-call(s32[4]{0:T(128)S(1)} %pad_add_fusion.place, f32[64,128]{1,0:T(8,128)S(1)} %get-tuple-element.66.halo, f32[64,1024]{1,0:T(8,128)S(1)} %collective-permute-done.7.near_image, f32[64,1024]{1,0:T(8,128)S(1)} %get-tuple-element.67.image, ...), custom_call_target="tpu_custom_call" | custom-call | bytes 9000000 | tf_op jit(solution)/shard_map/second/pallas_call | solution.py:678
  31.0 0.6 %collective-permute-start.17 = (f32[64,1024]{1,0:T(8,128)S(1)}, f32[64,1024]{1,0:T(8,128)S(1)}, u32[]{:S(2)}, u32[]{:S(2)}) collective-permute-start(f32[64,1024]{1,0:T(8,128)S(1)} %get-tuple-element.81), channel_id=1, source_target_pairs={{0,2},{1,3},{2,0},{3,1},{4,6},{5,7},{6,4},{7,5},{8,10},{9,11},{10,... | collective-permute-start | bytes 786440 | tf_op jit(solution)/shard_map/ppermute | solution.py:694
  31.6 0.0 collective-permute-done.8
  31.6 1.5 %products.1.after = f32[16,128]{1,0:T(8,128)S(1)} custom-call(s32[4]{0:T(128)S(1)} %pad_add_fusion.place, f32[32,2048]{1,0:T(8,128)S(1)} %get-tuple-element.43.refs_0_.vector, f32[64,1024]{1,0:T(8,128)S(1)} %get-tuple-element.65.load, f32[64,1024]{1,0:T(8,128)S(1)} %get-tuple-element.68.second_load, f32[64,1024]{1,0:T(8,128)S(1)} %get-tuple-element.67.image, ...), custom_call_target="tpu_custom_call" | custom-call | bytes 3000000 | tf_op jit(solution)/shard_map/products/pallas_call | solution.py:678
  33.1 0.6 %collective-permute-start.11 = (f32[16,128]{1,0:T(8,128)S(1)}, f32[16,128]{1,0:T(8,128)S(1)}, u32[]{:S(2)}, u32[]{:S(2)}) collective-permute-start(f32[16,128]{1,0:T(8,128)S(1)} %products.1.after), channel_id=1, source_target_pairs={{0,12},{4,8},{8,4},{12,0},{1,13},{5,9},{9,5},{13,1},{2,14},{6,10},... | collective-permute-start | bytes 24584 | tf_op jit(solution)/shard_map/ppermute | solution.py:707
  33.6 0.0 collective-permute-start.10
  33.6 3.8 %collective-permute-start.9 = (f32[16,128]{1,0:T(8,128)S(1)}, f32[16,128]{1,0:T(8,128)S(1)}, u32[]{:S(2)}, u32[]{:S(2)}) collective-permute-start(f32[16,128]{1,0:T(8,128)S(1)} %products.1.after), channel_id=1, source_target_pairs={{0,4},{4,0},{8,12},{12,8},{1,5},{5,1},{9,13},{13,9},{2,6},{6,2},{1... | collective-permute-start | bytes 24584 | tf_op jit(solution)/shard_map/ppermute | solution.py:707
  37.5 1.1 %collective-permute-done.11 = f32[16,128]{1,0:T(8,128)S(1)} collective-permute-done((f32[16,128]{1,0:T(8,128)S(1)}, f32[16,128]{1,0:T(8,128)S(1)}, u32[]{:S(2)}, u32[]{:S(2)}) %collective-permute-start.11) | collective-permute-done | bytes 8224 | tf_op jit(solution)/shard_map/ppermute | solution.py:707
  38.5 0.0 collective-permute-done.10
  38.5 0.6 %collective-permute-done.9 = f32[16,128]{1,0:T(8,128)S(1)} collective-permute-done((f32[16,128]{1,0:T(8,128)S(1)}, f32[16,128]{1,0:T(8,128)S(1)}, u32[]{:S(2)}, u32[]{:S(2)}) %collective-permute-start.9) | collective-permute-done | bytes 8224 | tf_op jit(solution)/shard_map/ppermute | solution.py:707
  39.1 0.0 collective-permute-start.14
  39.1 1.6 %collective-permute-start.13 = (f32[16,128]{1,0:T(8,128)S(1)}, f32[16,128]{1,0:T(8,128)S(1)}, u32[]{:S(2)}, u32[]{:S(2)}) collective-permute-start(f32[16,128]{1,0:T(8,128)S(1)} %add_add_fusion.1.after), channel_id=1, source_target_pairs={{0,2},{1,3},{2,0},{3,1},{4,6},{5,7},{6,4},{7,5},{8,10},{9,11},{10,... | collective-permute-start | bytes 24584 | tf_op jit(solution)/shard_map/ppermute | solution.py:707
  40.7 0.3 collective-permute-start.12
  41.0 0.0 collective-permute-done.15.arrived
  41.0 0.3 collective-permute-start.16
  41.3 0.2 collective-permute-done.17.arrived
  41.5 0.2 collective-permute-start.18
  41.7 0.5 %collective-permute-done.14 = f32[16,128]{1,0:T(8,128)S(1)} collective-permute-done((f32[16,128]{1,0:T(8,128)S(1)}, f32[16,128]{1,0:T(8,128)S(1)}, u32[]{:S(2)}, u32[]{:S(2)}) %collective-permute-start.14) | collective-permute-done | bytes 8224 | tf_op jit(solution)/shard_map/ppermute | solution.py:707
  42.2 0.6 %collective-permute-done.13 = f32[16,128]{1,0:T(8,128)S(1)} collective-permute-done((f32[16,128]{1,0:T(8,128)S(1)}, f32[16,128]{1,0:T(8,128)S(1)}, u32[]{:S(2)}, u32[]{:S(2)}) %collective-permute-start.13) | collective-permute-done | bytes 8224 | tf_op jit(solution)/shard_map/ppermute | solution.py:707
  42.8 0.0 collective-permute-done.12
  42.8 0.0 collective-permute-done.16.near_image
  42.8 1.1 %settle.1 = (f32[32,2048]{1,0:T(8,128)S(1)}, f32[32,2048]{1,0:T(8,128)S(1)}, f32[8,128]{1,0:T(8,128)S(1)}) custom-call(s32[4]{0:T(128)S(1)} %pad_add_fusion.place, f32[32,1024]{1,0:T(8,128)S(1)} %get-tuple-element.74.own_image, f32[32,1024]{1,0:T(8,128)S(1)} %collective-permute-done.16.near_image, f32[32,2048]{1,0:T(8,128)S(1)} %get-tuple-element.43.refs_0_.vector, ...), custom_call_target="tpu_custom_call" | custom-call | bytes 3000000 | tf_op jit(solution)/shard_map/settle/pallas_call | solution.py:678
  43.9 0.0 collective-permute-done.18.near_part
  43.9 1.6 %last.1 = (f32[32,2048]{1,0:T(8,128)}, f32[32,2048]{1,0:T(8,128)}) custom-call(f32[16,128]{1,0:T(8,128)S(1)} %add_add_fusion.gathered, f32[32,2048]{1,0:T(8,128)S(1)} %get-tuple-element.43.refs_0_.vector, f32[32,2048]{1,0:T(8,128)S(1)} %get-tuple-element.77.answer, f32[32,2048]{1,0:T(8,128)S(1)} %get-tuple-element.78.slope, ...), custom_call_target="tpu_custom_call" | custom-call | tf_op jit(solution)/shard_map/last/pallas_call | solution.py:923
  (7 shorter events, 0.1 us)
Async XLA Ops:
  0.6 12.1 %collective-permute-start = (f32[32,2048]{1,0:T(8,128)}, f32[32,2048]{1,0:T(8,128)S(1)}, u32[]{:S(2)}, u32[]{:S(2)}) collective-permute-start(f32[32,2048]{1,0:T(8,128)} %vector_in.1), channel_id=1, source_target_pairs={{0,2},{1,3},{2,0},{3,1},{4,6},{5,7},{6,4},{7,5},{8,10},{9,11},{10,... | collective-permute-start | bytes 786440 | tf_op jit(solution)/shard_map/ppermute | solution.py:694
  3.6 10.8 %collective-permute-start.1 = (f32[32,2048]{1,0:T(8,128)}, f32[32,2048]{1,0:T(8,128)S(1)}, u32[]{:S(2)}, u32[]{:S(2)}) collective-permute-start(f32[32,2048]{1,0:T(8,128)} %vector_in.1), channel_id=1, source_target_pairs={{0,1},{1,0},{2,3},{3,2},{4,5},{5,4},{6,7},{7,6},{8,9},{9,8},{10,11... | collective-permute-start | bytes 786440 | tf_op jit(solution)/shard_map/ppermute | solution.py:694
  3.6 9.2 %collective-permute-start.3 = (f32[32,2048]{1,0:T(8,128)}, f32[32,2048]{1,0:T(8,128)S(1)}, u32[]{:S(2)}, u32[]{:S(2)}) collective-permute-start(f32[32,2048]{1,0:T(8,128)} %operating_in.1), channel_id=1, source_target_pairs={{0,1},{1,0},{2,3},{3,2},{4,5},{5,4},{6,7},{7,6},{8,9},{9,8},{10,11... | collective-permute-start | bytes 786440 | tf_op jit(solution)/shard_map/ppermute | solution.py:694
  12.8 1.6 %collective-permute-start.2 = (f32[32,2048]{1,0:T(8,128)S(1)}, f32[32,2048]{1,0:T(8,128)S(1)}, u32[]{:S(2)}, u32[]{:S(2)}) collective-permute-start(f32[32,2048]{1,0:T(8,128)S(1)} %relay.1.refs_1_), channel_id=1, source_target_pairs={{0,1},{1,0},{2,3},{3,2},{4,5},{5,4},{6,7},{7,6},{8,9},{9,8},{10,11... | collective-permute-start | bytes 786440 | tf_op jit(solution)/shard_map/ppermute | solution.py:694
  15.6 6.7 %collective-permute-start.4 = (f32[48,128]{1,0:T(8,128)S(1)}, f32[48,128]{1,0:T(8,128)S(1)}, u32[]{:S(2)}, u32[]{:S(2)}) collective-permute-start(f32[48,128]{1,0:T(8,128)S(1)} %get-tuple-element.53), channel_id=1, source_target_pairs={{0,4},{4,0},{8,12},{12,8},{1,5},{5,1},{9,13},{13,9},{2,6},{6,2},{1... | collective-permute-start | bytes 73736 | tf_op jit(solution)/shard_map/ppermute | solution.py:699
  17.2 5.1 %collective-permute-start.5 = (f32[48,128]{1,0:T(8,128)S(1)}, f32[48,128]{1,0:T(8,128)S(1)}, u32[]{:S(2)}, u32[]{:S(2)}) collective-permute-start(f32[48,128]{1,0:T(8,128)S(1)} %get-tuple-element.54), channel_id=1, source_target_pairs={{0,8},{4,12},{8,0},{12,4},{1,9},{5,13},{9,1},{13,5},{2,10},{6,14},... | collective-permute-start | bytes 73736 | tf_op jit(solution)/shard_map/ppermute | solution.py:699
  19.8 5.6 %collective-permute-start.6 = (f32[48,128]{1,0:T(8,128)S(1)}, f32[48,128]{1,0:T(8,128)S(1)}, u32[]{:S(2)}, u32[]{:S(2)}) collective-permute-start(f32[48,128]{1,0:T(8,128)S(1)} %get-tuple-element.55), channel_id=1, source_target_pairs={{0,12},{4,8},{8,4},{12,0},{1,13},{5,9},{9,5},{13,1},{2,14},{6,10},... | collective-permute-start | bytes 73736 | tf_op jit(solution)/shard_map/ppermute | solution.py:699
  26.3 2.2 %collective-permute-start.7 = (f32[64,1024]{1,0:T(8,128)S(1)}, f32[64,1024]{1,0:T(8,128)S(1)}, u32[]{:S(2)}, u32[]{:S(2)}) collective-permute-start(f32[64,1024]{1,0:T(8,128)S(1)} %get-tuple-element.67.image), channel_id=1, source_target_pairs={{0,1},{1,0},{2,3},{3,2},{4,5},{5,4},{6,7},{7,6},{8,9},{9,8},{10,11... | collective-permute-start | bytes 786440 | tf_op jit(solution)/shard_map/ppermute | solution.py:694
  26.4 5.2 %collective-permute-start.8 = (f32[8,1024]{1,0:T(8,128)S(1)}, f32[8,1024]{1,0:T(8,128)S(1)}, u32[]{:S(2)}, u32[]{:S(2)}) collective-permute-start(f32[8,1024]{1,0:T(8,128)S(1)} %get-tuple-element.71), channel_id=1, source_target_pairs={{0,2},{1,3},{2,0},{3,1},{4,6},{5,7},{6,4},{7,5},{8,10},{9,11},{10,... | collective-permute-start | bytes 98312 | tf_op jit(solution)/shard_map/ppermute | solution.py:694
  27.0 14.0 %collective-permute-start.15 = (f32[64,1024]{1,0:T(8,128)S(1)}, f32[64,1024]{1,0:T(8,128)S(1)}, u32[]{:S(2)}, u32[]{:S(2)}) collective-permute-start(f32[64,1024]{1,0:T(8,128)S(1)} %get-tuple-element.73), channel_id=1, source_target_pairs={{0,2},{1,3},{2,0},{3,1},{4,6},{5,7},{6,4},{7,5},{8,10},{9,11},{10,... | collective-permute-start | bytes 786440 | tf_op jit(solution)/shard_map/ppermute | solution.py:694
  31.0 10.5 %collective-permute-start.17 = (f32[64,1024]{1,0:T(8,128)S(1)}, f32[64,1024]{1,0:T(8,128)S(1)}, u32[]{:S(2)}, u32[]{:S(2)}) collective-permute-start(f32[64,1024]{1,0:T(8,128)S(1)} %get-tuple-element.81), channel_id=1, source_target_pairs={{0,2},{1,3},{2,0},{3,1},{4,6},{5,7},{6,4},{7,5},{8,10},{9,11},{10,... | collective-permute-start | bytes 786440 | tf_op jit(solution)/shard_map/ppermute | solution.py:694
  33.1 5.5 %collective-permute-start.11 = (f32[16,128]{1,0:T(8,128)S(1)}, f32[16,128]{1,0:T(8,128)S(1)}, u32[]{:S(2)}, u32[]{:S(2)}) collective-permute-start(f32[16,128]{1,0:T(8,128)S(1)} %products.1.after), channel_id=1, source_target_pairs={{0,12},{4,8},{8,4},{12,0},{1,13},{5,9},{9,5},{13,1},{2,14},{6,10},... | collective-permute-start | bytes 24584 | tf_op jit(solution)/shard_map/ppermute | solution.py:707
  33.6 4.9 %collective-permute-start.10 = (f32[16,128]{1,0:T(8,128)S(1)}, f32[16,128]{1,0:T(8,128)S(1)}, u32[]{:S(2)}, u32[]{:S(2)}) collective-permute-start(f32[16,128]{1,0:T(8,128)S(1)} %products.1.after), channel_id=1, source_target_pairs={{0,8},{4,12},{8,0},{12,4},{1,9},{5,13},{9,1},{13,5},{2,10},{6,14},... | collective-permute-start | bytes 24584 | tf_op jit(solution)/shard_map/ppermute | solution.py:707
  33.6 5.5 %collective-permute-start.9 = (f32[16,128]{1,0:T(8,128)S(1)}, f32[16,128]{1,0:T(8,128)S(1)}, u32[]{:S(2)}, u32[]{:S(2)}) collective-permute-start(f32[16,128]{1,0:T(8,128)S(1)} %products.1.after), channel_id=1, source_target_pairs={{0,4},{4,0},{8,12},{12,8},{1,5},{5,1},{9,13},{13,9},{2,6},{6,2},{1... | collective-permute-start | bytes 24584 | tf_op jit(solution)/shard_map/ppermute | solution.py:707
  39.1 3.1 %collective-permute-start.14 = (f32[16,128]{1,0:T(8,128)S(1)}, f32[16,128]{1,0:T(8,128)S(1)}, u32[]{:S(2)}, u32[]{:S(2)}) collective-permute-start(f32[16,128]{1,0:T(8,128)S(1)} %add_add_fusion.1.after), channel_id=1, source_target_pairs={{0,3},{1,2},{2,1},{3,0},{4,7},{5,6},{6,5},{7,4},{8,11},{9,10},{10,... | collective-permute-start | bytes 24584 | tf_op jit(solution)/shard_map/ppermute | solution.py:707
  39.1 3.7 %collective-permute-start.13 = (f32[16,128]{1,0:T(8,128)S(1)}, f32[16,128]{1,0:T(8,128)S(1)}, u32[]{:S(2)}, u32[]{:S(2)}) collective-permute-start(f32[16,128]{1,0:T(8,128)S(1)} %add_add_fusion.1.after), channel_id=1, source_target_pairs={{0,2},{1,3},{2,0},{3,1},{4,6},{5,7},{6,4},{7,5},{8,10},{9,11},{10,... | collective-permute-start | bytes 24584 | tf_op jit(solution)/shard_map/ppermute | solution.py:707
  40.7 2.2 %collective-permute-start.12 = (f32[16,128]{1,0:T(8,128)S(1)}, f32[16,128]{1,0:T(8,128)S(1)}, u32[]{:S(2)}, u32[]{:S(2)}) collective-permute-start(f32[16,128]{1,0:T(8,128)S(1)} %add_add_fusion.1.after), channel_id=1, source_target_pairs={{0,1},{1,0},{2,3},{3,2},{4,5},{5,4},{6,7},{7,6},{8,9},{9,8},{10,11... | collective-permute-start | bytes 24584 | tf_op jit(solution)/shard_map/ppermute | solution.py:707
  41.0 1.8 %collective-permute-start.16 = (f32[32,1024]{1,0:T(8,128)S(1)}, f32[32,1024]{1,0:T(8,128)S(1)}, u32[]{:S(2)}, u32[]{:S(2)}) collective-permute-start(f32[32,1024]{1,0:T(8,128)S(1)} %get-tuple-element.75), channel_id=1, source_target_pairs={{0,1},{1,0},{2,3},{3,2},{4,5},{5,4},{6,7},{7,6},{8,9},{9,8},{10,11... | collective-permute-start | bytes 393224 | tf_op jit(solution)/shard_map/ppermute | solution.py:694
  41.5 2.4 %collective-permute-start.18 = (f32[32,1024]{1,0:T(8,128)S(1)}, f32[32,1024]{1,0:T(8,128)S(1)}, u32[]{:S(2)}, u32[]{:S(2)}) collective-permute-start(f32[32,1024]{1,0:T(8,128)S(1)} %get-tuple-element.83), channel_id=1, source_target_pairs={{0,1},{1,0},{2,3},{3,2},{4,5},{5,4},{6,7},{7,6},{8,9},{9,8},{10,11... | collective-permute-start | bytes 393224 | tf_op jit(solution)/shard_map/ppermute | solution.py:694

commit v5 on v4

--- a/solution.py
+++ b/solution.py
@@ -66,7 +66,7 @@
             )
         )
         sent = np.concatenate(
-            [block(place ^ (2 * group) ^ side) for group in range(parts // 2) for side in (0, 1)]
+            [block(place ^ mask ^ side) for side in (0, 1) for mask in range(0, parts, 2)]
         )
         back.append(analysis[np.ix_(sent, times)])
     return (
@@ -92,10 +92,16 @@
 
 
 def lane_sums(values):
-    blocks = values.shape[1] // LANES
-    total = values[:, :LANES]
-    for block in range(1, blocks):
-        total = total + values[:, block * LANES : (block + 1) * LANES]
+    rows, lanes = values.shape
+    step = 8 if rows % 8 == 0 else rows
+    total = functools.reduce(
+        jnp.add,
+        [
+            values[row : row + step, lane : lane + LANES]
+            for row in range(0, rows, step)
+            for lane in range(0, lanes, LANES)
+        ],
+    )
     return jnp.sum(total, axis=0, keepdims=True)
 
 
@@ -131,8 +137,9 @@
     return jnp.concatenate(pieces, axis=1)
 
 
-def prepare_kernel(
-    place,
+def fetch_kernel(
+    place_in,
+    vector_in,
     neighbours_in,
     weights_in,
     degree_in,
@@ -142,41 +149,40 @@
     boundary_in,
     table_in,
     operating_in,
-    vector_in,
     forward_in,
     back_in,
-    coupling_high,
-    coupling_low,
+    vector,
     picked,
     linear,
     capacity,
     capacity_all,
-    cut_halo,
     table,
     operating,
-    vector,
     forward,
     back,
+    entry_rows,
+    weight_rows,
+    place,
     neighbours,
     weights,
     degree,
     linear_all,
     send_list,
     boundary,
-    entry_rows,
-    weight_rows,
     copied,
 ):
+    for index in range(4):
+        place[index] = place_in[index]
     slots, nodes = neighbours.shape
-    sources, width = coupling_high.shape
     lanes = picked.shape[1]
-    half = width - lanes
+    half = linear.shape[1] - lanes
     node_groups = send_list.shape[0] // CAP
     side, part = place[0] % 2, place[1]
     copies = [
         pltpu.make_async_copy(source, target, copied.at[index])
         for index, (source, target) in enumerate(
             [
+                (vector_in, vector),
                 (send_list_in, send_list),
                 (boundary_in, boundary),
                 (neighbours_in, neighbours),
@@ -186,7 +192,6 @@
                 (capacity_in, capacity_all),
                 (table_in, table),
                 (operating_in, operating),
-                (vector_in, vector),
                 (forward_in.at[place[0]], forward),
                 (back_in.at[place[0]], back),
             ]
@@ -194,7 +199,7 @@
     ]
     for copy in copies:
         copy.start()
-    for copy in copies[:2]:
+    for copy in copies[1:3]:
         copy.wait()
 
     lane = lax.broadcasted_iota(I32, (8, lanes), 1)
@@ -210,7 +215,7 @@
     hit = lax.broadcasted_iota(I32, (nodes, lanes), 0) == cut_nodes[:1]
     picked[...] = jnp.where(hit, 1.0, 0.0).astype(BF16)
 
-    for copy in copies[2:7]:
+    for copy in copies[3:8]:
         copy.wait()
     mine = half_of(side, half)
     entry = neighbours[...]
@@ -249,7 +254,16 @@
     for slot in range(slots):
         entry_rows[slot : slot + 1, :] = entries[slot]
         weight_rows[slot : slot + 1, :] = gains[slot]
-
+    copies[0].wait()
+    for copy in copies[8:]:
+        copy.wait()
+
+
+def prepare_kernel(entry_rows, weight_rows, coupling_high, coupling_low, cut_halo):
+    slots, width = entry_rows.shape
+    sources = coupling_high.shape[0]
+    nodes = sources - cut_halo.shape[0]
+    half = width - cut_halo.shape[0]
     unroll = 4
 
     def column_block(block, carry):
@@ -291,9 +305,6 @@
         coupling_high[nodes:, half:].astype(F32) + coupling_low[nodes:, half:].astype(F32)
     )
 
-    for copy in copies[7:]:
-        copy.wait()
-
 
 def relay_kernel(*refs):
     count = (len(refs) - 1) // 2
@@ -322,8 +333,12 @@
     return shared, times if shared else 0
 
 
-def wave_kernel(*refs, pieces):
-    vectors = refs[:pieces]
+def packet_steps(steps):
+    return [(2,), (1, 3)] if steps == 3 else [(step,) for step in range(1, steps + 1)]
+
+
+def wave_kernel(*refs, pieces, steps):
+    vectors = refs[1 : 1 + pieces]
     (
         forward,
         conductances,
@@ -338,8 +353,9 @@
         wave,
         current,
         cut_current,
-    ) = refs[pieces : pieces + 13]
-    sent = refs[pieces + 13 :]
+    ) = refs[1 + pieces : 1 + pieces + 13]
+    sent = refs[1 + pieces + 13 :]
+    side = refs[0][0] % 2
     rows, nodes = vectors[0].shape
     lanes = picked.shape[1]
     times = wave.shape[0]
@@ -371,16 +387,16 @@
     )
     image = jnp.transpose(image)
     at_cut = jnp.transpose(conductances[:, nodes:])
-    slots = len(sent) * CAP
-    shared, start = packet_layout(len(sent), times)
-    for step, target in enumerate(sent):
-        at = slice(step * CAP, (step + 1) * CAP)
+    slots = steps * CAP
+    shared, start = packet_layout(steps, times)
+    for target, wanted in zip(sent, packet_steps(steps)):
         target[...] = jnp.zeros(target.shape, F32)
         if shared:
             target[:slots, :times] = cut_current[:slots]
-        target[:CAP, start : start + slots] = cut_halo[at, :slots]
-        target[CAP : 2 * CAP, start : start + times] = image[at]
-        target[2 * CAP : 3 * CAP, start : start + times] = at_cut[at]
+        for row, values, size in ((0, cut_halo, slots), (1, image, times), (2, at_cut, times)):
+            blocks = [values[(step - 1) * CAP : step * CAP, :size] for step in wanted]
+            block = blocks[0] if len(blocks) == 1 else jnp.where(side == 0, *blocks)
+            target[row * CAP : (row + 1) * CAP, start : start + size] = block
 
 
 def local_kernel(
@@ -422,15 +438,30 @@
 
 
 def signed_sums(values):
-    even = lax.broadcasted_iota(I32, values.shape, 0) % 2 == 0
+    rows = values.shape[0]
+    folded = functools.reduce(jnp.add, [values[row : row + 8] for row in range(0, rows, 8)])
+    even = lax.broadcasted_iota(I32, folded.shape, 0) % 2 == 0
     return (
-        jnp.sum(values, axis=0, keepdims=True),
-        jnp.sum(jnp.where(even, values, -values), axis=0, keepdims=True),
-    )
+        jnp.sum(folded, axis=0, keepdims=True),
+        jnp.sum(jnp.where(even, folded, -folded), axis=0, keepdims=True),
+    )
+
+
+def analysed(back, load):
+    spectrum = dot_split((back[0], back[1]), split(load))
+    middle = spectrum.shape[0] // 2
+    return spectrum[:middle], spectrum[middle:]
 
 
 def first_kernel(*refs, steps, apart):
-    arrived, others = refs[:steps], refs[steps : steps + apart]
+    side, arrived, others = refs[0][0] % 2, refs[1 : steps + 1], refs[steps + 1 : steps + 1 + apart]
+    if steps == 3:
+        both, own, near = (packet[...] for packet in arrived)
+        arrived = [
+            jnp.where(side == 0, own, near),
+            both,
+            jnp.where(side == 0, near, own),
+        ]
     (
         cut_current,
         local_load,
@@ -441,11 +472,11 @@
         coupling_low,
         image,
         load,
+        sums,
+        halo,
         kept,
         sent,
-        sums,
-        halo,
-    ) = refs[steps + apart :]
+    ) = refs[1 + steps + apart :]
     times, half = local_load.shape
     lanes = halo.shape[1]
     nodes = coupling_high.shape[0] - lanes
@@ -475,14 +506,11 @@
     load[...] = local_load[...] + share
     answer = load[...] + slope[...]
     image[...] = answer
-    spectrum = dot_split((back[0], back[1]), split(answer))
-    kept[...] = spectrum[:times]
-    if spectrum.shape[0] > times:
-        sent[...] = spectrum[times:]
+    kept[...], sent[...] = analysed(back, answer)
     lines = [*signed_sums(answer), *signed_sums(own_wave[...])]
     sums[...] = jnp.concatenate(lines + [jnp.zeros((4, half), F32)], axis=0)
 
-    blocks = []
+    currents = []
     for step in range(1, steps + 1):
         theirs = jnp.concatenate(
             [sender(step ^ block, block) for block in range(1, steps + 1)], axis=0
@@ -490,8 +518,8 @@
         gains = arrived[step - 1][:CAP, start : start + slots]
         image_part = arrived[step - 1][CAP : 2 * CAP, start : start + times]
         there = arrived[step - 1][2 * CAP : 3 * CAP, start : start + times]
-        blocks.append(there * (image_part + dot_split(split(gains), split(theirs))))
-    halo[...] = stack(blocks)
+        currents.append(there * (image_part + dot_split(split(gains), split(theirs))))
+    halo[...] = stack(currents)
 
 
 def second_kernel(
@@ -524,16 +552,14 @@
         load[:, lanes] += coupled(
             current[:times], current[...], coupling_high, coupling_low, slice(0, nodes), lanes
         ) + coupled(high, halo_stacked, coupling_high, coupling_low, slice(nodes, None), lanes)
-    spectrum = dot_split((back[0], back[1]), split(load[...]))
-    kept[...] = spectrum[:times]
-    if spectrum.shape[0] > times:
-        sent[...] = spectrum[times:]
-
-
-def merge_kernel(after, kept, arrived, own, near):
-    rows = own.shape[0]
-    own[...] = kept[:rows] + arrived[:rows]
-    near[...] = kept[rows:] + arrived[rows:]
+    kept[...], sent[...] = analysed(back, load[...])
+
+
+def sum_kernel(after, *refs):
+    total = refs[0][...]
+    for value in refs[1:-1]:
+        total = total + value[...]
+    refs[-1][...] = total
 
 
 def turned(field, first_pair, half_order):
@@ -545,10 +571,18 @@
     return scaling * jnp.where(row % 2 == 0, above, -below)
 
 
-def join(target, side, own, near):
-    half = own.shape[1]
-    target[:, half_of(side, half)] = own
-    target[:, half_of(1 - side, half)] = near
+def combine_kernel(after, place, kept, arrived, *targets):
+    half = kept.shape[1]
+    rows = targets[0].shape[0]
+    side = place[0] % 2
+    for index, target in enumerate(targets):
+        at = slice(index * rows, (index + 1) * rows)
+        target[:, half_of(side, half)] = kept[at]
+        target[:, half_of(1 - side, half)] = arrived[at]
+
+
+def joined(parts):
+    return functools.reduce(jnp.add, [part[...] for part in parts])
 
 
 def guess(cross, squares):
@@ -565,13 +599,14 @@
     wave,
     dual,
     dual_slope,
-    sums,
+    own_sums,
+    far_sums,
     scalars,
     *,
     length,
 ):
     start, first = wave[...], load[...]
-    field = vector[...]
+    field, sums = vector[...], own_sums[...] + far_sums[...]
     coeff = guess(scalar_sum(start * image[...]), scalar_sum(start * start))
     rest = image[...] - coeff * start
     change = second_load[...] - coeff * first
@@ -583,34 +618,37 @@
 
     def mixed(values, value_sums, others, other_ends):
         ends = value_sums[0] * other_ends[0] + value_sums[1] * other_ends[1]
-        return scalar_sum(values * others) * (2.0 / length) - scalar_sum(ends) * (
+        return lane_sums(values * others) * (2.0 / length) - lane_sums(ends) * (
             1.0 / length / length
         )
 
     found = [
-        coeff,
-        scalar_sum(field * field),
-        scalar_sum(dual[...] * rest),
-        scalar_sum(dual[...] * start),
+        lane_sums(field * field),
+        lane_sums(dual[...] * rest),
+        lane_sums(dual[...] * start),
         mixed(rest, rest_sums, rest, rest_ends),
         mixed(rest, rest_sums, start, start_ends) + mixed(start, start_sums, rest, rest_ends),
         mixed(start, start_sums, start, start_ends),
-        scalar_sum(dual[...] * change - dual_slope[...] * rest),
-        scalar_sum(dual[...] * first - dual_slope[...] * start),
+        lane_sums(dual[...] * change - dual_slope[...] * rest),
+        lane_sums(dual[...] * first - dual_slope[...] * start),
         mixed(rest, rest_sums, change, change_ends),
         mixed(rest, rest_sums, first, first_ends) + mixed(start, start_sums, change, change_ends),
         mixed(start, start_sums, first, first_ends),
     ]
     device = place[1] * place[3] + place[0]
     lane = lax.broadcasted_iota(I32, scalars.shape, 1)
-    column = jnp.concatenate(found + [jnp.zeros((4, 1), F32)], axis=0)
+    column = jnp.concatenate(found + [jnp.zeros((5, LANES), F32)], axis=0)
+    column = jnp.sum(column, axis=1, keepdims=True)
+    line = lax.broadcasted_iota(I32, column.shape, 0)
+    column = jnp.where(line == len(found), coeff, column)
     scalars[...] = jnp.where(lane == device, column, 0.0)
 
 
-def settle_kernel(place, own_image, near_image, vector, capacity, answer, slope, skew, *, length):
+def settle_kernel(place, vector, capacity, *refs, length):
+    *parts, answer, slope, skew = refs
     rows = vector.shape[0]
     first_pair = place[0] * (rows // 2)
-    join(answer, place[0] % 2, own_image[...], near_image[...])
+    answer[...] = joined(parts)
     field, start = answer[...], vector[...]
     slope[...] = capacity[...] * turned(field, first_pair, length // 2)
     start_slope = capacity[...] * turned(start, first_pair, length // 2)
@@ -629,27 +667,23 @@
     answer,
     slope,
     skew,
-    place,
-    own_part,
-    near_part,
-    basis_two,
-    next_residue,
-    *,
+    *refs,
     entries,
     devices,
 ):
-    side = place[0] % 2
+    *parts, basis_two, next_residue = refs
     own = [gathered[line : line + 1, :] for line in range(12)]
+    local = own.pop()
 
     def everywhere(values):
         return jnp.sum(values, axis=1, keepdims=True) / entries
 
-    scale_square = everywhere(own[1]) + EPSILON
-    coeff = everywhere(own[2] + own[0] * own[3]) / scale_square
-    near = own[0] - coeff
-    rest_square = everywhere(own[4] + near * (own[5] + near * own[6]))
-    along_one = everywhere(own[7] + near * own[8])
-    along_two = everywhere(own[9] + near * (own[10] + near * own[11]))
+    scale_square = everywhere(own[0]) + EPSILON
+    coeff = everywhere(own[1] + local * own[2]) / scale_square
+    near = local - coeff
+    rest_square = everywhere(own[3] + near * (own[4] + near * own[5]))
+    along_one = everywhere(own[6] + near * own[7])
+    along_two = everywhere(own[8] + near * (own[9] + near * own[10]))
     turn = skew[0:1, :1] - coeff * (skew[1:2, :1] - coeff * skew[2:3, :1])
     along_two = along_two + turn * (devices / entries)
     scale = jnp.sqrt(scale_square)
@@ -657,11 +691,10 @@
     inverse = 1.0 / (second_norm * scale)
     along_one = along_one * inverse / scale_square
     along_two = along_two * inverse * inverse
-    join(next_residue, side, own_part[...], near_part[...])
     second = (answer[...] - coeff * vector[...]) * inverse
     basis_two[...] = second
     next_residue[...] = (
-        (next_residue[...] + slope[...] - coeff * answer[...]) * inverse
+        (joined(parts) + slope[...] - coeff * answer[...]) * inverse
         - along_one * vector[...]
         - along_two * second
     )
@@ -674,12 +707,13 @@
 HBM = pl.BlockSpec(memory_space=pltpu.HBM)
 
 
-def run(kernel, name, specs, operands, outs, scratch=(), micros=1, room=12):
+def run(kernel, name, specs, operands, outs, scratch=(), micros=1, room=12, spaces=None):
+    spaces = spaces or [pltpu.VMEM] * len(outs)
     return pl.pallas_call(
         kernel,
-        out_shape=[pltpu.VMEM(shape, dtype) for shape, dtype in outs],
+        out_shape=[space(shape, dtype) for space, (shape, dtype) in zip(spaces, outs)],
         in_specs=specs,
-        out_specs=[VMEM] * len(outs),
+        out_specs=[pl.BlockSpec(memory_space=space) for space in spaces],
         scratch_shapes=list(scratch),
         compiler_params=pltpu.CompilerParams(vmem_limit_bytes=room * 2**20),
         cost_estimate=pl.CostEstimate(
@@ -694,44 +728,52 @@
     return lax.ppermute(value, "samples", [(at, at ^ mask) for at in range(count)])
 
 
-def trade(value, mask):
-    count = lax.axis_size("nodes")
-    return lax.ppermute(value, "nodes", [(at, at ^ mask) for at in range(count)])
-
-
-def total(value, axis):
-    count, stride = lax.axis_size(axis), 1
+def trade(value, masks):
+    count, parts = lax.axis_size("nodes"), lax.axis_size("samples")
+    pairs = [
+        (at * parts + which, (at ^ masks[which % len(masks)]) * parts + which)
+        for at in range(count)
+        for which in range(parts)
+    ]
+    return lax.ppermute(value, ("nodes", "samples"), pairs)
+
+
+def add(after, terms):
+    (value,) = run(
+        sum_kernel,
+        "sum",
+        [VMEM] * (len(terms) + 1),
+        (after, *terms),
+        [(terms[0].shape, F32)],
+    )
+    return value
+
+
+def exchange(value, axis, after):
+    count, stride, terms = lax.axis_size(axis), 1, [value]
     while stride < count:
+        if stride > 1:
+            value = add(after, terms)
         radix = 4 if count // stride % 4 == 0 else 2
-        others = [
+        terms = [value] + [
             lax.ppermute(value, axis, [(at, at ^ (step * stride)) for at in range(count)])
-            for step in range(1, radix)
+            for step in range(radix - 1, 0, -1)
         ]
-        value = value + functools.reduce(jnp.add, others)
         stride *= radix
-    return value
-
-
-def send_groups(kept, sent):
-    times = kept.shape[0]
+    return terms
+
+
+def hand_out(after, place, kept, arrived):
     count = lax.axis_size("samples") // 2
-    blocks = {0: kept}
-    for group in range(1, count):
-        blocks[group] = sent[(group - 1) * times : group * times] if count > 2 else sent
-    bit = count // 2
-    while bit > 1:
-        for group in [name for name in blocks if name & bit]:
-            blocks[group ^ bit] = blocks[group ^ bit] + swap(blocks.pop(group), 2 * bit)
-        bit //= 2
-    return blocks[0], swap(blocks[1], 2) if count > 1 else jnp.zeros_like(kept)
-
-
-def merge(after, kept, arrived):
-    half_block = ((kept.shape[0] // 2, kept.shape[1]), F32)
-    own, near = run(
-        merge_kernel, "merge", [VMEM] * 3, (after, kept, arrived), [half_block, half_block]
-    )
-    return own, swap(near, 1)
+    field = ((kept.shape[0] // count, 2 * kept.shape[1]), F32)
+    parts = run(
+        combine_kernel,
+        "combine",
+        [VMEM, SMEM] + [VMEM] * 2,
+        (after, place, kept, arrived),
+        [field] * count,
+    )
+    return [parts[0]] + [swap(part, 2 * mask) for mask, part in enumerate(parts) if mask]
 
 
 def shards(
@@ -760,41 +802,41 @@
 
     slot_count = weights.shape[0]
     (
-        coupling_high,
-        coupling_low,
+        own_vector,
         picked,
         linear_wide,
         capacity_wide,
         capacity,
-        cut_halo,
         table,
         own_operating,
-        own_vector,
         forward,
         back,
+        entry_rows,
+        weight_rows,
+        place,
     ) = run(
-        prepare_kernel,
-        "prepare",
+        fetch_kernel,
+        "fetch",
         [SMEM] + [HBM] * 12,
         (place,)
         + tuple(
             pltpu.with_memory_space_constraint(value, pltpu.HBM)
-            for value in (neighbours, weights, degree, linear, capacity, send_list, boundary)
-            + (table, operating, vector, forward, back)
+            for value in (vector, neighbours, weights, degree, linear, capacity, send_list)
+            + (boundary, table, operating, forward, back)
         ),
         [
-            ((sources, width), BF16),
-            ((sources, width), BF16),
+            ((rows, nodes), F32),
             ((nodes, lanes), BF16),
             ((1, width), F32),
             ((1, width), F32),
             ((1, nodes), F32),
-            ((lanes, lanes), F32),
             (table.shape, F32),
-            ((rows, nodes), F32),
             ((rows, nodes), F32),
             (forward.shape[1:], BF16),
             (back.shape[1:], BF16),
+            ((slot_count, width), I32),
+            ((slot_count, width), F32),
+            ((4,), I32),
         ],
         scratch=[
             pltpu.VMEM((slot_count, nodes), I32),
@@ -803,11 +845,18 @@
             pltpu.VMEM((1, nodes), F32),
             pltpu.SMEM(send_list.shape, I32),
             pltpu.SMEM(boundary.shape, I32),
-            pltpu.VMEM((slot_count, width), I32),
-            pltpu.VMEM((slot_count, width), F32),
             pltpu.SemaphoreType.DMA((12,)),
         ],
-        micros=8,
+        micros=2,
+        spaces=[pltpu.VMEM] * 11 + [pltpu.SMEM],
+    )
+    coupling_high, coupling_low, cut_halo = run(
+        prepare_kernel,
+        "prepare",
+        [VMEM] * 2,
+        (entry_rows, weight_rows),
+        [((sources, width), BF16), ((sources, width), BF16), ((lanes, lanes), F32)],
+        micros=7,
     )
     near_operating = swap(operating, 1)
     vectors, bit = [vector], parts // 2
@@ -841,10 +890,10 @@
         -(-(start + max(times, slots)) // LANES) * LANES,
     )
     field_high, field_low, wave, current, cut_current, *sent = run(
-        functools.partial(wave_kernel, pieces=parts),
+        functools.partial(wave_kernel, pieces=parts, steps=steps),
         "wave",
-        [VMEM] * (parts + 8),
-        (*vectors, forward, conductances, picked, coupling_high, coupling_low)
+        [SMEM] + [VMEM] * (parts + 8),
+        (place, *vectors, forward, conductances, picked, coupling_high, coupling_low)
         + (linear_wide, capacity_wide, cut_halo),
         [
             ((length, sources), BF16),
@@ -853,10 +902,12 @@
             ((2 * times, nodes), BF16),
             ((lanes, times), F32),
         ]
-        + [(packet, F32)] * steps,
+        + [(packet, F32)] * len(packet_steps(steps)),
         micros=2,
     )
-    arrived = [trade(packet, step + 1) for step, packet in enumerate(sent)]
+    arrived = [trade(packet, masks) for packet, masks in zip(sent, packet_steps(steps))]
+    if steps == 3:
+        arrived.append(swap(arrived[-1], 1))
     others = []
     if not shared:
         gathered = lax.all_gather(cut_current, "nodes")
@@ -871,53 +922,63 @@
         [wide] * 5,
         micros=3,
     )
-    rest = length - times
-    image, load, kept, sent, sums, halo = run(
+    block = ((length // 2, half), F32)
+    image, load, own_sums, halo, kept, sent = run(
         functools.partial(first_kernel, steps=steps, apart=len(others)),
         "first",
-        [VMEM] * (steps + len(others) + 7),
-        (*arrived, *others, cut_current, local_load, slope, own_wave, back, coupling_high, coupling_low),
-        [wide, wide, wide, ((max(rest, 8), half), F32), ((8, half), F32), ((times, lanes), F32)],
+        [SMEM] + [VMEM] * (steps + len(others) + 7),
+        (place, *arrived, *others, cut_current, local_load, slope, own_wave, back, coupling_high, coupling_low),
+        [wide, wide, ((8, half), F32), ((times, lanes), F32), block, block],
         micros=1,
     )
     near_image = swap(image, 1)
     bit = 2
-    while bit < parts:
-        sums = sums + swap(sums, bit)
+    while 2 * bit < parts:
+        own_sums = own_sums + swap(own_sums, bit)
         bit *= 2
-    kept, arrived = send_groups(kept, sent)
+    far_sums = swap(own_sums, bit) if bit < parts else jnp.zeros_like(own_sums)
+    arrived = swap(sent, 1)
+
     second_load, second_kept, second_sent = run(
         second_kernel,
         "second",
         [SMEM] + [VMEM] * 8,
         (place, halo, near_image, image, back, conductances)
         + (coupling_high, coupling_low, linear_wide),
-        [wide, wide, ((max(rest, 8), half), F32)],
+        [wide, block, block],
         scratch=[pltpu.VMEM((2 * times, nodes), BF16)],
         micros=3,
     )
+    answer_parts = hand_out(second_load, place, kept, arrived)
+    (second_sent,) = run(
+        relay_kernel,
+        "relay",
+        [VMEM] * 2,
+        (far_sums, second_sent),
+        [(second_sent.shape, F32)],
+    )
+    second_arrived = swap(second_sent, 1)
     gathered = -(-node_groups * parts // LANES) * LANES
     (scalars,) = run(
         functools.partial(products_kernel, length=length),
         "products",
-        [SMEM] + [VMEM] * 8,
-        (place, own_vector, load, second_load, image, own_wave, dual, dual_slope, sums),
+        [SMEM] + [VMEM] * 9,
+        (place, own_vector, load, second_load, image, own_wave, dual, dual_slope)
+        + (own_sums, far_sums),
         [((16, gathered), F32)],
         micros=1,
     )
-    second_kept, second_arrived = send_groups(second_kept, second_sent)
-    own_image, near_image = merge(scalars, kept, arrived)
-    scalars = total(scalars, "nodes")
+    second_parts = hand_out(scalars, place, second_kept, second_arrived)
+    scalars = add(cut_halo, exchange(scalars, "nodes", cut_halo))
     answer, slope, skew = run(
         functools.partial(settle_kernel, length=length),
         "settle",
-        [SMEM] + [VMEM] * 4,
-        (place, own_image, near_image, own_vector, capacity),
+        [SMEM] + [VMEM] * (len(answer_parts) + 2),
+        (place, own_vector, capacity, *answer_parts),
         [((rows, nodes), F32), ((rows, nodes), F32), ((8, LANES), F32)],
         micros=1,
     )
-    own_part, near_part = merge(scalars, second_kept, second_arrived)
-    scalars = total(scalars, "samples")
+    scalars = add(skew, exchange(scalars, "samples", cut_halo))
     field = jax.ShapeDtypeStruct((rows, nodes), F32)
     return tuple(
         pl.pallas_call(
@@ -925,11 +986,11 @@
                 last_kernel, entries=entries, devices=float(node_groups * parts)
             ),
             out_shape=[field, field],
-            in_specs=[VMEM] * 5 + [SMEM] + [VMEM] * 2,
+            in_specs=[VMEM] * (5 + len(second_parts)),
             out_specs=[VMEM] * 2,
             compiler_params=pltpu.CompilerParams(vmem_limit_bytes=12 * 2**20),
             name="last",
-        )(scalars, own_vector, answer, slope, skew, place, own_part, near_part)
+        )(scalars, own_vector, answer, slope, skew, *second_parts)
     )
 
 

time: 45.6 us -> 43.3 us (0.950)
  Pallas kernels: 21 us -> 17.3 us
  waiting for transfers between devices: 6.04 us -> 7.27 us
    pallas_call x11 -> x15, Pallas kernels: 19.4 us -> 16.3 us  [run(): pl.pallas_call(kernel, out_shape=[space(shape, dtype) for space, (shape,...]
    ppermute x10 -> x11, waiting for transfers between devices: 0.18 us -> 2.06 us  [swap(): lax.ppermute(value, 'samples', [(at, at ^ mask) for at in range(count)])]
    ppermute x9 -> x8, waiting for transfers between devices: 5.86 us -> 5.21 us  [the longest x6 4.88 us: exchange(): lax.ppermute(value, axis, [(at, at ^ step * stride) for at in range(count)])]
    pallas_call x1, Pallas kernels: 1.56 us -> 1.02 us  [shards(): pl.pallas_call(functools.partial(last_kernel, entries=entries, devices=fl...]
    ppermute x10 -> x11, starting transfers between devices: 6.82 us -> 7.18 us  [swap(): lax.ppermute(value, 'samples', [(at, at ^ mask) for at in range(count)])]
    ppermute x9 -> x8, starting transfers between devices: 10.7 us -> 10.5 us  [the longest x6 6.31 us: exchange(): lax.ppermute(value, axis, [(at, at ^ step * stride) for at in range(count)])]
  transfers between devices with their start and end apart: 19 -> 19, of which waited for: 6 -> 9; matrix products, arithmetic and copies ran while one was open for 0% -> 0% of each run, Pallas kernels for 38% -> 33%
where the time goes in v5:
time: 43.3 us; the launch traced here: 43.2 us
  starting transfers between devices  17.7 us (41%)
  Pallas kernels  17.3 us (40%)
  waiting for transfers between devices  7.27 us (17%)
  between operations  0.77 us (2%)
    pallas_call x15, Pallas kernels, run(): pl.pallas_call(kernel, out_shape=[space(shape, dtype) for space, (shape,...  16.3 us
    ppermute x11, starting transfers between devices, swap(): lax.ppermute(value, 'samples', [(at, at ^ mask) for at in range(count)])  7.18 us
    ppermute x6, starting transfers between devices, exchange(): lax.ppermute(value, axis, [(at, at ^ step * stride) for at in range(count)])  6.31 us
    ppermute x6, waiting for transfers between devices, exchange(): lax.ppermute(value, axis, [(at, at ^ step * stride) for at in range(count)])  4.88 us
    ppermute x2, starting transfers between devices, trade(): return lax.ppermute(value, ('nodes', 'samples'), pairs)  4.22 us
    ppermute x11, waiting for transfers between devices, swap(): lax.ppermute(value, 'samples', [(at, at ^ mask) for at in range(count)])  2.06 us
    pallas_call x1, Pallas kernels, shards(): pl.pallas_call(functools.partial(last_kernel, entries=entries, devices=fl...  1.02 us
  transfers between devices with their start and end apart: 19, of which 9 were waited for; matrix products, arithmetic and copies ran while one was open for 0% of the time, Pallas kernels for 33%

profile of v5, /device:TPU:0, one launch (start us, length us, event | category | flops | bytes accessed | tf_op | source)
XLA Modules:
  0.0 43.2 jit_solution(10356669463328432178)
XLA Ops:
  0.6 3.0 %collective-permute-start = (f32[32,2048]{1,0:T(8,128)}, f32[32,2048]{1,0:T(8,128)S(1)}, u32[]{:S(2)}, u32[]{:S(2)}) collective-permute-start(f32[32,2048]{1,0:T(8,128)} %vector_in.1), channel_id=1, source_target_pairs={{0,2},{1,3},{2,0},{3,1},{4,6},{5,7},{6,4},{7,5},{8,10},{9,11},{10,... | collective-permute-start | bytes 786440 | tf_op jit(solution)/shard_map/ppermute | solution.py:728
  3.6 0.0 collective-permute-start.1
  3.6 0.5 %collective-permute-start.3 = (f32[32,2048]{1,0:T(8,128)}, f32[32,2048]{1,0:T(8,128)S(1)}, u32[]{:S(2)}, u32[]{:S(2)}) collective-permute-start(f32[32,2048]{1,0:T(8,128)} %operating_in.1), channel_id=1, source_target_pairs={{0,1},{1,0},{2,3},{3,2},{4,5},{5,4},{6,7},{7,6},{8,9},{9,8},{10,11... | collective-permute-start | bytes 786440 | tf_op jit(solution)/shard_map/ppermute | solution.py:728
  4.1 0.1 pad_add_fusion.place_in
  4.2 2.3 %fetch.1 = (f32[32,2048]{1,0:T(8,128)S(1)}, bf16[2048,128]{1,0:T(8,128)(2,1)S(1)}, f32[1,1152]{1,0:T(1,128)S(1)}, f32[1,1152]{1,0:T(1,128)S(1)}, f32[1,2048]{1,0...) custom-call(s32[4]{0:T(128)S(1)} %pad_add_fusion.place_in, ...), custom_call_target="tpu_custom_call" | custom-call | bytes 6000000 | tf_op jit(solution)/shard_map/fetch/pallas_call | solution.py:712
  6.5 6.0 %prepare.1 = (bf16[2176,1152]{1,0:T(8,128)(2,1)S(1)}, bf16[2176,1152]{1,0:T(8,128)(2,1)S(1)}, f32[128,128]{1,0:T(8,128)S(1)}) custom-call(s32[8,1152]{1,0:T(8,128)S(1)} %get-tuple-element.48.entry_rows, f32[8,1152]{1,0:T(8,128)S(1)} %get-tuple-element.49.weight_rows), custom_call_target="tpu_custom_call" | custom-call | bytes 21000000 | tf_op jit(solution)/shard_map/prepare/pallas_call | solution.py:712
  12.5 0.0 collective-permute-done.refs_1_
  12.6 0.1 collective-permute-start.2
  12.6 0.0 collective-permute-done.3.near_operating
  12.6 1.0 %conductance.1.refs_6_.conductances = f32[64,2176]{1,0:T(8,128)S(1)} custom-call(s32[4]{0:T(128)S(4)} %get-tuple-element.45.place.refs_0_, f32[32,2048]{1,0:T(8,128)S(1)} %collective-permute-done.3.near_operating, f32[32,2048]{1,0:T(8,128)S(1)} %get-tuple-element.52.operating, f32[1,16]{1,0:T(1,128)S(1)} %get-tuple-element.53.table, ...), custom_call_target="tpu_custom_call" | custom-call | bytes 3000000 | tf_op jit(solution)/shard_map/conductance/pallas_call | solution.py:712
  13.6 0.0 collective-permute-done.1.refs_3_
  13.6 0.5 %collective-permute-done.2.refs_4_ = f32[32,2048]{1,0:T(8,128)S(1)} collective-permute-done((f32[32,2048]{1,0:T(8,128)S(1)}, f32[32,2048]{1,0:T(8,128)S(1)}, u32[]{:S(2)}, u32[]{:S(2)}) %collective-permute-start.2) | collective-permute-done | bytes 262176 | tf_op jit(solution)/shard_map/ppermute | solution.py:728
  14.2 1.1 %wave.1 = (bf16[128,2176]{1,0:T(8,128)(2,1)S(1)}, bf16[128,2176]{1,0:T(8,128)(2,1)S(1)}, f32[64,2176]{1,0:T(8,128)S(1)}, bf16[128,2048]{1,0:T(8,128)(2,1)S(1)}, ...) custom-call(s32[4]{0:T(128)S(4)} %get-tuple-element.45.place.refs_0_, ...), custom_call_target="tpu_custom_call" | custom-call | bytes 6000000 | tf_op jit(solution)/shard_map/wave/pallas_call | solution.py:712
  15.3 1.6 %collective-permute-start.5 = (f32[48,128]{1,0:T(8,128)S(1)}, f32[48,128]{1,0:T(8,128)S(1)}, u32[]{:S(2)}, u32[]{:S(2)}) collective-permute-start(f32[48,128]{1,0:T(8,128)S(1)} %get-tuple-element.60), channel_id=1, source_target_pairs={{0,4},{1,13},{2,6},{3,15},{4,0},{5,9},{6,2},{7,11},{8,12},{9,5},{1... | collective-permute-start | bytes 73736 | tf_op jit(solution)/shard_map/ppermute | solution.py:738
  16.9 2.6 %collective-permute-start.4 = (f32[48,128]{1,0:T(8,128)S(1)}, f32[48,128]{1,0:T(8,128)S(1)}, u32[]{:S(2)}, u32[]{:S(2)}) collective-permute-start(f32[48,128]{1,0:T(8,128)S(1)} %get-tuple-element.59), channel_id=1, source_target_pairs={{0,8},{1,9},{2,10},{3,11},{4,12},{5,13},{6,14},{7,15},{8,0},{9,1},... | collective-permute-start | bytes 73736 | tf_op jit(solution)/shard_map/ppermute | solution.py:738
  19.5 0.0 collective-permute-done.5.refs_2_
  19.5 0.5 %collective-permute-start.6 = (f32[48,128]{1,0:T(8,128)S(1)}, f32[48,128]{1,0:T(8,128)S(1)}, u32[]{:S(2)}, u32[]{:S(2)}) collective-permute-start(f32[48,128]{1,0:T(8,128)S(1)} %collective-permute-done.5.refs_2_), channel_id=1, source_target_pairs={{0,1},{1,0},{2,3},{3,2},{4,5},{5,4},{6,7},{7,6},{8,9},{9,8},{10,11... | collective-permute-start | bytes 73736 | tf_op jit(solution)/shard_map/ppermute | solution.py:728
  20.0 1.7 %local.1 = (f32[64,1024]{1,0:T(8,128)S(1)}, f32[64,1024]{1,0:T(8,128)S(1)}, f32[64,1024]{1,0:T(8,128)S(1)}, f32[64,1024]{1,0:T(8,128)S(1)}, f32[64,1024]{1,0:T(8,128)S(1)}) custom-call(bf16[128,2176]{1,0:T(8,128)(2,1)S(1)} %get-tuple-element.62.field_high, bf16[128,2176]{1,0:T(8,128)(2,1)S(1)} %get-tuple-element.63.field_low, ...), custom_call_target="tpu_custom_call" | custom-call | bytes 9000000 | tf_op jit(solution)/shard_map/local/pallas_call | solution.py:712
  21.7 0.3 collective-permute-done.4.refs_1_
  22.1 0.0 collective-permute-done.6.refs_3_
  22.1 0.9 %first.1 = (f32[64,1024]{1,0:T(8,128)S(1)}, f32[64,1024]{1,0:T(8,128)S(1)}, f32[8,1024]{1,0:T(8,128)S(1)}, f32[64,128]{1,0:T(8,128)S(1)}, f32[64,1024]{1,0:T(8,128)S(1)}, /*index=5*/f32[64,1024]{1,0:T(8,128)S(1)}) custom-call(s32[4]{0:T(128)S(4)} %get-tuple-element.45.place.refs_0_, f32[48,128]{1,0:T(8,128)S(1)} %collective-permute-done.4.refs_1_, ...), custom_call_target="tpu_custom_call" | custom-call | bytes 3000000 | tf_op jit(solution)/shard_map/first/pallas_call | solution.py:712
  22.9 0.4 collective-permute-start.7
  23.3 0.5 %collective-permute-start.10 = (f32[8,1024]{1,0:T(8,128)S(1)}, f32[8,1024]{1,0:T(8,128)S(1)}, u32[]{:S(2)}, u32[]{:S(2)}) collective-permute-start(f32[8,1024]{1,0:T(8,128)S(1)} %get-tuple-element.81.own_sums), channel_id=1, source_target_pairs={{0,2},{1,3},{2,0},{3,1},{4,6},{5,7},{6,4},{7,5},{8,10},{9,11},{10,... | collective-permute-start | bytes 98312 | tf_op jit(solution)/shard_map/ppermute | solution.py:728
  23.8 0.0 collective-permute-start.8
  23.8 0.7 %collective-permute-done.7.near_image = f32[64,1024]{1,0:T(8,128)S(1)} collective-permute-done((f32[64,1024]{1,0:T(8,128)S(1)}, f32[64,1024]{1,0:T(8,128)S(1)}, u32[]{:S(2)}, u32[]{:S(2)}) %collective-permute-start.7) | collective-permute-done | bytes 262176 | tf_op jit(solution)/shard_map/ppermute | solution.py:728
  24.5 1.9 %second.1 = (f32[64,1024]{1,0:T(8,128)S(1)}, f32[64,1024]{1,0:T(8,128)S(1)}, f32[64,1024]{1,0:T(8,128)S(1)}) custom-call(s32[4]{0:T(128)S(4)} %get-tuple-element.45.place.refs_0_, f32[64,128]{1,0:T(8,128)S(1)} %get-tuple-element.70.halo, f32[64,1024]{1,0:T(8,128)S(1)} %collective-permute-done.7.near_image, f32[64,1024]{1,0:T(8,128)S(1)} %get-tuple-element.71.image, ...), custom_call_target="tpu_custom_call" | custom-call | bytes 9000000 | tf_op jit(solution)/shard_map/second/pallas_call | solution.py:712
  26.4 0.8 %collective-permute-done.10.far_sums.refs_0_ = f32[8,1024]{1,0:T(8,128)S(1)} collective-permute-done((f32[8,1024]{1,0:T(8,128)S(1)}, f32[8,1024]{1,0:T(8,128)S(1)}, u32[]{:S(2)}, u32[]{:S(2)}) %collective-permute-start.10) | collective-permute-done | bytes 32800 | tf_op jit(solution)/shard_map/ppermute | solution.py:728
  27.2 0.1 collective-permute-start.17
  27.3 0.0 collective-permute-done.8.arrived
  27.4 0.6 %collective-permute-start.9 = (f32[32,2048]{1,0:T(8,128)S(1)}, f32[32,2048]{1,0:T(8,128)S(1)}, u32[]{:S(2)}, u32[]{:S(2)}) collective-permute-start(f32[32,2048]{1,0:T(8,128)S(1)} %get-tuple-element.76), channel_id=1, source_target_pairs={{0,2},{1,3},{2,0},{3,1},{4,6},{5,7},{6,4},{7,5},{8,10},{9,11},{10,... | collective-permute-start | bytes 786440 | tf_op jit(solution)/shard_map/ppermute | solution.py:728
  28.0 0.8 %products.1.refs_0_.after = f32[16,128]{1,0:T(8,128)S(1)} custom-call(s32[4]{0:T(128)S(4)} %get-tuple-element.45.place.refs_0_, f32[32,2048]{1,0:T(8,128)S(1)} %get-tuple-element.46.refs_1_.vector, f32[64,1024]{1,0:T(8,128)S(1)} %get-tuple-element.78.load, f32[64,1024]{1,0:T(8,128)S(1)} %get-tuple-element.72.after.second_load, ...), custom_call_target="tpu_custom_call" | custom-call | bytes 3000000 | tf_op jit(solution)/shard_map/products/pallas_call | solution.py:712
  28.8 0.1 collective-permute-done.17.arrived
  28.9 1.5 %collective-permute-start.18 = (f32[32,2048]{1,0:T(8,128)S(1)}, f32[32,2048]{1,0:T(8,128)S(1)}, u32[]{:S(2)}, u32[]{:S(2)}) collective-permute-start(f32[32,2048]{1,0:T(8,128)S(1)} %get-tuple-element.87), channel_id=1, source_target_pairs={{0,2},{1,3},{2,0},{3,1},{4,6},{5,7},{6,4},{7,5},{8,10},{9,11},{10,... | collective-permute-start | bytes 786440 | tf_op jit(solution)/shard_map/ppermute | solution.py:728
  30.4 3.0 %collective-permute-start.11 = (f32[16,128]{1,0:T(8,128)S(1)}, f32[16,128]{1,0:T(8,128)S(1)}, u32[]{:S(2)}, u32[]{:S(2)}) collective-permute-start(f32[16,128]{1,0:T(8,128)S(1)} %products.1.refs_0_.after), channel_id=1, source_target_pairs={{0,12},{4,8},{8,4},{12,0},{1,13},{5,9},{9,5},{13,1},{2,14},{6,10},... | collective-permute-start | bytes 24584 | tf_op jit(solution)/shard_map/ppermute | solution.py:759
  33.4 0.0 collective-permute-start.12
  33.4 1.4 %collective-permute-start.13 = (f32[16,128]{1,0:T(8,128)S(1)}, f32[16,128]{1,0:T(8,128)S(1)}, u32[]{:S(2)}, u32[]{:S(2)}) collective-permute-start(f32[16,128]{1,0:T(8,128)S(1)} %products.1.refs_0_.after), channel_id=1, source_target_pairs={{0,4},{4,0},{8,12},{12,8},{1,5},{5,1},{9,13},{13,9},{2,6},{6,2},{1... | collective-permute-start | bytes 24584 | tf_op jit(solution)/shard_map/ppermute | solution.py:759
  34.8 1.1 %collective-permute-done.11.refs_1_ = f32[16,128]{1,0:T(8,128)S(1)} collective-permute-done((f32[16,128]{1,0:T(8,128)S(1)}, f32[16,128]{1,0:T(8,128)S(1)}, u32[]{:S(2)}, u32[]{:S(2)}) %collective-permute-start.11) | collective-permute-done | bytes 8224 | tf_op jit(solution)/shard_map/ppermute | solution.py:759
  35.9 2.1 %collective-permute-done.12.refs_2_ = f32[16,128]{1,0:T(8,128)S(1)} collective-permute-done((f32[16,128]{1,0:T(8,128)S(1)}, f32[16,128]{1,0:T(8,128)S(1)}, u32[]{:S(2)}, u32[]{:S(2)}) %collective-permute-start.12) | collective-permute-done | bytes 8224 | tf_op jit(solution)/shard_map/ppermute | solution.py:759
  37.9 0.0 collective-permute-done.13.refs_3_
  37.9 0.1 collective-permute-start.14
  38.0 0.6 %collective-permute-start.15 = (f32[16,128]{1,0:T(8,128)S(1)}, f32[16,128]{1,0:T(8,128)S(1)}, u32[]{:S(2)}, u32[]{:S(2)}) collective-permute-start(f32[16,128]{1,0:T(8,128)S(1)} %sum.2.refs_0_), channel_id=1, source_target_pairs={{0,2},{1,3},{2,0},{3,1},{4,6},{5,7},{6,4},{7,5},{8,10},{9,11},{10,... | collective-permute-start | bytes 24584 | tf_op jit(solution)/shard_map/ppermute | solution.py:759
  38.7 1.2 %collective-permute-start.16 = (f32[16,128]{1,0:T(8,128)S(1)}, f32[16,128]{1,0:T(8,128)S(1)}, u32[]{:S(2)}, u32[]{:S(2)}) collective-permute-start(f32[16,128]{1,0:T(8,128)S(1)} %sum.2.refs_0_), channel_id=1, source_target_pairs={{0,1},{1,0},{2,3},{3,2},{4,5},{5,4},{6,7},{7,6},{8,9},{9,8},{10,11... | collective-permute-start | bytes 24584 | tf_op jit(solution)/shard_map/ppermute | solution.py:759
  39.9 0.0 collective-permute-done.9.refs_1_
  39.9 0.5 %settle.1 = (f32[32,2048]{1,0:T(8,128)S(1)}, f32[32,2048]{1,0:T(8,128)S(1)}, f32[8,128]{1,0:T(8,128)S(1)}) custom-call(s32[4]{0:T(128)S(4)} %get-tuple-element.45.place.refs_0_, f32[32,2048]{1,0:T(8,128)S(1)} %get-tuple-element.46.refs_1_.vector, f32[1,2048]{1,0:T(1,128)S(1)} %get-tuple-element.47.capacity, f32[32,2048]{1,0:T(8,128)S(1)} %get-tuple-element.75.refs_0_, ...), custom_call_target="tpu_custom_call" | custom-call | bytes 3000000 | tf_op jit(solution)/shard_map/settle/pallas_call | solution.py:712
  40.4 1.1 %collective-permute-done.14.refs_1_ = f32[16,128]{1,0:T(8,128)S(1)} collective-permute-done((f32[16,128]{1,0:T(8,128)S(1)}, f32[16,128]{1,0:T(8,128)S(1)}, u32[]{:S(2)}, u32[]{:S(2)}) %collective-permute-start.14) | collective-permute-done | bytes 8224 | tf_op jit(solution)/shard_map/ppermute | solution.py:759
  41.5 0.6 %collective-permute-done.15.refs_2_ = f32[16,128]{1,0:T(8,128)S(1)} collective-permute-done((f32[16,128]{1,0:T(8,128)S(1)}, f32[16,128]{1,0:T(8,128)S(1)}, u32[]{:S(2)}, u32[]{:S(2)}) %collective-permute-start.15) | collective-permute-done | bytes 8224 | tf_op jit(solution)/shard_map/ppermute | solution.py:759
  42.1 0.0 collective-permute-done.18.refs_1_
  42.1 1.0 %last.1 = (f32[32,2048]{1,0:T(8,128)}, f32[32,2048]{1,0:T(8,128)}) custom-call(f32[16,128]{1,0:T(8,128)S(1)} %sum.3.gathered, f32[32,2048]{1,0:T(8,128)S(1)} %get-tuple-element.46.refs_1_.vector, f32[32,2048]{1,0:T(8,128)S(1)} %get-tuple-element.82.answer, f32[32,2048]{1,0:T(8,128)S(1)} %get-tuple-element.83.slope, ...), custom_call_target="tpu_custom_call" | custom-call | tf_op jit(solution)/shard_map/last/pallas_call | solution.py:984
  (8 shorter events, 0.1 us)
Async XLA Ops:
  0.6 11.9 %collective-permute-start = (f32[32,2048]{1,0:T(8,128)}, f32[32,2048]{1,0:T(8,128)S(1)}, u32[]{:S(2)}, u32[]{:S(2)}) collective-permute-start(f32[32,2048]{1,0:T(8,128)} %vector_in.1), channel_id=1, source_target_pairs={{0,2},{1,3},{2,0},{3,1},{4,6},{5,7},{6,4},{7,5},{8,10},{9,11},{10,... | collective-permute-start | bytes 786440 | tf_op jit(solution)/shard_map/ppermute | solution.py:728
  3.6 10.0 %collective-permute-start.1 = (f32[32,2048]{1,0:T(8,128)}, f32[32,2048]{1,0:T(8,128)S(1)}, u32[]{:S(2)}, u32[]{:S(2)}) collective-permute-start(f32[32,2048]{1,0:T(8,128)} %vector_in.1), channel_id=1, source_target_pairs={{0,1},{1,0},{2,3},{3,2},{4,5},{5,4},{6,7},{7,6},{8,9},{9,8},{10,11... | collective-permute-start | bytes 786440 | tf_op jit(solution)/shard_map/ppermute | solution.py:728
  3.6 9.0 %collective-permute-start.3 = (f32[32,2048]{1,0:T(8,128)}, f32[32,2048]{1,0:T(8,128)S(1)}, u32[]{:S(2)}, u32[]{:S(2)}) collective-permute-start(f32[32,2048]{1,0:T(8,128)} %operating_in.1), channel_id=1, source_target_pairs={{0,1},{1,0},{2,3},{3,2},{4,5},{5,4},{6,7},{7,6},{8,9},{9,8},{10,11... | collective-permute-start | bytes 786440 | tf_op jit(solution)/shard_map/ppermute | solution.py:728
  12.6 1.6 %collective-permute-start.2 = (f32[32,2048]{1,0:T(8,128)S(1)}, f32[32,2048]{1,0:T(8,128)S(1)}, u32[]{:S(2)}, u32[]{:S(2)}) collective-permute-start(f32[32,2048]{1,0:T(8,128)S(1)} %relay.2.refs_2_), channel_id=1, source_target_pairs={{0,1},{1,0},{2,3},{3,2},{4,5},{5,4},{6,7},{7,6},{8,9},{9,8},{10,11... | collective-permute-start | bytes 786440 | tf_op jit(solution)/shard_map/ppermute | solution.py:728
  15.3 4.2 %collective-permute-start.5 = (f32[48,128]{1,0:T(8,128)S(1)}, f32[48,128]{1,0:T(8,128)S(1)}, u32[]{:S(2)}, u32[]{:S(2)}) collective-permute-start(f32[48,128]{1,0:T(8,128)S(1)} %get-tuple-element.60), channel_id=1, source_target_pairs={{0,4},{1,13},{2,6},{3,15},{4,0},{5,9},{6,2},{7,11},{8,12},{9,5},{1... | collective-permute-start | bytes 73736 | tf_op jit(solution)/shard_map/ppermute | solution.py:738
  16.9 5.1 %collective-permute-start.4 = (f32[48,128]{1,0:T(8,128)S(1)}, f32[48,128]{1,0:T(8,128)S(1)}, u32[]{:S(2)}, u32[]{:S(2)}) collective-permute-start(f32[48,128]{1,0:T(8,128)S(1)} %get-tuple-element.59), channel_id=1, source_target_pairs={{0,8},{1,9},{2,10},{3,11},{4,12},{5,13},{6,14},{7,15},{8,0},{9,1},... | collective-permute-start | bytes 73736 | tf_op jit(solution)/shard_map/ppermute | solution.py:738
  19.5 2.5 %collective-permute-start.6 = (f32[48,128]{1,0:T(8,128)S(1)}, f32[48,128]{1,0:T(8,128)S(1)}, u32[]{:S(2)}, u32[]{:S(2)}) collective-permute-start(f32[48,128]{1,0:T(8,128)S(1)} %collective-permute-done.5.refs_2_), channel_id=1, source_target_pairs={{0,1},{1,0},{2,3},{3,2},{4,5},{5,4},{6,7},{7,6},{8,9},{9,8},{10,11... | collective-permute-start | bytes 73736 | tf_op jit(solution)/shard_map/ppermute | solution.py:728
  22.9 1.6 %collective-permute-start.7 = (f32[64,1024]{1,0:T(8,128)S(1)}, f32[64,1024]{1,0:T(8,128)S(1)}, u32[]{:S(2)}, u32[]{:S(2)}) collective-permute-start(f32[64,1024]{1,0:T(8,128)S(1)} %get-tuple-element.71.image), channel_id=1, source_target_pairs={{0,1},{1,0},{2,3},{3,2},{4,5},{5,4},{6,7},{7,6},{8,9},{9,8},{10,11... | collective-permute-start | bytes 786440 | tf_op jit(solution)/shard_map/ppermute | solution.py:728
  23.3 3.9 %collective-permute-start.10 = (f32[8,1024]{1,0:T(8,128)S(1)}, f32[8,1024]{1,0:T(8,128)S(1)}, u32[]{:S(2)}, u32[]{:S(2)}) collective-permute-start(f32[8,1024]{1,0:T(8,128)S(1)} %get-tuple-element.81.own_sums), channel_id=1, source_target_pairs={{0,2},{1,3},{2,0},{3,1},{4,6},{5,7},{6,4},{7,5},{8,10},{9,11},{10,... | collective-permute-start | bytes 98312 | tf_op jit(solution)/shard_map/ppermute | solution.py:728
  23.8 3.5 %collective-permute-start.8 = (f32[64,1024]{1,0:T(8,128)S(1)}, f32[64,1024]{1,0:T(8,128)S(1)}, u32[]{:S(2)}, u32[]{:S(2)}) collective-permute-start(f32[64,1024]{1,0:T(8,128)S(1)} %get-tuple-element.74), channel_id=1, source_target_pairs={{0,1},{1,0},{2,3},{3,2},{4,5},{5,4},{6,7},{7,6},{8,9},{9,8},{10,11... | collective-permute-start | bytes 786440 | tf_op jit(solution)/shard_map/ppermute | solution.py:728
  27.2 1.6 %collective-permute-start.17 = (f32[64,1024]{1,0:T(8,128)S(1)}, f32[64,1024]{1,0:T(8,128)S(1)}, u32[]{:S(2)}, u32[]{:S(2)}) collective-permute-start(f32[64,1024]{1,0:T(8,128)S(1)} %relay.3), channel_id=1, source_target_pairs={{0,1},{1,0},{2,3},{3,2},{4,5},{5,4},{6,7},{7,6},{8,9},{9,8},{10,11... | collective-permute-start | bytes 786440 | tf_op jit(solution)/shard_map/ppermute | solution.py:728
  27.4 12.5 %collective-permute-start.9 = (f32[32,2048]{1,0:T(8,128)S(1)}, f32[32,2048]{1,0:T(8,128)S(1)}, u32[]{:S(2)}, u32[]{:S(2)}) collective-permute-start(f32[32,2048]{1,0:T(8,128)S(1)} %get-tuple-element.76), channel_id=1, source_target_pairs={{0,2},{1,3},{2,0},{3,1},{4,6},{5,7},{6,4},{7,5},{8,10},{9,11},{10,... | collective-permute-start | bytes 786440 | tf_op jit(solution)/shard_map/ppermute | solution.py:728
  28.9 13.2 %collective-permute-start.18 = (f32[32,2048]{1,0:T(8,128)S(1)}, f32[32,2048]{1,0:T(8,128)S(1)}, u32[]{:S(2)}, u32[]{:S(2)}) collective-permute-start(f32[32,2048]{1,0:T(8,128)S(1)} %get-tuple-element.87), channel_id=1, source_target_pairs={{0,2},{1,3},{2,0},{3,1},{4,6},{5,7},{6,4},{7,5},{8,10},{9,11},{10,... | collective-permute-start | bytes 786440 | tf_op jit(solution)/shard_map/ppermute | solution.py:728
  30.4 5.4 %collective-permute-start.11 = (f32[16,128]{1,0:T(8,128)S(1)}, f32[16,128]{1,0:T(8,128)S(1)}, u32[]{:S(2)}, u32[]{:S(2)}) collective-permute-start(f32[16,128]{1,0:T(8,128)S(1)} %products.1.refs_0_.after), channel_id=1, source_target_pairs={{0,12},{4,8},{8,4},{12,0},{1,13},{5,9},{9,5},{13,1},{2,14},{6,10},... | collective-permute-start | bytes 24584 | tf_op jit(solution)/shard_map/ppermute | solution.py:759
  33.4 4.5 %collective-permute-start.12 = (f32[16,128]{1,0:T(8,128)S(1)}, f32[16,128]{1,0:T(8,128)S(1)}, u32[]{:S(2)}, u32[]{:S(2)}) collective-permute-start(f32[16,128]{1,0:T(8,128)S(1)} %products.1.refs_0_.after), channel_id=1, source_target_pairs={{0,8},{4,12},{8,0},{12,4},{1,9},{5,13},{9,1},{13,5},{2,10},{6,14},... | collective-permute-start | bytes 24584 | tf_op jit(solution)/shard_map/ppermute | solution.py:759
  33.4 4.5 %collective-permute-start.13 = (f32[16,128]{1,0:T(8,128)S(1)}, f32[16,128]{1,0:T(8,128)S(1)}, u32[]{:S(2)}, u32[]{:S(2)}) collective-permute-start(f32[16,128]{1,0:T(8,128)S(1)} %products.1.refs_0_.after), channel_id=1, source_target_pairs={{0,4},{4,0},{8,12},{12,8},{1,5},{5,1},{9,13},{13,9},{2,6},{6,2},{1... | collective-permute-start | bytes 24584 | tf_op jit(solution)/shard_map/ppermute | solution.py:759
  37.9 3.6 %collective-permute-start.14 = (f32[16,128]{1,0:T(8,128)S(1)}, f32[16,128]{1,0:T(8,128)S(1)}, u32[]{:S(2)}, u32[]{:S(2)}) collective-permute-start(f32[16,128]{1,0:T(8,128)S(1)} %sum.2.refs_0_), channel_id=1, source_target_pairs={{0,3},{1,2},{2,1},{3,0},{4,7},{5,6},{6,5},{7,4},{8,11},{9,10},{10,... | collective-permute-start | bytes 24584 | tf_op jit(solution)/shard_map/ppermute | solution.py:759
  38.0 4.1 %collective-permute-start.15 = (f32[16,128]{1,0:T(8,128)S(1)}, f32[16,128]{1,0:T(8,128)S(1)}, u32[]{:S(2)}, u32[]{:S(2)}) collective-permute-start(f32[16,128]{1,0:T(8,128)S(1)} %sum.2.refs_0_), channel_id=1, source_target_pairs={{0,2},{1,3},{2,0},{3,1},{4,6},{5,7},{6,4},{7,5},{8,10},{9,11},{10,... | collective-permute-start | bytes 24584 | tf_op jit(solution)/shard_map/ppermute | solution.py:759
  38.7 3.4 %collective-permute-start.16 = (f32[16,128]{1,0:T(8,128)S(1)}, f32[16,128]{1,0:T(8,128)S(1)}, u32[]{:S(2)}, u32[]{:S(2)}) collective-permute-start(f32[16,128]{1,0:T(8,128)S(1)} %sum.2.refs_0_), channel_id=1, source_target_pairs={{0,1},{1,0},{2,3},{3,2},{4,5},{5,4},{6,7},{7,6},{8,9},{9,8},{10,11... | collective-permute-start | bytes 24584 | tf_op jit(solution)/shard_map/ppermute | solution.py:759

commit v6 on v5

--- a/solution.py
+++ b/solution.py
@@ -138,7 +138,6 @@
 
 
 def fetch_kernel(
-    place_in,
     vector_in,
     neighbours_in,
     weights_in,
@@ -171,8 +170,8 @@
     boundary,
     copied,
 ):
-    for index in range(4):
-        place[index] = place_in[index]
+    place[0], place[1] = lax.axis_index("samples"), lax.axis_index("nodes")
+    place[2], place[3] = lax.axis_size("nodes"), lax.axis_size("samples")
     slots, nodes = neighbours.shape
     lanes = picked.shape[1]
     half = linear.shape[1] - lanes
@@ -259,16 +258,15 @@
         copy.wait()
 
 
-def prepare_kernel(entry_rows, weight_rows, coupling_high, coupling_low, cut_halo):
+def build(entry_rows, weight_rows, coupling_high, coupling_low):
     slots, width = entry_rows.shape
     sources = coupling_high.shape[0]
-    nodes = sources - cut_halo.shape[0]
-    half = width - cut_halo.shape[0]
-    unroll = 4
+    blocks = sources // CAP
+    unroll = max(count for count in range(1, 35) if blocks % count == 0)
+    wide = (CAP, LANES)
 
     def column_block(block, carry):
         at_lanes = pl.ds(pl.multiple_of(block * LANES, LANES), LANES)
-        wide = (CAP, LANES)
         names = [
             jnp.broadcast_to(entry_rows[slot : slot + 1, at_lanes], wide).astype(jnp.int16)
             for slot in range(slots)
@@ -283,27 +281,36 @@
                 high = jnp.zeros(wide, BF16)
                 low = jnp.zeros(wide, BF16)
                 for slot in range(slots):
-                    hit = names[slot] == row
+                    hit = names[slot] == row + jnp.int16(CAP * inner)
                     high = jnp.where(hit, parts[slot][0], high)
                     low = jnp.where(hit, parts[slot][1], low)
-                at = pl.ds(pl.multiple_of((step * unroll + inner) * 16, 16), 16)
+                at = pl.ds(pl.multiple_of((step * unroll + inner) * CAP, CAP), CAP)
                 coupling_high[at, at_lanes] = high
                 coupling_low[at, at_lanes] = low
-                row = row + jnp.int16(16)
-            return row
+            return row + jnp.int16(CAP * unroll)
 
         lax.fori_loop(
             0,
-            sources // 16 // unroll,
+            blocks // unroll,
             source_rows,
             lax.broadcasted_iota(I32, wide, 0).astype(jnp.int16),
         )
         return carry
 
     lax.fori_loop(0, width // LANES, column_block, 0)
-    cut_halo[...] = jnp.transpose(
-        coupling_high[nodes:, half:].astype(F32) + coupling_low[nodes:, half:].astype(F32)
-    )
+
+
+def prepare_kernel(entry_rows, weight_rows, coupling_high, coupling_low):
+    half = coupling_high.shape[1]
+    build(entry_rows.at[:, :half], weight_rows.at[:, :half], coupling_high, coupling_low)
+
+
+def prepare_cut_kernel(after, entry_rows, weight_rows, cut_high, cut_low, cut_halo):
+    lanes = cut_high.shape[1]
+    half = entry_rows.shape[1] - lanes
+    build(entry_rows.at[:, half:], weight_rows.at[:, half:], cut_high, cut_low)
+    nodes = cut_high.shape[0] - lanes
+    cut_halo[...] = jnp.transpose(cut_high[nodes:].astype(F32) + cut_low[nodes:].astype(F32))
 
 
 def relay_kernel(*refs):
@@ -382,7 +389,7 @@
         + at_cut
         + capacity[:, half:] * slope
         + coupled(
-            high, current[...], coupling_high, coupling_low, slice(0, nodes), slice(half, None)
+            high, current[...], coupling_high, coupling_low, slice(0, nodes), slice(None)
         )
     )
     image = jnp.transpose(image)
@@ -453,8 +460,9 @@
     return spectrum[:middle], spectrum[middle:]
 
 
-def first_kernel(*refs, steps, apart):
-    side, arrived, others = refs[0][0] % 2, refs[1 : steps + 1], refs[steps + 1 : steps + 1 + apart]
+def unpack(side, arrived, others, cut_current, lanes):
+    steps = len(arrived)
+    times = cut_current.shape[1]
     if steps == 3:
         both, own, near = (packet[...] for packet in arrived)
         arrived = [
@@ -462,38 +470,39 @@
             both,
             jnp.where(side == 0, near, own),
         ]
+    slots = steps * CAP
+    blank = jnp.zeros((lanes - slots, times), F32)
+
+    def stack(blocks):
+        return jnp.transpose(jnp.concatenate([*blocks, blank], axis=0))
+
+    def sender(step, block):
+        at = slice((block - 1) * CAP, block * CAP)
+        if step == 0:
+            return cut_current[at]
+        return others[0][step, at] if others else arrived[step - 1][at, :times]
+
+    current = stack([sender(step, step) for step in range(1, steps + 1)])
+    return arrived, stack, sender, current
+
+
+def first_kernel(*refs, steps, apart):
+    arrived, others = refs[1 : steps + 1], refs[steps + 1 : steps + 1 + apart]
     (
         cut_current,
         local_load,
         slope,
         own_wave,
-        back,
         coupling_high,
         coupling_low,
         image,
         load,
         sums,
-        halo,
-        kept,
-        sent,
     ) = refs[1 + steps + apart :]
-    times, half = local_load.shape
-    lanes = halo.shape[1]
+    half = load.shape[1]
+    lanes = -(-steps * CAP // LANES) * LANES
     nodes = coupling_high.shape[0] - lanes
-    slots = steps * CAP
-    start = packet_layout(steps, times)[1]
-    blank = jnp.zeros((lanes - slots, times), F32)
-
-    def stack(blocks):
-        return jnp.transpose(jnp.concatenate([*blocks, blank], axis=0))
-
-    def sender(step, block):
-        at = slice((block - 1) * CAP, block * CAP)
-        if step == 0:
-            return cut_current[at]
-        return others[0][step, at] if apart else arrived[step - 1][at, :times]
-
-    current = stack([sender(step, step) for step in range(1, steps + 1)])
+    current = unpack(refs[0][0] % 2, arrived, others, cut_current, lanes)[-1]
     high, low = split(current)
     share = coupled(
         high,
@@ -506,10 +515,20 @@
     load[...] = local_load[...] + share
     answer = load[...] + slope[...]
     image[...] = answer
-    kept[...], sent[...] = analysed(back, answer)
     lines = [*signed_sums(answer), *signed_sums(own_wave[...])]
     sums[...] = jnp.concatenate(lines + [jnp.zeros((4, half), F32)], axis=0)
 
+
+def spread_kernel(*refs, steps, apart):
+    arrived, others = refs[1 : steps + 1], refs[steps + 1 : steps + 1 + apart]
+    cut_current, image, back, halo, kept, sent = refs[1 + steps + apart :]
+    times = image.shape[0]
+    slots = steps * CAP
+    start = packet_layout(steps, times)[1]
+    arrived, stack, sender, _ = unpack(
+        refs[0][0] % 2, arrived, others, cut_current, halo.shape[1]
+    )
+    kept[...], sent[...] = analysed(back, image[...])
     currents = []
     for step in range(1, steps + 1):
         theirs = jnp.concatenate(
@@ -757,7 +776,7 @@
         radix = 4 if count // stride % 4 == 0 else 2
         terms = [value] + [
             lax.ppermute(value, axis, [(at, at ^ (step * stride)) for at in range(count)])
-            for step in range(radix - 1, 0, -1)
+            for step in range(1, radix)
         ]
         stride *= radix
     return terms
@@ -787,14 +806,6 @@
     slots = steps * CAP
     lanes = -(-slots // LANES) * LANES
     sources, width = nodes + lanes, half + lanes
-    place = jnp.stack(
-        [
-            lax.axis_index("samples"),
-            lax.axis_index("nodes"),
-            jnp.int32(node_groups),
-            jnp.int32(parts),
-        ]
-    ).astype(I32)
     forward, back = (jnp.asarray(table) for table in transform_tables(length, parts))
     linear, capacity, degree, table = (
         value.reshape(1, -1) for value in (linear, capacity, degree, table)
@@ -817,9 +828,8 @@
     ) = run(
         fetch_kernel,
         "fetch",
-        [SMEM] + [HBM] * 12,
-        (place,)
-        + tuple(
+        [HBM] * 12,
+        tuple(
             pltpu.with_memory_space_constraint(value, pltpu.HBM)
             for value in (vector, neighbours, weights, degree, linear, capacity, send_list)
             + (boundary, table, operating, forward, back)
@@ -850,13 +860,13 @@
         micros=2,
         spaces=[pltpu.VMEM] * 11 + [pltpu.SMEM],
     )
-    coupling_high, coupling_low, cut_halo = run(
+    coupling_high, coupling_low = run(
         prepare_kernel,
         "prepare",
         [VMEM] * 2,
         (entry_rows, weight_rows),
-        [((sources, width), BF16), ((sources, width), BF16), ((lanes, lanes), F32)],
-        micros=7,
+        [((sources, half), BF16)] * 2,
+        micros=6,
     )
     near_operating = swap(operating, 1)
     vectors, bit = [vector], parts // 2
@@ -869,11 +879,19 @@
             relay_kernel,
             "relay",
             [VMEM] * (far + 1),
-            (cut_halo, *vectors[1:]),
+            (coupling_low, *vectors[1:]),
             [((rows, nodes), F32)] * far,
         )
     vectors = vectors + [swap(piece, 1) for piece in vectors]
     vectors[0] = own_vector
+    cut_high, cut_low, cut_halo = run(
+        prepare_cut_kernel,
+        "prepare_cut",
+        [VMEM] * 3,
+        (vectors[far], entry_rows, weight_rows),
+        [((sources, lanes), BF16), ((sources, lanes), BF16), ((lanes, lanes), F32)],
+        micros=1,
+    )
     (conductances,) = run(
         conductance_kernel,
         "conductance",
@@ -893,7 +911,7 @@
         functools.partial(wave_kernel, pieces=parts, steps=steps),
         "wave",
         [SMEM] + [VMEM] * (parts + 8),
-        (place, *vectors, forward, conductances, picked, coupling_high, coupling_low)
+        (place, *vectors, forward, conductances, picked, cut_high, cut_low)
         + (linear_wide, capacity_wide, cut_halo),
         [
             ((length, sources), BF16),
@@ -923,12 +941,22 @@
         micros=3,
     )
     block = ((length // 2, half), F32)
-    image, load, own_sums, halo, kept, sent = run(
+    packets = (place, *arrived, *others, cut_current)
+    packet_specs = [SMEM] + [VMEM] * (len(packets) - 1)
+    image, load, own_sums = run(
         functools.partial(first_kernel, steps=steps, apart=len(others)),
         "first",
-        [SMEM] + [VMEM] * (steps + len(others) + 7),
-        (place, *arrived, *others, cut_current, local_load, slope, own_wave, back, coupling_high, coupling_low),
-        [wide, wide, ((8, half), F32), ((times, lanes), F32), block, block],
+        packet_specs + [VMEM] * 5,
+        (*packets, local_load, slope, own_wave, coupling_high, coupling_low),
+        [wide, wide, ((8, half), F32)],
+        micros=1,
+    )
+    halo, kept, sent = run(
+        functools.partial(spread_kernel, steps=steps, apart=len(others)),
+        "spread",
+        packet_specs + [VMEM] * 2,
+        (*packets, image, back),
+        [((times, lanes), F32), block, block],
         micros=1,
     )
     near_image = swap(image, 1)

time: 43.3 us -> 41.6 us (0.961)
  waiting for transfers between devices: 7.27 us -> 4.72 us
  starting transfers between devices: 17.7 us -> 20.1 us
  Pallas kernels: 17.3 us -> 15.8 us
    ppermute x11, starting transfers between devices: 7.18 us -> 9.45 us  [swap(): lax.ppermute(value, 'samples', [(at, at ^ mask) for at in range(count)])]
    ppermute x11, waiting for transfers between devices: 2.06 us -> 0.03 us  [swap(): lax.ppermute(value, 'samples', [(at, at ^ mask) for at in range(count)])]
    pallas_call x15 -> x17, Pallas kernels: 16.3 us -> 14.8 us  [run(): pl.pallas_call(kernel, out_shape=[space(shape, dtype) for space, (shape,...]
  transfers between devices with their start and end apart: 19 -> 19, of which waited for: 9 -> 4; matrix products, arithmetic and copies ran while one was open for 0% -> 0% of each run, Pallas kernels for 33% -> 32%
where the time goes in v6:
time: 41.6 us; the launch traced here: 41.4 us
  starting transfers between devices  20.1 us (48%)
  Pallas kernels  15.8 us (38%)
  waiting for transfers between devices  4.72 us (11%)
  between operations  0.83 us (2%)
    pallas_call x17, Pallas kernels, run(): pl.pallas_call(kernel, out_shape=[space(shape, dtype) for space, (shape,...  14.8 us
    ppermute x11, starting transfers between devices, swap(): lax.ppermute(value, 'samples', [(at, at ^ mask) for at in range(count)])  9.45 us
    ppermute x6, starting transfers between devices, exchange(): lax.ppermute(value, axis, [(at, at ^ step * stride) for at in range(count)])  6.31 us
    ppermute x6, waiting for transfers between devices, exchange(): lax.ppermute(value, axis, [(at, at ^ step * stride) for at in range(count)])  4.69 us
    ppermute x2, starting transfers between devices, trade(): return lax.ppermute(value, ('nodes', 'samples'), pairs)  4.34 us
    pallas_call x1, Pallas kernels, shards(): pl.pallas_call(functools.partial(last_kernel, entries=entries, devices=fl...  1.02 us
  transfers between devices with their start and end apart: 19, of which 4 were waited for; matrix products, arithmetic and copies ran while one was open for 0% of the time, Pallas kernels for 32%

profile of v6, /device:TPU:0, one launch (start us, length us, event | category | flops | bytes accessed | tf_op | source)
XLA Modules:
  0.0 41.4 jit_solution(8408992566257197215)
XLA Ops:
  0.6 3.0 %collective-permute-start = (f32[32,2048]{1,0:T(8,128)}, f32[32,2048]{1,0:T(8,128)S(1)}, u32[]{:S(2)}, u32[]{:S(2)}) collective-permute-start(f32[32,2048]{1,0:T(8,128)} %vector_in.1), channel_id=1, source_target_pairs={{0,2},{1,3},{2,0},{3,1},{4,6},{5,7},{6,4},{7,5},{8,10},{9,11},{10,... | collective-permute-start | bytes 786440 | tf_op jit(solution)/shard_map/ppermute | solution.py:747
  3.6 0.0 collective-permute-start.1
  3.6 0.5 %collective-permute-start.3 = (f32[32,2048]{1,0:T(8,128)}, f32[32,2048]{1,0:T(8,128)S(1)}, u32[]{:S(2)}, u32[]{:S(2)}) collective-permute-start(f32[32,2048]{1,0:T(8,128)} %operating_in.1), channel_id=1, source_target_pairs={{0,1},{1,0},{2,3},{3,2},{4,5},{5,4},{6,7},{7,6},{8,9},{9,8},{10,11... | collective-permute-start | bytes 786440 | tf_op jit(solution)/shard_map/ppermute | solution.py:747
  4.1 1.7 %fetch.1 = (f32[32,2048]{1,0:T(8,128)S(1)}, bf16[2048,128]{1,0:T(8,128)(2,1)S(1)}, f32[1,1152]{1,0:T(1,128)S(1)}, f32[1,1152]{1,0:T(1,128)S(1)}, f32[1,2048]{1,0...) custom-call(f32[32,2048]{1,0:T(8,128)} %vector_in.1, ...), custom_call_target="tpu_custom_call" | custom-call | bytes 6000000 | tf_op jit(solution)/shard_map/fetch/pallas_call | solution.py:731
  5.9 4.4 %prepare.1 = (bf16[2176,1024]{1,0:T(8,128)(2,1)S(1)}, bf16[2176,1024]{1,0:T(8,128)(2,1)S(1)}) custom-call(s32[8,1152]{1,0:T(8,128)S(1)} %get-tuple-element.50.entry_rows, f32[8,1152]{1,0:T(8,128)S(1)} %get-tuple-element.51.weight_rows), custom_call_target="tpu_custom_call" | custom-call | bytes 18000000 | tf_op jit(solution)/shard_map/prepare/pallas_call | solution.py:731
  10.3 0.0 collective-permute-done.refs_1_
  10.3 0.1 collective-permute-start.2
  10.4 0.6 %prepare_cut.1 = (bf16[2176,128]{1,0:T(8,128)(2,1)S(1)}, bf16[2176,128]{1,0:T(8,128)(2,1)S(1)}, f32[128,128]{1,0:T(8,128)S(1)}) custom-call(f32[32,2048]{1,0:T(8,128)S(1)} %relay.2.after.refs_2_, s32[8,1152]{1,0:T(8,128)S(1)} %get-tuple-element.50.entry_rows, f32[8,1152]{1,0:T(8,128)S(1)} %get-tuple-element.51.weight_rows), custom_call_target="tpu_custom_call" | custom-call | bytes 3000000 | tf_op jit(solution)/shard_map/prepare_cut/pallas_call | solution.py:731
  11.0 0.0 collective-permute-done.3.near_operating
  11.0 1.0 %conductance.1.refs_6_.conductances = f32[64,2176]{1,0:T(8,128)S(1)} custom-call(s32[4]{0:T(128)S(4)} %get-tuple-element.47.place.refs_0_, f32[32,2048]{1,0:T(8,128)S(1)} %collective-permute-done.3.near_operating, f32[32,2048]{1,0:T(8,128)S(1)} %get-tuple-element.54.operating, f32[1,16]{1,0:T(1,128)S(1)} %get-tuple-element.55.table, ...), custom_call_target="tpu_custom_call" | custom-call | bytes 3000000 | tf_op jit(solution)/shard_map/conductance/pallas_call | solution.py:731
  12.0 0.0 collective-permute-done.1.refs_3_
  12.0 0.0 collective-permute-done.2.refs_4_
  12.0 1.1 %wave.1 = (bf16[128,2176]{1,0:T(8,128)(2,1)S(1)}, bf16[128,2176]{1,0:T(8,128)(2,1)S(1)}, f32[64,2176]{1,0:T(8,128)S(1)}, bf16[128,2048]{1,0:T(8,128)(2,1)S(1)}, ...) custom-call(s32[4]{0:T(128)S(4)} %get-tuple-element.47.place.refs_0_, ...), custom_call_target="tpu_custom_call" | custom-call | bytes 6000000 | tf_op jit(solution)/shard_map/wave/pallas_call | solution.py:731
  13.2 1.8 %collective-permute-start.5 = (f32[48,128]{1,0:T(8,128)S(1)}, f32[48,128]{1,0:T(8,128)S(1)}, u32[]{:S(2)}, u32[]{:S(2)}) collective-permute-start(f32[48,128]{1,0:T(8,128)S(1)} %get-tuple-element.63), channel_id=1, source_target_pairs={{0,4},{1,13},{2,6},{3,15},{4,0},{5,9},{6,2},{7,11},{8,12},{9,5},{1... | collective-permute-start | bytes 73736 | tf_op jit(solution)/shard_map/ppermute | solution.py:757
  14.9 2.6 %collective-permute-start.4 = (f32[48,128]{1,0:T(8,128)S(1)}, f32[48,128]{1,0:T(8,128)S(1)}, u32[]{:S(2)}, u32[]{:S(2)}) collective-permute-start(f32[48,128]{1,0:T(8,128)S(1)} %get-tuple-element.62), channel_id=1, source_target_pairs={{0,8},{1,9},{2,10},{3,11},{4,12},{5,13},{6,14},{7,15},{8,0},{9,1},... | collective-permute-start | bytes 73736 | tf_op jit(solution)/shard_map/ppermute | solution.py:757
  17.5 0.0 collective-permute-done.5.refs_2_
  17.5 0.9 %collective-permute-start.6 = (f32[48,128]{1,0:T(8,128)S(1)}, f32[48,128]{1,0:T(8,128)S(1)}, u32[]{:S(2)}, u32[]{:S(2)}) collective-permute-start(f32[48,128]{1,0:T(8,128)S(1)} %collective-permute-done.5.refs_2_), channel_id=1, source_target_pairs={{0,1},{1,0},{2,3},{3,2},{4,5},{5,4},{6,7},{7,6},{8,9},{9,8},{10,11... | collective-permute-start | bytes 73736 | tf_op jit(solution)/shard_map/ppermute | solution.py:747
  18.4 1.7 %local.1 = (f32[64,1024]{1,0:T(8,128)S(1)}, f32[64,1024]{1,0:T(8,128)S(1)}, f32[64,1024]{1,0:T(8,128)S(1)}, f32[64,1024]{1,0:T(8,128)S(1)}, f32[64,1024]{1,0:T(8,128)S(1)}) custom-call(bf16[128,2176]{1,0:T(8,128)(2,1)S(1)} %get-tuple-element.65.field_high, bf16[128,2176]{1,0:T(8,128)(2,1)S(1)} %get-tuple-element.66.field_low, ...), custom_call_target="tpu_custom_call" | custom-call | bytes 9000000 | tf_op jit(solution)/shard_map/local/pallas_call | solution.py:731
  20.1 0.0 collective-permute-done.4.refs_1_
  20.1 0.0 collective-permute-done.6.refs_3_
  20.2 0.3 first.1
  20.5 0.7 %collective-permute-start.7 = (f32[64,1024]{1,0:T(8,128)S(1)}, f32[64,1024]{1,0:T(8,128)S(1)}, u32[]{:S(2)}, u32[]{:S(2)}) collective-permute-start(f32[64,1024]{1,0:T(8,128)S(1)} %get-tuple-element.73.refs_5_.image), channel_id=1, source_target_pairs={{0,1},{1,0},{2,3},{3,2},{4,5},{5,4},{6,7},{7,6},{8,9},{9,8},{10,11... | collective-permute-start | bytes 786440 | tf_op jit(solution)/shard_map/ppermute | solution.py:747
  21.2 1.5 %collective-permute-start.10 = (f32[8,1024]{1,0:T(8,128)S(1)}, f32[8,1024]{1,0:T(8,128)S(1)}, u32[]{:S(2)}, u32[]{:S(2)}) collective-permute-start(f32[8,1024]{1,0:T(8,128)S(1)} %get-tuple-element.85.own_sums), channel_id=1, source_target_pairs={{0,2},{1,3},{2,0},{3,1},{4,6},{5,7},{6,4},{7,5},{8,10},{9,11},{10,... | collective-permute-start | bytes 98312 | tf_op jit(solution)/shard_map/ppermute | solution.py:747
  22.7 0.6 %spread.1 = (f32[64,128]{1,0:T(8,128)S(1)}, f32[64,1024]{1,0:T(8,128)S(1)}, f32[64,1024]{1,0:T(8,128)S(1)}) custom-call(s32[4]{0:T(128)S(4)} %get-tuple-element.47.place.refs_0_, f32[48,128]{1,0:T(8,128)S(1)} %collective-permute-done.4.refs_1_, f32[48,128]{1,0:T(8,128)S(1)} %collective-permute-done.5.refs_2_, f32[48,128]{1,0:T(8,128)S(1)} %collective-permute-done.6.refs_3_, ...), custom_call_target="tpu_custom_call" | custom-call | bytes 3000000 | tf_op jit(solution)/shard_map/spread/pallas_call | solution.py:731
  23.2 0.1 collective-permute-start.8
  23.3 0.0 collective-permute-done.7.near_image
  23.3 1.9 %second.1 = (f32[64,1024]{1,0:T(8,128)S(1)}, f32[64,1024]{1,0:T(8,128)S(1)}, f32[64,1024]{1,0:T(8,128)S(1)}) custom-call(s32[4]{0:T(128)S(4)} %get-tuple-element.47.place.refs_0_, f32[64,128]{1,0:T(8,128)S(1)} %get-tuple-element.75.halo, f32[64,1024]{1,0:T(8,128)S(1)} %collective-permute-done.7.near_image, f32[64,1024]{1,0:T(8,128)S(1)} %get-tuple-element.73.refs_5_.image, ...), custom_call_target="tpu_custom_call" | custom-call | bytes 9000000 | tf_op jit(solution)/shard_map/second/pallas_call | solution.py:731
  25.2 0.0 collective-permute-done.10.far_sums.refs_0_
  25.2 0.5 %collective-permute-start.17 = (f32[64,1024]{1,0:T(8,128)S(1)}, f32[64,1024]{1,0:T(8,128)S(1)}, u32[]{:S(2)}, u32[]{:S(2)}) collective-permute-start(f32[64,1024]{1,0:T(8,128)S(1)} %relay.3), channel_id=1, source_target_pairs={{0,1},{1,0},{2,3},{3,2},{4,5},{5,4},{6,7},{7,6},{8,9},{9,8},{10,11... | collective-permute-start | bytes 786440 | tf_op jit(solution)/shard_map/ppermute | solution.py:747
  25.8 0.0 collective-permute-done.8.arrived
  25.9 1.0 %collective-permute-start.9 = (f32[32,2048]{1,0:T(8,128)S(1)}, f32[32,2048]{1,0:T(8,128)S(1)}, u32[]{:S(2)}, u32[]{:S(2)}) collective-permute-start(f32[32,2048]{1,0:T(8,128)S(1)} %get-tuple-element.80), channel_id=1, source_target_pairs={{0,2},{1,3},{2,0},{3,1},{4,6},{5,7},{6,4},{7,5},{8,10},{9,11},{10,... | collective-permute-start | bytes 786440 | tf_op jit(solution)/shard_map/ppermute | solution.py:747
  26.8 0.8 %products.1.refs_0_.after = f32[16,128]{1,0:T(8,128)S(1)} custom-call(s32[4]{0:T(128)S(4)} %get-tuple-element.47.place.refs_0_, f32[32,2048]{1,0:T(8,128)S(1)} %get-tuple-element.48.refs_1_.vector, f32[64,1024]{1,0:T(8,128)S(1)} %get-tuple-element.82.load, f32[64,1024]{1,0:T(8,128)S(1)} %get-tuple-element.76.after.second_load, ...), custom_call_target="tpu_custom_call" | custom-call | bytes 3000000 | tf_op jit(solution)/shard_map/products/pallas_call | solution.py:731
  27.6 0.0 collective-permute-done.17.arrived
  27.7 1.2 %collective-permute-start.18 = (f32[32,2048]{1,0:T(8,128)S(1)}, f32[32,2048]{1,0:T(8,128)S(1)}, u32[]{:S(2)}, u32[]{:S(2)}) collective-permute-start(f32[32,2048]{1,0:T(8,128)S(1)} %get-tuple-element.91), channel_id=1, source_target_pairs={{0,2},{1,3},{2,0},{3,1},{4,6},{5,7},{6,4},{7,5},{8,10},{9,11},{10,... | collective-permute-start | bytes 786440 | tf_op jit(solution)/shard_map/ppermute | solution.py:747
  28.9 3.1 %collective-permute-start.13 = (f32[16,128]{1,0:T(8,128)S(1)}, f32[16,128]{1,0:T(8,128)S(1)}, u32[]{:S(2)}, u32[]{:S(2)}) collective-permute-start(f32[16,128]{1,0:T(8,128)S(1)} %products.1.refs_0_.after), channel_id=1, source_target_pairs={{0,12},{4,8},{8,4},{12,0},{1,13},{5,9},{9,5},{13,1},{2,14},{6,10},... | collective-permute-start | bytes 24584 | tf_op jit(solution)/shard_map/ppermute | solution.py:778
  31.9 0.0 collective-permute-start.12
  31.9 1.3 %collective-permute-start.11 = (f32[16,128]{1,0:T(8,128)S(1)}, f32[16,128]{1,0:T(8,128)S(1)}, u32[]{:S(2)}, u32[]{:S(2)}) collective-permute-start(f32[16,128]{1,0:T(8,128)S(1)} %products.1.refs_0_.after), channel_id=1, source_target_pairs={{0,4},{4,0},{8,12},{12,8},{1,5},{5,1},{9,13},{13,9},{2,6},{6,2},{1... | collective-permute-start | bytes 24584 | tf_op jit(solution)/shard_map/ppermute | solution.py:778
  33.2 1.1 %collective-permute-done.13.refs_3_ = f32[16,128]{1,0:T(8,128)S(1)} collective-permute-done((f32[16,128]{1,0:T(8,128)S(1)}, f32[16,128]{1,0:T(8,128)S(1)}, u32[]{:S(2)}, u32[]{:S(2)}) %collective-permute-start.13) | collective-permute-done | bytes 8224 | tf_op jit(solution)/shard_map/ppermute | solution.py:778
  34.3 2.2 %collective-permute-done.12.refs_2_ = f32[16,128]{1,0:T(8,128)S(1)} collective-permute-done((f32[16,128]{1,0:T(8,128)S(1)}, f32[16,128]{1,0:T(8,128)S(1)}, u32[]{:S(2)}, u32[]{:S(2)}) %collective-permute-start.12) | collective-permute-done | bytes 8224 | tf_op jit(solution)/shard_map/ppermute | solution.py:778
  36.5 0.0 collective-permute-done.11.refs_1_
  36.5 0.1 collective-permute-start.16
  36.6 1.0 %collective-permute-start.15 = (f32[16,128]{1,0:T(8,128)S(1)}, f32[16,128]{1,0:T(8,128)S(1)}, u32[]{:S(2)}, u32[]{:S(2)}) collective-permute-start(f32[16,128]{1,0:T(8,128)S(1)} %sum.2.refs_0_), channel_id=1, source_target_pairs={{0,2},{1,3},{2,0},{3,1},{4,6},{5,7},{6,4},{7,5},{8,10},{9,11},{10,... | collective-permute-start | bytes 24584 | tf_op jit(solution)/shard_map/ppermute | solution.py:778
  37.6 0.9 %collective-permute-start.14 = (f32[16,128]{1,0:T(8,128)S(1)}, f32[16,128]{1,0:T(8,128)S(1)}, u32[]{:S(2)}, u32[]{:S(2)}) collective-permute-start(f32[16,128]{1,0:T(8,128)S(1)} %sum.2.refs_0_), channel_id=1, source_target_pairs={{0,1},{1,0},{2,3},{3,2},{4,5},{5,4},{6,7},{7,6},{8,9},{9,8},{10,11... | collective-permute-start | bytes 24584 | tf_op jit(solution)/shard_map/ppermute | solution.py:778
  38.4 0.5 %settle.1 = (f32[32,2048]{1,0:T(8,128)S(1)}, f32[32,2048]{1,0:T(8,128)S(1)}, f32[8,128]{1,0:T(8,128)S(1)}) custom-call(s32[4]{0:T(128)S(4)} %get-tuple-element.47.place.refs_0_, f32[32,2048]{1,0:T(8,128)S(1)} %get-tuple-element.48.refs_1_.vector, f32[1,2048]{1,0:T(1,128)S(1)} %get-tuple-element.49.capacity, f32[32,2048]{1,0:T(8,128)S(1)} %get-tuple-element.79.refs_0_, ...), custom_call_target="tpu_custom_call" | custom-call | bytes 3000000 | tf_op jit(solution)/shard_map/settle/pallas_call | solution.py:731
  38.9 0.9 %collective-permute-done.16.refs_3_ = f32[16,128]{1,0:T(8,128)S(1)} collective-permute-done((f32[16,128]{1,0:T(8,128)S(1)}, f32[16,128]{1,0:T(8,128)S(1)}, u32[]{:S(2)}, u32[]{:S(2)}) %collective-permute-start.16) | collective-permute-done | bytes 8224 | tf_op jit(solution)/shard_map/ppermute | solution.py:778
  39.8 0.6 %collective-permute-done.15.refs_2_ = f32[16,128]{1,0:T(8,128)S(1)} collective-permute-done((f32[16,128]{1,0:T(8,128)S(1)}, f32[16,128]{1,0:T(8,128)S(1)}, u32[]{:S(2)}, u32[]{:S(2)}) %collective-permute-start.15) | collective-permute-done | bytes 8224 | tf_op jit(solution)/shard_map/ppermute | solution.py:778
  40.4 0.0 collective-permute-done.14.refs_1_
  40.4 1.0 %last.1 = (f32[32,2048]{1,0:T(8,128)}, f32[32,2048]{1,0:T(8,128)}) custom-call(f32[16,128]{1,0:T(8,128)S(1)} %sum.3.gathered, f32[32,2048]{1,0:T(8,128)S(1)} %get-tuple-element.48.refs_1_.vector, f32[32,2048]{1,0:T(8,128)S(1)} %get-tuple-element.86.answer, f32[32,2048]{1,0:T(8,128)S(1)} %get-tuple-element.87.slope, ...), custom_call_target="tpu_custom_call" | custom-call | tf_op jit(solution)/shard_map/last/pallas_call | solution.py:1012
  (8 shorter events, 0.1 us)
Async XLA Ops:
  0.6 9.6 %collective-permute-start = (f32[32,2048]{1,0:T(8,128)}, f32[32,2048]{1,0:T(8,128)S(1)}, u32[]{:S(2)}, u32[]{:S(2)}) collective-permute-start(f32[32,2048]{1,0:T(8,128)} %vector_in.1), channel_id=1, source_target_pairs={{0,2},{1,3},{2,0},{3,1},{4,6},{5,7},{6,4},{7,5},{8,10},{9,11},{10,... | collective-permute-start | bytes 786440 | tf_op jit(solution)/shard_map/ppermute | solution.py:747
  3.6 8.4 %collective-permute-start.1 = (f32[32,2048]{1,0:T(8,128)}, f32[32,2048]{1,0:T(8,128)S(1)}, u32[]{:S(2)}, u32[]{:S(2)}) collective-permute-start(f32[32,2048]{1,0:T(8,128)} %vector_in.1), channel_id=1, source_target_pairs={{0,1},{1,0},{2,3},{3,2},{4,5},{5,4},{6,7},{7,6},{8,9},{9,8},{10,11... | collective-permute-start | bytes 786440 | tf_op jit(solution)/shard_map/ppermute | solution.py:747
  3.6 7.4 %collective-permute-start.3 = (f32[32,2048]{1,0:T(8,128)}, f32[32,2048]{1,0:T(8,128)S(1)}, u32[]{:S(2)}, u32[]{:S(2)}) collective-permute-start(f32[32,2048]{1,0:T(8,128)} %operating_in.1), channel_id=1, source_target_pairs={{0,1},{1,0},{2,3},{3,2},{4,5},{5,4},{6,7},{7,6},{8,9},{9,8},{10,11... | collective-permute-start | bytes 786440 | tf_op jit(solution)/shard_map/ppermute | solution.py:747
  10.3 1.7 %collective-permute-start.2 = (f32[32,2048]{1,0:T(8,128)S(1)}, f32[32,2048]{1,0:T(8,128)S(1)}, u32[]{:S(2)}, u32[]{:S(2)}) collective-permute-start(f32[32,2048]{1,0:T(8,128)S(1)} %relay.2.after.refs_2_), channel_id=1, source_target_pairs={{0,1},{1,0},{2,3},{3,2},{4,5},{5,4},{6,7},{7,6},{8,9},{9,8},{10,11... | collective-permute-start | bytes 786440 | tf_op jit(solution)/shard_map/ppermute | solution.py:747
  13.2 4.3 %collective-permute-start.5 = (f32[48,128]{1,0:T(8,128)S(1)}, f32[48,128]{1,0:T(8,128)S(1)}, u32[]{:S(2)}, u32[]{:S(2)}) collective-permute-start(f32[48,128]{1,0:T(8,128)S(1)} %get-tuple-element.63), channel_id=1, source_target_pairs={{0,4},{1,13},{2,6},{3,15},{4,0},{5,9},{6,2},{7,11},{8,12},{9,5},{1... | collective-permute-start | bytes 73736 | tf_op jit(solution)/shard_map/ppermute | solution.py:757
  14.9 5.2 %collective-permute-start.4 = (f32[48,128]{1,0:T(8,128)S(1)}, f32[48,128]{1,0:T(8,128)S(1)}, u32[]{:S(2)}, u32[]{:S(2)}) collective-permute-start(f32[48,128]{1,0:T(8,128)S(1)} %get-tuple-element.62), channel_id=1, source_target_pairs={{0,8},{1,9},{2,10},{3,11},{4,12},{5,13},{6,14},{7,15},{8,0},{9,1},... | collective-permute-start | bytes 73736 | tf_op jit(solution)/shard_map/ppermute | solution.py:757
  17.5 2.6 %collective-permute-start.6 = (f32[48,128]{1,0:T(8,128)S(1)}, f32[48,128]{1,0:T(8,128)S(1)}, u32[]{:S(2)}, u32[]{:S(2)}) collective-permute-start(f32[48,128]{1,0:T(8,128)S(1)} %collective-permute-done.5.refs_2_), channel_id=1, source_target_pairs={{0,1},{1,0},{2,3},{3,2},{4,5},{5,4},{6,7},{7,6},{8,9},{9,8},{10,11... | collective-permute-start | bytes 73736 | tf_op jit(solution)/shard_map/ppermute | solution.py:747
  20.5 2.8 %collective-permute-start.7 = (f32[64,1024]{1,0:T(8,128)S(1)}, f32[64,1024]{1,0:T(8,128)S(1)}, u32[]{:S(2)}, u32[]{:S(2)}) collective-permute-start(f32[64,1024]{1,0:T(8,128)S(1)} %get-tuple-element.73.refs_5_.image), channel_id=1, source_target_pairs={{0,1},{1,0},{2,3},{3,2},{4,5},{5,4},{6,7},{7,6},{8,9},{9,8},{10,11... | collective-permute-start | bytes 786440 | tf_op jit(solution)/shard_map/ppermute | solution.py:747
  21.2 4.0 %collective-permute-start.10 = (f32[8,1024]{1,0:T(8,128)S(1)}, f32[8,1024]{1,0:T(8,128)S(1)}, u32[]{:S(2)}, u32[]{:S(2)}) collective-permute-start(f32[8,1024]{1,0:T(8,128)S(1)} %get-tuple-element.85.own_sums), channel_id=1, source_target_pairs={{0,2},{1,3},{2,0},{3,1},{4,6},{5,7},{6,4},{7,5},{8,10},{9,11},{10,... | collective-permute-start | bytes 98312 | tf_op jit(solution)/shard_map/ppermute | solution.py:747
  23.2 2.6 %collective-permute-start.8 = (f32[64,1024]{1,0:T(8,128)S(1)}, f32[64,1024]{1,0:T(8,128)S(1)}, u32[]{:S(2)}, u32[]{:S(2)}) collective-permute-start(f32[64,1024]{1,0:T(8,128)S(1)} %get-tuple-element.78), channel_id=1, source_target_pairs={{0,1},{1,0},{2,3},{3,2},{4,5},{5,4},{6,7},{7,6},{8,9},{9,8},{10,11... | collective-permute-start | bytes 786440 | tf_op jit(solution)/shard_map/ppermute | solution.py:747
  25.2 2.4 %collective-permute-start.17 = (f32[64,1024]{1,0:T(8,128)S(1)}, f32[64,1024]{1,0:T(8,128)S(1)}, u32[]{:S(2)}, u32[]{:S(2)}) collective-permute-start(f32[64,1024]{1,0:T(8,128)S(1)} %relay.3), channel_id=1, source_target_pairs={{0,1},{1,0},{2,3},{3,2},{4,5},{5,4},{6,7},{7,6},{8,9},{9,8},{10,11... | collective-permute-start | bytes 786440 | tf_op jit(solution)/shard_map/ppermute | solution.py:747
  25.9 12.6 %collective-permute-start.9 = (f32[32,2048]{1,0:T(8,128)S(1)}, f32[32,2048]{1,0:T(8,128)S(1)}, u32[]{:S(2)}, u32[]{:S(2)}) collective-permute-start(f32[32,2048]{1,0:T(8,128)S(1)} %get-tuple-element.80), channel_id=1, source_target_pairs={{0,2},{1,3},{2,0},{3,1},{4,6},{5,7},{6,4},{7,5},{8,10},{9,11},{10,... | collective-permute-start | bytes 786440 | tf_op jit(solution)/shard_map/ppermute | solution.py:747
  27.7 12.7 %collective-permute-start.18 = (f32[32,2048]{1,0:T(8,128)S(1)}, f32[32,2048]{1,0:T(8,128)S(1)}, u32[]{:S(2)}, u32[]{:S(2)}) collective-permute-start(f32[32,2048]{1,0:T(8,128)S(1)} %get-tuple-element.91), channel_id=1, source_target_pairs={{0,2},{1,3},{2,0},{3,1},{4,6},{5,7},{6,4},{7,5},{8,10},{9,11},{10,... | collective-permute-start | bytes 786440 | tf_op jit(solution)/shard_map/ppermute | solution.py:747
  28.9 5.4 %collective-permute-start.13 = (f32[16,128]{1,0:T(8,128)S(1)}, f32[16,128]{1,0:T(8,128)S(1)}, u32[]{:S(2)}, u32[]{:S(2)}) collective-permute-start(f32[16,128]{1,0:T(8,128)S(1)} %products.1.refs_0_.after), channel_id=1, source_target_pairs={{0,12},{4,8},{8,4},{12,0},{1,13},{5,9},{9,5},{13,1},{2,14},{6,10},... | collective-permute-start | bytes 24584 | tf_op jit(solution)/shard_map/ppermute | solution.py:778
  31.9 4.5 %collective-permute-start.12 = (f32[16,128]{1,0:T(8,128)S(1)}, f32[16,128]{1,0:T(8,128)S(1)}, u32[]{:S(2)}, u32[]{:S(2)}) collective-permute-start(f32[16,128]{1,0:T(8,128)S(1)} %products.1.refs_0_.after), channel_id=1, source_target_pairs={{0,8},{4,12},{8,0},{12,4},{1,9},{5,13},{9,1},{13,5},{2,10},{6,14},... | collective-permute-start | bytes 24584 | tf_op jit(solution)/shard_map/ppermute | solution.py:778
  31.9 4.5 %collective-permute-start.11 = (f32[16,128]{1,0:T(8,128)S(1)}, f32[16,128]{1,0:T(8,128)S(1)}, u32[]{:S(2)}, u32[]{:S(2)}) collective-permute-start(f32[16,128]{1,0:T(8,128)S(1)} %products.1.refs_0_.after), channel_id=1, source_target_pairs={{0,4},{4,0},{8,12},{12,8},{1,5},{5,1},{9,13},{13,9},{2,6},{6,2},{1... | collective-permute-start | bytes 24584 | tf_op jit(solution)/shard_map/ppermute | solution.py:778
  36.5 3.3 %collective-permute-start.16 = (f32[16,128]{1,0:T(8,128)S(1)}, f32[16,128]{1,0:T(8,128)S(1)}, u32[]{:S(2)}, u32[]{:S(2)}) collective-permute-start(f32[16,128]{1,0:T(8,128)S(1)} %sum.2.refs_0_), channel_id=1, source_target_pairs={{0,3},{1,2},{2,1},{3,0},{4,7},{5,6},{6,5},{7,4},{8,11},{9,10},{10,... | collective-permute-start | bytes 24584 | tf_op jit(solution)/shard_map/ppermute | solution.py:778
  36.6 3.8 %collective-permute-start.15 = (f32[16,128]{1,0:T(8,128)S(1)}, f32[16,128]{1,0:T(8,128)S(1)}, u32[]{:S(2)}, u32[]{:S(2)}) collective-permute-start(f32[16,128]{1,0:T(8,128)S(1)} %sum.2.refs_0_), channel_id=1, source_target_pairs={{0,2},{1,3},{2,0},{3,1},{4,6},{5,7},{6,4},{7,5},{8,10},{9,11},{10,... | collective-permute-start | bytes 24584 | tf_op jit(solution)/shard_map/ppermute | solution.py:778
  37.6 2.8 %collective-permute-start.14 = (f32[16,128]{1,0:T(8,128)S(1)}, f32[16,128]{1,0:T(8,128)S(1)}, u32[]{:S(2)}, u32[]{:S(2)}) collective-permute-start(f32[16,128]{1,0:T(8,128)S(1)} %sum.2.refs_0_), channel_id=1, source_target_pairs={{0,1},{1,0},{2,3},{3,2},{4,5},{5,4},{6,7},{7,6},{8,9},{9,8},{10,11... | collective-permute-start | bytes 24584 | tf_op jit(solution)/shard_map/ppermute | solution.py:778

commit v7 on v6

--- a/solution.py
+++ b/solution.py
@@ -435,13 +435,23 @@
     dual_slope[...] = capacity[:, :half] * others[2 * times :]
     own_wave[...] = wave[:, mine]
     load[...] = own_wave[...] * (linear[:, :half] + conductances[:, mine])
-    high = current[:times]
-    step = 256
-    for block in range(half // step):
-        lanes = slice(block * step, (block + 1) * step)
+    for lanes in blocks_of(0, half // 2):
         load[:, lanes] += coupled(
-            high, current[...], coupling_high, coupling_low, sources, lanes
-        )
+            current[:times], current[...], coupling_high, coupling_low, sources, lanes
+        )
+
+
+def local_rest_kernel(load, current, coupling_high, coupling_low, rest):
+    times, half = load.shape
+    sources = slice(0, current.shape[1])
+    for lanes, at in zip(blocks_of(half // 2, half), blocks_of(0, half // 2)):
+        rest[:, at] = load[:, lanes] + coupled(
+            current[:times], current[...], coupling_high, coupling_low, sources, lanes
+        )
+
+
+def blocks_of(start, stop, step=256):
+    return [slice(at, at + step) for at in range(start, stop, step)]
 
 
 def signed_sums(values):
@@ -491,6 +501,7 @@
     (
         cut_current,
         local_load,
+        local_rest,
         slope,
         own_wave,
         coupling_high,
@@ -512,7 +523,8 @@
         slice(nodes, None),
         slice(0, half),
     )
-    load[...] = local_load[...] + share
+    load[:, : half // 2] = local_load[:, : half // 2] + share[:, : half // 2]
+    load[:, half // 2 :] = local_rest[...] + share[:, half // 2 :]
     answer = load[...] + slope[...]
     image[...] = answer
     lines = [*signed_sums(answer), *signed_sums(own_wave[...])]
@@ -565,9 +577,7 @@
     load[...] = image[...] * (linear[:, :half] + conductances[:, mine])
     high, low = split(halo[...])
     halo_stacked = jnp.concatenate([high, low], axis=0)
-    step = 256
-    for block in range(half // step):
-        lanes = slice(block * step, (block + 1) * step)
+    for lanes in blocks_of(0, half):
         load[:, lanes] += coupled(
             current[:times], current[...], coupling_high, coupling_low, slice(0, nodes), lanes
         ) + coupled(high, halo_stacked, coupling_high, coupling_low, slice(nodes, None), lanes)
@@ -924,8 +934,6 @@
         micros=2,
     )
     arrived = [trade(packet, masks) for packet, masks in zip(sent, packet_steps(steps))]
-    if steps == 3:
-        arrived.append(swap(arrived[-1], 1))
     others = []
     if not shared:
         gathered = lax.all_gather(cut_current, "nodes")
@@ -940,14 +948,26 @@
         [wide] * 5,
         micros=3,
     )
+    if steps == 3:
+        (traded,) = run(
+            relay_kernel, "relay", [VMEM] * 2, (dual, arrived[-1]), [(packet, F32)]
+        )
+        arrived[-1:] = [traded, swap(traded, 1)]
+    (local_rest,) = run(
+        local_rest_kernel,
+        "local_rest",
+        [VMEM] * 4,
+        (local_load, current, coupling_high, coupling_low),
+        [((times, half // 2), F32)],
+    )
     block = ((length // 2, half), F32)
     packets = (place, *arrived, *others, cut_current)
     packet_specs = [SMEM] + [VMEM] * (len(packets) - 1)
     image, load, own_sums = run(
         functools.partial(first_kernel, steps=steps, apart=len(others)),
         "first",
-        packet_specs + [VMEM] * 5,
-        (*packets, local_load, slope, own_wave, coupling_high, coupling_low),
+        packet_specs + [VMEM] * 6,
+        (*packets, local_load, local_rest, slope, own_wave, coupling_high, coupling_low),
         [wide, wide, ((8, half), F32)],
         micros=1,
     )
@@ -977,7 +997,7 @@
         scratch=[pltpu.VMEM((2 * times, nodes), BF16)],
         micros=3,
     )
-    answer_parts = hand_out(second_load, place, kept, arrived)
+    answer_parts = hand_out(load, place, kept, arrived)
     (second_sent,) = run(
         relay_kernel,
         "relay",

time: 41.6 us -> 41.3 us (level)
  starting transfers between devices: 20.1 us -> 19.5 us
    ppermute x11, starting transfers between devices: 9.45 us -> 8.81 us  [swap(): lax.ppermute(value, 'samples', [(at, at ^ mask) for at in range(count)])]
    ppermute x2, waiting for transfers between devices: 0.01 us -> 0.54 us  [trade(): return lax.ppermute(value, ('nodes', 'samples'), pairs)]
    pallas_call x17 -> x19, Pallas kernels: 14.8 us -> 14.8 us  [run(): pl.pallas_call(kernel, out_shape=[space(shape, dtype) for space, (shape,...]
  transfers between devices with their start and end apart: 19 -> 19, of which waited for: 4 -> 5; matrix products, arithmetic and copies ran while one was open for 0% -> 0% of each run, Pallas kernels for 32% -> 32%
where the time goes in v7:
time: 41.3 us; the launch traced here: 41.2 us
  starting transfers between devices  19.5 us (47%)
  Pallas kernels  15.9 us (38%)
  waiting for transfers between devices  5.02 us (12%)
  between operations  0.84 us (2%)
    pallas_call x19, Pallas kernels, run(): pl.pallas_call(kernel, out_shape=[space(shape, dtype) for space, (shape,...  14.8 us
    ppermute x11, starting transfers between devices, swap(): lax.ppermute(value, 'samples', [(at, at ^ mask) for at in range(count)])  8.81 us
    ppermute x6, starting transfers between devices, exchange(): lax.ppermute(value, axis, [(at, at ^ step * stride) for at in range(count)])  6.31 us
    ppermute x6, waiting for transfers between devices, exchange(): lax.ppermute(value, axis, [(at, at ^ step * stride) for at in range(count)])  4.45 us
    ppermute x2, starting transfers between devices, trade(): return lax.ppermute(value, ('nodes', 'samples'), pairs)  4.34 us
    pallas_call x1, Pallas kernels, shards(): pl.pallas_call(functools.partial(last_kernel, entries=entries, devices=fl...  1.02 us
  transfers between devices with their start and end apart: 19, of which 5 were waited for; matrix products, arithmetic and copies ran while one was open for 0% of the time, Pallas kernels for 32%

profile of v7, /device:TPU:0, one launch (start us, length us, event | category | flops | bytes accessed | tf_op | source)
XLA Modules:
  0.0 41.2 jit_solution(10978519605471374861)
XLA Ops:
  0.6 3.0 %collective-permute-start = (f32[32,2048]{1,0:T(8,128)}, f32[32,2048]{1,0:T(8,128)S(1)}, u32[]{:S(2)}, u32[]{:S(2)}) collective-permute-start(f32[32,2048]{1,0:T(8,128)} %vector_in.1), channel_id=1, source_target_pairs={{0,2},{1,3},{2,0},{3,1},{4,6},{5,7},{6,4},{7,5},{8,10},{9,11},{10,... | collective-permute-start | bytes 786440 | tf_op jit(solution)/shard_map/ppermute | solution.py:757
  3.6 0.0 collective-permute-start.1
  3.6 0.5 %collective-permute-start.3 = (f32[32,2048]{1,0:T(8,128)}, f32[32,2048]{1,0:T(8,128)S(1)}, u32[]{:S(2)}, u32[]{:S(2)}) collective-permute-start(f32[32,2048]{1,0:T(8,128)} %operating_in.1), channel_id=1, source_target_pairs={{0,1},{1,0},{2,3},{3,2},{4,5},{5,4},{6,7},{7,6},{8,9},{9,8},{10,11... | collective-permute-start | bytes 786440 | tf_op jit(solution)/shard_map/ppermute | solution.py:757
  4.1 1.7 %fetch.1 = (f32[32,2048]{1,0:T(8,128)S(1)}, bf16[2048,128]{1,0:T(8,128)(2,1)S(1)}, f32[1,1152]{1,0:T(1,128)S(1)}, f32[1,1152]{1,0:T(1,128)S(1)}, f32[1,2048]{1,0...) custom-call(f32[32,2048]{1,0:T(8,128)} %vector_in.1, ...), custom_call_target="tpu_custom_call" | custom-call | bytes 6000000 | tf_op jit(solution)/shard_map/fetch/pallas_call | solution.py:741
  5.9 4.4 %prepare.1 = (bf16[2176,1024]{1,0:T(8,128)(2,1)S(1)}, bf16[2176,1024]{1,0:T(8,128)(2,1)S(1)}) custom-call(s32[8,1152]{1,0:T(8,128)S(1)} %get-tuple-element.50.entry_rows, f32[8,1152]{1,0:T(8,128)S(1)} %get-tuple-element.51.weight_rows), custom_call_target="tpu_custom_call" | custom-call | bytes 18000000 | tf_op jit(solution)/shard_map/prepare/pallas_call | solution.py:741
  10.3 0.0 collective-permute-done.refs_1_
  10.3 0.1 collective-permute-start.2
  10.4 0.6 %prepare_cut.1 = (bf16[2176,128]{1,0:T(8,128)(2,1)S(1)}, bf16[2176,128]{1,0:T(8,128)(2,1)S(1)}, f32[128,128]{1,0:T(8,128)S(1)}) custom-call(f32[32,2048]{1,0:T(8,128)S(1)} %relay.3.after.refs_2_, s32[8,1152]{1,0:T(8,128)S(1)} %get-tuple-element.50.entry_rows, f32[8,1152]{1,0:T(8,128)S(1)} %get-tuple-element.51.weight_rows), custom_call_target="tpu_custom_call" | custom-call | bytes 3000000 | tf_op jit(solution)/shard_map/prepare_cut/pallas_call | solution.py:741
  11.0 0.0 collective-permute-done.3.near_operating
  11.0 1.0 %conductance.1.refs_6_.conductances = f32[64,2176]{1,0:T(8,128)S(1)} custom-call(s32[4]{0:T(128)S(4)} %get-tuple-element.47.place.refs_0_, f32[32,2048]{1,0:T(8,128)S(1)} %collective-permute-done.3.near_operating, f32[32,2048]{1,0:T(8,128)S(1)} %get-tuple-element.54.operating, f32[1,16]{1,0:T(1,128)S(1)} %get-tuple-element.55.table, ...), custom_call_target="tpu_custom_call" | custom-call | bytes 3000000 | tf_op jit(solution)/shard_map/conductance/pallas_call | solution.py:741
  12.0 0.0 collective-permute-done.1.refs_3_
  12.0 1.1 %wave.1 = (bf16[128,2176]{1,0:T(8,128)(2,1)S(1)}, bf16[128,2176]{1,0:T(8,128)(2,1)S(1)}, f32[64,2176]{1,0:T(8,128)S(1)}, bf16[128,2048]{1,0:T(8,128)(2,1)S(1)}, ...) custom-call(s32[4]{0:T(128)S(4)} %get-tuple-element.47.place.refs_0_, ...), custom_call_target="tpu_custom_call" | custom-call | bytes 6000000 | tf_op jit(solution)/shard_map/wave/pallas_call | solution.py:741
  13.2 1.8 %collective-permute-start.5 = (f32[48,128]{1,0:T(8,128)S(1)}, f32[48,128]{1,0:T(8,128)S(1)}, u32[]{:S(2)}, u32[]{:S(2)}) collective-permute-start(f32[48,128]{1,0:T(8,128)S(1)} %get-tuple-element.69), channel_id=1, source_target_pairs={{0,4},{1,13},{2,6},{3,15},{4,0},{5,9},{6,2},{7,11},{8,12},{9,5},{1... | collective-permute-start | bytes 73736 | tf_op jit(solution)/shard_map/ppermute | solution.py:767
  14.9 2.6 %collective-permute-start.4 = (f32[48,128]{1,0:T(8,128)S(1)}, f32[48,128]{1,0:T(8,128)S(1)}, u32[]{:S(2)}, u32[]{:S(2)}) collective-permute-start(f32[48,128]{1,0:T(8,128)S(1)} %get-tuple-element.62), channel_id=1, source_target_pairs={{0,8},{1,9},{2,10},{3,11},{4,12},{5,13},{6,14},{7,15},{8,0},{9,1},... | collective-permute-start | bytes 73736 | tf_op jit(solution)/shard_map/ppermute | solution.py:767
  17.5 1.0 %local.1 = (f32[64,1024]{1,0:T(8,128)S(1)}, f32[64,1024]{1,0:T(8,128)S(1)}, f32[64,1024]{1,0:T(8,128)S(1)}, f32[64,1024]{1,0:T(8,128)S(1)}, f32[64,1024]{1,0:T(8,128)S(1)}) custom-call(bf16[128,2176]{1,0:T(8,128)(2,1)S(1)} %get-tuple-element.63.field_high, bf16[128,2176]{1,0:T(8,128)(2,1)S(1)} %get-tuple-element.64.field_low, ...), custom_call_target="tpu_custom_call" | custom-call | bytes 9000000 | tf_op jit(solution)/shard_map/local/pallas_call | solution.py:741
  18.5 0.0 collective-permute-done.5.refs_1_
  18.6 0.1 collective-permute-start.6
  18.6 0.8 %local_rest.1.refs_6_ = f32[64,512]{1,0:T(8,128)S(1)} custom-call(f32[64,1024]{1,0:T(8,128)S(1)} %get-tuple-element.71.load.refs_5_, bf16[128,2048]{1,0:T(8,128)(2,1)S(1)} %get-tuple-element.66.current, bf16[2176,1024]{1,0:T(8,128)(2,1)S(1)} %get-tuple-element.67.coupling_high.refs_9_, bf16[2176,1024]{1,0:T(8,128)(2,1)S(1)} %get-tuple-element.52.refs_0_.coupling_low.refs_10_), custom_call_target="tpu_custom_call" | custom-call | bytes 3000000 | tf_op jit(solution)/shard_map/local_rest/pallas_call | solution.py:741
  19.4 0.5 %collective-permute-done.4.refs_1_ = f32[48,128]{1,0:T(8,128)S(1)} collective-permute-done((f32[48,128]{1,0:T(8,128)S(1)}, f32[48,128]{1,0:T(8,128)S(1)}, u32[]{:S(2)}, u32[]{:S(2)}) %collective-permute-start.4) | collective-permute-done | bytes 24608 | tf_op jit(solution)/shard_map/ppermute | solution.py:767
  20.0 0.0 collective-permute-done.6.refs_3_
  20.0 0.3 first.1
  20.3 0.9 %collective-permute-start.9 = (f32[64,1024]{1,0:T(8,128)S(1)}, f32[64,1024]{1,0:T(8,128)S(1)}, u32[]{:S(2)}, u32[]{:S(2)}) collective-permute-start(f32[64,1024]{1,0:T(8,128)S(1)} %get-tuple-element.75.refs_5_.image), channel_id=1, source_target_pairs={{0,1},{1,0},{2,3},{3,2},{4,5},{5,4},{6,7},{7,6},{8,9},{9,8},{10,11... | collective-permute-start | bytes 786440 | tf_op jit(solution)/shard_map/ppermute | solution.py:757
  21.2 1.5 %collective-permute-start.10 = (f32[8,1024]{1,0:T(8,128)S(1)}, f32[8,1024]{1,0:T(8,128)S(1)}, u32[]{:S(2)}, u32[]{:S(2)}) collective-permute-start(f32[8,1024]{1,0:T(8,128)S(1)} %get-tuple-element.85.own_sums), channel_id=1, source_target_pairs={{0,2},{1,3},{2,0},{3,1},{4,6},{5,7},{6,4},{7,5},{8,10},{9,11},{10,... | collective-permute-start | bytes 98312 | tf_op jit(solution)/shard_map/ppermute | solution.py:757
  22.7 0.5 %spread.1 = (f32[64,128]{1,0:T(8,128)S(1)}, f32[64,1024]{1,0:T(8,128)S(1)}, f32[64,1024]{1,0:T(8,128)S(1)}) custom-call(s32[4]{0:T(128)S(4)} %get-tuple-element.47.place.refs_0_, f32[48,128]{1,0:T(8,128)S(1)} %collective-permute-done.4.refs_1_, f32[48,128]{1,0:T(8,128)S(1)} %relay.4.refs_2_, f32[48,128]{1,0:T(8,128)S(1)} %collective-permute-done.6.refs_3_, ...), custom_call_target="tpu_custom_call" | custom-call | bytes 3000000 | tf_op jit(solution)/shard_map/spread/pallas_call | solution.py:741
  23.2 0.1 collective-permute-start.7
  23.3 0.0 collective-permute-done.9.near_image
  23.3 1.9 %second.1 = (f32[64,1024]{1,0:T(8,128)S(1)}, f32[64,1024]{1,0:T(8,128)S(1)}, f32[64,1024]{1,0:T(8,128)S(1)}) custom-call(s32[4]{0:T(128)S(4)} %get-tuple-element.47.place.refs_0_, f32[64,128]{1,0:T(8,128)S(1)} %get-tuple-element.82.halo, f32[64,1024]{1,0:T(8,128)S(1)} %collective-permute-done.9.near_image, f32[64,1024]{1,0:T(8,128)S(1)} %get-tuple-element.75.refs_5_.image, ...), custom_call_target="tpu_custom_call" | custom-call | bytes 9000000 | tf_op jit(solution)/shard_map/second/pallas_call | solution.py:741
  25.2 0.0 collective-permute-done.10.far_sums.refs_0_
  25.2 0.6 %collective-permute-start.17 = (f32[64,1024]{1,0:T(8,128)S(1)}, f32[64,1024]{1,0:T(8,128)S(1)}, u32[]{:S(2)}, u32[]{:S(2)}) collective-permute-start(f32[64,1024]{1,0:T(8,128)S(1)} %relay.5), channel_id=1, source_target_pairs={{0,1},{1,0},{2,3},{3,2},{4,5},{5,4},{6,7},{7,6},{8,9},{9,8},{10,11... | collective-permute-start | bytes 786440 | tf_op jit(solution)/shard_map/ppermute | solution.py:757
  25.8 0.0 collective-permute-done.7.arrived
  25.9 1.0 %collective-permute-start.8 = (f32[32,2048]{1,0:T(8,128)S(1)}, f32[32,2048]{1,0:T(8,128)S(1)}, u32[]{:S(2)}, u32[]{:S(2)}) collective-permute-start(f32[32,2048]{1,0:T(8,128)S(1)} %get-tuple-element.80), channel_id=1, source_target_pairs={{0,2},{1,3},{2,0},{3,1},{4,6},{5,7},{6,4},{7,5},{8,10},{9,11},{10,... | collective-permute-start | bytes 786440 | tf_op jit(solution)/shard_map/ppermute | solution.py:757
  26.8 0.8 %products.1.refs_0_.after = f32[16,128]{1,0:T(8,128)S(1)} custom-call(s32[4]{0:T(128)S(4)} %get-tuple-element.47.place.refs_0_, f32[32,2048]{1,0:T(8,128)S(1)} %get-tuple-element.48.refs_1_.vector, f32[64,1024]{1,0:T(8,128)S(1)} %get-tuple-element.74.after.load, f32[64,1024]{1,0:T(8,128)S(1)} %get-tuple-element.83.second_load, ...), custom_call_target="tpu_custom_call" | custom-call | bytes 3000000 | tf_op jit(solution)/shard_map/products/pallas_call | solution.py:741
  27.6 0.0 collective-permute-done.17.arrived
  27.7 1.2 %collective-permute-start.18 = (f32[32,2048]{1,0:T(8,128)S(1)}, f32[32,2048]{1,0:T(8,128)S(1)}, u32[]{:S(2)}, u32[]{:S(2)}) collective-permute-start(f32[32,2048]{1,0:T(8,128)S(1)} %get-tuple-element.91), channel_id=1, source_target_pairs={{0,2},{1,3},{2,0},{3,1},{4,6},{5,7},{6,4},{7,5},{8,10},{9,11},{10,... | collective-permute-start | bytes 786440 | tf_op jit(solution)/shard_map/ppermute | solution.py:757
  28.8 2.5 %collective-permute-start.13 = (f32[16,128]{1,0:T(8,128)S(1)}, f32[16,128]{1,0:T(8,128)S(1)}, u32[]{:S(2)}, u32[]{:S(2)}) collective-permute-start(f32[16,128]{1,0:T(8,128)S(1)} %products.1.refs_0_.after), channel_id=1, source_target_pairs={{0,12},{4,8},{8,4},{12,0},{1,13},{5,9},{9,5},{13,1},{2,14},{6,10},... | collective-permute-start | bytes 24584 | tf_op jit(solution)/shard_map/ppermute | solution.py:788
  31.3 0.0 collective-permute-start.12
  31.3 1.9 %collective-permute-start.11 = (f32[16,128]{1,0:T(8,128)S(1)}, f32[16,128]{1,0:T(8,128)S(1)}, u32[]{:S(2)}, u32[]{:S(2)}) collective-permute-start(f32[16,128]{1,0:T(8,128)S(1)} %products.1.refs_0_.after), channel_id=1, source_target_pairs={{0,4},{4,0},{8,12},{12,8},{1,5},{5,1},{9,13},{13,9},{2,6},{6,2},{1... | collective-permute-start | bytes 24584 | tf_op jit(solution)/shard_map/ppermute | solution.py:788
  33.2 1.1 %collective-permute-done.13.refs_3_ = f32[16,128]{1,0:T(8,128)S(1)} collective-permute-done((f32[16,128]{1,0:T(8,128)S(1)}, f32[16,128]{1,0:T(8,128)S(1)}, u32[]{:S(2)}, u32[]{:S(2)}) %collective-permute-start.13) | collective-permute-done | bytes 8224 | tf_op jit(solution)/shard_map/ppermute | solution.py:788
  34.3 1.6 %collective-permute-done.12.refs_2_ = f32[16,128]{1,0:T(8,128)S(1)} collective-permute-done((f32[16,128]{1,0:T(8,128)S(1)}, f32[16,128]{1,0:T(8,128)S(1)}, u32[]{:S(2)}, u32[]{:S(2)}) %collective-permute-start.12) | collective-permute-done | bytes 8224 | tf_op jit(solution)/shard_map/ppermute | solution.py:788
  35.9 0.0 collective-permute-done.11.refs_1_
  35.9 0.1 collective-permute-start.16
  35.9 1.0 %collective-permute-start.15 = (f32[16,128]{1,0:T(8,128)S(1)}, f32[16,128]{1,0:T(8,128)S(1)}, u32[]{:S(2)}, u32[]{:S(2)}) collective-permute-start(f32[16,128]{1,0:T(8,128)S(1)} %sum.2.refs_0_), channel_id=1, source_target_pairs={{0,2},{1,3},{2,0},{3,1},{4,6},{5,7},{6,4},{7,5},{8,10},{9,11},{10,... | collective-permute-start | bytes 24584 | tf_op jit(solution)/shard_map/ppermute | solution.py:788
  36.9 0.9 %collective-permute-start.14 = (f32[16,128]{1,0:T(8,128)S(1)}, f32[16,128]{1,0:T(8,128)S(1)}, u32[]{:S(2)}, u32[]{:S(2)}) collective-permute-start(f32[16,128]{1,0:T(8,128)S(1)} %sum.2.refs_0_), channel_id=1, source_target_pairs={{0,1},{1,0},{2,3},{3,2},{4,5},{5,4},{6,7},{7,6},{8,9},{9,8},{10,11... | collective-permute-start | bytes 24584 | tf_op jit(solution)/shard_map/ppermute | solution.py:788
  37.8 0.5 %settle.1 = (f32[32,2048]{1,0:T(8,128)S(1)}, f32[32,2048]{1,0:T(8,128)S(1)}, f32[8,128]{1,0:T(8,128)S(1)}) custom-call(s32[4]{0:T(128)S(4)} %get-tuple-element.47.place.refs_0_, f32[32,2048]{1,0:T(8,128)S(1)} %get-tuple-element.48.refs_1_.vector, f32[1,2048]{1,0:T(1,128)S(1)} %get-tuple-element.49.capacity, f32[32,2048]{1,0:T(8,128)S(1)} %get-tuple-element.79.refs_0_, ...), custom_call_target="tpu_custom_call" | custom-call | bytes 3000000 | tf_op jit(solution)/shard_map/settle/pallas_call | solution.py:741
  38.3 0.9 %collective-permute-done.16.refs_3_ = f32[16,128]{1,0:T(8,128)S(1)} collective-permute-done((f32[16,128]{1,0:T(8,128)S(1)}, f32[16,128]{1,0:T(8,128)S(1)}, u32[]{:S(2)}, u32[]{:S(2)}) %collective-permute-start.16) | collective-permute-done | bytes 8224 | tf_op jit(solution)/shard_map/ppermute | solution.py:788
  39.2 1.0 %collective-permute-done.15.refs_2_ = f32[16,128]{1,0:T(8,128)S(1)} collective-permute-done((f32[16,128]{1,0:T(8,128)S(1)}, f32[16,128]{1,0:T(8,128)S(1)}, u32[]{:S(2)}, u32[]{:S(2)}) %collective-permute-start.15) | collective-permute-done | bytes 8224 | tf_op jit(solution)/shard_map/ppermute | solution.py:788
  40.1 0.0 collective-permute-done.14.refs_1_
  40.1 1.0 %last.1 = (f32[32,2048]{1,0:T(8,128)}, f32[32,2048]{1,0:T(8,128)}) custom-call(f32[16,128]{1,0:T(8,128)S(1)} %sum.3.gathered, f32[32,2048]{1,0:T(8,128)S(1)} %get-tuple-element.48.refs_1_.vector, f32[32,2048]{1,0:T(8,128)S(1)} %get-tuple-element.86.answer, f32[32,2048]{1,0:T(8,128)S(1)} %get-tuple-element.87.slope, ...), custom_call_target="tpu_custom_call" | custom-call | tf_op jit(solution)/shard_map/last/pallas_call | solution.py:1032
  (10 shorter events, 0.2 us)
Async XLA Ops:
  0.6 9.6 %collective-permute-start = (f32[32,2048]{1,0:T(8,128)}, f32[32,2048]{1,0:T(8,128)S(1)}, u32[]{:S(2)}, u32[]{:S(2)}) collective-permute-start(f32[32,2048]{1,0:T(8,128)} %vector_in.1), channel_id=1, source_target_pairs={{0,2},{1,3},{2,0},{3,1},{4,6},{5,7},{6,4},{7,5},{8,10},{9,11},{10,... | collective-permute-start | bytes 786440 | tf_op jit(solution)/shard_map/ppermute | solution.py:757
  3.6 8.4 %collective-permute-start.1 = (f32[32,2048]{1,0:T(8,128)}, f32[32,2048]{1,0:T(8,128)S(1)}, u32[]{:S(2)}, u32[]{:S(2)}) collective-permute-start(f32[32,2048]{1,0:T(8,128)} %vector_in.1), channel_id=1, source_target_pairs={{0,1},{1,0},{2,3},{3,2},{4,5},{5,4},{6,7},{7,6},{8,9},{9,8},{10,11... | collective-permute-start | bytes 786440 | tf_op jit(solution)/shard_map/ppermute | solution.py:757
  3.6 7.4 %collective-permute-start.3 = (f32[32,2048]{1,0:T(8,128)}, f32[32,2048]{1,0:T(8,128)S(1)}, u32[]{:S(2)}, u32[]{:S(2)}) collective-permute-start(f32[32,2048]{1,0:T(8,128)} %operating_in.1), channel_id=1, source_target_pairs={{0,1},{1,0},{2,3},{3,2},{4,5},{5,4},{6,7},{7,6},{8,9},{9,8},{10,11... | collective-permute-start | bytes 786440 | tf_op jit(solution)/shard_map/ppermute | solution.py:757
  10.3 1.7 %collective-permute-start.2 = (f32[32,2048]{1,0:T(8,128)S(1)}, f32[32,2048]{1,0:T(8,128)S(1)}, u32[]{:S(2)}, u32[]{:S(2)}) collective-permute-start(f32[32,2048]{1,0:T(8,128)S(1)} %relay.3.after.refs_2_), channel_id=1, source_target_pairs={{0,1},{1,0},{2,3},{3,2},{4,5},{5,4},{6,7},{7,6},{8,9},{9,8},{10,11... | collective-permute-start | bytes 786440 | tf_op jit(solution)/shard_map/ppermute | solution.py:757
  13.2 5.4 %collective-permute-start.5 = (f32[48,128]{1,0:T(8,128)S(1)}, f32[48,128]{1,0:T(8,128)S(1)}, u32[]{:S(2)}, u32[]{:S(2)}) collective-permute-start(f32[48,128]{1,0:T(8,128)S(1)} %get-tuple-element.69), channel_id=1, source_target_pairs={{0,4},{1,13},{2,6},{3,15},{4,0},{5,9},{6,2},{7,11},{8,12},{9,5},{1... | collective-permute-start | bytes 73736 | tf_op jit(solution)/shard_map/ppermute | solution.py:767
  14.9 5.1 %collective-permute-start.4 = (f32[48,128]{1,0:T(8,128)S(1)}, f32[48,128]{1,0:T(8,128)S(1)}, u32[]{:S(2)}, u32[]{:S(2)}) collective-permute-start(f32[48,128]{1,0:T(8,128)S(1)} %get-tuple-element.62), channel_id=1, source_target_pairs={{0,8},{1,9},{2,10},{3,11},{4,12},{5,13},{6,14},{7,15},{8,0},{9,1},... | collective-permute-start | bytes 73736 | tf_op jit(solution)/shard_map/ppermute | solution.py:767
  18.6 1.4 %collective-permute-start.6 = (f32[48,128]{1,0:T(8,128)S(1)}, f32[48,128]{1,0:T(8,128)S(1)}, u32[]{:S(2)}, u32[]{:S(2)}) collective-permute-start(f32[48,128]{1,0:T(8,128)S(1)} %relay.4.refs_2_), channel_id=1, source_target_pairs={{0,1},{1,0},{2,3},{3,2},{4,5},{5,4},{6,7},{7,6},{8,9},{9,8},{10,11... | collective-permute-start | bytes 73736 | tf_op jit(solution)/shard_map/ppermute | solution.py:757
  20.3 3.0 %collective-permute-start.9 = (f32[64,1024]{1,0:T(8,128)S(1)}, f32[64,1024]{1,0:T(8,128)S(1)}, u32[]{:S(2)}, u32[]{:S(2)}) collective-permute-start(f32[64,1024]{1,0:T(8,128)S(1)} %get-tuple-element.75.refs_5_.image), channel_id=1, source_target_pairs={{0,1},{1,0},{2,3},{3,2},{4,5},{5,4},{6,7},{7,6},{8,9},{9,8},{10,11... | collective-permute-start | bytes 786440 | tf_op jit(solution)/shard_map/ppermute | solution.py:757
  21.2 4.0 %collective-permute-start.10 = (f32[8,1024]{1,0:T(8,128)S(1)}, f32[8,1024]{1,0:T(8,128)S(1)}, u32[]{:S(2)}, u32[]{:S(2)}) collective-permute-start(f32[8,1024]{1,0:T(8,128)S(1)} %get-tuple-element.85.own_sums), channel_id=1, source_target_pairs={{0,2},{1,3},{2,0},{3,1},{4,6},{5,7},{6,4},{7,5},{8,10},{9,11},{10,... | collective-permute-start | bytes 98312 | tf_op jit(solution)/shard_map/ppermute | solution.py:757
  23.2 2.6 %collective-permute-start.7 = (f32[64,1024]{1,0:T(8,128)S(1)}, f32[64,1024]{1,0:T(8,128)S(1)}, u32[]{:S(2)}, u32[]{:S(2)}) collective-permute-start(f32[64,1024]{1,0:T(8,128)S(1)} %get-tuple-element.78), channel_id=1, source_target_pairs={{0,1},{1,0},{2,3},{3,2},{4,5},{5,4},{6,7},{7,6},{8,9},{9,8},{10,11... | collective-permute-start | bytes 786440 | tf_op jit(solution)/shard_map/ppermute | solution.py:757
  25.2 2.4 %collective-permute-start.17 = (f32[64,1024]{1,0:T(8,128)S(1)}, f32[64,1024]{1,0:T(8,128)S(1)}, u32[]{:S(2)}, u32[]{:S(2)}) collective-permute-start(f32[64,1024]{1,0:T(8,128)S(1)} %relay.5), channel_id=1, source_target_pairs={{0,1},{1,0},{2,3},{3,2},{4,5},{5,4},{6,7},{7,6},{8,9},{9,8},{10,11... | collective-permute-start | bytes 786440 | tf_op jit(solution)/shard_map/ppermute | solution.py:757
  25.9 11.9 %collective-permute-start.8 = (f32[32,2048]{1,0:T(8,128)S(1)}, f32[32,2048]{1,0:T(8,128)S(1)}, u32[]{:S(2)}, u32[]{:S(2)}) collective-permute-start(f32[32,2048]{1,0:T(8,128)S(1)} %get-tuple-element.80), channel_id=1, source_target_pairs={{0,2},{1,3},{2,0},{3,1},{4,6},{5,7},{6,4},{7,5},{8,10},{9,11},{10,... | collective-permute-start | bytes 786440 | tf_op jit(solution)/shard_map/ppermute | solution.py:757
  27.7 12.5 %collective-permute-start.18 = (f32[32,2048]{1,0:T(8,128)S(1)}, f32[32,2048]{1,0:T(8,128)S(1)}, u32[]{:S(2)}, u32[]{:S(2)}) collective-permute-start(f32[32,2048]{1,0:T(8,128)S(1)} %get-tuple-element.91), channel_id=1, source_target_pairs={{0,2},{1,3},{2,0},{3,1},{4,6},{5,7},{6,4},{7,5},{8,10},{9,11},{10,... | collective-permute-start | bytes 786440 | tf_op jit(solution)/shard_map/ppermute | solution.py:757
  28.8 5.4 %collective-permute-start.13 = (f32[16,128]{1,0:T(8,128)S(1)}, f32[16,128]{1,0:T(8,128)S(1)}, u32[]{:S(2)}, u32[]{:S(2)}) collective-permute-start(f32[16,128]{1,0:T(8,128)S(1)} %products.1.refs_0_.after), channel_id=1, source_target_pairs={{0,12},{4,8},{8,4},{12,0},{1,13},{5,9},{9,5},{13,1},{2,14},{6,10},... | collective-permute-start | bytes 24584 | tf_op jit(solution)/shard_map/ppermute | solution.py:788
  31.3 4.5 %collective-permute-start.12 = (f32[16,128]{1,0:T(8,128)S(1)}, f32[16,128]{1,0:T(8,128)S(1)}, u32[]{:S(2)}, u32[]{:S(2)}) collective-permute-start(f32[16,128]{1,0:T(8,128)S(1)} %products.1.refs_0_.after), channel_id=1, source_target_pairs={{0,8},{4,12},{8,0},{12,4},{1,9},{5,13},{9,1},{13,5},{2,10},{6,14},... | collective-permute-start | bytes 24584 | tf_op jit(solution)/shard_map/ppermute | solution.py:788
  31.3 4.5 %collective-permute-start.11 = (f32[16,128]{1,0:T(8,128)S(1)}, f32[16,128]{1,0:T(8,128)S(1)}, u32[]{:S(2)}, u32[]{:S(2)}) collective-permute-start(f32[16,128]{1,0:T(8,128)S(1)} %products.1.refs_0_.after), channel_id=1, source_target_pairs={{0,4},{4,0},{8,12},{12,8},{1,5},{5,1},{9,13},{13,9},{2,6},{6,2},{1... | collective-permute-start | bytes 24584 | tf_op jit(solution)/shard_map/ppermute | solution.py:788
  35.9 3.3 %collective-permute-start.16 = (f32[16,128]{1,0:T(8,128)S(1)}, f32[16,128]{1,0:T(8,128)S(1)}, u32[]{:S(2)}, u32[]{:S(2)}) collective-permute-start(f32[16,128]{1,0:T(8,128)S(1)} %sum.2.refs_0_), channel_id=1, source_target_pairs={{0,3},{1,2},{2,1},{3,0},{4,7},{5,6},{6,5},{7,4},{8,11},{9,10},{10,... | collective-permute-start | bytes 24584 | tf_op jit(solution)/shard_map/ppermute | solution.py:788
  35.9 4.2 %collective-permute-start.15 = (f32[16,128]{1,0:T(8,128)S(1)}, f32[16,128]{1,0:T(8,128)S(1)}, u32[]{:S(2)}, u32[]{:S(2)}) collective-permute-start(f32[16,128]{1,0:T(8,128)S(1)} %sum.2.refs_0_), channel_id=1, source_target_pairs={{0,2},{1,3},{2,0},{3,1},{4,6},{5,7},{6,4},{7,5},{8,10},{9,11},{10,... | collective-permute-start | bytes 24584 | tf_op jit(solution)/shard_map/ppermute | solution.py:788
  36.9 3.2 %collective-permute-start.14 = (f32[16,128]{1,0:T(8,128)S(1)}, f32[16,128]{1,0:T(8,128)S(1)}, u32[]{:S(2)}, u32[]{:S(2)}) collective-permute-start(f32[16,128]{1,0:T(8,128)S(1)} %sum.2.refs_0_), channel_id=1, source_target_pairs={{0,1},{1,0},{2,3},{3,2},{4,5},{5,4},{6,7},{7,6},{8,9},{9,8},{10,11... | collective-permute-start | bytes 24584 | tf_op jit(solution)/shard_map/ppermute | solution.py:788

commit v8 on v7

--- a/solution.py
+++ b/solution.py
@@ -138,7 +138,6 @@
 
 
 def fetch_kernel(
-    vector_in,
     neighbours_in,
     weights_in,
     degree_in,
@@ -148,20 +147,16 @@
     boundary_in,
     table_in,
     operating_in,
-    forward_in,
-    back_in,
-    vector,
     picked,
     linear,
     capacity,
     capacity_all,
+    entry_rows,
+    weight_rows,
+    own_conductances,
+    place,
     table,
     operating,
-    forward,
-    back,
-    entry_rows,
-    weight_rows,
-    place,
     neighbours,
     weights,
     degree,
@@ -181,7 +176,6 @@
         pltpu.make_async_copy(source, target, copied.at[index])
         for index, (source, target) in enumerate(
             [
-                (vector_in, vector),
                 (send_list_in, send_list),
                 (boundary_in, boundary),
                 (neighbours_in, neighbours),
@@ -191,14 +185,12 @@
                 (capacity_in, capacity_all),
                 (table_in, table),
                 (operating_in, operating),
-                (forward_in.at[place[0]], forward),
-                (back_in.at[place[0]], back),
             ]
         )
     ]
     for copy in copies:
         copy.start()
-    for copy in copies[1:3]:
+    for copy in copies[:2]:
         copy.wait()
 
     lane = lax.broadcasted_iota(I32, (8, lanes), 1)
@@ -214,7 +206,7 @@
     hit = lax.broadcasted_iota(I32, (nodes, lanes), 0) == cut_nodes[:1]
     picked[...] = jnp.where(hit, 1.0, 0.0).astype(BF16)
 
-    for copy in copies[3:8]:
+    for copy in copies[2:7]:
         copy.wait()
     mine = half_of(side, half)
     entry = neighbours[...]
@@ -253,9 +245,9 @@
     for slot in range(slots):
         entry_rows[slot : slot + 1, :] = entries[slot]
         weight_rows[slot : slot + 1, :] = gains[slot]
-    copies[0].wait()
-    for copy in copies[8:]:
+    for copy in copies[7:]:
         copy.wait()
+    own_conductances[...] = conductance(operating[...], table[...])
 
 
 def build(entry_rows, weight_rows, coupling_high, coupling_low):
@@ -300,17 +292,46 @@
     lax.fori_loop(0, width // LANES, column_block, 0)
 
 
-def prepare_kernel(entry_rows, weight_rows, coupling_high, coupling_low):
-    half = coupling_high.shape[1]
-    build(entry_rows.at[:, :half], weight_rows.at[:, :half], coupling_high, coupling_low)
-
-
-def prepare_cut_kernel(after, entry_rows, weight_rows, cut_high, cut_low, cut_halo):
-    lanes = cut_high.shape[1]
-    half = entry_rows.shape[1] - lanes
-    build(entry_rows.at[:, half:], weight_rows.at[:, half:], cut_high, cut_low)
-    nodes = cut_high.shape[0] - lanes
-    cut_halo[...] = jnp.transpose(cut_high[nodes:].astype(F32) + cut_low[nodes:].astype(F32))
+def prepare_kernel(
+    place,
+    entry_rows,
+    weight_rows,
+    vector_in,
+    forward_in,
+    back_in,
+    coupling_high,
+    coupling_low,
+    vector,
+    forward,
+    back,
+    copied,
+):
+    copies = [
+        pltpu.make_async_copy(source, target, copied.at[index])
+        for index, (source, target) in enumerate(
+            [
+                (vector_in, vector),
+                (forward_in.at[place[0]], forward),
+                (back_in.at[place[0]], back),
+            ]
+        )
+    ]
+    for copy in copies:
+        copy.start()
+    width = coupling_high.shape[1]
+    build(entry_rows.at[:, :width], weight_rows.at[:, :width], coupling_high, coupling_low)
+    for copy in copies:
+        copy.wait()
+
+
+def prepare_cut_kernel(after, entry_rows, weight_rows, tail_high, tail_low, cut_halo):
+    width = tail_high.shape[1]
+    start = entry_rows.shape[1] - width
+    build(entry_rows.at[:, start:], weight_rows.at[:, start:], tail_high, tail_low)
+    nodes = tail_high.shape[0] - (width - LANES)
+    cut_halo[...] = jnp.transpose(
+        tail_high[nodes:, LANES:].astype(F32) + tail_low[nodes:, LANES:].astype(F32)
+    )
 
 
 def relay_kernel(*refs):
@@ -319,20 +340,29 @@
         target[...] = source[...]
 
 
-def conductance_kernel(place, near_operating, operating, table, picked, conductances):
-    rows, nodes = operating.shape
+def conductance_kernel(place, near, own, picked, conductances):
+    rows, nodes = own.shape
     side = place[0] % 2
-    for at, values in ((side, operating), (1 - side, near_operating)):
-        conductances[pl.ds(pl.multiple_of(at * rows, 8), rows), :nodes] = conductance(
-            values[...], table[...]
-        )
+    for at, values in ((side, own), (1 - side, near)):
+        conductances[pl.ds(pl.multiple_of(at * rows, 8), rows), :nodes] = values[...]
     conductances[:, nodes:] = pick(conductances[:, :nodes], picked[...])
+
+
+def columns_of(coupling, sources, lanes):
+    main, tail = coupling
+    width = main.shape[1]
+    if lanes.stop <= width:
+        return main[sources, lanes]
+    last = tail[sources, max(lanes.start - width, 0) : lanes.stop - width]
+    if lanes.start >= width:
+        return last
+    return jnp.concatenate([main[sources, lanes.start : width], last], axis=1)
 
 
 def coupled(high, stacked, coupling_high, coupling_low, sources, lanes):
     rows = high.shape[0]
-    both = dot(stacked, coupling_high[sources, lanes])
-    return both[:rows] + both[rows:] + dot(high, coupling_low[sources, lanes])
+    both = dot(stacked, columns_of(coupling_high, sources, lanes))
+    return both[:rows] + both[rows:] + dot(high, columns_of(coupling_low, sources, lanes))
 
 
 def packet_layout(steps, times):
@@ -389,7 +419,12 @@
         + at_cut
         + capacity[:, half:] * slope
         + coupled(
-            high, current[...], coupling_high, coupling_low, slice(0, nodes), slice(None)
+            high,
+            current[...],
+            (coupling_high, coupling_high),
+            (coupling_low, coupling_low),
+            slice(0, nodes),
+            slice(LANES, LANES + lanes),
         )
     )
     image = jnp.transpose(image)
@@ -415,6 +450,8 @@
     conductances,
     coupling_high,
     coupling_low,
+    tail_high,
+    tail_low,
     linear,
     capacity,
     place,
@@ -426,6 +463,7 @@
 ):
     times, half = load.shape
     sources = slice(0, current.shape[1])
+    coupling = (coupling_high, tail_high), (coupling_low, tail_low)
     mine = half_of(place[0] % 2, half)
     others = dot_split(
         (forward[0, times:], forward[1, times:]), (field_high[:, mine], field_low[:, mine])
@@ -437,16 +475,17 @@
     load[...] = own_wave[...] * (linear[:, :half] + conductances[:, mine])
     for lanes in blocks_of(0, half // 2):
         load[:, lanes] += coupled(
-            current[:times], current[...], coupling_high, coupling_low, sources, lanes
+            current[:times], current[...], *coupling, sources, lanes
         )
 
 
-def local_rest_kernel(load, current, coupling_high, coupling_low, rest):
+def local_rest_kernel(load, current, coupling_high, coupling_low, tail_high, tail_low, rest):
     times, half = load.shape
+    coupling = (coupling_high, tail_high), (coupling_low, tail_low)
     sources = slice(0, current.shape[1])
     for lanes, at in zip(blocks_of(half // 2, half), blocks_of(0, half // 2)):
         rest[:, at] = load[:, lanes] + coupled(
-            current[:times], current[...], coupling_high, coupling_low, sources, lanes
+            current[:times], current[...], *coupling, sources, lanes
         )
 
 
@@ -506,6 +545,8 @@
         own_wave,
         coupling_high,
         coupling_low,
+        tail_high,
+        tail_low,
         image,
         load,
         sums,
@@ -518,8 +559,8 @@
     share = coupled(
         high,
         jnp.concatenate([high, low], axis=0),
-        coupling_high,
-        coupling_low,
+        (coupling_high, tail_high),
+        (coupling_low, tail_low),
         slice(nodes, None),
         slice(0, half),
     )
@@ -562,6 +603,8 @@
     conductances,
     coupling_high,
     coupling_low,
+    tail_high,
+    tail_low,
     linear,
     load,
     kept,
@@ -572,6 +615,7 @@
     nodes = current.shape[1]
     side = place[0] % 2
     mine, other = half_of(side, half), half_of(1 - side, half)
+    coupling = (coupling_high, tail_high), (coupling_low, tail_low)
     for at, field in ((mine, image), (other, near_image)):
         current[:times, at], current[times:, at] = split(conductances[:, at] * field[...])
     load[...] = image[...] * (linear[:, :half] + conductances[:, mine])
@@ -579,8 +623,8 @@
     halo_stacked = jnp.concatenate([high, low], axis=0)
     for lanes in blocks_of(0, half):
         load[:, lanes] += coupled(
-            current[:times], current[...], coupling_high, coupling_low, slice(0, nodes), lanes
-        ) + coupled(high, halo_stacked, coupling_high, coupling_low, slice(nodes, None), lanes)
+            current[:times], current[...], *coupling, slice(0, nodes), lanes
+        ) + coupled(high, halo_stacked, *coupling, slice(nodes, None), lanes)
     kept[...], sent[...] = analysed(back, load[...])
 
 
@@ -822,63 +866,64 @@
     )
 
     slot_count = weights.shape[0]
+    def kept_outside(*values):
+        return tuple(pltpu.with_memory_space_constraint(value, pltpu.HBM) for value in values)
+
     (
-        own_vector,
         picked,
         linear_wide,
         capacity_wide,
-        capacity,
-        table,
-        own_operating,
-        forward,
-        back,
+        capacity_all,
         entry_rows,
         weight_rows,
+        own_conductances,
         place,
     ) = run(
         fetch_kernel,
         "fetch",
-        [HBM] * 12,
-        tuple(
-            pltpu.with_memory_space_constraint(value, pltpu.HBM)
-            for value in (vector, neighbours, weights, degree, linear, capacity, send_list)
-            + (boundary, table, operating, forward, back)
-        ),
+        [HBM] * 9,
+        kept_outside(neighbours, weights, degree, linear, capacity, send_list, boundary)
+        + kept_outside(table, operating),
         [
-            ((rows, nodes), F32),
             ((nodes, lanes), BF16),
             ((1, width), F32),
             ((1, width), F32),
             ((1, nodes), F32),
-            (table.shape, F32),
-            ((rows, nodes), F32),
-            (forward.shape[1:], BF16),
-            (back.shape[1:], BF16),
             ((slot_count, width), I32),
             ((slot_count, width), F32),
+            ((rows, nodes), F32),
             ((4,), I32),
         ],
         scratch=[
+            pltpu.VMEM(table.shape, F32),
+            pltpu.VMEM((rows, nodes), F32),
             pltpu.VMEM((slot_count, nodes), I32),
             pltpu.VMEM((slot_count, nodes), F32),
             pltpu.VMEM((1, nodes), I32),
             pltpu.VMEM((1, nodes), F32),
             pltpu.SMEM(send_list.shape, I32),
             pltpu.SMEM(boundary.shape, I32),
-            pltpu.SemaphoreType.DMA((12,)),
+            pltpu.SemaphoreType.DMA((9,)),
         ],
         micros=2,
-        spaces=[pltpu.VMEM] * 11 + [pltpu.SMEM],
-    )
-    coupling_high, coupling_low = run(
+        spaces=[pltpu.VMEM] * 7 + [pltpu.SMEM],
+    )
+    coupling_high, coupling_low, own_vector, forward, back = run(
         prepare_kernel,
         "prepare",
-        [VMEM] * 2,
-        (entry_rows, weight_rows),
-        [((sources, half), BF16)] * 2,
+        [SMEM] + [VMEM] * 2 + [HBM] * 3,
+        (place, entry_rows, weight_rows) + kept_outside(vector, forward, back),
+        [
+            ((sources, half - LANES), BF16),
+            ((sources, half - LANES), BF16),
+            ((rows, nodes), F32),
+            (forward.shape[1:], BF16),
+            (back.shape[1:], BF16),
+        ],
+        scratch=[pltpu.SemaphoreType.DMA((3,))],
         micros=6,
     )
-    near_operating = swap(operating, 1)
+    near_conductances = swap(own_conductances, 1)
     vectors, bit = [vector], parts // 2
     while bit > 1:
         vectors = vectors + [swap(piece, bit) for piece in vectors]
@@ -894,19 +939,19 @@
         )
     vectors = vectors + [swap(piece, 1) for piece in vectors]
     vectors[0] = own_vector
-    cut_high, cut_low, cut_halo = run(
+    tail_high, tail_low, cut_halo = run(
         prepare_cut_kernel,
         "prepare_cut",
         [VMEM] * 3,
         (vectors[far], entry_rows, weight_rows),
-        [((sources, lanes), BF16), ((sources, lanes), BF16), ((lanes, lanes), F32)],
+        [((sources, LANES + lanes), BF16)] * 2 + [((lanes, lanes), F32)],
         micros=1,
     )
     (conductances,) = run(
         conductance_kernel,
         "conductance",
-        [SMEM] + [VMEM] * 4,
-        (place, near_operating, own_operating, table, picked),
+        [SMEM] + [VMEM] * 3,
+        (place, near_conductances, own_conductances, picked),
         [((times, sources), F32)],
         micros=1,
     )
@@ -921,7 +966,7 @@
         functools.partial(wave_kernel, pieces=parts, steps=steps),
         "wave",
         [SMEM] + [VMEM] * (parts + 8),
-        (place, *vectors, forward, conductances, picked, cut_high, cut_low)
+        (place, *vectors, forward, conductances, picked, tail_high, tail_low)
         + (linear_wide, capacity_wide, cut_halo),
         [
             ((length, sources), BF16),
@@ -942,9 +987,9 @@
     local_load, slope, own_wave, dual, dual_slope = run(
         local_kernel,
         "local",
-        [VMEM] * 10 + [SMEM],
+        [VMEM] * 12 + [SMEM],
         (field_high, field_low, forward, wave, current, conductances)
-        + (coupling_high, coupling_low, linear_wide, capacity_wide, place),
+        + (coupling_high, coupling_low, tail_high, tail_low, linear_wide, capacity_wide, place),
         [wide] * 5,
         micros=3,
     )
@@ -956,8 +1001,8 @@
     (local_rest,) = run(
         local_rest_kernel,
         "local_rest",
-        [VMEM] * 4,
-        (local_load, current, coupling_high, coupling_low),
+        [VMEM] * 6,
+        (local_load, current, coupling_high, coupling_low, tail_high, tail_low),
         [((times, half // 2), F32)],
     )
     block = ((length // 2, half), F32)
@@ -966,8 +1011,9 @@
     image, load, own_sums = run(
         functools.partial(first_kernel, steps=steps, apart=len(others)),
         "first",
-        packet_specs + [VMEM] * 6,
-        (*packets, local_load, local_rest, slope, own_wave, coupling_high, coupling_low),
+        packet_specs + [VMEM] * 8,
+        (*packets, local_load, local_rest, slope, own_wave)
+        + (coupling_high, coupling_low, tail_high, tail_low),
         [wide, wide, ((8, half), F32)],
         micros=1,
     )
@@ -990,9 +1036,9 @@
     second_load, second_kept, second_sent = run(
         second_kernel,
         "second",
-        [SMEM] + [VMEM] * 8,
+        [SMEM] + [VMEM] * 10,
         (place, halo, near_image, image, back, conductances)
-        + (coupling_high, coupling_low, linear_wide),
+        + (coupling_high, coupling_low, tail_high, tail_low, linear_wide),
         [wide, block, block],
         scratch=[pltpu.VMEM((2 * times, nodes), BF16)],
         micros=3,
@@ -1022,7 +1068,7 @@
         functools.partial(settle_kernel, length=length),
         "settle",
         [SMEM] + [VMEM] * (len(answer_parts) + 2),
-        (place, own_vector, capacity, *answer_parts),
+        (place, own_vector, capacity_all, *answer_parts),
         [((rows, nodes), F32), ((rows, nodes), F32), ((8, LANES), F32)],
         micros=1,
     )

time: 41.3 us -> 41.3 us (level)
  transfers between devices with their start and end apart: 19 -> 19, of which waited for: 5 -> 6; matrix products, arithmetic and copies ran while one was open for 0% -> 0% of each run, Pallas kernels for 32% -> 32%
where the time goes in v8:
time: 41.3 us; the launch traced here: 41.2 us
  starting transfers between devices  19.6 us (47%)
  Pallas kernels  15.6 us (38%)
  waiting for transfers between devices  5.11 us (12%)
  between operations  0.83 us (2%)
    pallas_call x19, Pallas kernels, run(): pl.pallas_call(kernel, out_shape=[space(shape, dtype) for space, (shape,...  14.6 us
    ppermute x11, starting transfers between devices, swap(): lax.ppermute(value, 'samples', [(at, at ^ mask) for at in range(count)])  8.81 us
    ppermute x6, starting transfers between devices, exchange(): lax.ppermute(value, axis, [(at, at ^ step * stride) for at in range(count)])  6.31 us
    ppermute x6, waiting for transfers between devices, exchange(): lax.ppermute(value, axis, [(at, at ^ step * stride) for at in range(count)])  4.46 us
    ppermute x2, starting transfers between devices, trade(): return lax.ppermute(value, ('nodes', 'samples'), pairs)  4.46 us
    pallas_call x1, Pallas kernels, shards(): pl.pallas_call(functools.partial(last_kernel, entries=entries, devices=fl...  1.02 us
  transfers between devices with their start and end apart: 19, of which 6 were waited for; matrix products, arithmetic and copies ran while one was open for 0% of the time, Pallas kernels for 32%

profile of v8, /device:TPU:0, one launch (start us, length us, event | category | flops | bytes accessed | tf_op | source)
XLA Modules:
  0.0 41.2 jit_solution(14448016401583409454)
XLA Ops:
  0.6 3.0 %collective-permute-start = (f32[32,2048]{1,0:T(8,128)}, f32[32,2048]{1,0:T(8,128)S(1)}, u32[]{:S(2)}, u32[]{:S(2)}) collective-permute-start(f32[32,2048]{1,0:T(8,128)} %vector_in.1), channel_id=1, source_target_pairs={{0,2},{1,3},{2,0},{3,1},{4,6},{5,7},{6,4},{7,5},{8,10},{9,11},{10,... | collective-permute-start | bytes 786440 | tf_op jit(solution)/shard_map/ppermute | solution.py:801
  3.6 0.0 collective-permute-start.1
  3.6 2.0 %fetch.1 = (bf16[2048,128]{1,0:T(8,128)(2,1)S(1)}, f32[1,1152]{1,0:T(1,128)S(1)}, f32[1,1152]{1,0:T(1,128)S(1)}, f32[1,2048]{1,0:T(1,128)S(1)}, s32[8,1152]{1,0:...) custom-call(s32[8,2048]{1,0:T(8,128)} %neighbours_in.1, f32[8,2048]{1,0:T(8,128)} %weights_in.1, ...), custom_call_target="tpu_custom_call" | custom-call | bytes 6000000 | tf_op jit(solution)/shard_map/fetch/pallas_call | solution.py:785
  5.6 0.6 %collective-permute-start.3 = (f32[32,2048]{1,0:T(8,128)S(1)}, f32[32,2048]{1,0:T(8,128)S(1)}, u32[]{:S(2)}, u32[]{:S(2)}) collective-permute-start(f32[32,2048]{1,0:T(8,128)S(1)} %get-tuple-element.53.own), channel_id=1, source_target_pairs={{0,1},{1,0},{2,3},{3,2},{4,5},{5,4},{6,7},{7,6},{8,9},{9,8},{10,11... | collective-permute-start | bytes 786440 | tf_op jit(solution)/shard_map/ppermute | solution.py:801
  6.2 3.8 %prepare.1 = (bf16[2176,896]{1,0:T(8,128)(2,1)S(1)}, bf16[2176,896]{1,0:T(8,128)(2,1)S(1)}, f32[32,2048]{1,0:T(8,128)S(1)}, bf16[2,256,128]{2,1,0:T(8,128)(2,1)S(1)}, bf16[2,128,64]{2,1,0:T(8,128)(2,1)S(1)}) custom-call(s32[4]{0:T(128)S(4)} %get-tuple-element.46.place.refs_0_, s32[8,1152]{1,0:T(8,128)S(1)} %get-tuple-element.47.entry_rows, ...), custom_call_target="tpu_custom_call" | custom-call | bytes 18000000 | tf_op jit(solution)/shard_map/prepare/pallas_call | solution.py:785
  10.1 0.1 collective-permute-done.refs_1_
  10.2 0.1 collective-permute-start.2
  10.3 1.2 %prepare_cut.1 = (bf16[2176,256]{1,0:T(8,128)(2,1)S(1)}, bf16[2176,256]{1,0:T(8,128)(2,1)S(1)}, f32[128,128]{1,0:T(8,128)S(1)}) custom-call(f32[32,2048]{1,0:T(8,128)S(1)} %relay.3.after.refs_2_, s32[8,1152]{1,0:T(8,128)S(1)} %get-tuple-element.47.entry_rows, f32[8,1152]{1,0:T(8,128)S(1)} %get-tuple-element.48.weight_rows), custom_call_target="tpu_custom_call" | custom-call | bytes 3000000 | tf_op jit(solution)/shard_map/prepare_cut/pallas_call | solution.py:785
  11.4 0.0 collective-permute-done.3.near
  11.5 0.4 conductance.1.refs_6_.conductances
  11.9 0.0 collective-permute-done.1.refs_3_
  11.9 0.0 collective-permute-done.2.refs_4_
  11.9 1.1 %wave.1 = (bf16[128,2176]{1,0:T(8,128)(2,1)S(1)}, bf16[128,2176]{1,0:T(8,128)(2,1)S(1)}, f32[64,2176]{1,0:T(8,128)S(1)}, bf16[128,2048]{1,0:T(8,128)(2,1)S(1)}, ...) custom-call(s32[4]{0:T(128)S(4)} %get-tuple-element.46.place.refs_0_, ...), custom_call_target="tpu_custom_call" | custom-call | bytes 6000000 | tf_op jit(solution)/shard_map/wave/pallas_call | solution.py:785
  13.0 1.9 %collective-permute-start.5 = (f32[48,128]{1,0:T(8,128)S(1)}, f32[48,128]{1,0:T(8,128)S(1)}, u32[]{:S(2)}, u32[]{:S(2)}) collective-permute-start(f32[48,128]{1,0:T(8,128)S(1)} %get-tuple-element.67), channel_id=1, source_target_pairs={{0,4},{1,13},{2,6},{3,15},{4,0},{5,9},{6,2},{7,11},{8,12},{9,5},{1... | collective-permute-start | bytes 73736 | tf_op jit(solution)/shard_map/ppermute | solution.py:811
  14.9 2.6 %collective-permute-start.4 = (f32[48,128]{1,0:T(8,128)S(1)}, f32[48,128]{1,0:T(8,128)S(1)}, u32[]{:S(2)}, u32[]{:S(2)}) collective-permute-start(f32[48,128]{1,0:T(8,128)S(1)} %get-tuple-element.60), channel_id=1, source_target_pairs={{0,8},{1,9},{2,10},{3,11},{4,12},{5,13},{6,14},{7,15},{8,0},{9,1},... | collective-permute-start | bytes 73736 | tf_op jit(solution)/shard_map/ppermute | solution.py:811
  17.5 1.0 %local.1 = (f32[64,1024]{1,0:T(8,128)S(1)}, f32[64,1024]{1,0:T(8,128)S(1)}, f32[64,1024]{1,0:T(8,128)S(1)}, f32[64,1024]{1,0:T(8,128)S(1)}, f32[64,1024]{1,0:T(8,128)S(1)}) custom-call(bf16[128,2176]{1,0:T(8,128)(2,1)S(1)} %get-tuple-element.61.field_high, bf16[128,2176]{1,0:T(8,128)(2,1)S(1)} %get-tuple-element.62.field_low, ...), custom_call_target="tpu_custom_call" | custom-call | bytes 9000000 | tf_op jit(solution)/shard_map/local/pallas_call | solution.py:785
  18.5 0.0 collective-permute-done.5.refs_1_
  18.5 0.1 collective-permute-start.6
  18.6 0.8 %local_rest.1.refs_6_ = f32[64,512]{1,0:T(8,128)S(1)} custom-call(f32[64,1024]{1,0:T(8,128)S(1)} %get-tuple-element.69.load.refs_5_, bf16[128,2048]{1,0:T(8,128)(2,1)S(1)} %get-tuple-element.64.current, bf16[2176,896]{1,0:T(8,128)(2,1)S(1)} %get-tuple-element.65.coupling_high.refs_9_, bf16[2176,896]{1,0:T(8,128)(2,1)S(1)} %get-tuple-element.51.refs_0_.coupling_low.refs_10_, ...), custom_call_target="tpu_custom_call" | custom-call | bytes 3000000 | tf_op jit(solution)/shard_map/local_rest/pallas_call | solution.py:785
  19.4 0.5 %collective-permute-done.4.refs_1_ = f32[48,128]{1,0:T(8,128)S(1)} collective-permute-done((f32[48,128]{1,0:T(8,128)S(1)}, f32[48,128]{1,0:T(8,128)S(1)}, u32[]{:S(2)}, u32[]{:S(2)}) %collective-permute-start.4) | collective-permute-done | bytes 24608 | tf_op jit(solution)/shard_map/ppermute | solution.py:811
  20.0 0.0 collective-permute-done.6.refs_3_
  20.0 0.3 first.1
  20.3 0.8 %collective-permute-start.9 = (f32[64,1024]{1,0:T(8,128)S(1)}, f32[64,1024]{1,0:T(8,128)S(1)}, u32[]{:S(2)}, u32[]{:S(2)}) collective-permute-start(f32[64,1024]{1,0:T(8,128)S(1)} %get-tuple-element.73.refs_5_.image), channel_id=1, source_target_pairs={{0,1},{1,0},{2,3},{3,2},{4,5},{5,4},{6,7},{7,6},{8,9},{9,8},{10,11... | collective-permute-start | bytes 786440 | tf_op jit(solution)/shard_map/ppermute | solution.py:801
  21.1 1.5 %collective-permute-start.10 = (f32[8,1024]{1,0:T(8,128)S(1)}, f32[8,1024]{1,0:T(8,128)S(1)}, u32[]{:S(2)}, u32[]{:S(2)}) collective-permute-start(f32[8,1024]{1,0:T(8,128)S(1)} %get-tuple-element.83.own_sums), channel_id=1, source_target_pairs={{0,2},{1,3},{2,0},{3,1},{4,6},{5,7},{6,4},{7,5},{8,10},{9,11},{10,... | collective-permute-start | bytes 98312 | tf_op jit(solution)/shard_map/ppermute | solution.py:801
  22.6 0.5 %spread.1 = (f32[64,128]{1,0:T(8,128)S(1)}, f32[64,1024]{1,0:T(8,128)S(1)}, f32[64,1024]{1,0:T(8,128)S(1)}) custom-call(s32[4]{0:T(128)S(4)} %get-tuple-element.46.place.refs_0_, f32[48,128]{1,0:T(8,128)S(1)} %collective-permute-done.4.refs_1_, f32[48,128]{1,0:T(8,128)S(1)} %relay.4.refs_2_, f32[48,128]{1,0:T(8,128)S(1)} %collective-permute-done.6.refs_3_, ...), custom_call_target="tpu_custom_call" | custom-call | bytes 3000000 | tf_op jit(solution)/shard_map/spread/pallas_call | solution.py:785
  23.2 0.1 collective-permute-start.7
  23.2 0.0 collective-permute-done.9.near_image
  23.2 1.9 %second.1 = (f32[64,1024]{1,0:T(8,128)S(1)}, f32[64,1024]{1,0:T(8,128)S(1)}, f32[64,1024]{1,0:T(8,128)S(1)}) custom-call(s32[4]{0:T(128)S(4)} %get-tuple-element.46.place.refs_0_, f32[64,128]{1,0:T(8,128)S(1)} %get-tuple-element.80.halo, f32[64,1024]{1,0:T(8,128)S(1)} %collective-permute-done.9.near_image, f32[64,1024]{1,0:T(8,128)S(1)} %get-tuple-element.73.refs_5_.image, ...), custom_call_target="tpu_custom_call" | custom-call | bytes 9000000 | tf_op jit(solution)/shard_map/second/pallas_call | solution.py:785
  25.2 0.0 collective-permute-done.10.far_sums.refs_0_
  25.2 0.6 %collective-permute-start.17 = (f32[64,1024]{1,0:T(8,128)S(1)}, f32[64,1024]{1,0:T(8,128)S(1)}, u32[]{:S(2)}, u32[]{:S(2)}) collective-permute-start(f32[64,1024]{1,0:T(8,128)S(1)} %relay.5), channel_id=1, source_target_pairs={{0,1},{1,0},{2,3},{3,2},{4,5},{5,4},{6,7},{7,6},{8,9},{9,8},{10,11... | collective-permute-start | bytes 786440 | tf_op jit(solution)/shard_map/ppermute | solution.py:801
  25.8 0.0 collective-permute-done.7.arrived
  25.8 0.9 %collective-permute-start.8 = (f32[32,2048]{1,0:T(8,128)S(1)}, f32[32,2048]{1,0:T(8,128)S(1)}, u32[]{:S(2)}, u32[]{:S(2)}) collective-permute-start(f32[32,2048]{1,0:T(8,128)S(1)} %get-tuple-element.78), channel_id=1, source_target_pairs={{0,2},{1,3},{2,0},{3,1},{4,6},{5,7},{6,4},{7,5},{8,10},{9,11},{10,... | collective-permute-start | bytes 786440 | tf_op jit(solution)/shard_map/ppermute | solution.py:801
  26.8 0.8 %products.1.refs_0_.after = f32[16,128]{1,0:T(8,128)S(1)} custom-call(s32[4]{0:T(128)S(4)} %get-tuple-element.46.place.refs_0_, f32[32,2048]{1,0:T(8,128)S(1)} %get-tuple-element.49.refs_1_.vector, f32[64,1024]{1,0:T(8,128)S(1)} %get-tuple-element.72.after.load, f32[64,1024]{1,0:T(8,128)S(1)} %get-tuple-element.81.second_load, ...), custom_call_target="tpu_custom_call" | custom-call | bytes 3000000 | tf_op jit(solution)/shard_map/products/pallas_call | solution.py:785
  27.5 0.0 collective-permute-done.17.arrived
  27.6 1.2 %collective-permute-start.18 = (f32[32,2048]{1,0:T(8,128)S(1)}, f32[32,2048]{1,0:T(8,128)S(1)}, u32[]{:S(2)}, u32[]{:S(2)}) collective-permute-start(f32[32,2048]{1,0:T(8,128)S(1)} %get-tuple-element.89), channel_id=1, source_target_pairs={{0,2},{1,3},{2,0},{3,1},{4,6},{5,7},{6,4},{7,5},{8,10},{9,11},{10,... | collective-permute-start | bytes 786440 | tf_op jit(solution)/shard_map/ppermute | solution.py:801
  28.8 2.4 %collective-permute-start.13 = (f32[16,128]{1,0:T(8,128)S(1)}, f32[16,128]{1,0:T(8,128)S(1)}, u32[]{:S(2)}, u32[]{:S(2)}) collective-permute-start(f32[16,128]{1,0:T(8,128)S(1)} %products.1.refs_0_.after), channel_id=1, source_target_pairs={{0,12},{4,8},{8,4},{12,0},{1,13},{5,9},{9,5},{13,1},{2,14},{6,10},... | collective-permute-start | bytes 24584 | tf_op jit(solution)/shard_map/ppermute | solution.py:832
  31.2 0.0 collective-permute-start.12
  31.2 2.0 %collective-permute-start.11 = (f32[16,128]{1,0:T(8,128)S(1)}, f32[16,128]{1,0:T(8,128)S(1)}, u32[]{:S(2)}, u32[]{:S(2)}) collective-permute-start(f32[16,128]{1,0:T(8,128)S(1)} %products.1.refs_0_.after), channel_id=1, source_target_pairs={{0,4},{4,0},{8,12},{12,8},{1,5},{5,1},{9,13},{13,9},{2,6},{6,2},{1... | collective-permute-start | bytes 24584 | tf_op jit(solution)/shard_map/ppermute | solution.py:832
  33.2 1.1 %collective-permute-done.13.refs_3_ = f32[16,128]{1,0:T(8,128)S(1)} collective-permute-done((f32[16,128]{1,0:T(8,128)S(1)}, f32[16,128]{1,0:T(8,128)S(1)}, u32[]{:S(2)}, u32[]{:S(2)}) %collective-permute-start.13) | collective-permute-done | bytes 8224 | tf_op jit(solution)/shard_map/ppermute | solution.py:832
  34.3 1.5 %collective-permute-done.12.refs_2_ = f32[16,128]{1,0:T(8,128)S(1)} collective-permute-done((f32[16,128]{1,0:T(8,128)S(1)}, f32[16,128]{1,0:T(8,128)S(1)}, u32[]{:S(2)}, u32[]{:S(2)}) %collective-permute-start.12) | collective-permute-done | bytes 8224 | tf_op jit(solution)/shard_map/ppermute | solution.py:832
  35.8 0.1 collective-permute-start.16
  35.8 0.9 %collective-permute-start.15 = (f32[16,128]{1,0:T(8,128)S(1)}, f32[16,128]{1,0:T(8,128)S(1)}, u32[]{:S(2)}, u32[]{:S(2)}) collective-permute-start(f32[16,128]{1,0:T(8,128)S(1)} %sum.2.refs_0_), channel_id=1, source_target_pairs={{0,2},{1,3},{2,0},{3,1},{4,6},{5,7},{6,4},{7,5},{8,10},{9,11},{10,... | collective-permute-start | bytes 24584 | tf_op jit(solution)/shard_map/ppermute | solution.py:832
  36.8 0.9 %collective-permute-start.14 = (f32[16,128]{1,0:T(8,128)S(1)}, f32[16,128]{1,0:T(8,128)S(1)}, u32[]{:S(2)}, u32[]{:S(2)}) collective-permute-start(f32[16,128]{1,0:T(8,128)S(1)} %sum.2.refs_0_), channel_id=1, source_target_pairs={{0,1},{1,0},{2,3},{3,2},{4,5},{5,4},{6,7},{7,6},{8,9},{9,8},{10,11... | collective-permute-start | bytes 24584 | tf_op jit(solution)/shard_map/ppermute | solution.py:832
  37.7 0.5 %settle.1 = (f32[32,2048]{1,0:T(8,128)S(1)}, f32[32,2048]{1,0:T(8,128)S(1)}, f32[8,128]{1,0:T(8,128)S(1)}) custom-call(s32[4]{0:T(128)S(4)} %get-tuple-element.46.place.refs_0_, f32[32,2048]{1,0:T(8,128)S(1)} %get-tuple-element.49.refs_1_.vector, f32[1,2048]{1,0:T(1,128)S(1)} %get-tuple-element.50.capacity, f32[32,2048]{1,0:T(8,128)S(1)} %get-tuple-element.77.refs_0_, ...), custom_call_target="tpu_custom_call" | custom-call | bytes 3000000 | tf_op jit(solution)/shard_map/settle/pallas_call | solution.py:785
  38.2 0.8 %collective-permute-done.16.refs_3_ = f32[16,128]{1,0:T(8,128)S(1)} collective-permute-done((f32[16,128]{1,0:T(8,128)S(1)}, f32[16,128]{1,0:T(8,128)S(1)}, u32[]{:S(2)}, u32[]{:S(2)}) %collective-permute-start.16) | collective-permute-done | bytes 8224 | tf_op jit(solution)/shard_map/ppermute | solution.py:832
  39.0 1.1 %collective-permute-done.15.refs_2_ = f32[16,128]{1,0:T(8,128)S(1)} collective-permute-done((f32[16,128]{1,0:T(8,128)S(1)}, f32[16,128]{1,0:T(8,128)S(1)}, u32[]{:S(2)}, u32[]{:S(2)}) %collective-permute-start.15) | collective-permute-done | bytes 8224 | tf_op jit(solution)/shard_map/ppermute | solution.py:832
  40.1 0.0 collective-permute-done.14.refs_1_
  40.1 1.0 %last.1 = (f32[32,2048]{1,0:T(8,128)}, f32[32,2048]{1,0:T(8,128)}) custom-call(f32[16,128]{1,0:T(8,128)S(1)} %sum.3.gathered, f32[32,2048]{1,0:T(8,128)S(1)} %get-tuple-element.49.refs_1_.vector, f32[32,2048]{1,0:T(8,128)S(1)} %get-tuple-element.84.answer, f32[32,2048]{1,0:T(8,128)S(1)} %get-tuple-element.85.slope, ...), custom_call_target="tpu_custom_call" | custom-call | tf_op jit(solution)/shard_map/last/pallas_call | solution.py:1078
  (10 shorter events, 0.1 us)
Async XLA Ops:
  0.6 9.5 %collective-permute-start = (f32[32,2048]{1,0:T(8,128)}, f32[32,2048]{1,0:T(8,128)S(1)}, u32[]{:S(2)}, u32[]{:S(2)}) collective-permute-start(f32[32,2048]{1,0:T(8,128)} %vector_in.1), channel_id=1, source_target_pairs={{0,2},{1,3},{2,0},{3,1},{4,6},{5,7},{6,4},{7,5},{8,10},{9,11},{10,... | collective-permute-start | bytes 786440 | tf_op jit(solution)/shard_map/ppermute | solution.py:801
  3.6 8.2 %collective-permute-start.1 = (f32[32,2048]{1,0:T(8,128)}, f32[32,2048]{1,0:T(8,128)S(1)}, u32[]{:S(2)}, u32[]{:S(2)}) collective-permute-start(f32[32,2048]{1,0:T(8,128)} %vector_in.1), channel_id=1, source_target_pairs={{0,1},{1,0},{2,3},{3,2},{4,5},{5,4},{6,7},{7,6},{8,9},{9,8},{10,11... | collective-permute-start | bytes 786440 | tf_op jit(solution)/shard_map/ppermute | solution.py:801
  5.6 5.8 %collective-permute-start.3 = (f32[32,2048]{1,0:T(8,128)S(1)}, f32[32,2048]{1,0:T(8,128)S(1)}, u32[]{:S(2)}, u32[]{:S(2)}) collective-permute-start(f32[32,2048]{1,0:T(8,128)S(1)} %get-tuple-element.53.own), channel_id=1, source_target_pairs={{0,1},{1,0},{2,3},{3,2},{4,5},{5,4},{6,7},{7,6},{8,9},{9,8},{10,11... | collective-permute-start | bytes 786440 | tf_op jit(solution)/shard_map/ppermute | solution.py:801
  10.2 1.7 %collective-permute-start.2 = (f32[32,2048]{1,0:T(8,128)S(1)}, f32[32,2048]{1,0:T(8,128)S(1)}, u32[]{:S(2)}, u32[]{:S(2)}) collective-permute-start(f32[32,2048]{1,0:T(8,128)S(1)} %relay.3.after.refs_2_), channel_id=1, source_target_pairs={{0,1},{1,0},{2,3},{3,2},{4,5},{5,4},{6,7},{7,6},{8,9},{9,8},{10,11... | collective-permute-start | bytes 786440 | tf_op jit(solution)/shard_map/ppermute | solution.py:801
  13.0 5.5 %collective-permute-start.5 = (f32[48,128]{1,0:T(8,128)S(1)}, f32[48,128]{1,0:T(8,128)S(1)}, u32[]{:S(2)}, u32[]{:S(2)}) collective-permute-start(f32[48,128]{1,0:T(8,128)S(1)} %get-tuple-element.67), channel_id=1, source_target_pairs={{0,4},{1,13},{2,6},{3,15},{4,0},{5,9},{6,2},{7,11},{8,12},{9,5},{1... | collective-permute-start | bytes 73736 | tf_op jit(solution)/shard_map/ppermute | solution.py:811
  14.9 5.1 %collective-permute-start.4 = (f32[48,128]{1,0:T(8,128)S(1)}, f32[48,128]{1,0:T(8,128)S(1)}, u32[]{:S(2)}, u32[]{:S(2)}) collective-permute-start(f32[48,128]{1,0:T(8,128)S(1)} %get-tuple-element.60), channel_id=1, source_target_pairs={{0,8},{1,9},{2,10},{3,11},{4,12},{5,13},{6,14},{7,15},{8,0},{9,1},... | collective-permute-start | bytes 73736 | tf_op jit(solution)/shard_map/ppermute | solution.py:811
  18.5 1.4 %collective-permute-start.6 = (f32[48,128]{1,0:T(8,128)S(1)}, f32[48,128]{1,0:T(8,128)S(1)}, u32[]{:S(2)}, u32[]{:S(2)}) collective-permute-start(f32[48,128]{1,0:T(8,128)S(1)} %relay.4.refs_2_), channel_id=1, source_target_pairs={{0,1},{1,0},{2,3},{3,2},{4,5},{5,4},{6,7},{7,6},{8,9},{9,8},{10,11... | collective-permute-start | bytes 73736 | tf_op jit(solution)/shard_map/ppermute | solution.py:801
  20.3 2.9 %collective-permute-start.9 = (f32[64,1024]{1,0:T(8,128)S(1)}, f32[64,1024]{1,0:T(8,128)S(1)}, u32[]{:S(2)}, u32[]{:S(2)}) collective-permute-start(f32[64,1024]{1,0:T(8,128)S(1)} %get-tuple-element.73.refs_5_.image), channel_id=1, source_target_pairs={{0,1},{1,0},{2,3},{3,2},{4,5},{5,4},{6,7},{7,6},{8,9},{9,8},{10,11... | collective-permute-start | bytes 786440 | tf_op jit(solution)/shard_map/ppermute | solution.py:801
  21.1 4.1 %collective-permute-start.10 = (f32[8,1024]{1,0:T(8,128)S(1)}, f32[8,1024]{1,0:T(8,128)S(1)}, u32[]{:S(2)}, u32[]{:S(2)}) collective-permute-start(f32[8,1024]{1,0:T(8,128)S(1)} %get-tuple-element.83.own_sums), channel_id=1, source_target_pairs={{0,2},{1,3},{2,0},{3,1},{4,6},{5,7},{6,4},{7,5},{8,10},{9,11},{10,... | collective-permute-start | bytes 98312 | tf_op jit(solution)/shard_map/ppermute | solution.py:801
  23.2 2.6 %collective-permute-start.7 = (f32[64,1024]{1,0:T(8,128)S(1)}, f32[64,1024]{1,0:T(8,128)S(1)}, u32[]{:S(2)}, u32[]{:S(2)}) collective-permute-start(f32[64,1024]{1,0:T(8,128)S(1)} %get-tuple-element.76), channel_id=1, source_target_pairs={{0,1},{1,0},{2,3},{3,2},{4,5},{5,4},{6,7},{7,6},{8,9},{9,8},{10,11... | collective-permute-start | bytes 786440 | tf_op jit(solution)/shard_map/ppermute | solution.py:801
  25.2 2.3 %collective-permute-start.17 = (f32[64,1024]{1,0:T(8,128)S(1)}, f32[64,1024]{1,0:T(8,128)S(1)}, u32[]{:S(2)}, u32[]{:S(2)}) collective-permute-start(f32[64,1024]{1,0:T(8,128)S(1)} %relay.5), channel_id=1, source_target_pairs={{0,1},{1,0},{2,3},{3,2},{4,5},{5,4},{6,7},{7,6},{8,9},{9,8},{10,11... | collective-permute-start | bytes 786440 | tf_op jit(solution)/shard_map/ppermute | solution.py:801
  25.8 11.8 %collective-permute-start.8 = (f32[32,2048]{1,0:T(8,128)S(1)}, f32[32,2048]{1,0:T(8,128)S(1)}, u32[]{:S(2)}, u32[]{:S(2)}) collective-permute-start(f32[32,2048]{1,0:T(8,128)S(1)} %get-tuple-element.78), channel_id=1, source_target_pairs={{0,2},{1,3},{2,0},{3,1},{4,6},{5,7},{6,4},{7,5},{8,10},{9,11},{10,... | collective-permute-start | bytes 786440 | tf_op jit(solution)/shard_map/ppermute | solution.py:801
  27.6 12.5 %collective-permute-start.18 = (f32[32,2048]{1,0:T(8,128)S(1)}, f32[32,2048]{1,0:T(8,128)S(1)}, u32[]{:S(2)}, u32[]{:S(2)}) collective-permute-start(f32[32,2048]{1,0:T(8,128)S(1)} %get-tuple-element.89), channel_id=1, source_target_pairs={{0,2},{1,3},{2,0},{3,1},{4,6},{5,7},{6,4},{7,5},{8,10},{9,11},{10,... | collective-permute-start | bytes 786440 | tf_op jit(solution)/shard_map/ppermute | solution.py:801
  28.8 5.4 %collective-permute-start.13 = (f32[16,128]{1,0:T(8,128)S(1)}, f32[16,128]{1,0:T(8,128)S(1)}, u32[]{:S(2)}, u32[]{:S(2)}) collective-permute-start(f32[16,128]{1,0:T(8,128)S(1)} %products.1.refs_0_.after), channel_id=1, source_target_pairs={{0,12},{4,8},{8,4},{12,0},{1,13},{5,9},{9,5},{13,1},{2,14},{6,10},... | collective-permute-start | bytes 24584 | tf_op jit(solution)/shard_map/ppermute | solution.py:832
  31.2 4.5 %collective-permute-start.12 = (f32[16,128]{1,0:T(8,128)S(1)}, f32[16,128]{1,0:T(8,128)S(1)}, u32[]{:S(2)}, u32[]{:S(2)}) collective-permute-start(f32[16,128]{1,0:T(8,128)S(1)} %products.1.refs_0_.after), channel_id=1, source_target_pairs={{0,8},{4,12},{8,0},{12,4},{1,9},{5,13},{9,1},{13,5},{2,10},{6,14},... | collective-permute-start | bytes 24584 | tf_op jit(solution)/shard_map/ppermute | solution.py:832
  31.2 4.5 %collective-permute-start.11 = (f32[16,128]{1,0:T(8,128)S(1)}, f32[16,128]{1,0:T(8,128)S(1)}, u32[]{:S(2)}, u32[]{:S(2)}) collective-permute-start(f32[16,128]{1,0:T(8,128)S(1)} %products.1.refs_0_.after), channel_id=1, source_target_pairs={{0,4},{4,0},{8,12},{12,8},{1,5},{5,1},{9,13},{13,9},{2,6},{6,2},{1... | collective-permute-start | bytes 24584 | tf_op jit(solution)/shard_map/ppermute | solution.py:832
  35.8 3.2 %collective-permute-start.16 = (f32[16,128]{1,0:T(8,128)S(1)}, f32[16,128]{1,0:T(8,128)S(1)}, u32[]{:S(2)}, u32[]{:S(2)}) collective-permute-start(f32[16,128]{1,0:T(8,128)S(1)} %sum.2.refs_0_), channel_id=1, source_target_pairs={{0,3},{1,2},{2,1},{3,0},{4,7},{5,6},{6,5},{7,4},{8,11},{9,10},{10,... | collective-permute-start | bytes 24584 | tf_op jit(solution)/shard_map/ppermute | solution.py:832
  35.8 4.3 %collective-permute-start.15 = (f32[16,128]{1,0:T(8,128)S(1)}, f32[16,128]{1,0:T(8,128)S(1)}, u32[]{:S(2)}, u32[]{:S(2)}) collective-permute-start(f32[16,128]{1,0:T(8,128)S(1)} %sum.2.refs_0_), channel_id=1, source_target_pairs={{0,2},{1,3},{2,0},{3,1},{4,6},{5,7},{6,4},{7,5},{8,10},{9,11},{10,... | collective-permute-start | bytes 24584 | tf_op jit(solution)/shard_map/ppermute | solution.py:832
  36.8 3.3 %collective-permute-start.14 = (f32[16,128]{1,0:T(8,128)S(1)}, f32[16,128]{1,0:T(8,128)S(1)}, u32[]{:S(2)}, u32[]{:S(2)}) collective-permute-start(f32[16,128]{1,0:T(8,128)S(1)} %sum.2.refs_0_), channel_id=1, source_target_pairs={{0,1},{1,0},{2,3},{3,2},{4,5},{5,4},{6,7},{7,6},{8,9},{9,8},{10,11... | collective-permute-start | bytes 24584 | tf_op jit(solution)/shard_map/ppermute | solution.py:832

commit v9 on v7

--- a/solution.py
+++ b/solution.py
@@ -32,10 +32,12 @@
     return synthesis, analysis, turn
 
 
-def halves(table):
-    high = table.astype(np.float32).astype(BF16)
-    low = (table - high.astype(np.float64)).astype(np.float32).astype(BF16)
-    return np.stack([high, low])
+def thirds(table):
+    parts = []
+    for _ in range(3):
+        parts.append(table.astype(np.float32).astype(BF16))
+        table = table - parts[-1].astype(np.float64)
+    return np.stack(parts)
 
 
 def piece_order(count):
@@ -70,14 +72,21 @@
         )
         back.append(analysis[np.ix_(sent, times)])
     return (
-        np.moveaxis(halves(np.stack(forward)), 0, 1),
-        np.moveaxis(halves(np.stack(back)), 0, 1),
+        np.moveaxis(thirds(np.stack(forward)), 0, 1),
+        np.moveaxis(thirds(np.stack(back)), 0, 1),
     )
 
 
 def split(values):
     high = values.astype(BF16)
     return high, (values - high.astype(F32)).astype(BF16)
+
+
+def split_three(values):
+    high = values.astype(BF16)
+    rest = values - high.astype(F32)
+    middle = rest.astype(BF16)
+    return high, middle, (rest - middle.astype(F32)).astype(BF16)
 
 
 def dot(first, second):
@@ -89,6 +98,14 @@
     rows = first_high.shape[0]
     both = dot(jnp.concatenate([first_high, first_low], axis=0), second_high)
     return both[:rows] + both[rows:] + dot(first_high, second_low)
+
+
+def dot_three(first, second):
+    rows = first[0].shape[0]
+    one = dot(jnp.concatenate(first, axis=0), second[0])
+    two = dot(jnp.concatenate(first[:2], axis=0), second[1])
+    small = one[2 * rows :] + two[rows:] + dot(first[0], second[2])
+    return one[:rows] + ((one[rows : 2 * rows] + two[:rows]) + small)
 
 
 def lane_sums(values):
@@ -361,7 +378,7 @@
         current,
         cut_current,
     ) = refs[1 + pieces : 1 + pieces + 13]
-    sent = refs[1 + pieces + 13 :]
+    *sent, field_last = refs[1 + pieces + 13 :]
     side = refs[0][0] % 2
     rows, nodes = vectors[0].shape
     lanes = picked.shape[1]
@@ -369,11 +386,14 @@
     half = linear.shape[1] - lanes
     for index in range(pieces):
         at = slice(index * rows, (index + 1) * rows)
-        field_high[at, :nodes], field_low[at, :nodes] = split(vectors[index][...])
+        parts = split_three(vectors[index][...])
+        field_high[at, :nodes], field_low[at, :nodes], field_last[at, :nodes] = parts
     field_high[:, nodes:] = dot(field_high[:, :nodes], picked[...]).astype(BF16)
     field_low[:, nodes:] = dot(field_low[:, :nodes], picked[...]).astype(BF16)
-    wave[...] = dot_split(
-        (forward[0, :times], forward[1, :times]), (field_high[...], field_low[...])
+    field_last[:, nodes:] = dot(field_last[:, :nodes], picked[...]).astype(BF16)
+    wave[...] = dot_three(
+        [forward[part, :times] for part in range(3)],
+        (field_high[...], field_low[...], field_last[...]),
     )
     slope = dot_split(
         (forward[0, times : 2 * times], forward[1, times : 2 * times]),
@@ -465,7 +485,7 @@
 
 
 def analysed(back, load):
-    spectrum = dot_split((back[0], back[1]), split(load))
+    spectrum = dot_three([back[part] for part in range(3)], split_three(load))
     middle = spectrum.shape[0] // 2
     return spectrum[:middle], spectrum[middle:]
 
@@ -931,6 +951,7 @@
             ((lanes, times), F32),
         ]
         + [(packet, F32)] * len(packet_steps(steps)),
+        scratch=[pltpu.VMEM((length, sources), BF16)],
         micros=2,
     )
     arrived = [trade(packet, masks) for packet, masks in zip(sent, packet_steps(steps))]

time: 41.3 us -> 42.1 us (1.019)
  Pallas kernels: 15.9 us -> 16.6 us
    pallas_call x19, Pallas kernels: 14.8 us -> 15.6 us  [run(): pl.pallas_call(kernel, out_shape=[space(shape, dtype) for space, (shape,...]
  transfers between devices with their start and end apart: 19 -> 19, of which waited for: 5 -> 5; matrix products, arithmetic and copies ran while one was open for 0% -> 0% of each run, Pallas kernels for 32% -> 33%
where the time goes in v9:
time: 42.1 us; the launch traced here: 41.9 us
  starting transfers between devices  19.4 us (46%)
  Pallas kernels  16.6 us (39%)
  waiting for transfers between devices  5.02 us (12%)
  between operations  0.84 us (2%)
    pallas_call x19, Pallas kernels, run(): pl.pallas_call(kernel, out_shape=[space(shape, dtype) for space, (shape,...  15.6 us
    ppermute x11, starting transfers between devices, swap(): lax.ppermute(value, 'samples', [(at, at ^ mask) for at in range(count)])  8.78 us
    ppermute x6, starting transfers between devices, exchange(): lax.ppermute(value, axis, [(at, at ^ step * stride) for at in range(count)])  6.31 us
    ppermute x6, waiting for transfers between devices, exchange(): lax.ppermute(value, axis, [(at, at ^ step * stride) for at in range(count)])  4.45 us
    ppermute x2, starting transfers between devices, trade(): return lax.ppermute(value, ('nodes', 'samples'), pairs)  4.34 us
    pallas_call x1, Pallas kernels, shards(): pl.pallas_call(functools.partial(last_kernel, entries=entries, devices=fl...  1.02 us
  transfers between devices with their start and end apart: 19, of which 5 were waited for; matrix products, arithmetic and copies ran while one was open for 0% of the time, Pallas kernels for 33%

profile of v9, /device:TPU:0, one launch (start us, length us, event | category | flops | bytes accessed | tf_op | source)
XLA Modules:
  0.0 41.9 jit_solution(12141883648681908608)
XLA Ops:
  0.6 3.0 %collective-permute-start = (f32[32,2048]{1,0:T(8,128)}, f32[32,2048]{1,0:T(8,128)S(1)}, u32[]{:S(2)}, u32[]{:S(2)}) collective-permute-start(f32[32,2048]{1,0:T(8,128)} %vector_in.1), channel_id=1, source_target_pairs={{0,2},{1,3},{2,0},{3,1},{4,6},{5,7},{6,4},{7,5},{8,10},{9,11},{10,... | collective-permute-start | bytes 786440 | tf_op jit(solution)/shard_map/ppermute | solution.py:777
  3.6 0.0 collective-permute-start.1
  3.6 0.5 %collective-permute-start.3 = (f32[32,2048]{1,0:T(8,128)}, f32[32,2048]{1,0:T(8,128)S(1)}, u32[]{:S(2)}, u32[]{:S(2)}) collective-permute-start(f32[32,2048]{1,0:T(8,128)} %operating_in.1), channel_id=1, source_target_pairs={{0,1},{1,0},{2,3},{3,2},{4,5},{5,4},{6,7},{7,6},{8,9},{9,8},{10,11... | collective-permute-start | bytes 786440 | tf_op jit(solution)/shard_map/ppermute | solution.py:777
  4.1 1.7 %fetch.1 = (f32[32,2048]{1,0:T(8,128)S(1)}, bf16[2048,128]{1,0:T(8,128)(2,1)S(1)}, f32[1,1152]{1,0:T(1,128)S(1)}, f32[1,1152]{1,0:T(1,128)S(1)}, f32[1,2048]{1,0...) custom-call(f32[32,2048]{1,0:T(8,128)} %vector_in.1, ...), custom_call_target="tpu_custom_call" | custom-call | bytes 6000000 | tf_op jit(solution)/shard_map/fetch/pallas_call | solution.py:761
  5.9 4.4 %prepare.1 = (bf16[2176,1024]{1,0:T(8,128)(2,1)S(1)}, bf16[2176,1024]{1,0:T(8,128)(2,1)S(1)}) custom-call(s32[8,1152]{1,0:T(8,128)S(1)} %get-tuple-element.50.entry_rows, f32[8,1152]{1,0:T(8,128)S(1)} %get-tuple-element.51.weight_rows), custom_call_target="tpu_custom_call" | custom-call | bytes 18000000 | tf_op jit(solution)/shard_map/prepare/pallas_call | solution.py:761
  10.3 0.0 collective-permute-done.refs_1_
  10.3 0.1 collective-permute-start.2
  10.4 0.6 %prepare_cut.1 = (bf16[2176,128]{1,0:T(8,128)(2,1)S(1)}, bf16[2176,128]{1,0:T(8,128)(2,1)S(1)}, f32[128,128]{1,0:T(8,128)S(1)}) custom-call(f32[32,2048]{1,0:T(8,128)S(1)} %relay.3.after.refs_2_, s32[8,1152]{1,0:T(8,128)S(1)} %get-tuple-element.50.entry_rows, f32[8,1152]{1,0:T(8,128)S(1)} %get-tuple-element.51.weight_rows), custom_call_target="tpu_custom_call" | custom-call | bytes 3000000 | tf_op jit(solution)/shard_map/prepare_cut/pallas_call | solution.py:761
  11.0 0.0 collective-permute-done.3.near_operating
  11.0 1.0 %conductance.1.refs_6_.conductances = f32[64,2176]{1,0:T(8,128)S(1)} custom-call(s32[4]{0:T(128)S(4)} %get-tuple-element.47.place.refs_0_, f32[32,2048]{1,0:T(8,128)S(1)} %collective-permute-done.3.near_operating, f32[32,2048]{1,0:T(8,128)S(1)} %get-tuple-element.54.operating, f32[1,16]{1,0:T(1,128)S(1)} %get-tuple-element.55.table, ...), custom_call_target="tpu_custom_call" | custom-call | bytes 3000000 | tf_op jit(solution)/shard_map/conductance/pallas_call | solution.py:761
  12.0 0.0 collective-permute-done.1.refs_3_
  12.0 0.0 collective-permute-done.2.refs_4_
  12.0 1.5 %wave.1 = (bf16[128,2176]{1,0:T(8,128)(2,1)S(1)}, bf16[128,2176]{1,0:T(8,128)(2,1)S(1)}, f32[64,2176]{1,0:T(8,128)S(1)}, bf16[128,2048]{1,0:T(8,128)(2,1)S(1)}, ...) custom-call(s32[4]{0:T(128)S(4)} %get-tuple-element.47.place.refs_0_, ...), custom_call_target="tpu_custom_call" | custom-call | bytes 6000000 | tf_op jit(solution)/shard_map/wave/pallas_call | solution.py:761
  13.5 1.8 %collective-permute-start.5 = (f32[48,128]{1,0:T(8,128)S(1)}, f32[48,128]{1,0:T(8,128)S(1)}, u32[]{:S(2)}, u32[]{:S(2)}) collective-permute-start(f32[48,128]{1,0:T(8,128)S(1)} %get-tuple-element.69), channel_id=1, source_target_pairs={{0,4},{1,13},{2,6},{3,15},{4,0},{5,9},{6,2},{7,11},{8,12},{9,5},{1... | collective-permute-start | bytes 73736 | tf_op jit(solution)/shard_map/ppermute | solution.py:787
  15.3 2.6 %collective-permute-start.4 = (f32[48,128]{1,0:T(8,128)S(1)}, f32[48,128]{1,0:T(8,128)S(1)}, u32[]{:S(2)}, u32[]{:S(2)}) collective-permute-start(f32[48,128]{1,0:T(8,128)S(1)} %get-tuple-element.62), channel_id=1, source_target_pairs={{0,8},{1,9},{2,10},{3,11},{4,12},{5,13},{6,14},{7,15},{8,0},{9,1},... | collective-permute-start | bytes 73736 | tf_op jit(solution)/shard_map/ppermute | solution.py:787
  17.9 1.0 %local.1 = (f32[64,1024]{1,0:T(8,128)S(1)}, f32[64,1024]{1,0:T(8,128)S(1)}, f32[64,1024]{1,0:T(8,128)S(1)}, f32[64,1024]{1,0:T(8,128)S(1)}, f32[64,1024]{1,0:T(8,128)S(1)}) custom-call(bf16[128,2176]{1,0:T(8,128)(2,1)S(1)} %get-tuple-element.63.field_high, bf16[128,2176]{1,0:T(8,128)(2,1)S(1)} %get-tuple-element.64.field_low, ...), custom_call_target="tpu_custom_call" | custom-call | bytes 9000000 | tf_op jit(solution)/shard_map/local/pallas_call | solution.py:761
  18.9 0.0 collective-permute-done.5.refs_1_
  19.0 0.1 collective-permute-start.6
  19.0 0.8 %local_rest.1.refs_6_ = f32[64,512]{1,0:T(8,128)S(1)} custom-call(f32[64,1024]{1,0:T(8,128)S(1)} %get-tuple-element.71.load.refs_5_, bf16[128,2048]{1,0:T(8,128)(2,1)S(1)} %get-tuple-element.66.current, bf16[2176,1024]{1,0:T(8,128)(2,1)S(1)} %get-tuple-element.67.coupling_high.refs_9_, bf16[2176,1024]{1,0:T(8,128)(2,1)S(1)} %get-tuple-element.52.refs_0_.coupling_low.refs_10_), custom_call_target="tpu_custom_call" | custom-call | bytes 3000000 | tf_op jit(solution)/shard_map/local_rest/pallas_call | solution.py:761
  19.8 0.5 %collective-permute-done.4.refs_1_ = f32[48,128]{1,0:T(8,128)S(1)} collective-permute-done((f32[48,128]{1,0:T(8,128)S(1)}, f32[48,128]{1,0:T(8,128)S(1)}, u32[]{:S(2)}, u32[]{:S(2)}) %collective-permute-start.4) | collective-permute-done | bytes 24608 | tf_op jit(solution)/shard_map/ppermute | solution.py:787
  20.4 0.3 first.1
  20.7 0.9 %collective-permute-start.9 = (f32[64,1024]{1,0:T(8,128)S(1)}, f32[64,1024]{1,0:T(8,128)S(1)}, u32[]{:S(2)}, u32[]{:S(2)}) collective-permute-start(f32[64,1024]{1,0:T(8,128)S(1)} %get-tuple-element.75.refs_5_.image), channel_id=1, source_target_pairs={{0,1},{1,0},{2,3},{3,2},{4,5},{5,4},{6,7},{7,6},{8,9},{9,8},{10,11... | collective-permute-start | bytes 786440 | tf_op jit(solution)/shard_map/ppermute | solution.py:777
  21.6 1.5 %collective-permute-start.10 = (f32[8,1024]{1,0:T(8,128)S(1)}, f32[8,1024]{1,0:T(8,128)S(1)}, u32[]{:S(2)}, u32[]{:S(2)}) collective-permute-start(f32[8,1024]{1,0:T(8,128)S(1)} %get-tuple-element.85.own_sums), channel_id=1, source_target_pairs={{0,2},{1,3},{2,0},{3,1},{4,6},{5,7},{6,4},{7,5},{8,10},{9,11},{10,... | collective-permute-start | bytes 98312 | tf_op jit(solution)/shard_map/ppermute | solution.py:777
  23.1 0.8 %spread.1 = (f32[64,128]{1,0:T(8,128)S(1)}, f32[64,1024]{1,0:T(8,128)S(1)}, f32[64,1024]{1,0:T(8,128)S(1)}) custom-call(s32[4]{0:T(128)S(4)} %get-tuple-element.47.place.refs_0_, f32[48,128]{1,0:T(8,128)S(1)} %collective-permute-done.4.refs_1_, f32[48,128]{1,0:T(8,128)S(1)} %relay.4.refs_2_, f32[48,128]{1,0:T(8,128)S(1)} %collective-permute-done.6.refs_3_, ...), custom_call_target="tpu_custom_call" | custom-call | bytes 3000000 | tf_op jit(solution)/shard_map/spread/pallas_call | solution.py:761
  23.8 0.1 collective-permute-start.7
  23.9 2.0 %second.1 = (f32[64,1024]{1,0:T(8,128)S(1)}, f32[64,1024]{1,0:T(8,128)S(1)}, f32[64,1024]{1,0:T(8,128)S(1)}) custom-call(s32[4]{0:T(128)S(4)} %get-tuple-element.47.place.refs_0_, f32[64,128]{1,0:T(8,128)S(1)} %get-tuple-element.82.halo, f32[64,1024]{1,0:T(8,128)S(1)} %collective-permute-done.9.near_image, f32[64,1024]{1,0:T(8,128)S(1)} %get-tuple-element.75.refs_5_.image, ...), custom_call_target="tpu_custom_call" | custom-call | bytes 9000000 | tf_op jit(solution)/shard_map/second/pallas_call | solution.py:761
  26.0 0.0 collective-permute-done.10.far_sums.refs_0_
  26.0 0.5 %collective-permute-start.17 = (f32[64,1024]{1,0:T(8,128)S(1)}, f32[64,1024]{1,0:T(8,128)S(1)}, u32[]{:S(2)}, u32[]{:S(2)}) collective-permute-start(f32[64,1024]{1,0:T(8,128)S(1)} %relay.5), channel_id=1, source_target_pairs={{0,1},{1,0},{2,3},{3,2},{4,5},{5,4},{6,7},{7,6},{8,9},{9,8},{10,11... | collective-permute-start | bytes 786440 | tf_op jit(solution)/shard_map/ppermute | solution.py:777
  26.5 0.0 collective-permute-done.7.arrived
  26.6 0.6 %collective-permute-start.8 = (f32[32,2048]{1,0:T(8,128)S(1)}, f32[32,2048]{1,0:T(8,128)S(1)}, u32[]{:S(2)}, u32[]{:S(2)}) collective-permute-start(f32[32,2048]{1,0:T(8,128)S(1)} %get-tuple-element.80), channel_id=1, source_target_pairs={{0,2},{1,3},{2,0},{3,1},{4,6},{5,7},{6,4},{7,5},{8,10},{9,11},{10,... | collective-permute-start | bytes 786440 | tf_op jit(solution)/shard_map/ppermute | solution.py:777
  27.2 0.8 %products.1.refs_0_.after = f32[16,128]{1,0:T(8,128)S(1)} custom-call(s32[4]{0:T(128)S(4)} %get-tuple-element.47.place.refs_0_, f32[32,2048]{1,0:T(8,128)S(1)} %get-tuple-element.48.refs_1_.vector, f32[64,1024]{1,0:T(8,128)S(1)} %get-tuple-element.74.after.load, f32[64,1024]{1,0:T(8,128)S(1)} %get-tuple-element.83.second_load, ...), custom_call_target="tpu_custom_call" | custom-call | bytes 3000000 | tf_op jit(solution)/shard_map/products/pallas_call | solution.py:761
  28.0 0.0 collective-permute-done.17.arrived
  28.0 1.5 %collective-permute-start.18 = (f32[32,2048]{1,0:T(8,128)S(1)}, f32[32,2048]{1,0:T(8,128)S(1)}, u32[]{:S(2)}, u32[]{:S(2)}) collective-permute-start(f32[32,2048]{1,0:T(8,128)S(1)} %get-tuple-element.91), channel_id=1, source_target_pairs={{0,2},{1,3},{2,0},{3,1},{4,6},{5,7},{6,4},{7,5},{8,10},{9,11},{10,... | collective-permute-start | bytes 786440 | tf_op jit(solution)/shard_map/ppermute | solution.py:777
  29.6 2.5 %collective-permute-start.13 = (f32[16,128]{1,0:T(8,128)S(1)}, f32[16,128]{1,0:T(8,128)S(1)}, u32[]{:S(2)}, u32[]{:S(2)}) collective-permute-start(f32[16,128]{1,0:T(8,128)S(1)} %products.1.refs_0_.after), channel_id=1, source_target_pairs={{0,12},{4,8},{8,4},{12,0},{1,13},{5,9},{9,5},{13,1},{2,14},{6,10},... | collective-permute-start | bytes 24584 | tf_op jit(solution)/shard_map/ppermute | solution.py:808
  32.0 0.0 collective-permute-start.12
  32.0 1.9 %collective-permute-start.11 = (f32[16,128]{1,0:T(8,128)S(1)}, f32[16,128]{1,0:T(8,128)S(1)}, u32[]{:S(2)}, u32[]{:S(2)}) collective-permute-start(f32[16,128]{1,0:T(8,128)S(1)} %products.1.refs_0_.after), channel_id=1, source_target_pairs={{0,4},{4,0},{8,12},{12,8},{1,5},{5,1},{9,13},{13,9},{2,6},{6,2},{1... | collective-permute-start | bytes 24584 | tf_op jit(solution)/shard_map/ppermute | solution.py:808
  34.0 1.1 %collective-permute-done.13.refs_3_ = f32[16,128]{1,0:T(8,128)S(1)} collective-permute-done((f32[16,128]{1,0:T(8,128)S(1)}, f32[16,128]{1,0:T(8,128)S(1)}, u32[]{:S(2)}, u32[]{:S(2)}) %collective-permute-start.13) | collective-permute-done | bytes 8224 | tf_op jit(solution)/shard_map/ppermute | solution.py:808
  35.0 1.6 %collective-permute-done.12.refs_2_ = f32[16,128]{1,0:T(8,128)S(1)} collective-permute-done((f32[16,128]{1,0:T(8,128)S(1)}, f32[16,128]{1,0:T(8,128)S(1)}, u32[]{:S(2)}, u32[]{:S(2)}) %collective-permute-start.12) | collective-permute-done | bytes 8224 | tf_op jit(solution)/shard_map/ppermute | solution.py:808
  36.6 0.0 collective-permute-done.11.refs_1_
  36.6 0.1 collective-permute-start.16
  36.7 0.6 %collective-permute-start.15 = (f32[16,128]{1,0:T(8,128)S(1)}, f32[16,128]{1,0:T(8,128)S(1)}, u32[]{:S(2)}, u32[]{:S(2)}) collective-permute-start(f32[16,128]{1,0:T(8,128)S(1)} %sum.2.refs_0_), channel_id=1, source_target_pairs={{0,2},{1,3},{2,0},{3,1},{4,6},{5,7},{6,4},{7,5},{8,10},{9,11},{10,... | collective-permute-start | bytes 24584 | tf_op jit(solution)/shard_map/ppermute | solution.py:808
  37.3 1.2 %collective-permute-start.14 = (f32[16,128]{1,0:T(8,128)S(1)}, f32[16,128]{1,0:T(8,128)S(1)}, u32[]{:S(2)}, u32[]{:S(2)}) collective-permute-start(f32[16,128]{1,0:T(8,128)S(1)} %sum.2.refs_0_), channel_id=1, source_target_pairs={{0,1},{1,0},{2,3},{3,2},{4,5},{5,4},{6,7},{7,6},{8,9},{9,8},{10,11... | collective-permute-start | bytes 24584 | tf_op jit(solution)/shard_map/ppermute | solution.py:808
  38.5 0.0 collective-permute-done.8.refs_1_
  38.5 0.5 %settle.1 = (f32[32,2048]{1,0:T(8,128)S(1)}, f32[32,2048]{1,0:T(8,128)S(1)}, f32[8,128]{1,0:T(8,128)S(1)}) custom-call(s32[4]{0:T(128)S(4)} %get-tuple-element.47.place.refs_0_, f32[32,2048]{1,0:T(8,128)S(1)} %get-tuple-element.48.refs_1_.vector, f32[1,2048]{1,0:T(1,128)S(1)} %get-tuple-element.49.capacity, f32[32,2048]{1,0:T(8,128)S(1)} %get-tuple-element.79.refs_0_, ...), custom_call_target="tpu_custom_call" | custom-call | bytes 3000000 | tf_op jit(solution)/shard_map/settle/pallas_call | solution.py:761
  39.0 0.9 %collective-permute-done.16.refs_3_ = f32[16,128]{1,0:T(8,128)S(1)} collective-permute-done((f32[16,128]{1,0:T(8,128)S(1)}, f32[16,128]{1,0:T(8,128)S(1)}, u32[]{:S(2)}, u32[]{:S(2)}) %collective-permute-start.16) | collective-permute-done | bytes 8224 | tf_op jit(solution)/shard_map/ppermute | solution.py:808
  39.9 1.0 %collective-permute-done.15.refs_2_ = f32[16,128]{1,0:T(8,128)S(1)} collective-permute-done((f32[16,128]{1,0:T(8,128)S(1)}, f32[16,128]{1,0:T(8,128)S(1)}, u32[]{:S(2)}, u32[]{:S(2)}) %collective-permute-start.15) | collective-permute-done | bytes 8224 | tf_op jit(solution)/shard_map/ppermute | solution.py:808
  40.9 0.0 collective-permute-done.18.refs_1_
  40.9 1.0 %last.1 = (f32[32,2048]{1,0:T(8,128)}, f32[32,2048]{1,0:T(8,128)}) custom-call(f32[16,128]{1,0:T(8,128)S(1)} %sum.3.gathered, f32[32,2048]{1,0:T(8,128)S(1)} %get-tuple-element.48.refs_1_.vector, f32[32,2048]{1,0:T(8,128)S(1)} %get-tuple-element.86.answer, f32[32,2048]{1,0:T(8,128)S(1)} %get-tuple-element.87.slope, ...), custom_call_target="tpu_custom_call" | custom-call | tf_op jit(solution)/shard_map/last/pallas_call | solution.py:1053
  (10 shorter events, 0.2 us)
Async XLA Ops:
  0.6 9.6 %collective-permute-start = (f32[32,2048]{1,0:T(8,128)}, f32[32,2048]{1,0:T(8,128)S(1)}, u32[]{:S(2)}, u32[]{:S(2)}) collective-permute-start(f32[32,2048]{1,0:T(8,128)} %vector_in.1), channel_id=1, source_target_pairs={{0,2},{1,3},{2,0},{3,1},{4,6},{5,7},{6,4},{7,5},{8,10},{9,11},{10,... | collective-permute-start | bytes 786440 | tf_op jit(solution)/shard_map/ppermute | solution.py:777
  3.6 8.4 %collective-permute-start.1 = (f32[32,2048]{1,0:T(8,128)}, f32[32,2048]{1,0:T(8,128)S(1)}, u32[]{:S(2)}, u32[]{:S(2)}) collective-permute-start(f32[32,2048]{1,0:T(8,128)} %vector_in.1), channel_id=1, source_target_pairs={{0,1},{1,0},{2,3},{3,2},{4,5},{5,4},{6,7},{7,6},{8,9},{9,8},{10,11... | collective-permute-start | bytes 786440 | tf_op jit(solution)/shard_map/ppermute | solution.py:777
  3.6 7.4 %collective-permute-start.3 = (f32[32,2048]{1,0:T(8,128)}, f32[32,2048]{1,0:T(8,128)S(1)}, u32[]{:S(2)}, u32[]{:S(2)}) collective-permute-start(f32[32,2048]{1,0:T(8,128)} %operating_in.1), channel_id=1, source_target_pairs={{0,1},{1,0},{2,3},{3,2},{4,5},{5,4},{6,7},{7,6},{8,9},{9,8},{10,11... | collective-permute-start | bytes 786440 | tf_op jit(solution)/shard_map/ppermute | solution.py:777
  10.3 1.7 %collective-permute-start.2 = (f32[32,2048]{1,0:T(8,128)S(1)}, f32[32,2048]{1,0:T(8,128)S(1)}, u32[]{:S(2)}, u32[]{:S(2)}) collective-permute-start(f32[32,2048]{1,0:T(8,128)S(1)} %relay.3.after.refs_2_), channel_id=1, source_target_pairs={{0,1},{1,0},{2,3},{3,2},{4,5},{5,4},{6,7},{7,6},{8,9},{9,8},{10,11... | collective-permute-start | bytes 786440 | tf_op jit(solution)/shard_map/ppermute | solution.py:777
  13.5 5.4 %collective-permute-start.5 = (f32[48,128]{1,0:T(8,128)S(1)}, f32[48,128]{1,0:T(8,128)S(1)}, u32[]{:S(2)}, u32[]{:S(2)}) collective-permute-start(f32[48,128]{1,0:T(8,128)S(1)} %get-tuple-element.69), channel_id=1, source_target_pairs={{0,4},{1,13},{2,6},{3,15},{4,0},{5,9},{6,2},{7,11},{8,12},{9,5},{1... | collective-permute-start | bytes 73736 | tf_op jit(solution)/shard_map/ppermute | solution.py:787
  15.3 5.1 %collective-permute-start.4 = (f32[48,128]{1,0:T(8,128)S(1)}, f32[48,128]{1,0:T(8,128)S(1)}, u32[]{:S(2)}, u32[]{:S(2)}) collective-permute-start(f32[48,128]{1,0:T(8,128)S(1)} %get-tuple-element.62), channel_id=1, source_target_pairs={{0,8},{1,9},{2,10},{3,11},{4,12},{5,13},{6,14},{7,15},{8,0},{9,1},... | collective-permute-start | bytes 73736 | tf_op jit(solution)/shard_map/ppermute | solution.py:787
  19.0 1.4 %collective-permute-start.6 = (f32[48,128]{1,0:T(8,128)S(1)}, f32[48,128]{1,0:T(8,128)S(1)}, u32[]{:S(2)}, u32[]{:S(2)}) collective-permute-start(f32[48,128]{1,0:T(8,128)S(1)} %relay.4.refs_2_), channel_id=1, source_target_pairs={{0,1},{1,0},{2,3},{3,2},{4,5},{5,4},{6,7},{7,6},{8,9},{9,8},{10,11... | collective-permute-start | bytes 73736 | tf_op jit(solution)/shard_map/ppermute | solution.py:777
  20.7 3.2 %collective-permute-start.9 = (f32[64,1024]{1,0:T(8,128)S(1)}, f32[64,1024]{1,0:T(8,128)S(1)}, u32[]{:S(2)}, u32[]{:S(2)}) collective-permute-start(f32[64,1024]{1,0:T(8,128)S(1)} %get-tuple-element.75.refs_5_.image), channel_id=1, source_target_pairs={{0,1},{1,0},{2,3},{3,2},{4,5},{5,4},{6,7},{7,6},{8,9},{9,8},{10,11... | collective-permute-start | bytes 786440 | tf_op jit(solution)/shard_map/ppermute | solution.py:777
  21.6 4.4 %collective-permute-start.10 = (f32[8,1024]{1,0:T(8,128)S(1)}, f32[8,1024]{1,0:T(8,128)S(1)}, u32[]{:S(2)}, u32[]{:S(2)}) collective-permute-start(f32[8,1024]{1,0:T(8,128)S(1)} %get-tuple-element.85.own_sums), channel_id=1, source_target_pairs={{0,2},{1,3},{2,0},{3,1},{4,6},{5,7},{6,4},{7,5},{8,10},{9,11},{10,... | collective-permute-start | bytes 98312 | tf_op jit(solution)/shard_map/ppermute | solution.py:777
  23.8 2.7 %collective-permute-start.7 = (f32[64,1024]{1,0:T(8,128)S(1)}, f32[64,1024]{1,0:T(8,128)S(1)}, u32[]{:S(2)}, u32[]{:S(2)}) collective-permute-start(f32[64,1024]{1,0:T(8,128)S(1)} %get-tuple-element.78), channel_id=1, source_target_pairs={{0,1},{1,0},{2,3},{3,2},{4,5},{5,4},{6,7},{7,6},{8,9},{9,8},{10,11... | collective-permute-start | bytes 786440 | tf_op jit(solution)/shard_map/ppermute | solution.py:777
  26.0 2.0 %collective-permute-start.17 = (f32[64,1024]{1,0:T(8,128)S(1)}, f32[64,1024]{1,0:T(8,128)S(1)}, u32[]{:S(2)}, u32[]{:S(2)}) collective-permute-start(f32[64,1024]{1,0:T(8,128)S(1)} %relay.5), channel_id=1, source_target_pairs={{0,1},{1,0},{2,3},{3,2},{4,5},{5,4},{6,7},{7,6},{8,9},{9,8},{10,11... | collective-permute-start | bytes 786440 | tf_op jit(solution)/shard_map/ppermute | solution.py:777
  26.6 11.9 %collective-permute-start.8 = (f32[32,2048]{1,0:T(8,128)S(1)}, f32[32,2048]{1,0:T(8,128)S(1)}, u32[]{:S(2)}, u32[]{:S(2)}) collective-permute-start(f32[32,2048]{1,0:T(8,128)S(1)} %get-tuple-element.80), channel_id=1, source_target_pairs={{0,2},{1,3},{2,0},{3,1},{4,6},{5,7},{6,4},{7,5},{8,10},{9,11},{10,... | collective-permute-start | bytes 786440 | tf_op jit(solution)/shard_map/ppermute | solution.py:777
  28.0 12.8 %collective-permute-start.18 = (f32[32,2048]{1,0:T(8,128)S(1)}, f32[32,2048]{1,0:T(8,128)S(1)}, u32[]{:S(2)}, u32[]{:S(2)}) collective-permute-start(f32[32,2048]{1,0:T(8,128)S(1)} %get-tuple-element.91), channel_id=1, source_target_pairs={{0,2},{1,3},{2,0},{3,1},{4,6},{5,7},{6,4},{7,5},{8,10},{9,11},{10,... | collective-permute-start | bytes 786440 | tf_op jit(solution)/shard_map/ppermute | solution.py:777
  29.6 5.4 %collective-permute-start.13 = (f32[16,128]{1,0:T(8,128)S(1)}, f32[16,128]{1,0:T(8,128)S(1)}, u32[]{:S(2)}, u32[]{:S(2)}) collective-permute-start(f32[16,128]{1,0:T(8,128)S(1)} %products.1.refs_0_.after), channel_id=1, source_target_pairs={{0,12},{4,8},{8,4},{12,0},{1,13},{5,9},{9,5},{13,1},{2,14},{6,10},... | collective-permute-start | bytes 24584 | tf_op jit(solution)/shard_map/ppermute | solution.py:808
  32.0 4.5 %collective-permute-start.12 = (f32[16,128]{1,0:T(8,128)S(1)}, f32[16,128]{1,0:T(8,128)S(1)}, u32[]{:S(2)}, u32[]{:S(2)}) collective-permute-start(f32[16,128]{1,0:T(8,128)S(1)} %products.1.refs_0_.after), channel_id=1, source_target_pairs={{0,8},{4,12},{8,0},{12,4},{1,9},{5,13},{9,1},{13,5},{2,10},{6,14},... | collective-permute-start | bytes 24584 | tf_op jit(solution)/shard_map/ppermute | solution.py:808
  32.0 4.5 %collective-permute-start.11 = (f32[16,128]{1,0:T(8,128)S(1)}, f32[16,128]{1,0:T(8,128)S(1)}, u32[]{:S(2)}, u32[]{:S(2)}) collective-permute-start(f32[16,128]{1,0:T(8,128)S(1)} %products.1.refs_0_.after), channel_id=1, source_target_pairs={{0,4},{4,0},{8,12},{12,8},{1,5},{5,1},{9,13},{13,9},{2,6},{6,2},{1... | collective-permute-start | bytes 24584 | tf_op jit(solution)/shard_map/ppermute | solution.py:808
  36.6 3.3 %collective-permute-start.16 = (f32[16,128]{1,0:T(8,128)S(1)}, f32[16,128]{1,0:T(8,128)S(1)}, u32[]{:S(2)}, u32[]{:S(2)}) collective-permute-start(f32[16,128]{1,0:T(8,128)S(1)} %sum.2.refs_0_), channel_id=1, source_target_pairs={{0,3},{1,2},{2,1},{3,0},{4,7},{5,6},{6,5},{7,4},{8,11},{9,10},{10,... | collective-permute-start | bytes 24584 | tf_op jit(solution)/shard_map/ppermute | solution.py:808
  36.7 4.2 %collective-permute-start.15 = (f32[16,128]{1,0:T(8,128)S(1)}, f32[16,128]{1,0:T(8,128)S(1)}, u32[]{:S(2)}, u32[]{:S(2)}) collective-permute-start(f32[16,128]{1,0:T(8,128)S(1)} %sum.2.refs_0_), channel_id=1, source_target_pairs={{0,2},{1,3},{2,0},{3,1},{4,6},{5,7},{6,4},{7,5},{8,10},{9,11},{10,... | collective-permute-start | bytes 24584 | tf_op jit(solution)/shard_map/ppermute | solution.py:808
  37.3 3.6 %collective-permute-start.14 = (f32[16,128]{1,0:T(8,128)S(1)}, f32[16,128]{1,0:T(8,128)S(1)}, u32[]{:S(2)}, u32[]{:S(2)}) collective-permute-start(f32[16,128]{1,0:T(8,128)S(1)} %sum.2.refs_0_), channel_id=1, source_target_pairs={{0,1},{1,0},{2,3},{3,2},{4,5},{5,4},{6,7},{7,6},{8,9},{9,8},{10,11... | collective-permute-start | bytes 24584 | tf_op jit(solution)/shard_map/ppermute | solution.py:808

commit v10 on v9

--- a/solution.py
+++ b/solution.py
@@ -387,18 +387,18 @@
     for index in range(pieces):
         at = slice(index * rows, (index + 1) * rows)
         parts = split_three(vectors[index][...])
-        field_high[at, :nodes], field_low[at, :nodes], field_last[at, :nodes] = parts
+        field_high[at, :nodes], field_low[at, :nodes], field_last[at] = parts
     field_high[:, nodes:] = dot(field_high[:, :nodes], picked[...]).astype(BF16)
     field_low[:, nodes:] = dot(field_low[:, :nodes], picked[...]).astype(BF16)
-    field_last[:, nodes:] = dot(field_last[:, :nodes], picked[...]).astype(BF16)
-    wave[...] = dot_three(
+    wave[:, :nodes] = dot_three(
         [forward[part, :times] for part in range(3)],
-        (field_high[...], field_low[...], field_last[...]),
-    )
-    slope = dot_split(
-        (forward[0, times : 2 * times], forward[1, times : 2 * times]),
+        (field_high[:, :nodes], field_low[:, :nodes], field_last[...]),
+    )
+    both = dot_split(
+        (forward[0, : 2 * times], forward[1, : 2 * times]),
         (field_high[:, nodes:], field_low[:, nodes:]),
     )
+    wave[:, nodes:], slope = both[:times], both[times:]
     high, low = split(conductances[:, :nodes] * wave[:, :nodes])
     current[:times] = high
     current[times:] = low
@@ -951,7 +951,7 @@
             ((lanes, times), F32),
         ]
         + [(packet, F32)] * len(packet_steps(steps)),
-        scratch=[pltpu.VMEM((length, sources), BF16)],
+        scratch=[pltpu.VMEM((length, nodes), BF16)],
         micros=2,
     )
     arrived = [trade(packet, masks) for packet, masks in zip(sent, packet_steps(steps))]

time: 42.1 us -> 41.9 us (level)
  no operation moved by 1% of the time
where the time goes in v10:
time: 41.9 us; the launch traced here: 41.8 us
  starting transfers between devices  19.4 us (46%)
  Pallas kernels  16.5 us (39%)
  waiting for transfers between devices  5.03 us (12%)
  between operations  0.84 us (2%)
    pallas_call x19, Pallas kernels, run(): pl.pallas_call(kernel, out_shape=[space(shape, dtype) for space, (shape,...  15.4 us
    ppermute x11, starting transfers between devices, swap(): lax.ppermute(value, 'samples', [(at, at ^ mask) for at in range(count)])  8.78 us
    ppermute x6, starting transfers between devices, exchange(): lax.ppermute(value, axis, [(at, at ^ step * stride) for at in range(count)])  6.31 us
    ppermute x6, waiting for transfers between devices, exchange(): lax.ppermute(value, axis, [(at, at ^ step * stride) for at in range(count)])  4.45 us
    ppermute x2, starting transfers between devices, trade(): return lax.ppermute(value, ('nodes', 'samples'), pairs)  4.34 us
    pallas_call x1, Pallas kernels, shards(): pl.pallas_call(functools.partial(last_kernel, entries=entries, devices=fl...  1.02 us
  transfers between devices with their start and end apart: 19, of which 5 were waited for; matrix products, arithmetic and copies ran while one was open for 0% of the time, Pallas kernels for 33%

profile of v10, /device:TPU:0, one launch (start us, length us, event | category | flops | bytes accessed | tf_op | source)
XLA Modules:
  0.0 41.8 jit_solution(13444507221872479414)
XLA Ops:
  0.6 3.0 %collective-permute-start = (f32[32,2048]{1,0:T(8,128)}, f32[32,2048]{1,0:T(8,128)S(1)}, u32[]{:S(2)}, u32[]{:S(2)}) collective-permute-start(f32[32,2048]{1,0:T(8,128)} %vector_in.1), channel_id=1, source_target_pairs={{0,2},{1,3},{2,0},{3,1},{4,6},{5,7},{6,4},{7,5},{8,10},{9,11},{10,... | collective-permute-start | bytes 786440 | tf_op jit(solution)/shard_map/ppermute | solution.py:777
  3.6 0.0 collective-permute-start.1
  3.6 0.5 %collective-permute-start.3 = (f32[32,2048]{1,0:T(8,128)}, f32[32,2048]{1,0:T(8,128)S(1)}, u32[]{:S(2)}, u32[]{:S(2)}) collective-permute-start(f32[32,2048]{1,0:T(8,128)} %operating_in.1), channel_id=1, source_target_pairs={{0,1},{1,0},{2,3},{3,2},{4,5},{5,4},{6,7},{7,6},{8,9},{9,8},{10,11... | collective-permute-start | bytes 786440 | tf_op jit(solution)/shard_map/ppermute | solution.py:777
  4.1 1.7 %fetch.1 = (f32[32,2048]{1,0:T(8,128)S(1)}, bf16[2048,128]{1,0:T(8,128)(2,1)S(1)}, f32[1,1152]{1,0:T(1,128)S(1)}, f32[1,1152]{1,0:T(1,128)S(1)}, f32[1,2048]{1,0...) custom-call(f32[32,2048]{1,0:T(8,128)} %vector_in.1, ...), custom_call_target="tpu_custom_call" | custom-call | bytes 6000000 | tf_op jit(solution)/shard_map/fetch/pallas_call | solution.py:761
  5.9 4.4 %prepare.1 = (bf16[2176,1024]{1,0:T(8,128)(2,1)S(1)}, bf16[2176,1024]{1,0:T(8,128)(2,1)S(1)}) custom-call(s32[8,1152]{1,0:T(8,128)S(1)} %get-tuple-element.50.entry_rows, f32[8,1152]{1,0:T(8,128)S(1)} %get-tuple-element.51.weight_rows), custom_call_target="tpu_custom_call" | custom-call | bytes 18000000 | tf_op jit(solution)/shard_map/prepare/pallas_call | solution.py:761
  10.3 0.0 collective-permute-done.refs_1_
  10.3 0.1 collective-permute-start.2
  10.4 0.6 %prepare_cut.1 = (bf16[2176,128]{1,0:T(8,128)(2,1)S(1)}, bf16[2176,128]{1,0:T(8,128)(2,1)S(1)}, f32[128,128]{1,0:T(8,128)S(1)}) custom-call(f32[32,2048]{1,0:T(8,128)S(1)} %relay.3.after.refs_2_, s32[8,1152]{1,0:T(8,128)S(1)} %get-tuple-element.50.entry_rows, f32[8,1152]{1,0:T(8,128)S(1)} %get-tuple-element.51.weight_rows), custom_call_target="tpu_custom_call" | custom-call | bytes 3000000 | tf_op jit(solution)/shard_map/prepare_cut/pallas_call | solution.py:761
  11.0 0.0 collective-permute-done.3.near_operating
  11.0 1.0 %conductance.1.refs_6_.conductances = f32[64,2176]{1,0:T(8,128)S(1)} custom-call(s32[4]{0:T(128)S(4)} %get-tuple-element.47.place.refs_0_, f32[32,2048]{1,0:T(8,128)S(1)} %collective-permute-done.3.near_operating, f32[32,2048]{1,0:T(8,128)S(1)} %get-tuple-element.54.operating, f32[1,16]{1,0:T(1,128)S(1)} %get-tuple-element.55.table, ...), custom_call_target="tpu_custom_call" | custom-call | bytes 3000000 | tf_op jit(solution)/shard_map/conductance/pallas_call | solution.py:761
  12.0 0.0 collective-permute-done.1.refs_3_
  12.0 0.0 collective-permute-done.2.refs_4_
  12.0 1.4 %wave.1 = (bf16[128,2176]{1,0:T(8,128)(2,1)S(1)}, bf16[128,2176]{1,0:T(8,128)(2,1)S(1)}, f32[64,2176]{1,0:T(8,128)S(1)}, bf16[128,2048]{1,0:T(8,128)(2,1)S(1)}, ...) custom-call(s32[4]{0:T(128)S(4)} %get-tuple-element.47.place.refs_0_, ...), custom_call_target="tpu_custom_call" | custom-call | bytes 6000000 | tf_op jit(solution)/shard_map/wave/pallas_call | solution.py:761
  13.4 1.8 %collective-permute-start.5 = (f32[48,128]{1,0:T(8,128)S(1)}, f32[48,128]{1,0:T(8,128)S(1)}, u32[]{:S(2)}, u32[]{:S(2)}) collective-permute-start(f32[48,128]{1,0:T(8,128)S(1)} %get-tuple-element.69), channel_id=1, source_target_pairs={{0,4},{1,13},{2,6},{3,15},{4,0},{5,9},{6,2},{7,11},{8,12},{9,5},{1... | collective-permute-start | bytes 73736 | tf_op jit(solution)/shard_map/ppermute | solution.py:787
  15.2 2.6 %collective-permute-start.4 = (f32[48,128]{1,0:T(8,128)S(1)}, f32[48,128]{1,0:T(8,128)S(1)}, u32[]{:S(2)}, u32[]{:S(2)}) collective-permute-start(f32[48,128]{1,0:T(8,128)S(1)} %get-tuple-element.62), channel_id=1, source_target_pairs={{0,8},{1,9},{2,10},{3,11},{4,12},{5,13},{6,14},{7,15},{8,0},{9,1},... | collective-permute-start | bytes 73736 | tf_op jit(solution)/shard_map/ppermute | solution.py:787
  17.7 1.0 %local.1 = (f32[64,1024]{1,0:T(8,128)S(1)}, f32[64,1024]{1,0:T(8,128)S(1)}, f32[64,1024]{1,0:T(8,128)S(1)}, f32[64,1024]{1,0:T(8,128)S(1)}, f32[64,1024]{1,0:T(8,128)S(1)}) custom-call(bf16[128,2176]{1,0:T(8,128)(2,1)S(1)} %get-tuple-element.63.field_high, bf16[128,2176]{1,0:T(8,128)(2,1)S(1)} %get-tuple-element.64.field_low, ...), custom_call_target="tpu_custom_call" | custom-call | bytes 9000000 | tf_op jit(solution)/shard_map/local/pallas_call | solution.py:761
  18.8 0.0 collective-permute-done.5.refs_1_
  18.8 0.1 collective-permute-start.6
  18.9 0.8 %local_rest.1.refs_6_ = f32[64,512]{1,0:T(8,128)S(1)} custom-call(f32[64,1024]{1,0:T(8,128)S(1)} %get-tuple-element.71.load.refs_5_, bf16[128,2048]{1,0:T(8,128)(2,1)S(1)} %get-tuple-element.66.current, bf16[2176,1024]{1,0:T(8,128)(2,1)S(1)} %get-tuple-element.67.coupling_high.refs_9_, bf16[2176,1024]{1,0:T(8,128)(2,1)S(1)} %get-tuple-element.52.refs_0_.coupling_low.refs_10_), custom_call_target="tpu_custom_call" | custom-call | bytes 3000000 | tf_op jit(solution)/shard_map/local_rest/pallas_call | solution.py:761
  19.7 0.5 %collective-permute-done.4.refs_1_ = f32[48,128]{1,0:T(8,128)S(1)} collective-permute-done((f32[48,128]{1,0:T(8,128)S(1)}, f32[48,128]{1,0:T(8,128)S(1)}, u32[]{:S(2)}, u32[]{:S(2)}) %collective-permute-start.4) | collective-permute-done | bytes 24608 | tf_op jit(solution)/shard_map/ppermute | solution.py:787
  20.2 0.0 collective-permute-done.6.refs_3_
  20.2 0.3 first.1
  20.6 0.9 %collective-permute-start.9 = (f32[64,1024]{1,0:T(8,128)S(1)}, f32[64,1024]{1,0:T(8,128)S(1)}, u32[]{:S(2)}, u32[]{:S(2)}) collective-permute-start(f32[64,1024]{1,0:T(8,128)S(1)} %get-tuple-element.75.refs_5_.image), channel_id=1, source_target_pairs={{0,1},{1,0},{2,3},{3,2},{4,5},{5,4},{6,7},{7,6},{8,9},{9,8},{10,11... | collective-permute-start | bytes 786440 | tf_op jit(solution)/shard_map/ppermute | solution.py:777
  21.4 1.5 %collective-permute-start.10 = (f32[8,1024]{1,0:T(8,128)S(1)}, f32[8,1024]{1,0:T(8,128)S(1)}, u32[]{:S(2)}, u32[]{:S(2)}) collective-permute-start(f32[8,1024]{1,0:T(8,128)S(1)} %get-tuple-element.85.own_sums), channel_id=1, source_target_pairs={{0,2},{1,3},{2,0},{3,1},{4,6},{5,7},{6,4},{7,5},{8,10},{9,11},{10,... | collective-permute-start | bytes 98312 | tf_op jit(solution)/shard_map/ppermute | solution.py:777
  22.9 0.8 %spread.1 = (f32[64,128]{1,0:T(8,128)S(1)}, f32[64,1024]{1,0:T(8,128)S(1)}, f32[64,1024]{1,0:T(8,128)S(1)}) custom-call(s32[4]{0:T(128)S(4)} %get-tuple-element.47.place.refs_0_, f32[48,128]{1,0:T(8,128)S(1)} %collective-permute-done.4.refs_1_, f32[48,128]{1,0:T(8,128)S(1)} %relay.4.refs_2_, f32[48,128]{1,0:T(8,128)S(1)} %collective-permute-done.6.refs_3_, ...), custom_call_target="tpu_custom_call" | custom-call | bytes 3000000 | tf_op jit(solution)/shard_map/spread/pallas_call | solution.py:761
  23.7 0.1 collective-permute-start.7
  23.8 0.0 collective-permute-done.9.near_image
  23.8 2.0 %second.1 = (f32[64,1024]{1,0:T(8,128)S(1)}, f32[64,1024]{1,0:T(8,128)S(1)}, f32[64,1024]{1,0:T(8,128)S(1)}) custom-call(s32[4]{0:T(128)S(4)} %get-tuple-element.47.place.refs_0_, f32[64,128]{1,0:T(8,128)S(1)} %get-tuple-element.82.halo, f32[64,1024]{1,0:T(8,128)S(1)} %collective-permute-done.9.near_image, f32[64,1024]{1,0:T(8,128)S(1)} %get-tuple-element.75.refs_5_.image, ...), custom_call_target="tpu_custom_call" | custom-call | bytes 9000000 | tf_op jit(solution)/shard_map/second/pallas_call | solution.py:761
  25.8 0.0 collective-permute-done.10.far_sums.refs_0_
  25.8 0.6 %collective-permute-start.17 = (f32[64,1024]{1,0:T(8,128)S(1)}, f32[64,1024]{1,0:T(8,128)S(1)}, u32[]{:S(2)}, u32[]{:S(2)}) collective-permute-start(f32[64,1024]{1,0:T(8,128)S(1)} %relay.5), channel_id=1, source_target_pairs={{0,1},{1,0},{2,3},{3,2},{4,5},{5,4},{6,7},{7,6},{8,9},{9,8},{10,11... | collective-permute-start | bytes 786440 | tf_op jit(solution)/shard_map/ppermute | solution.py:777
  26.4 0.0 collective-permute-done.7.arrived
  26.4 0.6 %collective-permute-start.8 = (f32[32,2048]{1,0:T(8,128)S(1)}, f32[32,2048]{1,0:T(8,128)S(1)}, u32[]{:S(2)}, u32[]{:S(2)}) collective-permute-start(f32[32,2048]{1,0:T(8,128)S(1)} %get-tuple-element.80), channel_id=1, source_target_pairs={{0,2},{1,3},{2,0},{3,1},{4,6},{5,7},{6,4},{7,5},{8,10},{9,11},{10,... | collective-permute-start | bytes 786440 | tf_op jit(solution)/shard_map/ppermute | solution.py:777
  27.1 0.8 %products.1.refs_0_.after = f32[16,128]{1,0:T(8,128)S(1)} custom-call(s32[4]{0:T(128)S(4)} %get-tuple-element.47.place.refs_0_, f32[32,2048]{1,0:T(8,128)S(1)} %get-tuple-element.48.refs_1_.vector, f32[64,1024]{1,0:T(8,128)S(1)} %get-tuple-element.74.after.load, f32[64,1024]{1,0:T(8,128)S(1)} %get-tuple-element.83.second_load, ...), custom_call_target="tpu_custom_call" | custom-call | bytes 3000000 | tf_op jit(solution)/shard_map/products/pallas_call | solution.py:761
  27.9 1.5 %collective-permute-start.18 = (f32[32,2048]{1,0:T(8,128)S(1)}, f32[32,2048]{1,0:T(8,128)S(1)}, u32[]{:S(2)}, u32[]{:S(2)}) collective-permute-start(f32[32,2048]{1,0:T(8,128)S(1)} %get-tuple-element.91), channel_id=1, source_target_pairs={{0,2},{1,3},{2,0},{3,1},{4,6},{5,7},{6,4},{7,5},{8,10},{9,11},{10,... | collective-permute-start | bytes 786440 | tf_op jit(solution)/shard_map/ppermute | solution.py:777
  29.4 2.5 %collective-permute-start.13 = (f32[16,128]{1,0:T(8,128)S(1)}, f32[16,128]{1,0:T(8,128)S(1)}, u32[]{:S(2)}, u32[]{:S(2)}) collective-permute-start(f32[16,128]{1,0:T(8,128)S(1)} %products.1.refs_0_.after), channel_id=1, source_target_pairs={{0,12},{4,8},{8,4},{12,0},{1,13},{5,9},{9,5},{13,1},{2,14},{6,10},... | collective-permute-start | bytes 24584 | tf_op jit(solution)/shard_map/ppermute | solution.py:808
  31.9 1.9 %collective-permute-start.11 = (f32[16,128]{1,0:T(8,128)S(1)}, f32[16,128]{1,0:T(8,128)S(1)}, u32[]{:S(2)}, u32[]{:S(2)}) collective-permute-start(f32[16,128]{1,0:T(8,128)S(1)} %products.1.refs_0_.after), channel_id=1, source_target_pairs={{0,4},{4,0},{8,12},{12,8},{1,5},{5,1},{9,13},{13,9},{2,6},{6,2},{1... | collective-permute-start | bytes 24584 | tf_op jit(solution)/shard_map/ppermute | solution.py:808
  33.8 1.1 %collective-permute-done.13.refs_3_ = f32[16,128]{1,0:T(8,128)S(1)} collective-permute-done((f32[16,128]{1,0:T(8,128)S(1)}, f32[16,128]{1,0:T(8,128)S(1)}, u32[]{:S(2)}, u32[]{:S(2)}) %collective-permute-start.13) | collective-permute-done | bytes 8224 | tf_op jit(solution)/shard_map/ppermute | solution.py:808
  34.9 1.6 %collective-permute-done.12.refs_2_ = f32[16,128]{1,0:T(8,128)S(1)} collective-permute-done((f32[16,128]{1,0:T(8,128)S(1)}, f32[16,128]{1,0:T(8,128)S(1)}, u32[]{:S(2)}, u32[]{:S(2)}) %collective-permute-start.12) | collective-permute-done | bytes 8224 | tf_op jit(solution)/shard_map/ppermute | solution.py:808
  36.5 0.0 collective-permute-done.11.refs_1_
  36.5 0.1 collective-permute-start.16
  36.5 0.6 %collective-permute-start.15 = (f32[16,128]{1,0:T(8,128)S(1)}, f32[16,128]{1,0:T(8,128)S(1)}, u32[]{:S(2)}, u32[]{:S(2)}) collective-permute-start(f32[16,128]{1,0:T(8,128)S(1)} %sum.2.refs_0_), channel_id=1, source_target_pairs={{0,2},{1,3},{2,0},{3,1},{4,6},{5,7},{6,4},{7,5},{8,10},{9,11},{10,... | collective-permute-start | bytes 24584 | tf_op jit(solution)/shard_map/ppermute | solution.py:808
  37.2 1.2 %collective-permute-start.14 = (f32[16,128]{1,0:T(8,128)S(1)}, f32[16,128]{1,0:T(8,128)S(1)}, u32[]{:S(2)}, u32[]{:S(2)}) collective-permute-start(f32[16,128]{1,0:T(8,128)S(1)} %sum.2.refs_0_), channel_id=1, source_target_pairs={{0,1},{1,0},{2,3},{3,2},{4,5},{5,4},{6,7},{7,6},{8,9},{9,8},{10,11... | collective-permute-start | bytes 24584 | tf_op jit(solution)/shard_map/ppermute | solution.py:808
  38.4 0.0 collective-permute-done.8.refs_1_
  38.4 0.5 %settle.1 = (f32[32,2048]{1,0:T(8,128)S(1)}, f32[32,2048]{1,0:T(8,128)S(1)}, f32[8,128]{1,0:T(8,128)S(1)}) custom-call(s32[4]{0:T(128)S(4)} %get-tuple-element.47.place.refs_0_, f32[32,2048]{1,0:T(8,128)S(1)} %get-tuple-element.48.refs_1_.vector, f32[1,2048]{1,0:T(1,128)S(1)} %get-tuple-element.49.capacity, f32[32,2048]{1,0:T(8,128)S(1)} %get-tuple-element.79.refs_0_, ...), custom_call_target="tpu_custom_call" | custom-call | bytes 3000000 | tf_op jit(solution)/shard_map/settle/pallas_call | solution.py:761
  38.9 0.9 %collective-permute-done.16.refs_3_ = f32[16,128]{1,0:T(8,128)S(1)} collective-permute-done((f32[16,128]{1,0:T(8,128)S(1)}, f32[16,128]{1,0:T(8,128)S(1)}, u32[]{:S(2)}, u32[]{:S(2)}) %collective-permute-start.16) | collective-permute-done | bytes 8224 | tf_op jit(solution)/shard_map/ppermute | solution.py:808
  39.8 1.0 %collective-permute-done.15.refs_2_ = f32[16,128]{1,0:T(8,128)S(1)} collective-permute-done((f32[16,128]{1,0:T(8,128)S(1)}, f32[16,128]{1,0:T(8,128)S(1)}, u32[]{:S(2)}, u32[]{:S(2)}) %collective-permute-start.15) | collective-permute-done | bytes 8224 | tf_op jit(solution)/shard_map/ppermute | solution.py:808
  40.7 0.0 collective-permute-done.18.refs_1_
  40.7 1.0 %last.1 = (f32[32,2048]{1,0:T(8,128)}, f32[32,2048]{1,0:T(8,128)}) custom-call(f32[16,128]{1,0:T(8,128)S(1)} %sum.3.gathered, f32[32,2048]{1,0:T(8,128)S(1)} %get-tuple-element.48.refs_1_.vector, f32[32,2048]{1,0:T(8,128)S(1)} %get-tuple-element.86.answer, f32[32,2048]{1,0:T(8,128)S(1)} %get-tuple-element.87.slope, ...), custom_call_target="tpu_custom_call" | custom-call | tf_op jit(solution)/shard_map/last/pallas_call | solution.py:1053
  (10 shorter events, 0.2 us)
Async XLA Ops:
  0.6 9.6 %collective-permute-start = (f32[32,2048]{1,0:T(8,128)}, f32[32,2048]{1,0:T(8,128)S(1)}, u32[]{:S(2)}, u32[]{:S(2)}) collective-permute-start(f32[32,2048]{1,0:T(8,128)} %vector_in.1), channel_id=1, source_target_pairs={{0,2},{1,3},{2,0},{3,1},{4,6},{5,7},{6,4},{7,5},{8,10},{9,11},{10,... | collective-permute-start | bytes 786440 | tf_op jit(solution)/shard_map/ppermute | solution.py:777
  3.6 8.4 %collective-permute-start.1 = (f32[32,2048]{1,0:T(8,128)}, f32[32,2048]{1,0:T(8,128)S(1)}, u32[]{:S(2)}, u32[]{:S(2)}) collective-permute-start(f32[32,2048]{1,0:T(8,128)} %vector_in.1), channel_id=1, source_target_pairs={{0,1},{1,0},{2,3},{3,2},{4,5},{5,4},{6,7},{7,6},{8,9},{9,8},{10,11... | collective-permute-start | bytes 786440 | tf_op jit(solution)/shard_map/ppermute | solution.py:777
  3.6 7.4 %collective-permute-start.3 = (f32[32,2048]{1,0:T(8,128)}, f32[32,2048]{1,0:T(8,128)S(1)}, u32[]{:S(2)}, u32[]{:S(2)}) collective-permute-start(f32[32,2048]{1,0:T(8,128)} %operating_in.1), channel_id=1, source_target_pairs={{0,1},{1,0},{2,3},{3,2},{4,5},{5,4},{6,7},{7,6},{8,9},{9,8},{10,11... | collective-permute-start | bytes 786440 | tf_op jit(solution)/shard_map/ppermute | solution.py:777
  10.3 1.7 %collective-permute-start.2 = (f32[32,2048]{1,0:T(8,128)S(1)}, f32[32,2048]{1,0:T(8,128)S(1)}, u32[]{:S(2)}, u32[]{:S(2)}) collective-permute-start(f32[32,2048]{1,0:T(8,128)S(1)} %relay.3.after.refs_2_), channel_id=1, source_target_pairs={{0,1},{1,0},{2,3},{3,2},{4,5},{5,4},{6,7},{7,6},{8,9},{9,8},{10,11... | collective-permute-start | bytes 786440 | tf_op jit(solution)/shard_map/ppermute | solution.py:777
  13.4 5.4 %collective-permute-start.5 = (f32[48,128]{1,0:T(8,128)S(1)}, f32[48,128]{1,0:T(8,128)S(1)}, u32[]{:S(2)}, u32[]{:S(2)}) collective-permute-start(f32[48,128]{1,0:T(8,128)S(1)} %get-tuple-element.69), channel_id=1, source_target_pairs={{0,4},{1,13},{2,6},{3,15},{4,0},{5,9},{6,2},{7,11},{8,12},{9,5},{1... | collective-permute-start | bytes 73736 | tf_op jit(solution)/shard_map/ppermute | solution.py:787
  15.2 5.1 %collective-permute-start.4 = (f32[48,128]{1,0:T(8,128)S(1)}, f32[48,128]{1,0:T(8,128)S(1)}, u32[]{:S(2)}, u32[]{:S(2)}) collective-permute-start(f32[48,128]{1,0:T(8,128)S(1)} %get-tuple-element.62), channel_id=1, source_target_pairs={{0,8},{1,9},{2,10},{3,11},{4,12},{5,13},{6,14},{7,15},{8,0},{9,1},... | collective-permute-start | bytes 73736 | tf_op jit(solution)/shard_map/ppermute | solution.py:787
  18.8 1.4 %collective-permute-start.6 = (f32[48,128]{1,0:T(8,128)S(1)}, f32[48,128]{1,0:T(8,128)S(1)}, u32[]{:S(2)}, u32[]{:S(2)}) collective-permute-start(f32[48,128]{1,0:T(8,128)S(1)} %relay.4.refs_2_), channel_id=1, source_target_pairs={{0,1},{1,0},{2,3},{3,2},{4,5},{5,4},{6,7},{7,6},{8,9},{9,8},{10,11... | collective-permute-start | bytes 73736 | tf_op jit(solution)/shard_map/ppermute | solution.py:777
  20.6 3.2 %collective-permute-start.9 = (f32[64,1024]{1,0:T(8,128)S(1)}, f32[64,1024]{1,0:T(8,128)S(1)}, u32[]{:S(2)}, u32[]{:S(2)}) collective-permute-start(f32[64,1024]{1,0:T(8,128)S(1)} %get-tuple-element.75.refs_5_.image), channel_id=1, source_target_pairs={{0,1},{1,0},{2,3},{3,2},{4,5},{5,4},{6,7},{7,6},{8,9},{9,8},{10,11... | collective-permute-start | bytes 786440 | tf_op jit(solution)/shard_map/ppermute | solution.py:777
  21.4 4.4 %collective-permute-start.10 = (f32[8,1024]{1,0:T(8,128)S(1)}, f32[8,1024]{1,0:T(8,128)S(1)}, u32[]{:S(2)}, u32[]{:S(2)}) collective-permute-start(f32[8,1024]{1,0:T(8,128)S(1)} %get-tuple-element.85.own_sums), channel_id=1, source_target_pairs={{0,2},{1,3},{2,0},{3,1},{4,6},{5,7},{6,4},{7,5},{8,10},{9,11},{10,... | collective-permute-start | bytes 98312 | tf_op jit(solution)/shard_map/ppermute | solution.py:777
  23.7 2.7 %collective-permute-start.7 = (f32[64,1024]{1,0:T(8,128)S(1)}, f32[64,1024]{1,0:T(8,128)S(1)}, u32[]{:S(2)}, u32[]{:S(2)}) collective-permute-start(f32[64,1024]{1,0:T(8,128)S(1)} %get-tuple-element.78), channel_id=1, source_target_pairs={{0,1},{1,0},{2,3},{3,2},{4,5},{5,4},{6,7},{7,6},{8,9},{9,8},{10,11... | collective-permute-start | bytes 786440 | tf_op jit(solution)/shard_map/ppermute | solution.py:777
  25.8 2.0 %collective-permute-start.17 = (f32[64,1024]{1,0:T(8,128)S(1)}, f32[64,1024]{1,0:T(8,128)S(1)}, u32[]{:S(2)}, u32[]{:S(2)}) collective-permute-start(f32[64,1024]{1,0:T(8,128)S(1)} %relay.5), channel_id=1, source_target_pairs={{0,1},{1,0},{2,3},{3,2},{4,5},{5,4},{6,7},{7,6},{8,9},{9,8},{10,11... | collective-permute-start | bytes 786440 | tf_op jit(solution)/shard_map/ppermute | solution.py:777
  26.4 12.0 %collective-permute-start.8 = (f32[32,2048]{1,0:T(8,128)S(1)}, f32[32,2048]{1,0:T(8,128)S(1)}, u32[]{:S(2)}, u32[]{:S(2)}) collective-permute-start(f32[32,2048]{1,0:T(8,128)S(1)} %get-tuple-element.80), channel_id=1, source_target_pairs={{0,2},{1,3},{2,0},{3,1},{4,6},{5,7},{6,4},{7,5},{8,10},{9,11},{10,... | collective-permute-start | bytes 786440 | tf_op jit(solution)/shard_map/ppermute | solution.py:777
  27.9 12.8 %collective-permute-start.18 = (f32[32,2048]{1,0:T(8,128)S(1)}, f32[32,2048]{1,0:T(8,128)S(1)}, u32[]{:S(2)}, u32[]{:S(2)}) collective-permute-start(f32[32,2048]{1,0:T(8,128)S(1)} %get-tuple-element.91), channel_id=1, source_target_pairs={{0,2},{1,3},{2,0},{3,1},{4,6},{5,7},{6,4},{7,5},{8,10},{9,11},{10,... | collective-permute-start | bytes 786440 | tf_op jit(solution)/shard_map/ppermute | solution.py:777
  29.4 5.4 %collective-permute-start.13 = (f32[16,128]{1,0:T(8,128)S(1)}, f32[16,128]{1,0:T(8,128)S(1)}, u32[]{:S(2)}, u32[]{:S(2)}) collective-permute-start(f32[16,128]{1,0:T(8,128)S(1)} %products.1.refs_0_.after), channel_id=1, source_target_pairs={{0,12},{4,8},{8,4},{12,0},{1,13},{5,9},{9,5},{13,1},{2,14},{6,10},... | collective-permute-start | bytes 24584 | tf_op jit(solution)/shard_map/ppermute | solution.py:808
  31.9 4.5 %collective-permute-start.12 = (f32[16,128]{1,0:T(8,128)S(1)}, f32[16,128]{1,0:T(8,128)S(1)}, u32[]{:S(2)}, u32[]{:S(2)}) collective-permute-start(f32[16,128]{1,0:T(8,128)S(1)} %products.1.refs_0_.after), channel_id=1, source_target_pairs={{0,8},{4,12},{8,0},{12,4},{1,9},{5,13},{9,1},{13,5},{2,10},{6,14},... | collective-permute-start | bytes 24584 | tf_op jit(solution)/shard_map/ppermute | solution.py:808
  31.9 4.5 %collective-permute-start.11 = (f32[16,128]{1,0:T(8,128)S(1)}, f32[16,128]{1,0:T(8,128)S(1)}, u32[]{:S(2)}, u32[]{:S(2)}) collective-permute-start(f32[16,128]{1,0:T(8,128)S(1)} %products.1.refs_0_.after), channel_id=1, source_target_pairs={{0,4},{4,0},{8,12},{12,8},{1,5},{5,1},{9,13},{13,9},{2,6},{6,2},{1... | collective-permute-start | bytes 24584 | tf_op jit(solution)/shard_map/ppermute | solution.py:808
  36.5 3.3 %collective-permute-start.16 = (f32[16,128]{1,0:T(8,128)S(1)}, f32[16,128]{1,0:T(8,128)S(1)}, u32[]{:S(2)}, u32[]{:S(2)}) collective-permute-start(f32[16,128]{1,0:T(8,128)S(1)} %sum.2.refs_0_), channel_id=1, source_target_pairs={{0,3},{1,2},{2,1},{3,0},{4,7},{5,6},{6,5},{7,4},{8,11},{9,10},{10,... | collective-permute-start | bytes 24584 | tf_op jit(solution)/shard_map/ppermute | solution.py:808
  36.5 4.2 %collective-permute-start.15 = (f32[16,128]{1,0:T(8,128)S(1)}, f32[16,128]{1,0:T(8,128)S(1)}, u32[]{:S(2)}, u32[]{:S(2)}) collective-permute-start(f32[16,128]{1,0:T(8,128)S(1)} %sum.2.refs_0_), channel_id=1, source_target_pairs={{0,2},{1,3},{2,0},{3,1},{4,6},{5,7},{6,4},{7,5},{8,10},{9,11},{10,... | collective-permute-start | bytes 24584 | tf_op jit(solution)/shard_map/ppermute | solution.py:808
  37.2 3.6 %collective-permute-start.14 = (f32[16,128]{1,0:T(8,128)S(1)}, f32[16,128]{1,0:T(8,128)S(1)}, u32[]{:S(2)}, u32[]{:S(2)}) collective-permute-start(f32[16,128]{1,0:T(8,128)S(1)} %sum.2.refs_0_), channel_id=1, source_target_pairs={{0,1},{1,0},{2,3},{3,2},{4,5},{5,4},{6,7},{7,6},{8,9},{9,8},{10,11... | collective-permute-start | bytes 24584 | tf_op jit(solution)/shard_map/ppermute | solution.py:808

commit v11 on v9

--- a/solution.py
+++ b/solution.py
@@ -1037,7 +1037,7 @@
         [((16, gathered), F32)],
         micros=1,
     )
-    second_parts = hand_out(scalars, place, second_kept, second_arrived)
+    second_parts = hand_out(answer_parts[0], place, second_kept, second_arrived)
     scalars = add(cut_halo, exchange(scalars, "nodes", cut_halo))
     answer, slope, skew = run(
         functools.partial(settle_kernel, length=length),

time: 42.1 us -> 42.1 us (level)
  waiting for transfers between devices: 5.02 us -> 5.53 us
    ppermute x11, waiting for transfers between devices: 0.03 us -> 0.53 us  [swap(): lax.ppermute(value, 'samples', [(at, at ^ mask) for at in range(count)])]
    ppermute x11, starting transfers between devices: 8.78 us -> 8.3 us  [swap(): lax.ppermute(value, 'samples', [(at, at ^ mask) for at in range(count)])]
  transfers between devices with their start and end apart: 19 -> 19, of which waited for: 5 -> 6; matrix products, arithmetic and copies ran while one was open for 0% -> 0% of each run, Pallas kernels for 33% -> 33%
where the time goes in v11:
time: 42.1 us; the launch traced here: 41.9 us
  starting transfers between devices  19 us (45%)
  Pallas kernels  16.6 us (39%)
  waiting for transfers between devices  5.53 us (13%)
  between operations  0.84 us (2%)
    pallas_call x19, Pallas kernels, run(): pl.pallas_call(kernel, out_shape=[space(shape, dtype) for space, (shape,...  15.6 us
    ppermute x11, starting transfers between devices, swap(): lax.ppermute(value, 'samples', [(at, at ^ mask) for at in range(count)])  8.3 us
    ppermute x6, starting transfers between devices, exchange(): lax.ppermute(value, axis, [(at, at ^ step * stride) for at in range(count)])  6.31 us
    ppermute x6, waiting for transfers between devices, exchange(): lax.ppermute(value, axis, [(at, at ^ step * stride) for at in range(count)])  4.46 us
    ppermute x2, starting transfers between devices, trade(): return lax.ppermute(value, ('nodes', 'samples'), pairs)  4.35 us
    pallas_call x1, Pallas kernels, shards(): pl.pallas_call(functools.partial(last_kernel, entries=entries, devices=fl...  1.03 us
  transfers between devices with their start and end apart: 19, of which 6 were waited for; matrix products, arithmetic and copies ran while one was open for 0% of the time, Pallas kernels for 33%

profile of v11, /device:TPU:0, one launch (start us, length us, event | category | flops | bytes accessed | tf_op | source)
XLA Modules:
  0.0 41.9 jit_solution(18234704009880178292)
XLA Ops:
  0.6 3.0 %collective-permute-start = (f32[32,2048]{1,0:T(8,128)}, f32[32,2048]{1,0:T(8,128)S(1)}, u32[]{:S(2)}, u32[]{:S(2)}) collective-permute-start(f32[32,2048]{1,0:T(8,128)} %vector_in.1), channel_id=1, source_target_pairs={{0,2},{1,3},{2,0},{3,1},{4,6},{5,7},{6,4},{7,5},{8,10},{9,11},{10,... | collective-permute-start | bytes 786440 | tf_op jit(solution)/shard_map/ppermute | solution.py:777
  3.6 0.0 collective-permute-start.1
  3.6 0.5 %collective-permute-start.3 = (f32[32,2048]{1,0:T(8,128)}, f32[32,2048]{1,0:T(8,128)S(1)}, u32[]{:S(2)}, u32[]{:S(2)}) collective-permute-start(f32[32,2048]{1,0:T(8,128)} %operating_in.1), channel_id=1, source_target_pairs={{0,1},{1,0},{2,3},{3,2},{4,5},{5,4},{6,7},{7,6},{8,9},{9,8},{10,11... | collective-permute-start | bytes 786440 | tf_op jit(solution)/shard_map/ppermute | solution.py:777
  4.1 1.7 %fetch.1 = (f32[32,2048]{1,0:T(8,128)S(1)}, bf16[2048,128]{1,0:T(8,128)(2,1)S(1)}, f32[1,1152]{1,0:T(1,128)S(1)}, f32[1,1152]{1,0:T(1,128)S(1)}, f32[1,2048]{1,0...) custom-call(f32[32,2048]{1,0:T(8,128)} %vector_in.1, ...), custom_call_target="tpu_custom_call" | custom-call | bytes 6000000 | tf_op jit(solution)/shard_map/fetch/pallas_call | solution.py:761
  5.9 4.4 %prepare.1 = (bf16[2176,1024]{1,0:T(8,128)(2,1)S(1)}, bf16[2176,1024]{1,0:T(8,128)(2,1)S(1)}) custom-call(s32[8,1152]{1,0:T(8,128)S(1)} %get-tuple-element.50.entry_rows, f32[8,1152]{1,0:T(8,128)S(1)} %get-tuple-element.51.weight_rows), custom_call_target="tpu_custom_call" | custom-call | bytes 18000000 | tf_op jit(solution)/shard_map/prepare/pallas_call | solution.py:761
  10.3 0.0 collective-permute-done.refs_1_
  10.3 0.1 collective-permute-start.2
  10.4 0.6 %prepare_cut.1 = (bf16[2176,128]{1,0:T(8,128)(2,1)S(1)}, bf16[2176,128]{1,0:T(8,128)(2,1)S(1)}, f32[128,128]{1,0:T(8,128)S(1)}) custom-call(f32[32,2048]{1,0:T(8,128)S(1)} %relay.3.after.refs_2_, s32[8,1152]{1,0:T(8,128)S(1)} %get-tuple-element.50.entry_rows, f32[8,1152]{1,0:T(8,128)S(1)} %get-tuple-element.51.weight_rows), custom_call_target="tpu_custom_call" | custom-call | bytes 3000000 | tf_op jit(solution)/shard_map/prepare_cut/pallas_call | solution.py:761
  11.0 0.0 collective-permute-done.3.near_operating
  11.0 1.0 %conductance.1.refs_6_.conductances = f32[64,2176]{1,0:T(8,128)S(1)} custom-call(s32[4]{0:T(128)S(4)} %get-tuple-element.47.place.refs_0_, f32[32,2048]{1,0:T(8,128)S(1)} %collective-permute-done.3.near_operating, f32[32,2048]{1,0:T(8,128)S(1)} %get-tuple-element.54.operating, f32[1,16]{1,0:T(1,128)S(1)} %get-tuple-element.55.table, ...), custom_call_target="tpu_custom_call" | custom-call | bytes 3000000 | tf_op jit(solution)/shard_map/conductance/pallas_call | solution.py:761
  12.0 0.0 collective-permute-done.1.refs_3_
  12.0 0.0 collective-permute-done.2.refs_4_
  12.0 1.5 %wave.1 = (bf16[128,2176]{1,0:T(8,128)(2,1)S(1)}, bf16[128,2176]{1,0:T(8,128)(2,1)S(1)}, f32[64,2176]{1,0:T(8,128)S(1)}, bf16[128,2048]{1,0:T(8,128)(2,1)S(1)}, ...) custom-call(s32[4]{0:T(128)S(4)} %get-tuple-element.47.place.refs_0_, ...), custom_call_target="tpu_custom_call" | custom-call | bytes 6000000 | tf_op jit(solution)/shard_map/wave/pallas_call | solution.py:761
  13.5 1.8 %collective-permute-start.5 = (f32[48,128]{1,0:T(8,128)S(1)}, f32[48,128]{1,0:T(8,128)S(1)}, u32[]{:S(2)}, u32[]{:S(2)}) collective-permute-start(f32[48,128]{1,0:T(8,128)S(1)} %get-tuple-element.69), channel_id=1, source_target_pairs={{0,4},{1,13},{2,6},{3,15},{4,0},{5,9},{6,2},{7,11},{8,12},{9,5},{1... | collective-permute-start | bytes 73736 | tf_op jit(solution)/shard_map/ppermute | solution.py:787
  15.3 2.6 %collective-permute-start.4 = (f32[48,128]{1,0:T(8,128)S(1)}, f32[48,128]{1,0:T(8,128)S(1)}, u32[]{:S(2)}, u32[]{:S(2)}) collective-permute-start(f32[48,128]{1,0:T(8,128)S(1)} %get-tuple-element.62), channel_id=1, source_target_pairs={{0,8},{1,9},{2,10},{3,11},{4,12},{5,13},{6,14},{7,15},{8,0},{9,1},... | collective-permute-start | bytes 73736 | tf_op jit(solution)/shard_map/ppermute | solution.py:787
  17.9 1.0 %local.1 = (f32[64,1024]{1,0:T(8,128)S(1)}, f32[64,1024]{1,0:T(8,128)S(1)}, f32[64,1024]{1,0:T(8,128)S(1)}, f32[64,1024]{1,0:T(8,128)S(1)}, f32[64,1024]{1,0:T(8,128)S(1)}) custom-call(bf16[128,2176]{1,0:T(8,128)(2,1)S(1)} %get-tuple-element.63.field_high, bf16[128,2176]{1,0:T(8,128)(2,1)S(1)} %get-tuple-element.64.field_low, ...), custom_call_target="tpu_custom_call" | custom-call | bytes 9000000 | tf_op jit(solution)/shard_map/local/pallas_call | solution.py:761
  18.9 0.0 collective-permute-done.5.refs_1_
  19.0 0.1 collective-permute-start.6
  19.0 0.8 %local_rest.1.refs_6_ = f32[64,512]{1,0:T(8,128)S(1)} custom-call(f32[64,1024]{1,0:T(8,128)S(1)} %get-tuple-element.71.load.refs_5_, bf16[128,2048]{1,0:T(8,128)(2,1)S(1)} %get-tuple-element.66.current, bf16[2176,1024]{1,0:T(8,128)(2,1)S(1)} %get-tuple-element.67.coupling_high.refs_9_, bf16[2176,1024]{1,0:T(8,128)(2,1)S(1)} %get-tuple-element.52.refs_0_.coupling_low.refs_10_), custom_call_target="tpu_custom_call" | custom-call | bytes 3000000 | tf_op jit(solution)/shard_map/local_rest/pallas_call | solution.py:761
  19.8 0.5 %collective-permute-done.4.refs_1_ = f32[48,128]{1,0:T(8,128)S(1)} collective-permute-done((f32[48,128]{1,0:T(8,128)S(1)}, f32[48,128]{1,0:T(8,128)S(1)}, u32[]{:S(2)}, u32[]{:S(2)}) %collective-permute-start.4) | collective-permute-done | bytes 24608 | tf_op jit(solution)/shard_map/ppermute | solution.py:787
  20.4 0.3 first.1
  20.7 0.9 %collective-permute-start.9 = (f32[64,1024]{1,0:T(8,128)S(1)}, f32[64,1024]{1,0:T(8,128)S(1)}, u32[]{:S(2)}, u32[]{:S(2)}) collective-permute-start(f32[64,1024]{1,0:T(8,128)S(1)} %get-tuple-element.75.refs_5_.image), channel_id=1, source_target_pairs={{0,1},{1,0},{2,3},{3,2},{4,5},{5,4},{6,7},{7,6},{8,9},{9,8},{10,11... | collective-permute-start | bytes 786440 | tf_op jit(solution)/shard_map/ppermute | solution.py:777
  21.6 1.5 %collective-permute-start.10 = (f32[8,1024]{1,0:T(8,128)S(1)}, f32[8,1024]{1,0:T(8,128)S(1)}, u32[]{:S(2)}, u32[]{:S(2)}) collective-permute-start(f32[8,1024]{1,0:T(8,128)S(1)} %get-tuple-element.85.own_sums), channel_id=1, source_target_pairs={{0,2},{1,3},{2,0},{3,1},{4,6},{5,7},{6,4},{7,5},{8,10},{9,11},{10,... | collective-permute-start | bytes 98312 | tf_op jit(solution)/shard_map/ppermute | solution.py:777
  23.1 0.8 %spread.1 = (f32[64,128]{1,0:T(8,128)S(1)}, f32[64,1024]{1,0:T(8,128)S(1)}, f32[64,1024]{1,0:T(8,128)S(1)}) custom-call(s32[4]{0:T(128)S(4)} %get-tuple-element.47.place.refs_0_, f32[48,128]{1,0:T(8,128)S(1)} %collective-permute-done.4.refs_1_, f32[48,128]{1,0:T(8,128)S(1)} %relay.4.refs_2_, f32[48,128]{1,0:T(8,128)S(1)} %collective-permute-done.6.refs_3_, ...), custom_call_target="tpu_custom_call" | custom-call | bytes 3000000 | tf_op jit(solution)/shard_map/spread/pallas_call | solution.py:761
  23.8 0.1 collective-permute-start.7
  23.9 0.0 collective-permute-done.9.near_image
  23.9 2.0 %second.1 = (f32[64,1024]{1,0:T(8,128)S(1)}, f32[64,1024]{1,0:T(8,128)S(1)}, f32[64,1024]{1,0:T(8,128)S(1)}) custom-call(s32[4]{0:T(128)S(4)} %get-tuple-element.47.place.refs_0_, f32[64,128]{1,0:T(8,128)S(1)} %get-tuple-element.82.halo, f32[64,1024]{1,0:T(8,128)S(1)} %collective-permute-done.9.near_image, f32[64,1024]{1,0:T(8,128)S(1)} %get-tuple-element.75.refs_5_.image, ...), custom_call_target="tpu_custom_call" | custom-call | bytes 9000000 | tf_op jit(solution)/shard_map/second/pallas_call | solution.py:761
  26.0 0.0 collective-permute-done.10.far_sums.refs_0_
  26.0 0.6 %collective-permute-start.17 = (f32[64,1024]{1,0:T(8,128)S(1)}, f32[64,1024]{1,0:T(8,128)S(1)}, u32[]{:S(2)}, u32[]{:S(2)}) collective-permute-start(f32[64,1024]{1,0:T(8,128)S(1)} %relay.5), channel_id=1, source_target_pairs={{0,1},{1,0},{2,3},{3,2},{4,5},{5,4},{6,7},{7,6},{8,9},{9,8},{10,11... | collective-permute-start | bytes 786440 | tf_op jit(solution)/shard_map/ppermute | solution.py:777
  26.6 0.6 %collective-permute-start.8 = (f32[32,2048]{1,0:T(8,128)S(1)}, f32[32,2048]{1,0:T(8,128)S(1)}, u32[]{:S(2)}, u32[]{:S(2)}) collective-permute-start(f32[32,2048]{1,0:T(8,128)S(1)} %get-tuple-element.80), channel_id=1, source_target_pairs={{0,2},{1,3},{2,0},{3,1},{4,6},{5,7},{6,4},{7,5},{8,10},{9,11},{10,... | collective-permute-start | bytes 786440 | tf_op jit(solution)/shard_map/ppermute | solution.py:777
  27.2 0.5 %collective-permute-done.17.arrived = f32[64,1024]{1,0:T(8,128)S(1)} collective-permute-done((f32[64,1024]{1,0:T(8,128)S(1)}, f32[64,1024]{1,0:T(8,128)S(1)}, u32[]{:S(2)}, u32[]{:S(2)}) %collective-permute-start.17) | collective-permute-done | bytes 262176 | tf_op jit(solution)/shard_map/ppermute | solution.py:777
  27.8 1.1 %collective-permute-start.18 = (f32[32,2048]{1,0:T(8,128)S(1)}, f32[32,2048]{1,0:T(8,128)S(1)}, u32[]{:S(2)}, u32[]{:S(2)}) collective-permute-start(f32[32,2048]{1,0:T(8,128)S(1)} %get-tuple-element.91), channel_id=1, source_target_pairs={{0,2},{1,3},{2,0},{3,1},{4,6},{5,7},{6,4},{7,5},{8,10},{9,11},{10,... | collective-permute-start | bytes 786440 | tf_op jit(solution)/shard_map/ppermute | solution.py:777
  28.8 0.8 %products.1.refs_0_ = f32[16,128]{1,0:T(8,128)S(1)} custom-call(s32[4]{0:T(128)S(4)} %get-tuple-element.47.place.refs_0_, f32[32,2048]{1,0:T(8,128)S(1)} %get-tuple-element.48.refs_1_.vector, f32[64,1024]{1,0:T(8,128)S(1)} %get-tuple-element.74.after.load, f32[64,1024]{1,0:T(8,128)S(1)} %get-tuple-element.83.second_load, ...), custom_call_target="tpu_custom_call" | custom-call | bytes 3000000 | tf_op jit(solution)/shard_map/products/pallas_call | solution.py:761
  29.6 2.5 %collective-permute-start.13 = (f32[16,128]{1,0:T(8,128)S(1)}, f32[16,128]{1,0:T(8,128)S(1)}, u32[]{:S(2)}, u32[]{:S(2)}) collective-permute-start(f32[16,128]{1,0:T(8,128)S(1)} %products.1.refs_0_), channel_id=1, source_target_pairs={{0,12},{4,8},{8,4},{12,0},{1,13},{5,9},{9,5},{13,1},{2,14},{6,10},... | collective-permute-start | bytes 24584 | tf_op jit(solution)/shard_map/ppermute | solution.py:808
  32.1 0.0 collective-permute-start.12
  32.1 1.9 %collective-permute-start.11 = (f32[16,128]{1,0:T(8,128)S(1)}, f32[16,128]{1,0:T(8,128)S(1)}, u32[]{:S(2)}, u32[]{:S(2)}) collective-permute-start(f32[16,128]{1,0:T(8,128)S(1)} %products.1.refs_0_), channel_id=1, source_target_pairs={{0,4},{4,0},{8,12},{12,8},{1,5},{5,1},{9,13},{13,9},{2,6},{6,2},{1... | collective-permute-start | bytes 24584 | tf_op jit(solution)/shard_map/ppermute | solution.py:808
  34.0 1.1 %collective-permute-done.13.refs_3_ = f32[16,128]{1,0:T(8,128)S(1)} collective-permute-done((f32[16,128]{1,0:T(8,128)S(1)}, f32[16,128]{1,0:T(8,128)S(1)}, u32[]{:S(2)}, u32[]{:S(2)}) %collective-permute-start.13) | collective-permute-done | bytes 8224 | tf_op jit(solution)/shard_map/ppermute | solution.py:808
  35.0 1.6 %collective-permute-done.12.refs_2_ = f32[16,128]{1,0:T(8,128)S(1)} collective-permute-done((f32[16,128]{1,0:T(8,128)S(1)}, f32[16,128]{1,0:T(8,128)S(1)}, u32[]{:S(2)}, u32[]{:S(2)}) %collective-permute-start.12) | collective-permute-done | bytes 8224 | tf_op jit(solution)/shard_map/ppermute | solution.py:808
  36.6 0.0 collective-permute-done.11.refs_1_
  36.6 0.1 collective-permute-start.16
  36.7 1.1 %collective-permute-start.15 = (f32[16,128]{1,0:T(8,128)S(1)}, f32[16,128]{1,0:T(8,128)S(1)}, u32[]{:S(2)}, u32[]{:S(2)}) collective-permute-start(f32[16,128]{1,0:T(8,128)S(1)} %sum.2.refs_0_), channel_id=1, source_target_pairs={{0,2},{1,3},{2,0},{3,1},{4,6},{5,7},{6,4},{7,5},{8,10},{9,11},{10,... | collective-permute-start | bytes 24584 | tf_op jit(solution)/shard_map/ppermute | solution.py:808
  37.8 0.7 %collective-permute-start.14 = (f32[16,128]{1,0:T(8,128)S(1)}, f32[16,128]{1,0:T(8,128)S(1)}, u32[]{:S(2)}, u32[]{:S(2)}) collective-permute-start(f32[16,128]{1,0:T(8,128)S(1)} %sum.2.refs_0_), channel_id=1, source_target_pairs={{0,1},{1,0},{2,3},{3,2},{4,5},{5,4},{6,7},{7,6},{8,9},{9,8},{10,11... | collective-permute-start | bytes 24584 | tf_op jit(solution)/shard_map/ppermute | solution.py:808
  38.6 0.5 %settle.1 = (f32[32,2048]{1,0:T(8,128)S(1)}, f32[32,2048]{1,0:T(8,128)S(1)}, f32[8,128]{1,0:T(8,128)S(1)}) custom-call(s32[4]{0:T(128)S(4)} %get-tuple-element.47.place.refs_0_, f32[32,2048]{1,0:T(8,128)S(1)} %get-tuple-element.48.refs_1_.vector, f32[1,2048]{1,0:T(1,128)S(1)} %get-tuple-element.49.capacity, f32[32,2048]{1,0:T(8,128)S(1)} %get-tuple-element.79.refs_0_.after, ...), custom_call_target="tpu_custom_call" | custom-call | bytes 3000000 | tf_op jit(solution)/shard_map/settle/pallas_call | solution.py:761
  39.1 0.9 %collective-permute-done.16.refs_3_ = f32[16,128]{1,0:T(8,128)S(1)} collective-permute-done((f32[16,128]{1,0:T(8,128)S(1)}, f32[16,128]{1,0:T(8,128)S(1)}, u32[]{:S(2)}, u32[]{:S(2)}) %collective-permute-start.16) | collective-permute-done | bytes 8224 | tf_op jit(solution)/shard_map/ppermute | solution.py:808
  39.9 1.0 %collective-permute-done.15.refs_2_ = f32[16,128]{1,0:T(8,128)S(1)} collective-permute-done((f32[16,128]{1,0:T(8,128)S(1)}, f32[16,128]{1,0:T(8,128)S(1)}, u32[]{:S(2)}, u32[]{:S(2)}) %collective-permute-start.15) | collective-permute-done | bytes 8224 | tf_op jit(solution)/shard_map/ppermute | solution.py:808
  40.9 0.0 collective-permute-done.14.refs_1_
  40.9 0.0 collective-permute-done.18.refs_1_
  40.9 1.0 %last.1 = (f32[32,2048]{1,0:T(8,128)}, f32[32,2048]{1,0:T(8,128)}) custom-call(f32[16,128]{1,0:T(8,128)S(1)} %sum.3.gathered, f32[32,2048]{1,0:T(8,128)S(1)} %get-tuple-element.48.refs_1_.vector, f32[32,2048]{1,0:T(8,128)S(1)} %get-tuple-element.86.answer, f32[32,2048]{1,0:T(8,128)S(1)} %get-tuple-element.87.slope, ...), custom_call_target="tpu_custom_call" | custom-call | tf_op jit(solution)/shard_map/last/pallas_call | solution.py:1053
  (10 shorter events, 0.1 us)
Async XLA Ops:
  0.6 9.6 %collective-permute-start = (f32[32,2048]{1,0:T(8,128)}, f32[32,2048]{1,0:T(8,128)S(1)}, u32[]{:S(2)}, u32[]{:S(2)}) collective-permute-start(f32[32,2048]{1,0:T(8,128)} %vector_in.1), channel_id=1, source_target_pairs={{0,2},{1,3},{2,0},{3,1},{4,6},{5,7},{6,4},{7,5},{8,10},{9,11},{10,... | collective-permute-start | bytes 786440 | tf_op jit(solution)/shard_map/ppermute | solution.py:777
  3.6 8.4 %collective-permute-start.1 = (f32[32,2048]{1,0:T(8,128)}, f32[32,2048]{1,0:T(8,128)S(1)}, u32[]{:S(2)}, u32[]{:S(2)}) collective-permute-start(f32[32,2048]{1,0:T(8,128)} %vector_in.1), channel_id=1, source_target_pairs={{0,1},{1,0},{2,3},{3,2},{4,5},{5,4},{6,7},{7,6},{8,9},{9,8},{10,11... | collective-permute-start | bytes 786440 | tf_op jit(solution)/shard_map/ppermute | solution.py:777
  3.6 7.4 %collective-permute-start.3 = (f32[32,2048]{1,0:T(8,128)}, f32[32,2048]{1,0:T(8,128)S(1)}, u32[]{:S(2)}, u32[]{:S(2)}) collective-permute-start(f32[32,2048]{1,0:T(8,128)} %operating_in.1), channel_id=1, source_target_pairs={{0,1},{1,0},{2,3},{3,2},{4,5},{5,4},{6,7},{7,6},{8,9},{9,8},{10,11... | collective-permute-start | bytes 786440 | tf_op jit(solution)/shard_map/ppermute | solution.py:777
  10.3 1.7 %collective-permute-start.2 = (f32[32,2048]{1,0:T(8,128)S(1)}, f32[32,2048]{1,0:T(8,128)S(1)}, u32[]{:S(2)}, u32[]{:S(2)}) collective-permute-start(f32[32,2048]{1,0:T(8,128)S(1)} %relay.3.after.refs_2_), channel_id=1, source_target_pairs={{0,1},{1,0},{2,3},{3,2},{4,5},{5,4},{6,7},{7,6},{8,9},{9,8},{10,11... | collective-permute-start | bytes 786440 | tf_op jit(solution)/shard_map/ppermute | solution.py:777
  13.5 5.4 %collective-permute-start.5 = (f32[48,128]{1,0:T(8,128)S(1)}, f32[48,128]{1,0:T(8,128)S(1)}, u32[]{:S(2)}, u32[]{:S(2)}) collective-permute-start(f32[48,128]{1,0:T(8,128)S(1)} %get-tuple-element.69), channel_id=1, source_target_pairs={{0,4},{1,13},{2,6},{3,15},{4,0},{5,9},{6,2},{7,11},{8,12},{9,5},{1... | collective-permute-start | bytes 73736 | tf_op jit(solution)/shard_map/ppermute | solution.py:787
  15.3 5.1 %collective-permute-start.4 = (f32[48,128]{1,0:T(8,128)S(1)}, f32[48,128]{1,0:T(8,128)S(1)}, u32[]{:S(2)}, u32[]{:S(2)}) collective-permute-start(f32[48,128]{1,0:T(8,128)S(1)} %get-tuple-element.62), channel_id=1, source_target_pairs={{0,8},{1,9},{2,10},{3,11},{4,12},{5,13},{6,14},{7,15},{8,0},{9,1},... | collective-permute-start | bytes 73736 | tf_op jit(solution)/shard_map/ppermute | solution.py:787
  19.0 1.4 %collective-permute-start.6 = (f32[48,128]{1,0:T(8,128)S(1)}, f32[48,128]{1,0:T(8,128)S(1)}, u32[]{:S(2)}, u32[]{:S(2)}) collective-permute-start(f32[48,128]{1,0:T(8,128)S(1)} %relay.4.refs_2_), channel_id=1, source_target_pairs={{0,1},{1,0},{2,3},{3,2},{4,5},{5,4},{6,7},{7,6},{8,9},{9,8},{10,11... | collective-permute-start | bytes 73736 | tf_op jit(solution)/shard_map/ppermute | solution.py:777
  20.7 3.2 %collective-permute-start.9 = (f32[64,1024]{1,0:T(8,128)S(1)}, f32[64,1024]{1,0:T(8,128)S(1)}, u32[]{:S(2)}, u32[]{:S(2)}) collective-permute-start(f32[64,1024]{1,0:T(8,128)S(1)} %get-tuple-element.75.refs_5_.image), channel_id=1, source_target_pairs={{0,1},{1,0},{2,3},{3,2},{4,5},{5,4},{6,7},{7,6},{8,9},{9,8},{10,11... | collective-permute-start | bytes 786440 | tf_op jit(solution)/shard_map/ppermute | solution.py:777
  21.6 4.4 %collective-permute-start.10 = (f32[8,1024]{1,0:T(8,128)S(1)}, f32[8,1024]{1,0:T(8,128)S(1)}, u32[]{:S(2)}, u32[]{:S(2)}) collective-permute-start(f32[8,1024]{1,0:T(8,128)S(1)} %get-tuple-element.85.own_sums), channel_id=1, source_target_pairs={{0,2},{1,3},{2,0},{3,1},{4,6},{5,7},{6,4},{7,5},{8,10},{9,11},{10,... | collective-permute-start | bytes 98312 | tf_op jit(solution)/shard_map/ppermute | solution.py:777
  23.8 2.7 %collective-permute-start.7 = (f32[64,1024]{1,0:T(8,128)S(1)}, f32[64,1024]{1,0:T(8,128)S(1)}, u32[]{:S(2)}, u32[]{:S(2)}) collective-permute-start(f32[64,1024]{1,0:T(8,128)S(1)} %get-tuple-element.78), channel_id=1, source_target_pairs={{0,1},{1,0},{2,3},{3,2},{4,5},{5,4},{6,7},{7,6},{8,9},{9,8},{10,11... | collective-permute-start | bytes 786440 | tf_op jit(solution)/shard_map/ppermute | solution.py:777
  26.0 1.7 %collective-permute-start.17 = (f32[64,1024]{1,0:T(8,128)S(1)}, f32[64,1024]{1,0:T(8,128)S(1)}, u32[]{:S(2)}, u32[]{:S(2)}) collective-permute-start(f32[64,1024]{1,0:T(8,128)S(1)} %relay.5), channel_id=1, source_target_pairs={{0,1},{1,0},{2,3},{3,2},{4,5},{5,4},{6,7},{7,6},{8,9},{9,8},{10,11... | collective-permute-start | bytes 786440 | tf_op jit(solution)/shard_map/ppermute | solution.py:777
  26.6 11.9 %collective-permute-start.8 = (f32[32,2048]{1,0:T(8,128)S(1)}, f32[32,2048]{1,0:T(8,128)S(1)}, u32[]{:S(2)}, u32[]{:S(2)}) collective-permute-start(f32[32,2048]{1,0:T(8,128)S(1)} %get-tuple-element.80), channel_id=1, source_target_pairs={{0,2},{1,3},{2,0},{3,1},{4,6},{5,7},{6,4},{7,5},{8,10},{9,11},{10,... | collective-permute-start | bytes 786440 | tf_op jit(solution)/shard_map/ppermute | solution.py:777
  27.8 13.1 %collective-permute-start.18 = (f32[32,2048]{1,0:T(8,128)S(1)}, f32[32,2048]{1,0:T(8,128)S(1)}, u32[]{:S(2)}, u32[]{:S(2)}) collective-permute-start(f32[32,2048]{1,0:T(8,128)S(1)} %get-tuple-element.91), channel_id=1, source_target_pairs={{0,2},{1,3},{2,0},{3,1},{4,6},{5,7},{6,4},{7,5},{8,10},{9,11},{10,... | collective-permute-start | bytes 786440 | tf_op jit(solution)/shard_map/ppermute | solution.py:777
  29.6 5.4 %collective-permute-start.13 = (f32[16,128]{1,0:T(8,128)S(1)}, f32[16,128]{1,0:T(8,128)S(1)}, u32[]{:S(2)}, u32[]{:S(2)}) collective-permute-start(f32[16,128]{1,0:T(8,128)S(1)} %products.1.refs_0_), channel_id=1, source_target_pairs={{0,12},{4,8},{8,4},{12,0},{1,13},{5,9},{9,5},{13,1},{2,14},{6,10},... | collective-permute-start | bytes 24584 | tf_op jit(solution)/shard_map/ppermute | solution.py:808
  32.1 4.5 %collective-permute-start.12 = (f32[16,128]{1,0:T(8,128)S(1)}, f32[16,128]{1,0:T(8,128)S(1)}, u32[]{:S(2)}, u32[]{:S(2)}) collective-permute-start(f32[16,128]{1,0:T(8,128)S(1)} %products.1.refs_0_), channel_id=1, source_target_pairs={{0,8},{4,12},{8,0},{12,4},{1,9},{5,13},{9,1},{13,5},{2,10},{6,14},... | collective-permute-start | bytes 24584 | tf_op jit(solution)/shard_map/ppermute | solution.py:808
  32.1 4.5 %collective-permute-start.11 = (f32[16,128]{1,0:T(8,128)S(1)}, f32[16,128]{1,0:T(8,128)S(1)}, u32[]{:S(2)}, u32[]{:S(2)}) collective-permute-start(f32[16,128]{1,0:T(8,128)S(1)} %products.1.refs_0_), channel_id=1, source_target_pairs={{0,4},{4,0},{8,12},{12,8},{1,5},{5,1},{9,13},{13,9},{2,6},{6,2},{1... | collective-permute-start | bytes 24584 | tf_op jit(solution)/shard_map/ppermute | solution.py:808
  36.6 3.3 %collective-permute-start.16 = (f32[16,128]{1,0:T(8,128)S(1)}, f32[16,128]{1,0:T(8,128)S(1)}, u32[]{:S(2)}, u32[]{:S(2)}) collective-permute-start(f32[16,128]{1,0:T(8,128)S(1)} %sum.2.refs_0_), channel_id=1, source_target_pairs={{0,3},{1,2},{2,1},{3,0},{4,7},{5,6},{6,5},{7,4},{8,11},{9,10},{10,... | collective-permute-start | bytes 24584 | tf_op jit(solution)/shard_map/ppermute | solution.py:808
  36.7 4.2 %collective-permute-start.15 = (f32[16,128]{1,0:T(8,128)S(1)}, f32[16,128]{1,0:T(8,128)S(1)}, u32[]{:S(2)}, u32[]{:S(2)}) collective-permute-start(f32[16,128]{1,0:T(8,128)S(1)} %sum.2.refs_0_), channel_id=1, source_target_pairs={{0,2},{1,3},{2,0},{3,1},{4,6},{5,7},{6,4},{7,5},{8,10},{9,11},{10,... | collective-permute-start | bytes 24584 | tf_op jit(solution)/shard_map/ppermute | solution.py:808
  37.8 3.1 %collective-permute-start.14 = (f32[16,128]{1,0:T(8,128)S(1)}, f32[16,128]{1,0:T(8,128)S(1)}, u32[]{:S(2)}, u32[]{:S(2)}) collective-permute-start(f32[16,128]{1,0:T(8,128)S(1)} %sum.2.refs_0_), channel_id=1, source_target_pairs={{0,1},{1,0},{2,3},{3,2},{4,5},{5,4},{6,7},{7,6},{8,9},{9,8},{10,11... | collective-permute-start | bytes 24584 | tf_op jit(solution)/shard_map/ppermute | solution.py:808
